TPU v7x, 32 devices: a whole 2x2x4 slice. The times are simulated.
32 devices in a mesh: mem: 4 (over y, x), space: 8 (over z, core).
Axes of the slice: x: 2, y: 2, z: 4, core: 2. Of those that a mesh axis runs over, the one named last changes fastest.
Arguments:
- ensemble: bfloat16 [16, 16, 92160], P('mem', None, 'space'), may hold values from -100 to 100
- cotangent: bfloat16 [16, 16, 92160], P('mem', None, 'space'), may hold values from -6 to 6
- w_query: bfloat16 [16, 16], replicated, may hold values from -2 to 2
- w_key: bfloat16 [16, 16], replicated, may hold values from -2 to 2
- w_value: bfloat16 [16, 16], replicated, may hold values from -1.5 to 1.5
- w_out: bfloat16 [16, 16], replicated, may hold values from -1.5 to 1.5
Outputs:
- updated: float32 [16, 16, 92160], P('mem', None, 'space')
- ensemble_grad: float32 [16, 16, 92160], P('mem', None, 'space')
All inputs are finite; a program needn't handle non-finite values.
Results may differ from a plain program's by a relative error of at most 0.0044.
Values may be sent and summed in bfloat16 or wider, within the bound.
No kernel may reach another device: no remote copies, remote signals or barrier semaphores. Data moves between devices by JAX's collectives and lax.ppermute only.
A program may use at most 128 MiB of HBM per device.

v0:
```python
import math

import jax
import jax.numpy as jnp
from jax import lax
from jax.sharding import PartitionSpec as P


def project(weight, field):
    return jnp.einsum("cd,mdp->mcp", weight, field, preferred_element_type=jnp.float32)


def project_back(weight, field):
    return jnp.einsum("cd,mcp->mdp", weight, field, preferred_element_type=jnp.float32)


def flatten(field):
    return field.reshape(field.shape[0], field.shape[1] * field.shape[2])


def pair_sum(left, right):
    return lax.dot_general(
        flatten(left), flatten(right), (((1,), (1,)), ((), ())), preferred_element_type=jnp.float32
    )


def normalize(scores):
    row_peak = jnp.max(scores, axis=1, keepdims=True)
    exponent = jnp.exp(scores - row_peak)
    return exponent / jnp.sum(exponent, axis=1, keepdims=True)


def combine(weights_half, field):
    mixed = jnp.dot(weights_half, flatten(field), preferred_element_type=jnp.float32)
    return mixed.astype(jnp.bfloat16).reshape(field.shape)


def shards(ensemble, cotangent, w_query, w_key, w_value, w_out):
    mem_count = lax.axis_size("mem")
    space_count = lax.axis_size("space")
    fields, grad_fields = (
        lax.all_to_all(ensemble, "mem", split_axis=2, concat_axis=0, tiled=True),
        lax.all_to_all(cotangent, "mem", split_axis=2, concat_axis=0, tiled=True),
    )
    members, channels, cell_count = fields.shape
    score_scale = 1.0 / (cell_count * mem_count * space_count * math.sqrt(channels))
    queries = project(w_query, fields).astype(jnp.bfloat16)
    key_field = project(w_key, fields).astype(jnp.bfloat16)
    value_field = project(w_value, fields).astype(jnp.bfloat16)
    partial_scores = pair_sum(queries, key_field)
    total_scores = lax.psum(partial_scores, ("mem", "space"))
    weights = normalize(score_scale * total_scores)
    weights_half = weights.astype(jnp.bfloat16)
    mixed = combine(weights_half, value_field)
    branch = project(w_out, mixed).astype(jnp.bfloat16)
    grad_mixed = project_back(w_out, grad_fields).astype(jnp.bfloat16)
    partial_pairs = pair_sum(grad_mixed, value_field)
    total_pairs = lax.psum(partial_pairs, ("mem", "space"))
    grad_scores = weights * (total_pairs - jnp.sum(weights * total_pairs, axis=1, keepdims=True))
    grad_scaled = (score_scale * grad_scores).astype(jnp.bfloat16)
    grad_queries = combine(grad_scaled, key_field)
    grad_keys = combine(grad_scaled.T, queries)
    grad_values = combine(weights_half.T, grad_mixed)
    grad_branch = (
        project_back(w_query, grad_queries)
        + project_back(w_key, grad_keys)
        + project_back(w_value, grad_values)
    ).astype(jnp.bfloat16)
    branch_home, grad_home = (
        lax.all_to_all(branch, "mem", split_axis=0, concat_axis=2, tiled=True),
        lax.all_to_all(grad_branch, "mem", split_axis=0, concat_axis=2, tiled=True),
    )
    updated = ensemble.astype(jnp.float32) + branch_home.astype(jnp.float32)
    ensemble_grad = cotangent.astype(jnp.float32) + grad_home.astype(jnp.float32)
    return (updated, ensemble_grad)


def solution(mesh):
    placed = (P("mem", None, "space"), P("mem", None, "space"), P(), P(), P(), P())
    return jax.shard_map(
        shards,
        mesh=mesh,
        in_specs=placed,
        out_specs=(P("mem", None, "space"), P("mem", None, "space")),
        check_vma=False,
    )
```

profile of v0, /device:TPU:0, one launch (start us, length us, event | category | flops | bytes accessed | tf_op | source)
XLA Modules:
  0.0 252.4 jit_solution(17271797960007357516)
XLA Ops:
  0.6 13.9 %copy.20 = bf16[4,16,11520]{1,0,2:T(4,128)(2,1)} copy(bf16[4,16,11520]{2,1,0:T(8,128)(2,1)} %param.6) | data formatting | bytes 2949120 | tf_op args[0]
  14.5 14.7 %reshape.65 = bf16[4,2,92160]{2,1,0:T(2,128)(2,1)} reshape(bf16[11520,4,16]{2,1,0:T(4,128)(2,1)} %bitcast.74) | data formatting | bytes 2949120
  29.3 5.3 %all-to-all-start = ((bf16[4,2,92160]{2,1,0:T(2,128)(2,1)}), bf16[4,2,92160]{2,1,0:T(2,128)(2,1)S(1)}, u32[]{:S(2)}, u32[]{:S(2)}) async-start(bf16[4,2,92160]{2,1,0:T(2,128)(2,1)} %reshape.65), calls=%async_computation | async-start | bytes 2949120 | tf_op jit(solution)/shard_map/all_to_all | solution.py:42
  34.6 10.9 %copy.25 = bf16[4,16,11520]{1,0,2:T(4,128)(2,1)} copy(bf16[4,16,11520]{2,1,0:T(8,128)(2,1)S(1)} %copy-done.4) | data formatting | bytes 2949120 | tf_op args[1]
  45.4 14.8 %reshape.67 = bf16[4,2,92160]{2,1,0:T(2,128)(2,1)} reshape(bf16[11520,4,16]{2,1,0:T(4,128)(2,1)} %bitcast.75) | data formatting | bytes 2949120
  60.2 4.5 %all-to-all-start.2 = ((bf16[4,2,92160]{2,1,0:T(2,128)(2,1)}), bf16[4,2,92160]{2,1,0:T(2,128)(2,1)}, u32[]{:S(2)}, u32[]{:S(2)}) async-start(bf16[4,2,92160]{2,1,0:T(2,128)(2,1)} %reshape.67), calls=%async_computation.2 | async-start | bytes 2949120 | tf_op jit(solution)/shard_map/all_to_all | solution.py:43
  64.7 9.6 %reshape.66 = bf16[11520,4,16]{2,1,0:T(4,128)(2,1)} reshape(bf16[4,2,92160]{2,1,0:T(2,128)(2,1)S(1)} %all-to-all-done) | data formatting | bytes 2949120
  74.3 14.4 %copy.21 = bf16[4,16,4,2880]{3,1,0,2:T(8,128)(2,1)S(1)} copy(bf16[4,16,4,2880]{1,0,3,2:T(4,128)(2,1)} %bitcast.72) | data formatting | bytes 2949120 | tf_op jit(solution)/shard_map/all_to_all | solution.py:42
  89.3 2.5 %reshape.45 = bf16[16,46080]{1,0:T(8,128)(2,1)} reshape(bf16[16,16,2880]{2,1,0:T(8,128)(2,1)S(1)} %fusion.3) | data formatting | bytes 2949120 | tf_op jit(solution)/shard_map/reshape | solution.py:18
  93.5 3.5 %reshape.47 = bf16[16,46080]{1,0:T(8,128)(2,1)} reshape(bf16[16,16,2880]{2,1,0:T(8,128)(2,1)} %fusion.2) | data formatting | bytes 2949120 | tf_op jit(solution)/shard_map/reshape | solution.py:18
  97.0 2.3 fusion.13
  99.8 10.9 %reshape.68 = bf16[11520,4,16]{2,1,0:T(4,128)(2,1)} reshape(bf16[4,2,92160]{2,1,0:T(2,128)(2,1)} %all-to-all-done.2) | data formatting | bytes 2949120
  110.7 15.4 %copy.26 = bf16[4,16,4,2880]{3,1,0,2:T(8,128)(2,1)} copy(bf16[4,16,4,2880]{1,0,3,2:T(4,128)(2,1)} %bitcast.73) | data formatting | bytes 2949120 | tf_op jit(solution)/shard_map/all_to_all | solution.py:43
  128.1 2.5 %reshape.49 = bf16[16,46080]{1,0:T(8,128)(2,1)} reshape(bf16[16,16,2880]{2,1,0:T(8,128)(2,1)S(1)} %fusion.1) | data formatting | bytes 2949120 | tf_op jit(solution)/shard_map/reshape | solution.py:18
  131.5 41.3 %all-reduce = (f32[16,16]{1,0:T(8,128)S(1)}, f32[16,16]{1,0:T(8,128)S(1)}) all-reduce(f32[16,16]{1,0:T(8,128)S(1)} %fusion.13, f32[16,16]{1,0:T(8,128)S(1)} %fusion.18), channel_id=1, replica_groups=mesh['mem'=4,'space'=8] {'mem','space'}, use_global_device_ids=true, to_apply=%region_0.0 | all-reduce | flops 512 | bytes 4096 | tf_op jit(solution)/shard_map/psum | solution.py:51
  173.3 2.0 convolution_convert_fusion.2
  175.3 2.2 reshape.46
  177.5 2.1 fusion.31
  181.3 3.3 %reshape.48 = bf16[16,16,2880]{2,1,0:T(8,128)(2,1)} reshape(bf16[16,46080]{1,0:T(8,128)(2,1)} %convolution_convert_fusion.1) | data formatting | bytes 2949120 | tf_op jit(solution)/shard_map/reshape | solution.py:35
  184.7 3.2 %convolution_convert_fusion = bf16[16,46080]{1,0:T(8,128)(2,1)} fusion(bf16[16,46080]{1,0:T(8,128)(2,1)} %reshape.49, f32[16,16]{1,0:T(8,128)S(1)} %get-tuple-element.2, f32[16]{0:T(128)S(1)} %fusion.24, f32[16]{0:T(128)S(1)} %multiply_reduce_fusion.1), kind=kOutput, calls=%fused_computation | convolution fusion | flops 24331264 | bytes 2950272 | tf_op jit(solution)/shard_map/dot_general | solution.py:34
  187.8 3.3 %reshape.50 = bf16[16,16,2880]{2,1,0:T(8,128)(2,1)} reshape(bf16[16,46080]{1,0:T(8,128)(2,1)} %convolution_convert_fusion) | data formatting | bytes 2949120 | tf_op jit(solution)/shard_map/reshape | solution.py:35
  191.2 2.1 convolution_add_fusion.1
  195.0 3.8 %all-to-all-start.3 = ((bf16[16,16,2880]{2,1,0:T(8,128)(2,1)}), bf16[16,16,2880]{2,1,0:T(8,128)(2,1)S(1)}, u32[]{:S(2)}, u32[]{:S(2)}) async-start(bf16[16,16,2880]{2,1,0:T(8,128)(2,1)} %fusion.6), calls=%async_computation.3 | async-start | bytes 3014656 | tf_op jit(solution)/shard_map/all_to_all | solution.py:71
  198.8 2.5 reshape.43
  201.3 3.1 %convolution_convert_fusion.3 = bf16[16,46080]{1,0:T(8,128)(2,1)} fusion(bf16[16,46080]{1,0:T(8,128)(2,1)} %reshape.43, f32[16,16]{1,0:T(8,128)S(1)} %get-tuple-element.2, f32[16]{0:T(128)S(1)} %fusion.24, f32[16]{0:T(128)S(1)} %multiply_reduce_fusion.1), kind=kOutput, calls=%fused_computation.3 | convolution fusion | flops 24331264 | bytes 2950272 | tf_op jit(solution)/shard_map/dot_general | solution.py:34
  204.4 2.5 reshape.44
  208.5 8.2 %all-to-all-done.3 = bf16[16,16,2880]{2,1,0:T(8,128)(2,1)S(1)} async-done(((bf16[16,16,2880]{2,1,0:T(8,128)(2,1)}), bf16[16,16,2880]{2,1,0:T(8,128)(2,1)S(1)}, u32[]{:S(2)}, u32[]{:S(2)}) %all-to-all-start.3) | async-done | bytes 1474592 | tf_op jit(solution)/shard_map/all_to_all | solution.py:71
  216.7 4.6 %all-to-all-start.1 = ((bf16[16,16,2880]{2,1,0:T(8,128)(2,1)}), bf16[16,16,2880]{2,1,0:T(8,128)(2,1)}, u32[]{:S(2)}, u32[]{:S(2)}) async-start(bf16[16,16,2880]{2,1,0:T(8,128)(2,1)} %fusion.5), calls=%async_computation.1 | async-start | bytes 3014656 | tf_op jit(solution)/shard_map/all_to_all | solution.py:70
  223.6 3.0 %reshape.52 = f32[4,16,11520]{2,1,0:T(8,128)} reshape(f32[4,16,4,2880]{3,2,1,0:T(4,128)S(1)} %copy.33) | data formatting | bytes 5898240 | tf_op jit(solution)/shard_map/convert_element_type | solution.py:74
  226.5 12.6 %all-to-all-done.1 = bf16[16,16,2880]{2,1,0:T(8,128)(2,1)} async-done(((bf16[16,16,2880]{2,1,0:T(8,128)(2,1)}), bf16[16,16,2880]{2,1,0:T(8,128)(2,1)}, u32[]{:S(2)}, u32[]{:S(2)}) %all-to-all-start.1) | async-done | bytes 1474592 | tf_op jit(solution)/shard_map/all_to_all | solution.py:70
  242.7 3.0 %reshape.51 = f32[4,16,11520]{2,1,0:T(8,128)} reshape(f32[4,16,4,2880]{3,2,1,0:T(4,128)S(1)} %copy.24) | data formatting | bytes 5898240 | tf_op jit(solution)/shard_map/convert_element_type | solution.py:73
  245.7 6.6 %convert_add_fusion = (f32[4,16,11520]{2,1,0:T(8,128)}, f32[4,16,11520]{2,1,0:T(8,128)}) fusion(f32[4,16,11520]{2,1,0:T(8,128)} %reshape.52, bf16[4,16,11520]{2,1,0:T(8,128)(2,1)} %param.7, f32[4,16,11520]{2,1,0:T(8,128)} %reshape.51, bf16[4,16,11520]{2,1,0:T(8,128)(2,1)} %param.6), kind=kLoop, calls=%fused_computation.20 | loop fusion | flops 2949120 | bytes 14745600 | tf_op jit(solution)/shard_map/add | solution.py:74
  (35 shorter events, 17.0 us)
Async XLA Ops:
  0.6 91.2 %copy-start = (bf16[16,16]{1,0:T(8,128)(2,1)S(1)}, bf16[16,16]{1,0:T(8,128)(2,1)}, u32[]{:S(2)}) copy-start(bf16[16,16]{1,0:T(8,128)(2,1)} %param.8) | copy-start | bytes 1540
  29.3 5.3 %copy-start.4 = (bf16[4,16,11520]{2,1,0:T(8,128)(2,1)S(1)}, bf16[4,16,11520]{2,1,0:T(8,128)(2,1)}, u32[]{:S(2)}) copy-start(bf16[4,16,11520]{2,1,0:T(8,128)(2,1)} %param.7) | copy-start | bytes 4423684
  29.3 30.9 %all-to-all-start = ((bf16[4,2,92160]{2,1,0:T(2,128)(2,1)}), bf16[4,2,92160]{2,1,0:T(2,128)(2,1)S(1)}, u32[]{:S(2)}, u32[]{:S(2)}) async-start(bf16[4,2,92160]{2,1,0:T(2,128)(2,1)} %reshape.65), calls=%async_computation | async-start | bytes 2949120 | tf_op jit(solution)/shard_map/all_to_all | solution.py:42
  60.2 39.6 %all-to-all-start.2 = ((bf16[4,2,92160]{2,1,0:T(2,128)(2,1)}), bf16[4,2,92160]{2,1,0:T(2,128)(2,1)}, u32[]{:S(2)}, u32[]{:S(2)}) async-start(bf16[4,2,92160]{2,1,0:T(2,128)(2,1)} %reshape.67), calls=%async_computation.2 | async-start | bytes 2949120 | tf_op jit(solution)/shard_map/all_to_all | solution.py:43
  74.3 14.5 %copy-start.6 = (bf16[16,16]{1,0:T(8,128)(2,1)S(1)}, bf16[16,16]{1,0:T(8,128)(2,1)}, u32[]{:S(2)}) copy-start(bf16[16,16]{1,0:T(8,128)(2,1)} %param.9) | copy-start | bytes 1540
  97.0 2.3 copy-start.7
  99.8 30.8 %copy-start.1 = (bf16[16,16,2880]{2,1,0:T(8,128)(2,1)}, bf16[16,16,2880]{2,1,0:T(8,128)(2,1)S(1)}, u32[]{:S(2)}) copy-start(bf16[16,16,2880]{2,1,0:T(8,128)(2,1)S(1)} %fusion.4) | copy-start | bytes 4423684
  110.7 15.4 %copy-start.8 = (bf16[16,16]{1,0:T(8,128)(2,1)S(1)}, bf16[16,16]{1,0:T(8,128)(2,1)}, u32[]{:S(2)}) copy-start(bf16[16,16]{1,0:T(8,128)(2,1)} %param.11) | copy-start | bytes 1540
  177.5 2.1 copy-start.5
  191.2 2.1 copy-start.3
  195.0 3.8 %copy-start.2 = (bf16[16,16,2880]{2,1,0:T(8,128)(2,1)S(1)}, bf16[16,16,2880]{2,1,0:T(8,128)(2,1)}, u32[]{:S(2)}) copy-start(bf16[16,16,2880]{2,1,0:T(8,128)(2,1)} %copy-done.1) | copy-start | bytes 4423684
  195.0 21.7 %all-to-all-start.3 = ((bf16[16,16,2880]{2,1,0:T(8,128)(2,1)}), bf16[16,16,2880]{2,1,0:T(8,128)(2,1)S(1)}, u32[]{:S(2)}, u32[]{:S(2)}) async-start(bf16[16,16,2880]{2,1,0:T(8,128)(2,1)} %fusion.6), calls=%async_computation.3 | async-start | bytes 3014656 | tf_op jit(solution)/shard_map/all_to_all | solution.py:71
  216.7 22.4 %all-to-all-start.1 = ((bf16[16,16,2880]{2,1,0:T(8,128)(2,1)}), bf16[16,16,2880]{2,1,0:T(8,128)(2,1)}, u32[]{:S(2)}, u32[]{:S(2)}) async-start(bf16[16,16,2880]{2,1,0:T(8,128)(2,1)} %fusion.5), calls=%async_computation.1 | async-start | bytes 3014656 | tf_op jit(solution)/shard_map/all_to_all | solution.py:70
where the time goes:
time: 255 us; the launch traced here: 252 us
  local copies, waits for them, and re-layouts  137 us (54%)
  blocking collectives  41.3 us (16%)
  matrix products  25.4 us (10%)
  waiting for transfers between devices  20.8 us (8%)
  starting transfers between devices  18.2 us (7%)
  other arithmetic  9.04 us (4%)
    unnamed x24, local copies, waits for them, and re-layouts  74.8 us
    psum x1, blocking collectives, shards(): total_scores = lax.psum(partial_scores, ('mem', 'space'))  41.3 us
    all_to_all x1, local copies, waits for them, and re-layouts, shards(): lax.all_to_all(cotangent, 'mem', split_axis=2, concat_axis=0, tiled=True)  15.4 us
    all_to_all x1, local copies, waits for them, and re-layouts, shards(): lax.all_to_all(ensemble, 'mem', split_axis=2, concat_axis=0, tiled=True)  14.4 us
    all_to_all x1, waiting for transfers between devices, shards(): lax.all_to_all(branch, 'mem', split_axis=0, concat_axis=2, tiled=True)  12.6 us
    reshape x4, local copies, waits for them, and re-layouts, combine(): return mixed.astype(jnp.bfloat16).reshape(field.shape)  11.3 us
    reshape x4, local copies, waits for them, and re-layouts, flatten(): return field.reshape(field.shape[0], field.shape[1] * field.shape[2])  11.1 us
    dot_general x4, matrix products, combine(): jnp.dot(weights_half, flatten(field), preferred_element_type=jnp.float32)  10 us
  transfers between devices with their start and end apart: 4, of which 2 were waited for; matrix products, arithmetic and copies ran while one was open for 30% of the time, Pallas kernels for 0%

commit v1 on v0

v1 whole, which is shorter than its diff:
```python
import functools
import math

import jax
import jax.numpy as jnp
from jax import lax
from jax.experimental import pallas as pl
from jax.experimental.pallas import tpu as pltpu
from jax.sharding import PartitionSpec as P

LANES = 128
HIGH = lax.Precision.HIGHEST
VMEM = pltpu.MemorySpace.VMEM


def mm(a, b, dims, precision=None):
    return lax.dot_general(
        a, b, (dims, ((), ())), precision=precision, preferred_element_type=jnp.float32
    )


def chunk_start(index, chunk, length):
    return pl.multiple_of(jnp.minimum(index * chunk, length - chunk), LANES)


def partner(me, step):
    return me ^ step


def lane_tiles(width, step=512):
    return [(at, min(step, width - at)) for at in range(0, width, step)]


def member_of_row(me, rows, channels, members, group):
    row = lax.broadcasted_iota(jnp.int32, (rows, members), 0)
    col = lax.broadcasted_iota(jnp.int32, (rows, members), 1)
    per_group = group * channels
    owner = (row // per_group) ^ me
    member = owner * group + (row % per_group) // channels
    return (member == col).astype(jnp.float32)


def split_kernel(me_of, count, chunk, length, x_ref, *rest):
    outs, sem = rest[:count], rest[count]
    me = me_of()
    copies = [
        pltpu.make_async_copy(
            x_ref.at[:, pl.ds(chunk_start(partner(me, s), chunk, length), chunk)],
            outs[s],
            sem.at[s],
        )
        for s in range(count)
    ]
    for copy in copies:
        copy.start()
    for copy in copies:
        copy.wait()


def tiled(small, rows, channels):
    tall = jnp.concatenate([small] * (rows // channels), axis=0)
    col = lax.broadcasted_iota(jnp.int32, (channels, rows), 1)
    row = lax.broadcasted_iota(jnp.int32, (channels, rows), 0)
    spread = (col % channels == row).astype(jnp.float32)
    return mm(tall, spread, ((1,), (0,)), HIGH)


def split_weights_kernel(
    me_of, count, chunk, length, rows, channels,
    x_ref, dep_ref, wq_ref, wk_ref, wv_ref, wo_ref, *rest,
):
    outs = rest[:count]
    qk_ref, qkt_ref, ov_ref, ovt_ref, sem = rest[count:]
    me = me_of()
    copies = [
        pltpu.make_async_copy(
            x_ref.at[:, pl.ds(chunk_start(partner(me, s), chunk, length), chunk)],
            outs[s],
            sem.at[s],
        )
        for s in range(count)
    ]
    for copy in copies:
        copy.start()
    wq, wk = wq_ref[...].astype(jnp.float32), wk_ref[...].astype(jnp.float32)
    wv, wo = wv_ref[...].astype(jnp.float32), wo_ref[...].astype(jnp.float32)
    wqt, wkt, wvt, wot = wq.T, wk.T, wv.T, wo.T
    qk_ref[...] = tiled(mm(wqt, wk, ((1,), (0,)), HIGH), rows, channels)
    qkt_ref[...] = tiled(mm(wkt, wq, ((1,), (0,)), HIGH), rows, channels)
    ov_ref[...] = tiled(mm(wo, wv, ((1,), (0,)), HIGH), rows, channels)
    ovt_ref[...] = tiled(mm(wvt, wot, ((1,), (0,)), HIGH), rows, channels)
    for copy in copies:
        copy.wait()


def gather_tile(refs, at, width):
    return jnp.concatenate([r[:, at:at + width] for r in refs], axis=0)


def fold(weighted, picks):
    half = mm(weighted, picks, ((1,), (0,)), HIGH)
    return mm(picks, half, ((0,), (0,)), HIGH)


def gram_kernel(me_of, count, chunk, length, group, channels, members, same, *refs):
    me = me_of()
    left = refs[:count]
    right = left if same else refs[count:2 * count]
    tile_ref, out_ref = refs[-2], refs[-1]
    rows = count * left[0].shape[0]
    skip = me * chunk - chunk_start(me, chunk, length)
    total = jnp.zeros((rows, rows), jnp.float32)
    for at, width in lane_tiles(chunk):
        b = gather_tile(right, at, width)
        a = b if same else gather_tile(left, at, width)
        lane = lax.broadcasted_iota(jnp.int32, (rows, width), 1) + at
        a = jnp.where(lane >= skip, a.astype(jnp.float32), 0.0).astype(jnp.bfloat16)
        total = total + mm(a, b, ((1,), (1,)))
    picks = member_of_row(me, rows, channels, members, group)
    out_ref[...] = fold(total * tile_ref[...], picks)


def softmax(scores):
    peak = jnp.max(scores, axis=1, keepdims=True)
    exponent = jnp.exp(scores - peak)
    return exponent / jnp.sum(exponent, axis=1, keepdims=True)


def spread(small, picks):
    tall = mm(picks, small.astype(jnp.bfloat16), ((1,), (0,))).astype(jnp.bfloat16)
    return mm(tall, picks, ((1,), (1,)))


def spread_t(small, picks):
    tall = mm(picks, small.astype(jnp.bfloat16), ((1,), (1,))).astype(jnp.bfloat16)
    return mm(tall, picks, ((1,), (1,)))


def two_parts(value):
    high = value.astype(jnp.bfloat16)
    return high, (value - high.astype(jnp.float32)).astype(jnp.bfloat16)


def branch_kernel(me_of, count, chunk, group, channels, members, scale, s_ref, ov_ref, *refs):
    me = me_of()
    fields, outs = refs[:count], refs[count:]
    per = fields[0].shape[0]
    rows = count * per
    picks = member_of_row(me, rows, channels, members, group).astype(jnp.bfloat16)
    weights = softmax(s_ref[...] * scale)
    high, low = two_parts(spread(weights, picks) * ov_ref[...])
    for at, width in lane_tiles(chunk):
        e = gather_tile(fields, at, width)
        b = (mm(high, e, ((1,), (0,))) + mm(low, e, ((1,), (0,)))).astype(jnp.bfloat16)
        for s in range(count):
            outs[s][:, at:at + width] = b[s * per:(s + 1) * per]


def grad_kernel(
    me_of, count, chunk, group, channels, members, scale,
    s_ref, p_ref, qk_ref, qkt_ref, ovt_ref, *refs,
):
    me = me_of()
    fields, grads, outs = refs[:count], refs[count:2 * count], refs[2 * count:]
    per = fields[0].shape[0]
    rows = count * per
    picks = member_of_row(me, rows, channels, members, group).astype(jnp.bfloat16)
    weights = softmax(s_ref[...] * scale)
    pairs = p_ref[...]
    slope = weights * (pairs - jnp.sum(weights * pairs, axis=1, keepdims=True)) * scale
    d_high, d_low = two_parts(
        spread(slope, picks) * qk_ref[...] + spread_t(slope, picks) * qkt_ref[...]
    )
    a_high, a_low = two_parts(spread_t(weights, picks) * ovt_ref[...])
    for at, width in lane_tiles(chunk):
        e = gather_tile(fields, at, width)
        c = gather_tile(grads, at, width)
        b = (
            mm(d_high, e, ((1,), (0,))) + mm(d_low, e, ((1,), (0,)))
            + mm(a_high, c, ((1,), (0,))) + mm(a_low, c, ((1,), (0,)))
        ).astype(jnp.bfloat16)
        for s in range(count):
            outs[s][:, at:at + width] = b[s * per:(s + 1) * per]


def finish_kernel(me_of, count, chunk, length, *refs):
    me = me_of()
    base, extra, out_ref = refs[:count], refs[count:2 * count], refs[-1]
    for s in range(count):
        start = chunk_start(partner(me, s), chunk, length)
        out_ref[:, pl.ds(start, chunk)] = base[s][...].astype(jnp.float32) + extra[
            s
        ][...].astype(jnp.float32)


def exchange(parts):
    count = len(parts)
    return [parts[0]] + [
        lax.ppermute(parts[s], "mem", [(i, i ^ s) for i in range(count)])
        for s in range(1, count)
    ]


def sum_over(value, name):
    size = lax.axis_size(name)
    step = 1
    while step < size:
        value = value + lax.ppermute(value, name, [(i, i ^ step) for i in range(size)])
        step *= 2
    return value


def shards(ensemble, cotangent, w_query, w_key, w_value, w_out):
    count = lax.axis_size("mem")
    group, channels, length = ensemble.shape
    members = group * count
    per = group * channels
    rows = per * count
    chunk = -(-length // (LANES * count)) * LANES
    scale = 1.0 / (length * lax.axis_size("space") * math.sqrt(channels))
    me_of = lambda: lax.axis_index("mem")
    bf, f32 = jnp.bfloat16, jnp.float32
    whole = pl.BlockSpec(memory_space=VMEM)
    anywhere = pl.BlockSpec(memory_space=pl.ANY)
    params = pltpu.CompilerParams(vmem_limit_bytes=40 * 1024 * 1024)
    part = jax.ShapeDtypeStruct((per, chunk), bf)
    square = jax.ShapeDtypeStruct((rows, rows), f32)
    pair = jax.ShapeDtypeStruct((members, members), f32)
    fields = ensemble.reshape(per, length)
    grads = cotangent.reshape(per, length)

    def cost(flops, moved):
        return pl.CostEstimate(flops=flops, bytes_accessed=moved, transcendentals=0)

    e_mine = pl.pallas_call(
        functools.partial(split_kernel, me_of, count, chunk, length),
        out_shape=[part] * count,
        in_specs=[anywhere],
        out_specs=[anywhere] * count,
        scratch_shapes=[pltpu.SemaphoreType.DMA((count,))],
        compiler_params=params,
        name="split_fields",
    )(fields)
    outcome = pl.pallas_call(
        functools.partial(split_weights_kernel, me_of, count, chunk, length, rows, channels),
        out_shape=[part] * count + [square] * 4,
        in_specs=[anywhere, anywhere] + [whole] * 4,
        out_specs=[anywhere] * count + [whole] * 4,
        scratch_shapes=[pltpu.SemaphoreType.DMA((count,))],
        compiler_params=params,
        name="split_grads",
    )(grads, e_mine[0], w_query, w_key, w_value, w_out)
    c_mine, (qk, qkt, ov, ovt) = outcome[:count], outcome[count:]

    e_cells = exchange(e_mine)
    c_cells = exchange(c_mine)

    def gram(left, right, tile, name):
        same = left is right
        operands = list(left) if same else list(left) + list(right)
        return pl.pallas_call(
            functools.partial(
                gram_kernel, me_of, count, chunk, length, group, channels, members, same
            ),
            out_shape=pair,
            in_specs=[whole] * (len(operands) + 1),
            out_specs=whole,
            compiler_params=params,
            cost_estimate=cost(2 * rows * rows * chunk, 2 * len(operands) * per * chunk),
            name=name,
        )(*operands, tile)

    scores = gram(e_cells, e_cells, qk, "score_sums")
    scores = sum_over(sum_over(scores, "space"), "mem")
    branch = pl.pallas_call(
        functools.partial(branch_kernel, me_of, count, chunk, group, channels, members, scale),
        out_shape=[part] * count,
        in_specs=[whole] * (count + 2),
        out_specs=[whole] * count,
        compiler_params=params,
        cost_estimate=cost(4 * rows * rows * chunk, 4 * rows * chunk),
        name="branch",
    )(scores, ov, *e_cells)
    branch_home = exchange(branch)

    pairs = gram(c_cells, e_cells, ov, "pair_sums")
    pairs = sum_over(sum_over(pairs, "mem"), "space")
    grad = pl.pallas_call(
        functools.partial(grad_kernel, me_of, count, chunk, group, channels, members, scale),
        out_shape=[part] * count,
        in_specs=[whole] * (2 * count + 5),
        out_specs=[whole] * count,
        compiler_params=params,
        cost_estimate=cost(8 * rows * rows * chunk, 6 * rows * chunk),
        name="input_gradient",
    )(scores, pairs, qk, qkt, ovt, *e_cells, *c_cells)
    grad_home = exchange(grad)

    def finish(base, extra, name):
        return pl.pallas_call(
            functools.partial(finish_kernel, me_of, count, chunk, length),
            out_shape=jax.ShapeDtypeStruct((per, length), f32),
            in_specs=[whole] * (2 * count),
            out_specs=whole,
            compiler_params=params,
            cost_estimate=cost(per * length, 8 * per * length),
            name=name,
        )(*base, *extra).reshape(group, channels, length)

    updated = finish(e_mine, branch_home, "updated")
    ensemble_grad = finish(c_mine, grad_home, "ensemble_grad")
    return (updated, ensemble_grad)


def solution(mesh):
    split = P("mem", None, "space")
    return jax.shard_map(
        shards,
        mesh=mesh,
        in_specs=(split, split, P(), P(), P(), P()),
        out_specs=(split, split),
        check_vma=False,
    )
```

time: 255 us -> 104 us (0.41); the launches traced: 252 us -> 104 us
  local copies, waits for them, and re-layouts: 137 us -> 5.48 us
  blocking collectives: 41.3 us -> 0 us
  waiting for transfers between devices: 20.8 us -> 56.7 us
  matrix products: 25.4 us -> 0 us
  Pallas kernels: 0 us -> 12.2 us
  starting transfers between devices: 18.2 us -> 29 us
  other arithmetic: 9.04 us -> 0.03 us
    unnamed x24 -> x12, local copies, waits for them, and re-layouts: 74.8 us -> 5.48 us
    ppermute x0 -> x22, waiting for transfers between devices: none -> 56.7 us  [the longest x12 48.9 us: exchange(): lax.ppermute(parts[s], 'mem', [(i, i ^ s) for i in range(count)])]
    psum x1 -> x0, blocking collectives: 41.3 us -> none  [shards(): total_scores = lax.psum(partial_scores, ('mem', 'space'))]
    all_to_all x2 -> x0, local copies, waits for them, and re-layouts: 29.8 us -> none  [the longest x1 15.4 us: shards(): lax.all_to_all(cotangent, 'mem', split_axis=2, concat_axis=0, tiled=True)]
    ppermute x0 -> x22, starting transfers between devices: none -> 29 us  [the longest x12 17.6 us: exchange(): lax.ppermute(parts[s], 'mem', [(i, i ^ s) for i in range(count)])]
    dot_general x14 -> x0, matrix products: 25.4 us -> none  [the longest x4 10 us: combine(): jnp.dot(weights_half, flatten(field), preferred_element_type=jnp.float32)]
    reshape x8 -> x0, local copies, waits for them, and re-layouts: 22.4 us -> none  [the longest x4 11.3 us: combine(): return mixed.astype(jnp.bfloat16).reshape(field.shape)]
    all_to_all x4 -> x0, waiting for transfers between devices: 20.8 us -> none  [the longest x1 12.6 us: shards(): lax.all_to_all(branch, 'mem', split_axis=0, concat_axis=2, tiled=True)]
  transfers between devices with their start and end apart: 4 -> 22, of which waited for: 2 -> 16; matrix products, arithmetic and copies ran while one was open for 30% -> 0% of each run, Pallas kernels for 0% -> 5%
where the time goes in v1:
time: 104 us
  waiting for transfers between devices  56.7 us (55%)
  starting transfers between devices  29 us (28%)
  Pallas kernels  12.2 us (12%)
  local copies, waits for them, and re-layouts  5.48 us (5%)
    ppermute x12, waiting for transfers between devices, exchange(): lax.ppermute(parts[s], 'mem', [(i, i ^ s) for i in range(count)])  48.9 us
    ppermute x12, starting transfers between devices, exchange(): lax.ppermute(parts[s], 'mem', [(i, i ^ s) for i in range(count)])  17.6 us
    ppermute x10, starting transfers between devices, sum_over(): lax.ppermute(value, name, [(i, i ^ step) for i in range(size)])  11.4 us
    ppermute x10, waiting for transfers between devices, sum_over(): lax.ppermute(value, name, [(i, i ^ step) for i in range(size)])  7.84 us
    unnamed x12, local copies, waits for them, and re-layouts  5.48 us
    pallas_call x2, Pallas kernels, finish(): pl.pallas_call(functools.partial(finish_kernel, me_of, count, chunk, leng...  3.8 us
    pallas_call x2, Pallas kernels, gram(): pl.pallas_call(functools.partial(gram_kernel, me_of, count, chunk, length...  2.93 us
    pallas_call x1, Pallas kernels, shards(): pl.pallas_call(functools.partial(grad_kernel, me_of, count, chunk, group,...  2.43 us
  transfers between devices with their start and end apart: 22, of which 16 were waited for; matrix products, arithmetic and copies ran while one was open for 0% of the time, Pallas kernels for 5%

profile of v1, /device:TPU:0, one launch (start us, length us, event | category | flops | bytes accessed | tf_op | source)
XLA Modules:
  0.0 104.1 jit_solution(5880646757130660446)
XLA Ops:
  0.6 1.4 %copy-done.1 = bf16[4,16,11520]{2,1,0:T(8,128)(2,1)S(1)} copy-done((bf16[4,16,11520]{2,1,0:T(8,128)(2,1)S(1)}, bf16[4,16,11520]{2,1,0:T(8,128)(2,1)}, u32[]{:S(2)}) %copy-start.1) | copy-done | bytes 1474584
  2.2 1.4 %copy-done = bf16[4,16,11520]{2,1,0:T(8,128)(2,1)S(1)} copy-done((bf16[4,16,11520]{2,1,0:T(8,128)(2,1)S(1)}, bf16[4,16,11520]{2,1,0:T(8,128)(2,1)}, u32[]{:S(2)}) %copy-start) | copy-done | bytes 1474584
  6.3 1.5 %split_grads.1 = (bf16[64,2944]{1,0:T(8,128)(2,1)S(1)}, bf16[64,2944]{1,0:T(8,128)(2,1)S(1)}, bf16[64,2944]{1,0:T(8,128)(2,1)S(1)}, bf16[64,2944]{1,0:T(8,128)(2...) custom-call(bf16[64,11520]{1,0:T(8,128)(2,1)S(1)} %bitcast.4, ...), custom_call_target="tpu_custom_call" | custom-call | tf_op jit(solution)/shard_map/split_grads/pallas_call | solution.py:244
  7.8 3.0 %collective-permute-start.11 = (bf16[64,2944]{1,0:T(8,128)(2,1)S(1)}, bf16[64,2944]{1,0:T(8,128)(2,1)S(1)}, u32[]{:S(2)}, u32[]{:S(2)}) collective-permute-start(bf16[64,2944]{1,0:T(8,128)(2,1)S(1)} %get-tuple-element.33.refs_1_), channel_id=1, source_target_pairs={{0,8},{8,0},{16,24},{24,16},{1,9},{9,1},{17,25},{25,17},{2,10},{10... | collective-permute-start | bytes 1130504 | tf_op jit(solution)/shard_map/ppermute | solution.py:199
  10.8 1.5 %collective-permute-start.12 = (bf16[64,2944]{1,0:T(8,128)(2,1)S(1)}, bf16[64,2944]{1,0:T(8,128)(2,1)S(1)}, u32[]{:S(2)}, u32[]{:S(2)}) collective-permute-start(bf16[64,2944]{1,0:T(8,128)(2,1)S(1)} %get-tuple-element.34.refs_2_), channel_id=1, source_target_pairs={{0,16},{8,24},{16,0},{24,8},{1,17},{9,25},{17,1},{25,9},{2,18},{10... | collective-permute-start | bytes 1130504 | tf_op jit(solution)/shard_map/ppermute | solution.py:199
  12.4 1.9 %collective-permute-start = (bf16[64,2944]{1,0:T(8,128)(2,1)S(1)}, bf16[64,2944]{1,0:T(8,128)(2,1)S(1)}, u32[]{:S(2)}, u32[]{:S(2)}) collective-permute-start(bf16[64,2944]{1,0:T(8,128)(2,1)S(1)} %get-tuple-element.23.refs_1_), channel_id=1, source_target_pairs={{0,8},{8,0},{16,24},{24,16},{1,9},{9,1},{17,25},{25,17},{2,10},{10... | collective-permute-start | bytes 1130504 | tf_op jit(solution)/shard_map/ppermute | solution.py:199
  14.3 1.5 %collective-permute-start.1 = (bf16[64,2944]{1,0:T(8,128)(2,1)S(1)}, bf16[64,2944]{1,0:T(8,128)(2,1)S(1)}, u32[]{:S(2)}, u32[]{:S(2)}) collective-permute-start(bf16[64,2944]{1,0:T(8,128)(2,1)S(1)} %get-tuple-element.24.refs_2_), channel_id=1, source_target_pairs={{0,16},{8,24},{16,0},{24,8},{1,17},{9,25},{17,1},{25,9},{2,18},{10... | collective-permute-start | bytes 1130504 | tf_op jit(solution)/shard_map/ppermute | solution.py:199
  15.8 4.6 %collective-permute-done.11.refs_1_.refs_5_ = bf16[64,2944]{1,0:T(8,128)(2,1)S(1)} collective-permute-done((bf16[64,2944]{1,0:T(8,128)(2,1)S(1)}, bf16[64,2944]{1,0:T(8,128)(2,1)S(1)}, u32[]{:S(2)}, u32[]{:S(2)}) %collective-permute-start.11) | collective-permute-done | bytes 376864 | tf_op jit(solution)/shard_map/ppermute | solution.py:199
  20.4 3.0 %collective-permute-start.2 = (bf16[64,2944]{1,0:T(8,128)(2,1)S(1)}, bf16[64,2944]{1,0:T(8,128)(2,1)S(1)}, u32[]{:S(2)}, u32[]{:S(2)}) collective-permute-start(bf16[64,2944]{1,0:T(8,128)(2,1)S(1)} %get-tuple-element.25.refs_3_), channel_id=1, source_target_pairs={{0,24},{8,16},{16,8},{24,0},{1,25},{9,17},{17,9},{25,1},{2,26},{10... | collective-permute-start | bytes 1130504 | tf_op jit(solution)/shard_map/ppermute | solution.py:199
  23.4 7.2 %collective-permute-done.12.refs_2_.refs_6_ = bf16[64,2944]{1,0:T(8,128)(2,1)S(1)} collective-permute-done((bf16[64,2944]{1,0:T(8,128)(2,1)S(1)}, bf16[64,2944]{1,0:T(8,128)(2,1)S(1)}, u32[]{:S(2)}, u32[]{:S(2)}) %collective-permute-start.12) | collective-permute-done | bytes 376864 | tf_op jit(solution)/shard_map/ppermute | solution.py:199
  30.6 6.0 %collective-permute-done.refs_1_.refs_5_ = bf16[64,2944]{1,0:T(8,128)(2,1)S(1)} collective-permute-done((bf16[64,2944]{1,0:T(8,128)(2,1)S(1)}, bf16[64,2944]{1,0:T(8,128)(2,1)S(1)}, u32[]{:S(2)}, u32[]{:S(2)}) %collective-permute-start) | collective-permute-done | bytes 376864 | tf_op jit(solution)/shard_map/ppermute | solution.py:199
  36.6 8.7 %collective-permute-done.1.refs_2_.refs_6_ = bf16[64,2944]{1,0:T(8,128)(2,1)S(1)} collective-permute-done((bf16[64,2944]{1,0:T(8,128)(2,1)S(1)}, bf16[64,2944]{1,0:T(8,128)(2,1)S(1)}, u32[]{:S(2)}, u32[]{:S(2)}) %collective-permute-start.1) | collective-permute-done | bytes 376864 | tf_op jit(solution)/shard_map/ppermute | solution.py:199
  45.3 1.5 %pair_sums.1 = f32[16,16]{1,0:T(8,128)S(1)} custom-call(bf16[64,2944]{1,0:T(8,128)(2,1)S(1)} %get-tuple-element.32.refs_0_.refs_4_, bf16[64,2944]{1,0:T(8,128)(2,1)S(1)} %collective-permute-done.11.refs_1_.refs_5_, bf16[64,2944]{1,0:T(8,128)(2,1)S(1)} %collective-permute-done.12.refs_2_.refs_6_, ...), custom_call_target="tpu_custom_call" | custom-call | flops 385875968 | bytes 3014656 | tf_op jit(solution)/shard_map/pair_sums/pallas_call | solution.py:261
  46.8 1.3 %collective-permute-start.14 = (f32[16,16]{1,0:T(8,128)S(1)}, f32[16,16]{1,0:T(8,128)S(1)}, u32[]{:S(2)}, u32[]{:S(2)}) collective-permute-start(f32[16,16]{1,0:T(8,128)S(1)} %pair_sums.1), channel_id=1, source_target_pairs={{0,8},{8,0},{16,24},{24,16},{1,9},{9,1},{17,25},{25,17},{2,10},{10... | collective-permute-start | bytes 3080 | tf_op jit(solution)/shard_map/ppermute | solution.py:208
  48.1 1.5 %score_sums.1 = f32[16,16]{1,0:T(8,128)S(1)} custom-call(bf16[64,2944]{1,0:T(8,128)(2,1)S(1)} %get-tuple-element.22.dep_ref.refs_0_.refs_4_, bf16[64,2944]{1,0:T(8,128)(2,1)S(1)} %collective-permute-done.refs_1_.refs_5_, bf16[64,2944]{1,0:T(8,128)(2,1)S(1)} %collective-permute-done.1.refs_2_.refs_6_, ...), custom_call_target="tpu_custom_call" | custom-call | flops 385875968 | bytes 1507328 | tf_op jit(solution)/shard_map/score_sums/pallas_call | solution.py:261
  50.5 1.5 %collective-permute-start.15 = (f32[16,16]{1,0:T(8,128)S(1)}, f32[16,16]{1,0:T(8,128)S(1)}, u32[]{:S(2)}, u32[]{:S(2)}) collective-permute-start(f32[16,16]{1,0:T(8,128)S(1)} %add.35), channel_id=1, source_target_pairs={{0,16},{8,24},{16,0},{24,8},{1,17},{9,25},{17,1},{25,9},{2,18},{10... | collective-permute-start | bytes 3080 | tf_op jit(solution)/shard_map/ppermute | solution.py:208
  52.0 1.6 %collective-permute-start.4 = (f32[16,16]{1,0:T(8,128)S(1)}, f32[16,16]{1,0:T(8,128)S(1)}, u32[]{:S(2)}, u32[]{:S(2)}) collective-permute-start(f32[16,16]{1,0:T(8,128)S(1)} %add.30), channel_id=1, source_target_pairs={{0,2},{1,3},{2,0},{3,1},{4,6},{5,7},{6,4},{7,5},{8,10},{9,11},{10,... | collective-permute-start | bytes 3080 | tf_op jit(solution)/shard_map/ppermute | solution.py:208
  54.1 1.5 %collective-permute-done.4 = f32[16,16]{1,0:T(8,128)S(1)} collective-permute-done((f32[16,16]{1,0:T(8,128)S(1)}, f32[16,16]{1,0:T(8,128)S(1)}, u32[]{:S(2)}, u32[]{:S(2)}) %collective-permute-start.4) | collective-permute-done | bytes 1056 | tf_op jit(solution)/shard_map/ppermute | solution.py:208
  55.7 2.6 %collective-permute-start.5 = (f32[16,16]{1,0:T(8,128)S(1)}, f32[16,16]{1,0:T(8,128)S(1)}, u32[]{:S(2)}, u32[]{:S(2)}) collective-permute-start(f32[16,16]{1,0:T(8,128)S(1)} %add.31), channel_id=1, source_target_pairs={{0,4},{1,5},{2,6},{3,7},{4,0},{5,1},{6,2},{7,3},{8,12},{9,13},{10,... | collective-permute-start | bytes 3080 | tf_op jit(solution)/shard_map/ppermute | solution.py:208
  58.2 1.6 %collective-permute-start.17 = (f32[16,16]{1,0:T(8,128)S(1)}, f32[16,16]{1,0:T(8,128)S(1)}, u32[]{:S(2)}, u32[]{:S(2)}) collective-permute-start(f32[16,16]{1,0:T(8,128)S(1)} %add.37), channel_id=1, source_target_pairs={{0,2},{1,3},{2,0},{3,1},{4,6},{5,7},{6,4},{7,5},{8,10},{9,11},{10,... | collective-permute-start | bytes 3080 | tf_op jit(solution)/shard_map/ppermute | solution.py:208
  60.7 1.2 %collective-permute-done.17 = f32[16,16]{1,0:T(8,128)S(1)} collective-permute-done((f32[16,16]{1,0:T(8,128)S(1)}, f32[16,16]{1,0:T(8,128)S(1)}, u32[]{:S(2)}, u32[]{:S(2)}) %collective-permute-start.17) | collective-permute-done | bytes 1056 | tf_op jit(solution)/shard_map/ppermute | solution.py:208
  61.9 1.5 %collective-permute-start.18 = (f32[16,16]{1,0:T(8,128)S(1)}, f32[16,16]{1,0:T(8,128)S(1)}, u32[]{:S(2)}, u32[]{:S(2)}) collective-permute-start(f32[16,16]{1,0:T(8,128)S(1)} %add.38), channel_id=1, source_target_pairs={{0,4},{1,5},{2,6},{3,7},{4,0},{5,1},{6,2},{7,3},{8,12},{9,13},{10,... | collective-permute-start | bytes 3080 | tf_op jit(solution)/shard_map/ppermute | solution.py:208
  64.6 1.9 %collective-permute-done.18 = f32[16,16]{1,0:T(8,128)S(1)} collective-permute-done((f32[16,16]{1,0:T(8,128)S(1)}, f32[16,16]{1,0:T(8,128)S(1)}, u32[]{:S(2)}, u32[]{:S(2)}) %collective-permute-start.18) | collective-permute-done | bytes 1056 | tf_op jit(solution)/shard_map/ppermute | solution.py:208
  67.5 2.4 %input_gradient.1 = (bf16[64,2944]{1,0:T(8,128)(2,1)S(1)}, bf16[64,2944]{1,0:T(8,128)(2,1)S(1)}, bf16[64,2944]{1,0:T(8,128)(2,1)S(1)}, bf16[64,2944]{1,0:T(8,128)(2,1)S(1)}) custom-call(f32[16,16]{1,0:T(8,128)S(1)} %add.34.s_ref, f32[16,16]{1,0:T(8,128)S(1)} %add.39.p_ref, f32[256,256]{1,0:T(8,128)S(1)} %get-tuple-element.26.refs_4_.qk_ref, ...), custom_call_target="tpu_custom_call" | custom-call | flops 1543503872 | bytes 4521984 | tf_op jit(solution)/shard_map/input_gradient/pallas_call | solution.py:288
  71.8 1.7 %collective-permute-start.21 = (bf16[64,2944]{1,0:T(8,128)(2,1)S(1)}, bf16[64,2944]{1,0:T(8,128)(2,1)S(1)}, u32[]{:S(2)}, u32[]{:S(2)}) collective-permute-start(bf16[64,2944]{1,0:T(8,128)(2,1)S(1)} %get-tuple-element.41), channel_id=1, source_target_pairs={{0,24},{8,16},{16,8},{24,0},{1,25},{9,17},{17,9},{25,1},{2,26},{10... | collective-permute-start | bytes 1130504 | tf_op jit(solution)/shard_map/ppermute | solution.py:199
  73.5 1.4 %branch.1 = (bf16[64,2944]{1,0:T(8,128)(2,1)S(1)}, bf16[64,2944]{1,0:T(8,128)(2,1)S(1)}, bf16[64,2944]{1,0:T(8,128)(2,1)S(1)}, bf16[64,2944]{1,0:T(8,128)(2,1)S(1)}) custom-call(f32[16,16]{1,0:T(8,128)S(1)} %add.34.s_ref, f32[256,256]{1,0:T(8,128)S(1)} %get-tuple-element.27.ov_ref.refs_8_, bf16[64,2944]{1,0:T(8,128)(2,1)S(1)} %get-tuple-element.22.dep_ref.refs_0_.refs_4_, ...), custom_call_target="tpu_custom_call" | custom-call | flops 771751936 | bytes 3014656 | tf_op jit(solution)/shard_map/branch/pallas_call | solution.py:275
  74.9 1.3 %collective-permute-start.10 = (bf16[64,2944]{1,0:T(8,128)(2,1)S(1)}, bf16[64,2944]{1,0:T(8,128)(2,1)S(1)}, u32[]{:S(2)}, u32[]{:S(2)}) collective-permute-start(bf16[64,2944]{1,0:T(8,128)(2,1)S(1)} %get-tuple-element.31), channel_id=1, source_target_pairs={{0,24},{8,16},{16,8},{24,0},{1,25},{9,17},{17,9},{25,1},{2,26},{10... | collective-permute-start | bytes 1130504 | tf_op jit(solution)/shard_map/ppermute | solution.py:199
  77.1 4.6 %collective-permute-done.19.refs_5_ = bf16[64,2944]{1,0:T(8,128)(2,1)S(1)} collective-permute-done((bf16[64,2944]{1,0:T(8,128)(2,1)S(1)}, bf16[64,2944]{1,0:T(8,128)(2,1)S(1)}, u32[]{:S(2)}, u32[]{:S(2)}) %collective-permute-start.19) | collective-permute-done | bytes 376864 | tf_op jit(solution)/shard_map/ppermute | solution.py:199
  82.5 14.9 %collective-permute-done.20.refs_6_ = bf16[64,2944]{1,0:T(8,128)(2,1)S(1)} collective-permute-done((bf16[64,2944]{1,0:T(8,128)(2,1)S(1)}, bf16[64,2944]{1,0:T(8,128)(2,1)S(1)}, u32[]{:S(2)}, u32[]{:S(2)}) %collective-permute-start.20) | collective-permute-done | bytes 376864 | tf_op jit(solution)/shard_map/ppermute | solution.py:199
  97.4 1.9 %ensemble_grad.1 = f32[64,11520]{1,0:T(8,128)} custom-call(bf16[64,2944]{1,0:T(8,128)(2,1)S(1)} %get-tuple-element.32.refs_0_.refs_4_, bf16[64,2944]{1,0:T(8,128)(2,1)S(1)} %get-tuple-element.33.refs_1_, bf16[64,2944]{1,0:T(8,128)(2,1)S(1)} %get-tuple-element.34.refs_2_, bf16[64,2944]{1,0:T(8,128)(2,1)S(1)} %get-tuple-element.35.refs_3_, ...), custom_call_target="tpu_custom_call" | custom-call | flops 737280 | bytes 5898240 | tf_op jit(solution)/shard_map/ensemble_grad/pallas_call | solution.py:300
  99.3 2.1 %collective-permute-done.8.refs_5_ = bf16[64,2944]{1,0:T(8,128)(2,1)S(1)} collective-permute-done((bf16[64,2944]{1,0:T(8,128)(2,1)S(1)}, bf16[64,2944]{1,0:T(8,128)(2,1)S(1)}, u32[]{:S(2)}, u32[]{:S(2)}) %collective-permute-start.8) | collective-permute-done | bytes 376864 | tf_op jit(solution)/shard_map/ppermute | solution.py:199
  102.2 1.9 %updated.1 = f32[64,11520]{1,0:T(8,128)} custom-call(bf16[64,2944]{1,0:T(8,128)(2,1)S(1)} %get-tuple-element.22.dep_ref.refs_0_.refs_4_, bf16[64,2944]{1,0:T(8,128)(2,1)S(1)} %get-tuple-element.23.refs_1_, bf16[64,2944]{1,0:T(8,128)(2,1)S(1)} %get-tuple-element.24.refs_2_, bf16[64,2944]{1,0:T(8,128)(2,1)S(1)} %get-tuple-element.25.refs_3_, ...), custom_call_target="tpu_custom_call" | custom-call | flops 737280 | bytes 5898240 | tf_op jit(solution)/shard_map/updated/pallas_call | solution.py:300
  (42 shorter events, 12.0 us)
Async XLA Ops:
  0.6 1.4 %copy-start.1 = (bf16[4,16,11520]{2,1,0:T(8,128)(2,1)S(1)}, bf16[4,16,11520]{2,1,0:T(8,128)(2,1)}, u32[]{:S(2)}) copy-start(bf16[4,16,11520]{2,1,0:T(8,128)(2,1)} %param.6) | copy-start | bytes 4423684
  2.2 1.4 %copy-start = (bf16[4,16,11520]{2,1,0:T(8,128)(2,1)S(1)}, bf16[4,16,11520]{2,1,0:T(8,128)(2,1)}, u32[]{:S(2)}) copy-start(bf16[4,16,11520]{2,1,0:T(8,128)(2,1)} %param.7) | copy-start | bytes 4423684
  3.6 0.7 copy-start.2
  4.3 0.7 copy-start.3
  4.9 0.7 copy-start.4
  5.6 0.7 copy-start.5
  7.8 12.6 %collective-permute-start.11 = (bf16[64,2944]{1,0:T(8,128)(2,1)S(1)}, bf16[64,2944]{1,0:T(8,128)(2,1)S(1)}, u32[]{:S(2)}, u32[]{:S(2)}) collective-permute-start(bf16[64,2944]{1,0:T(8,128)(2,1)S(1)} %get-tuple-element.33.refs_1_), channel_id=1, source_target_pairs={{0,8},{8,0},{16,24},{24,16},{1,9},{9,1},{17,25},{25,17},{2,10},{10... | collective-permute-start | bytes 1130504 | tf_op jit(solution)/shard_map/ppermute | solution.py:199
  10.8 19.8 %collective-permute-start.12 = (bf16[64,2944]{1,0:T(8,128)(2,1)S(1)}, bf16[64,2944]{1,0:T(8,128)(2,1)S(1)}, u32[]{:S(2)}, u32[]{:S(2)}) collective-permute-start(bf16[64,2944]{1,0:T(8,128)(2,1)S(1)} %get-tuple-element.34.refs_2_), channel_id=1, source_target_pairs={{0,16},{8,24},{16,0},{24,8},{1,17},{9,25},{17,1},{25,9},{2,18},{10... | collective-permute-start | bytes 1130504 | tf_op jit(solution)/shard_map/ppermute | solution.py:199
  12.4 18.2 %collective-permute-start.13 = (bf16[64,2944]{1,0:T(8,128)(2,1)S(1)}, bf16[64,2944]{1,0:T(8,128)(2,1)S(1)}, u32[]{:S(2)}, u32[]{:S(2)}) collective-permute-start(bf16[64,2944]{1,0:T(8,128)(2,1)S(1)} %get-tuple-element.35.refs_3_), channel_id=1, source_target_pairs={{0,24},{8,16},{16,8},{24,0},{1,25},{9,17},{17,9},{25,1},{2,26},{10... | collective-permute-start | bytes 1130504 | tf_op jit(solution)/shard_map/ppermute | solution.py:199
  12.4 24.2 %collective-permute-start = (bf16[64,2944]{1,0:T(8,128)(2,1)S(1)}, bf16[64,2944]{1,0:T(8,128)(2,1)S(1)}, u32[]{:S(2)}, u32[]{:S(2)}) collective-permute-start(bf16[64,2944]{1,0:T(8,128)(2,1)S(1)} %get-tuple-element.23.refs_1_), channel_id=1, source_target_pairs={{0,8},{8,0},{16,24},{24,16},{1,9},{9,1},{17,25},{25,17},{2,10},{10... | collective-permute-start | bytes 1130504 | tf_op jit(solution)/shard_map/ppermute | solution.py:199
  14.3 31.0 %collective-permute-start.1 = (bf16[64,2944]{1,0:T(8,128)(2,1)S(1)}, bf16[64,2944]{1,0:T(8,128)(2,1)S(1)}, u32[]{:S(2)}, u32[]{:S(2)}) collective-permute-start(bf16[64,2944]{1,0:T(8,128)(2,1)S(1)} %get-tuple-element.24.refs_2_), channel_id=1, source_target_pairs={{0,16},{8,24},{16,0},{24,8},{1,17},{9,25},{17,1},{25,9},{2,18},{10... | collective-permute-start | bytes 1130504 | tf_op jit(solution)/shard_map/ppermute | solution.py:199
  20.4 24.9 %collective-permute-start.2 = (bf16[64,2944]{1,0:T(8,128)(2,1)S(1)}, bf16[64,2944]{1,0:T(8,128)(2,1)S(1)}, u32[]{:S(2)}, u32[]{:S(2)}) collective-permute-start(bf16[64,2944]{1,0:T(8,128)(2,1)S(1)} %get-tuple-element.25.refs_3_), channel_id=1, source_target_pairs={{0,24},{8,16},{16,8},{24,0},{1,25},{9,17},{17,9},{25,1},{2,26},{10... | collective-permute-start | bytes 1130504 | tf_op jit(solution)/shard_map/ppermute | solution.py:199
  46.8 3.7 %collective-permute-start.14 = (f32[16,16]{1,0:T(8,128)S(1)}, f32[16,16]{1,0:T(8,128)S(1)}, u32[]{:S(2)}, u32[]{:S(2)}) collective-permute-start(f32[16,16]{1,0:T(8,128)S(1)} %pair_sums.1), channel_id=1, source_target_pairs={{0,8},{8,0},{16,24},{24,16},{1,9},{9,1},{17,25},{25,17},{2,10},{10... | collective-permute-start | bytes 3080 | tf_op jit(solution)/shard_map/ppermute | solution.py:208
  49.6 2.4 %collective-permute-start.3 = (f32[16,16]{1,0:T(8,128)S(1)}, f32[16,16]{1,0:T(8,128)S(1)}, u32[]{:S(2)}, u32[]{:S(2)}) collective-permute-start(f32[16,16]{1,0:T(8,128)S(1)} %score_sums.1), channel_id=1, source_target_pairs={{0,1},{1,0},{2,3},{3,2},{4,5},{5,4},{6,7},{7,6},{8,9},{9,8},{10,11... | collective-permute-start | bytes 3080 | tf_op jit(solution)/shard_map/ppermute | solution.py:208
  50.5 3.7 %collective-permute-start.15 = (f32[16,16]{1,0:T(8,128)S(1)}, f32[16,16]{1,0:T(8,128)S(1)}, u32[]{:S(2)}, u32[]{:S(2)}) collective-permute-start(f32[16,16]{1,0:T(8,128)S(1)} %add.35), channel_id=1, source_target_pairs={{0,16},{8,24},{16,0},{24,8},{1,17},{9,25},{17,1},{25,9},{2,18},{10... | collective-permute-start | bytes 3080 | tf_op jit(solution)/shard_map/ppermute | solution.py:208
  52.0 3.7 %collective-permute-start.4 = (f32[16,16]{1,0:T(8,128)S(1)}, f32[16,16]{1,0:T(8,128)S(1)}, u32[]{:S(2)}, u32[]{:S(2)}) collective-permute-start(f32[16,16]{1,0:T(8,128)S(1)} %add.30), channel_id=1, source_target_pairs={{0,2},{1,3},{2,0},{3,1},{4,6},{5,7},{6,4},{7,5},{8,10},{9,11},{10,... | collective-permute-start | bytes 3080 | tf_op jit(solution)/shard_map/ppermute | solution.py:208
  54.1 4.1 %collective-permute-start.16 = (f32[16,16]{1,0:T(8,128)S(1)}, f32[16,16]{1,0:T(8,128)S(1)}, u32[]{:S(2)}, u32[]{:S(2)}) collective-permute-start(f32[16,16]{1,0:T(8,128)S(1)} %add.36), channel_id=1, source_target_pairs={{0,1},{1,0},{2,3},{3,2},{4,5},{5,4},{6,7},{7,6},{8,9},{9,8},{10,11... | collective-permute-start | bytes 3080 | tf_op jit(solution)/shard_map/ppermute | solution.py:208
  55.7 4.5 %collective-permute-start.5 = (f32[16,16]{1,0:T(8,128)S(1)}, f32[16,16]{1,0:T(8,128)S(1)}, u32[]{:S(2)}, u32[]{:S(2)}) collective-permute-start(f32[16,16]{1,0:T(8,128)S(1)} %add.31), channel_id=1, source_target_pairs={{0,4},{1,5},{2,6},{3,7},{4,0},{5,1},{6,2},{7,3},{8,12},{9,13},{10,... | collective-permute-start | bytes 3080 | tf_op jit(solution)/shard_map/ppermute | solution.py:208
  58.2 3.7 %collective-permute-start.17 = (f32[16,16]{1,0:T(8,128)S(1)}, f32[16,16]{1,0:T(8,128)S(1)}, u32[]{:S(2)}, u32[]{:S(2)}) collective-permute-start(f32[16,16]{1,0:T(8,128)S(1)} %add.37), channel_id=1, source_target_pairs={{0,2},{1,3},{2,0},{3,1},{4,6},{5,7},{6,4},{7,5},{8,10},{9,11},{10,... | collective-permute-start | bytes 3080 | tf_op jit(solution)/shard_map/ppermute | solution.py:208
  60.2 3.7 %collective-permute-start.6 = (f32[16,16]{1,0:T(8,128)S(1)}, f32[16,16]{1,0:T(8,128)S(1)}, u32[]{:S(2)}, u32[]{:S(2)}) collective-permute-start(f32[16,16]{1,0:T(8,128)S(1)} %add.32), channel_id=1, source_target_pairs={{0,8},{8,0},{16,24},{24,16},{1,9},{9,1},{17,25},{25,17},{2,10},{10... | collective-permute-start | bytes 3080 | tf_op jit(solution)/shard_map/ppermute | solution.py:208
  61.9 4.5 %collective-permute-start.18 = (f32[16,16]{1,0:T(8,128)S(1)}, f32[16,16]{1,0:T(8,128)S(1)}, u32[]{:S(2)}, u32[]{:S(2)}) collective-permute-start(f32[16,16]{1,0:T(8,128)S(1)} %add.38), channel_id=1, source_target_pairs={{0,4},{1,5},{2,6},{3,7},{4,0},{5,1},{6,2},{7,3},{8,12},{9,13},{10,... | collective-permute-start | bytes 3080 | tf_op jit(solution)/shard_map/ppermute | solution.py:208
  63.9 3.7 %collective-permute-start.7 = (f32[16,16]{1,0:T(8,128)S(1)}, f32[16,16]{1,0:T(8,128)S(1)}, u32[]{:S(2)}, u32[]{:S(2)}) collective-permute-start(f32[16,16]{1,0:T(8,128)S(1)} %add.33), channel_id=1, source_target_pairs={{0,16},{8,24},{16,0},{24,8},{1,17},{9,25},{17,1},{25,9},{2,18},{10... | collective-permute-start | bytes 3080 | tf_op jit(solution)/shard_map/ppermute | solution.py:208
  70.0 11.8 %collective-permute-start.19 = (bf16[64,2944]{1,0:T(8,128)(2,1)S(1)}, bf16[64,2944]{1,0:T(8,128)(2,1)S(1)}, u32[]{:S(2)}, u32[]{:S(2)}) collective-permute-start(bf16[64,2944]{1,0:T(8,128)(2,1)S(1)} %get-tuple-element.39), channel_id=1, source_target_pairs={{0,8},{8,0},{16,24},{24,16},{1,9},{9,1},{17,25},{25,17},{2,10},{10... | collective-permute-start | bytes 1130504 | tf_op jit(solution)/shard_map/ppermute | solution.py:199
  71.0 26.4 %collective-permute-start.20 = (bf16[64,2944]{1,0:T(8,128)(2,1)S(1)}, bf16[64,2944]{1,0:T(8,128)(2,1)S(1)}, u32[]{:S(2)}, u32[]{:S(2)}) collective-permute-start(bf16[64,2944]{1,0:T(8,128)(2,1)S(1)} %get-tuple-element.40), channel_id=1, source_target_pairs={{0,16},{8,24},{16,0},{24,8},{1,17},{9,25},{17,1},{25,9},{2,18},{10... | collective-permute-start | bytes 1130504 | tf_op jit(solution)/shard_map/ppermute | solution.py:199
  71.8 25.6 %collective-permute-start.21 = (bf16[64,2944]{1,0:T(8,128)(2,1)S(1)}, bf16[64,2944]{1,0:T(8,128)(2,1)S(1)}, u32[]{:S(2)}, u32[]{:S(2)}) collective-permute-start(bf16[64,2944]{1,0:T(8,128)(2,1)S(1)} %get-tuple-element.41), channel_id=1, source_target_pairs={{0,24},{8,16},{16,8},{24,0},{1,25},{9,17},{17,9},{25,1},{2,26},{10... | collective-permute-start | bytes 1130504 | tf_op jit(solution)/shard_map/ppermute | solution.py:199
  74.9 24.4 %collective-permute-start.10 = (bf16[64,2944]{1,0:T(8,128)(2,1)S(1)}, bf16[64,2944]{1,0:T(8,128)(2,1)S(1)}, u32[]{:S(2)}, u32[]{:S(2)}) collective-permute-start(bf16[64,2944]{1,0:T(8,128)(2,1)S(1)} %get-tuple-element.31), channel_id=1, source_target_pairs={{0,24},{8,16},{16,8},{24,0},{1,25},{9,17},{17,9},{25,1},{2,26},{10... | collective-permute-start | bytes 1130504 | tf_op jit(solution)/shard_map/ppermute | solution.py:199
  76.2 25.2 %collective-permute-start.8 = (bf16[64,2944]{1,0:T(8,128)(2,1)S(1)}, bf16[64,2944]{1,0:T(8,128)(2,1)S(1)}, u32[]{:S(2)}, u32[]{:S(2)}) collective-permute-start(bf16[64,2944]{1,0:T(8,128)(2,1)S(1)} %get-tuple-element.29), channel_id=1, source_target_pairs={{0,8},{8,0},{16,24},{24,16},{1,9},{9,1},{17,25},{25,17},{2,10},{10... | collective-permute-start | bytes 1130504 | tf_op jit(solution)/shard_map/ppermute | solution.py:199
  81.7 20.5 %collective-permute-start.9 = (bf16[64,2944]{1,0:T(8,128)(2,1)S(1)}, bf16[64,2944]{1,0:T(8,128)(2,1)S(1)}, u32[]{:S(2)}, u32[]{:S(2)}) collective-permute-start(bf16[64,2944]{1,0:T(8,128)(2,1)S(1)} %get-tuple-element.30), channel_id=1, source_target_pairs={{0,16},{8,24},{16,0},{24,8},{1,17},{9,25},{17,1},{25,9},{2,18},{10... | collective-permute-start | bytes 1130504 | tf_op jit(solution)/shard_map/ppermute | solution.py:199

commit v2 on v1

v2 whole, which is shorter than its diff:
```python
import functools
import math

import jax
import jax.numpy as jnp
from jax import lax
from jax.experimental import pallas as pl
from jax.experimental.pallas import tpu as pltpu
from jax.sharding import PartitionSpec as P

LANES = 128
HIGH = lax.Precision.HIGHEST
VMEM = pltpu.MemorySpace.VMEM


def mm(a, b, dims, precision=None):
    return lax.dot_general(
        a, b, (dims, ((), ())), precision=precision, preferred_element_type=jnp.float32
    )


def chunk_start(index, chunk, length):
    return pl.multiple_of(jnp.minimum(index * chunk, length - chunk), LANES)


def partner(me, step):
    return me ^ step


def lane_tiles(width, step=512):
    return [(at, min(step, width - at)) for at in range(0, width, step)]


def half_of(chunk):
    return -(-chunk // (2 * LANES)) * LANES


def whole_pieces(count, chunk):
    return [(s, 0, chunk) for s in range(count)]


def last_cut(count, chunk):
    pieces = whole_pieces(count, chunk)
    half = half_of(chunk)
    return pieces[:-1] + [(count - 1, 0, half), (count - 1, half, chunk - half)]


def store_pieces(outs, pieces, value, at, width, per):
    for out, (s, low, size) in zip(outs, pieces):
        a, b = max(at, low), min(at + width, low + size)
        if a < b:
            out[:, a - low:b - low] = value[s * per:(s + 1) * per, a - at:b - at]


def member_of_row(me, rows, channels, members, group):
    row = lax.broadcasted_iota(jnp.int32, (rows, members), 0)
    col = lax.broadcasted_iota(jnp.int32, (rows, members), 1)
    per_group = group * channels
    owner = (row // per_group) ^ me
    member = owner * group + (row % per_group) // channels
    return (member == col).astype(jnp.float32)


def split_kernel(me_of, count, chunk, length, x_ref, *rest):
    outs, sem = rest[-count - 1:-1], rest[-1]
    me = me_of()
    copies = [
        pltpu.make_async_copy(
            x_ref.at[:, pl.ds(chunk_start(partner(me, s), chunk, length), chunk)],
            outs[s],
            sem.at[s],
        )
        for s in range(count)
    ]
    for copy in copies:
        copy.start()
    for copy in copies:
        copy.wait()


def tiled(small, rows, channels):
    tall = jnp.concatenate([small] * (rows // channels), axis=0)
    col = lax.broadcasted_iota(jnp.int32, (channels, rows), 1)
    row = lax.broadcasted_iota(jnp.int32, (channels, rows), 0)
    spread = (col % channels == row).astype(jnp.float32)
    return mm(tall, spread, ((1,), (0,)), HIGH)


def tiles_kernel(rows, channels, wq_ref, wk_ref, wv_ref, wo_ref, qk_ref, qkt_ref, ov_ref, ovt_ref):
    wq, wk = wq_ref[...].astype(jnp.float32), wk_ref[...].astype(jnp.float32)
    wv, wo = wv_ref[...].astype(jnp.float32), wo_ref[...].astype(jnp.float32)
    wqt, wkt, wvt, wot = wq.T, wk.T, wv.T, wo.T
    qk_ref[...] = tiled(mm(wqt, wk, ((1,), (0,)), HIGH), rows, channels)
    qkt_ref[...] = tiled(mm(wkt, wq, ((1,), (0,)), HIGH), rows, channels)
    ov_ref[...] = tiled(mm(wo, wv, ((1,), (0,)), HIGH), rows, channels)
    ovt_ref[...] = tiled(mm(wvt, wot, ((1,), (0,)), HIGH), rows, channels)


def gather_tile(refs, at, width):
    return jnp.concatenate([r[:, at:at + width] for r in refs], axis=0)


def fold(weighted, picks):
    half = mm(weighted, picks, ((1,), (0,)), HIGH)
    return mm(picks, half, ((0,), (0,)), HIGH)


def masked_gram(me, count, chunk, length, left, right):
    rows = count * right[0].shape[0]
    skip = me * chunk - chunk_start(me, chunk, length)
    total = jnp.zeros((rows, rows), jnp.float32)
    for at, width in lane_tiles(chunk):
        b = gather_tile(right, at, width)
        a = b if left is right else gather_tile(left, at, width)
        lane = lax.broadcasted_iota(jnp.int32, (rows, width), 1) + at
        a = jnp.where(lane >= skip, a.astype(jnp.float32), 0.0).astype(jnp.bfloat16)
        total = total + mm(a, b, ((1,), (1,)))
    return total


def score_kernel(me_of, count, chunk, length, group, channels, members, tile_ref, *refs):
    me = me_of()
    fields, out_ref = refs[:count], refs[-1]
    rows = count * fields[0].shape[0]
    total = masked_gram(me, count, chunk, length, fields, fields)
    picks = member_of_row(me, rows, channels, members, group)
    out_ref[...] = fold(total * tile_ref[...], picks)


def pair_kernel(me_of, count, chunk, length, group, channels, members, tile_ref, s_ref, *refs):
    me = me_of()
    fields, grads, out_ref = refs[:count], refs[count:2 * count], refs[-1]
    rows = count * fields[0].shape[0]
    total = masked_gram(me, count, chunk, length, grads, fields)
    picks = member_of_row(me, rows, channels, members, group)
    out_ref[:members, :] = s_ref[...]
    out_ref[members:, :] = fold(total * tile_ref[...], picks)


def softmax(scores):
    peak = jnp.max(scores, axis=1, keepdims=True)
    exponent = jnp.exp(scores - peak)
    return exponent / jnp.sum(exponent, axis=1, keepdims=True)


def spread(small, picks):
    tall = mm(picks, small.astype(jnp.bfloat16), ((1,), (0,))).astype(jnp.bfloat16)
    return mm(tall, picks, ((1,), (1,)))


def spread_t(small, picks):
    tall = mm(picks, small.astype(jnp.bfloat16), ((1,), (1,))).astype(jnp.bfloat16)
    return mm(tall, picks, ((1,), (1,)))


def two_parts(value):
    high = value.astype(jnp.bfloat16)
    return high, (value - high.astype(jnp.float32)).astype(jnp.bfloat16)


def branch_kernel(
    me_of, count, chunk, group, channels, members, scale, pieces, ov_ref, *refs
):
    me = me_of()
    sums, fields = refs[:count], refs[count:2 * count]
    total_ref, outs = refs[2 * count], refs[2 * count + 1:]
    per = fields[0].shape[0]
    rows = count * per
    total = sums[0][...]
    for other in sums[1:]:
        total = total + other[...]
    total_ref[...] = total
    picks = member_of_row(me, rows, channels, members, group).astype(jnp.bfloat16)
    weights = softmax(total[:members, :] * scale)
    high, low = two_parts(spread(weights, picks) * ov_ref[...])
    for at, width in lane_tiles(chunk):
        e = gather_tile(fields, at, width)
        b = (mm(high, e, ((1,), (0,))) + mm(low, e, ((1,), (0,)))).astype(jnp.bfloat16)
        store_pieces(outs, pieces, b, at, width, per)


def grad_kernel(
    me_of, count, chunk, group, channels, members, scale, low, size, waits,
    s_ref, p_ref, qk_ref, qkt_ref, ovt_ref, *refs,
):
    me = me_of()
    fields, grads, outs = refs[:count], refs[count:2 * count], refs[2 * count + waits:]
    per = fields[0].shape[0]
    rows = count * per
    picks = member_of_row(me, rows, channels, members, group).astype(jnp.bfloat16)
    weights = softmax(s_ref[:members, :] * scale)
    pairs = p_ref[members:, :]
    slope = weights * (pairs - jnp.sum(weights * pairs, axis=1, keepdims=True)) * scale
    d_high, d_low = two_parts(
        spread(slope, picks) * qk_ref[...] + spread_t(slope, picks) * qkt_ref[...]
    )
    a_high, a_low = two_parts(spread_t(weights, picks) * ovt_ref[...])
    for at, width in lane_tiles(size):
        e = gather_tile(fields, low + at, width)
        c = gather_tile(grads, low + at, width)
        b = (
            mm(d_high, e, ((1,), (0,))) + mm(d_low, e, ((1,), (0,)))
            + mm(a_high, c, ((1,), (0,))) + mm(a_low, c, ((1,), (0,)))
        ).astype(jnp.bfloat16)
        for s in range(count):
            outs[s][:, at:at + width] = b[s * per:(s + 1) * per]


def finish_kernel(me_of, count, chunk, length, pieces, dep_ref, *refs):
    me = me_of()
    base, extra = refs[:count], refs[count:count + len(pieces)]
    out_ref, held, sem = refs[count + len(pieces):]
    per = base[0].shape[0]
    rows = 16
    copies = []
    for at in range(0, per, rows):
        for more, (s, low, size) in zip(extra, pieces):
            start = chunk_start(partner(me, s), chunk, length) + low
            held[at:at + rows, pl.ds(pl.multiple_of(start, LANES), size)] = base[s][
                at:at + rows, low:low + size
            ].astype(jnp.float32) + more[at:at + rows, :].astype(jnp.float32)
        copy = pltpu.make_async_copy(
            held.at[at:at + rows], out_ref.at[at:at + rows], sem.at[at // rows]
        )
        copy.start()
        copies.append(copy)
    for copy in copies:
        copy.wait()


def swap(value, step, count):
    return lax.ppermute(value, "mem", [(i, i ^ step) for i in range(count)])


def exchange(parts, pieces, count):
    return [
        part if s == 0 else swap(part, s, count) for part, (s, _, _) in zip(parts, pieces)
    ]


def sum_steps(value, name, steps):
    size = lax.axis_size(name)
    for step in steps:
        value = value + lax.ppermute(value, name, [(i, i ^ step) for i in range(size)])
    return value


def doubling(size):
    steps, step = [], 1
    while step < size:
        steps.append(step)
        step *= 2
    return steps


def shards(ensemble, cotangent, w_query, w_key, w_value, w_out):
    count = lax.axis_size("mem")
    group, channels, length = ensemble.shape
    members = group * count
    per = group * channels
    rows = per * count
    chunk = -(-length // (LANES * count)) * LANES
    scale = 1.0 / (length * lax.axis_size("space") * math.sqrt(channels))
    me_of = lambda: lax.axis_index("mem")
    bf, f32 = jnp.bfloat16, jnp.float32
    whole = pl.BlockSpec(memory_space=VMEM)
    anywhere = pl.BlockSpec(memory_space=pl.ANY)
    in_hbm = pl.BlockSpec(memory_space=pltpu.MemorySpace.HBM)
    params = pltpu.CompilerParams(vmem_limit_bytes=40 * 1024 * 1024)
    part = jax.ShapeDtypeStruct((per, chunk), bf)
    square = jax.ShapeDtypeStruct((rows, rows), f32)
    pair = jax.ShapeDtypeStruct((members, members), f32)
    fields = ensemble.reshape(per, length)
    grads = cotangent.reshape(per, length)

    def cost(flops, moved):
        return pl.CostEstimate(flops=flops, bytes_accessed=moved, transcendentals=0)

    first = min(1, count - 1)
    plain = whole_pieces(count, chunk)
    cut = last_cut(count, chunk)

    def shapes(pieces):
        return [jax.ShapeDtypeStruct((per, size), bf) for _, _, size in pieces]

    def split(operands, name):
        return pl.pallas_call(
            functools.partial(split_kernel, me_of, count, chunk, length),
            out_shape=[part] * count,
            in_specs=[anywhere] * len(operands),
            out_specs=[anywhere] * count,
            scratch_shapes=[pltpu.SemaphoreType.DMA((count,))],
            compiler_params=params,
            name=name,
        )(*operands)

    e_mine = split([fields], "split_fields")
    e_cells = exchange(e_mine, plain, count)
    qk, qkt, ov, ovt = pl.pallas_call(
        functools.partial(tiles_kernel, rows, channels),
        out_shape=[square] * 4,
        in_specs=[whole] * 4,
        out_specs=[whole] * 4,
        compiler_params=params,
        cost_estimate=cost(10**8, 4 * 4 * rows * rows),
        name="weight_tiles",
    )(w_query, w_key, w_value, w_out)
    c_mine = split([grads, e_cells[first], qk], "split_grads")
    c_cells = exchange(c_mine, plain, count)
    space_steps = doubling(lax.axis_size("space"))

    scores = pl.pallas_call(
        functools.partial(
            score_kernel, me_of, count, chunk, length, group, channels, members
        ),
        out_shape=pair,
        in_specs=[whole] * (count + 1),
        out_specs=whole,
        compiler_params=params,
        cost_estimate=cost(2 * rows * rows * chunk, 2 * rows * chunk),
        name="score_sums",
    )(qk, *e_cells)
    scores = sum_steps(scores, "space", space_steps)
    both = pl.pallas_call(
        functools.partial(
            pair_kernel, me_of, count, chunk, length, group, channels, members
        ),
        out_shape=jax.ShapeDtypeStruct((2 * members, members), f32),
        in_specs=[whole] * (2 * count + 2),
        out_specs=whole,
        compiler_params=params,
        cost_estimate=cost(2 * rows * rows * chunk, 4 * rows * chunk),
        name="pair_sums",
    )(ov, scores, *e_cells, *c_cells)
    order = sorted(range(1, count), key=lambda s: (s & (s - 1) != 0, -s))
    sums = [both] + [swap(both, s, count) for s in order]

    outcome = pl.pallas_call(
        functools.partial(
            branch_kernel, me_of, count, chunk, group, channels, members, scale, cut
        ),
        out_shape=[jax.ShapeDtypeStruct((2 * members, members), f32)] + shapes(cut),
        in_specs=[whole] * (2 * count + 1),
        out_specs=[whole] * (len(cut) + 1),
        compiler_params=params,
        cost_estimate=cost(4 * rows * rows * chunk, 4 * rows * chunk),
        name="branch",
    )(ov, *sums, *e_cells)
    mem_sums, branch = outcome[0], outcome[1:]
    pairs = sum_steps(mem_sums, "space", space_steps)
    branch_home = exchange(branch, cut, count)

    def gradient(low, size, awaited, name):
        parts = pl.pallas_call(
            functools.partial(
                grad_kernel, me_of, count, chunk, group, channels, members, scale, low,
                size, len(awaited),
            ),
            out_shape=[jax.ShapeDtypeStruct((per, size), bf)] * count,
            in_specs=[whole] * (2 * count + 5) + [anywhere] * len(awaited),
            out_specs=[whole] * count,
            compiler_params=params,
            cost_estimate=cost(8 * rows * rows * size, 6 * rows * size),
            name=name,
        )(mem_sums, pairs, qk, qkt, ovt, *e_cells, *c_cells, *awaited)
        pieces = [(s, low, size) for s in range(count)]
        return pieces, exchange(parts, pieces, count)

    half = half_of(chunk)
    pieces_a, grad_a = gradient(0, half, branch_home[1:-1], "input_gradient_a")
    pieces_b, grad_b = gradient(half, chunk - half, branch_home[-1:], "input_gradient_b")

    def finish(base, extra, pieces, after, name):
        return pl.pallas_call(
            functools.partial(finish_kernel, me_of, count, chunk, length, pieces),
            out_shape=jax.ShapeDtypeStruct((per, length), f32),
            in_specs=[anywhere] + [whole] * (count + len(pieces)),
            out_specs=in_hbm,
            scratch_shapes=[
                pltpu.VMEM((per, length), f32),
                pltpu.SemaphoreType.DMA((per // 16,)),
            ],
            compiler_params=params,
            cost_estimate=cost(per * length, 8 * per * length),
            name=name,
        )(after, *base, *extra).reshape(group, channels, length)

    updated = finish(e_mine, branch_home, cut, grad_a[first], "updated")
    ensemble_grad = finish(
        c_mine, grad_a + grad_b, pieces_a + pieces_b, grad_a[0], "ensemble_grad"
    )
    return (updated, ensemble_grad)


def solution(mesh):
    split = P("mem", None, "space")
    return jax.shard_map(
        shards,
        mesh=mesh,
        in_specs=(split, split, P(), P(), P(), P()),
        out_specs=(split, split),
        check_vma=False,
    )
```

time: 104 us -> 85.1 us (0.82)
  waiting for transfers between devices: 56.7 us -> 33.3 us
  starting transfers between devices: 29 us -> 32.6 us
    ppermute x22 -> x25, waiting for transfers between devices: 56.7 us -> 33.3 us  [the longest x19 24 us: swap(): return lax.ppermute(value, 'mem', [(i, i ^ step) for i in range(count)])]
    ppermute x22 -> x25, starting transfers between devices: 29 us -> 32.6 us  [the longest x19 24.2 us: swap(): return lax.ppermute(value, 'mem', [(i, i ^ step) for i in range(count)])]
    pallas_call x5 -> x7, Pallas kernels: 7.05 us -> 7.82 us  [the longest x2 3.2 us: gradient(): pl.pallas_call(functools.partial(grad_kernel, me_of, count, chunk, group,...]
  transfers between devices with their start and end apart: 22 -> 25, of which waited for: 16 -> 19; matrix products, arithmetic and copies ran while one was open for 0% -> 0% of each run, Pallas kernels for 5% -> 9%
where the time goes in v2:
time: 85.1 us; the launch traced here: 84.8 us
  waiting for transfers between devices  33.3 us (39%)
  starting transfers between devices  32.6 us (38%)
  Pallas kernels  12.6 us (15%)
  local copies, waits for them, and re-layouts  5.48 us (6%)
    ppermute x19, starting transfers between devices, swap(): return lax.ppermute(value, 'mem', [(i, i ^ step) for i in range(count)])  24.2 us
    ppermute x19, waiting for transfers between devices, swap(): return lax.ppermute(value, 'mem', [(i, i ^ step) for i in range(count)])  24 us
    ppermute x6, waiting for transfers between devices, sum_steps(): lax.ppermute(value, name, [(i, i ^ step) for i in range(size)])  9.37 us
    ppermute x6, starting transfers between devices, sum_steps(): lax.ppermute(value, name, [(i, i ^ step) for i in range(size)])  8.4 us
    unnamed x12, local copies, waits for them, and re-layouts  5.48 us
    pallas_call x2, Pallas kernels, finish(): pl.pallas_call(functools.partial(finish_kernel, me_of, count, chunk, leng...  3.4 us
    pallas_call x2, Pallas kernels, gradient(): pl.pallas_call(functools.partial(grad_kernel, me_of, count, chunk, group,...  3.2 us
  transfers between devices with their start and end apart: 25, of which 19 were waited for; matrix products, arithmetic and copies ran while one was open for 0% of the time, Pallas kernels for 9%

profile of v2, /device:TPU:0, one launch (start us, length us, event | category | flops | bytes accessed | tf_op | source)
XLA Modules:
  0.0 84.8 jit_solution(1478977427744355068)
XLA Ops:
  0.6 1.4 %copy-done = bf16[4,16,11520]{2,1,0:T(8,128)(2,1)S(1)} copy-done((bf16[4,16,11520]{2,1,0:T(8,128)(2,1)S(1)}, bf16[4,16,11520]{2,1,0:T(8,128)(2,1)}, u32[]{:S(2)}) %copy-start) | copy-done | bytes 1474584
  2.2 3.0 %collective-permute-start = (bf16[64,2944]{1,0:T(8,128)(2,1)S(1)}, bf16[64,2944]{1,0:T(8,128)(2,1)S(1)}, u32[]{:S(2)}, u32[]{:S(2)}) collective-permute-start(bf16[64,2944]{1,0:T(8,128)(2,1)S(1)} %get-tuple-element.31.refs_1_), channel_id=1, source_target_pairs={{0,8},{8,0},{16,24},{24,16},{1,9},{9,1},{17,25},{25,17},{2,10},{10... | collective-permute-start | bytes 1130504 | tf_op jit(solution)/shard_map/ppermute | solution.py:232
  5.2 1.5 %collective-permute-start.1 = (bf16[64,2944]{1,0:T(8,128)(2,1)S(1)}, bf16[64,2944]{1,0:T(8,128)(2,1)S(1)}, u32[]{:S(2)}, u32[]{:S(2)}) collective-permute-start(bf16[64,2944]{1,0:T(8,128)(2,1)S(1)} %get-tuple-element.32.refs_2_), channel_id=1, source_target_pairs={{0,16},{8,24},{16,0},{24,8},{1,17},{9,25},{17,1},{25,9},{2,18},{10... | collective-permute-start | bytes 1130504 | tf_op jit(solution)/shard_map/ppermute | solution.py:232
  10.8 4.0 %collective-permute-done.refs_1_.rest_0_.refs_5_ = bf16[64,2944]{1,0:T(8,128)(2,1)S(1)} collective-permute-done((bf16[64,2944]{1,0:T(8,128)(2,1)S(1)}, bf16[64,2944]{1,0:T(8,128)(2,1)S(1)}, u32[]{:S(2)}, u32[]{:S(2)}) %collective-permute-start) | collective-permute-done | bytes 376864 | tf_op jit(solution)/shard_map/ppermute | solution.py:232
  14.8 1.4 %copy-done.1 = bf16[4,16,11520]{2,1,0:T(8,128)(2,1)S(1)} copy-done((bf16[4,16,11520]{2,1,0:T(8,128)(2,1)S(1)}, bf16[4,16,11520]{2,1,0:T(8,128)(2,1)}, u32[]{:S(2)}) %copy-start.1) | copy-done | bytes 1474584
  16.4 2.1 %collective-permute-start.6 = (bf16[64,2944]{1,0:T(8,128)(2,1)S(1)}, bf16[64,2944]{1,0:T(8,128)(2,1)S(1)}, u32[]{:S(2)}, u32[]{:S(2)}) collective-permute-start(bf16[64,2944]{1,0:T(8,128)(2,1)S(1)} %get-tuple-element.35.refs_1_), channel_id=1, source_target_pairs={{0,8},{8,0},{16,24},{24,16},{1,9},{9,1},{17,25},{25,17},{2,10},{10... | collective-permute-start | bytes 1130504 | tf_op jit(solution)/shard_map/ppermute | solution.py:232
  18.5 1.5 %collective-permute-start.7 = (bf16[64,2944]{1,0:T(8,128)(2,1)S(1)}, bf16[64,2944]{1,0:T(8,128)(2,1)S(1)}, u32[]{:S(2)}, u32[]{:S(2)}) collective-permute-start(bf16[64,2944]{1,0:T(8,128)(2,1)S(1)} %get-tuple-element.36.refs_2_), channel_id=1, source_target_pairs={{0,16},{8,24},{16,0},{24,8},{1,17},{9,25},{17,1},{25,9},{2,18},{10... | collective-permute-start | bytes 1130504 | tf_op jit(solution)/shard_map/ppermute | solution.py:232
  20.0 3.9 %collective-permute-done.1.refs_2_.refs_6_ = bf16[64,2944]{1,0:T(8,128)(2,1)S(1)} collective-permute-done((bf16[64,2944]{1,0:T(8,128)(2,1)S(1)}, bf16[64,2944]{1,0:T(8,128)(2,1)S(1)}, u32[]{:S(2)}, u32[]{:S(2)}) %collective-permute-start.1) | collective-permute-done | bytes 376864 | tf_op jit(solution)/shard_map/ppermute | solution.py:232
  24.4 1.5 %score_sums.1 = f32[16,16]{1,0:T(8,128)S(1)} custom-call(f32[256,256]{1,0:T(8,128)S(1)} %get-tuple-element.29.tile_ref.rest_1_.qk_ref, bf16[64,2944]{1,0:T(8,128)(2,1)S(1)} %get-tuple-element.30.refs_0_.refs_4_, bf16[64,2944]{1,0:T(8,128)(2,1)S(1)} %collective-permute-done.refs_1_.rest_0_.refs_5_, ...), custom_call_target="tpu_custom_call" | custom-call | flops 385875968 | bytes 1507328 | tf_op jit(solution)/shard_map/score_sums/pallas_call | solution.py:312
  27.1 1.6 %collective-permute-start.4 = (f32[16,16]{1,0:T(8,128)S(1)}, f32[16,16]{1,0:T(8,128)S(1)}, u32[]{:S(2)}, u32[]{:S(2)}) collective-permute-start(f32[16,16]{1,0:T(8,128)S(1)} %add.18), channel_id=1, source_target_pairs={{0,2},{1,3},{2,0},{3,1},{4,6},{5,7},{6,4},{7,5},{8,10},{9,11},{10,... | collective-permute-start | bytes 3080 | tf_op jit(solution)/shard_map/ppermute | solution.py:244
  28.7 2.1 %collective-permute-done.4 = f32[16,16]{1,0:T(8,128)S(1)} collective-permute-done((f32[16,16]{1,0:T(8,128)S(1)}, f32[16,16]{1,0:T(8,128)S(1)}, u32[]{:S(2)}, u32[]{:S(2)}) %collective-permute-start.4) | collective-permute-done | bytes 1056 | tf_op jit(solution)/shard_map/ppermute | solution.py:244
  30.8 2.6 %collective-permute-start.5 = (f32[16,16]{1,0:T(8,128)S(1)}, f32[16,16]{1,0:T(8,128)S(1)}, u32[]{:S(2)}, u32[]{:S(2)}) collective-permute-start(f32[16,16]{1,0:T(8,128)S(1)} %add.19), channel_id=1, source_target_pairs={{0,4},{1,5},{2,6},{3,7},{4,0},{5,1},{6,2},{7,3},{8,12},{9,13},{10,... | collective-permute-start | bytes 3080 | tf_op jit(solution)/shard_map/ppermute | solution.py:244
  33.4 2.0 %collective-permute-done.5 = f32[16,16]{1,0:T(8,128)S(1)} collective-permute-done((f32[16,16]{1,0:T(8,128)S(1)}, f32[16,16]{1,0:T(8,128)S(1)}, u32[]{:S(2)}, u32[]{:S(2)}) %collective-permute-start.5) | collective-permute-done | bytes 1056 | tf_op jit(solution)/shard_map/ppermute | solution.py:244
  35.3 4.3 %collective-permute-done.7.refs_6_ = bf16[64,2944]{1,0:T(8,128)(2,1)S(1)} collective-permute-done((bf16[64,2944]{1,0:T(8,128)(2,1)S(1)}, bf16[64,2944]{1,0:T(8,128)(2,1)S(1)}, u32[]{:S(2)}, u32[]{:S(2)}) %collective-permute-start.7) | collective-permute-done | bytes 376864 | tf_op jit(solution)/shard_map/ppermute | solution.py:232
  39.6 1.5 %pair_sums.1.refs_0_ = f32[32,16]{1,0:T(8,128)S(1)} custom-call(f32[256,256]{1,0:T(8,128)S(1)} %get-tuple-element.28.tile_ref.ov_ref, f32[16,16]{1,0:T(8,128)S(1)} %add.20.s_ref, bf16[64,2944]{1,0:T(8,128)(2,1)S(1)} %get-tuple-element.30.refs_0_.refs_4_, bf16[64,2944]{1,0:T(8,128)(2,1)S(1)} %collective-permute-done.refs_1_.rest_0_.refs_5_, ...), custom_call_target="tpu_custom_call" | custom-call | flops 385875968 | bytes 3014656 | tf_op jit(solution)/shard_map/pair_sums/pallas_call | solution.py:324
  41.1 1.6 %collective-permute-start.11 = (f32[32,16]{1,0:T(8,128)S(1)}, f32[32,16]{1,0:T(8,128)S(1)}, u32[]{:S(2)}, u32[]{:S(2)}) collective-permute-start(f32[32,16]{1,0:T(8,128)S(1)} %pair_sums.1.refs_0_), channel_id=1, source_target_pairs={{0,24},{8,16},{16,8},{24,0},{1,25},{9,17},{17,9},{25,1},{2,26},{10... | collective-permute-start | bytes 6152 | tf_op jit(solution)/shard_map/ppermute | solution.py:232
  42.7 1.5 %collective-permute-start.10 = (f32[32,16]{1,0:T(8,128)S(1)}, f32[32,16]{1,0:T(8,128)S(1)}, u32[]{:S(2)}, u32[]{:S(2)}) collective-permute-start(f32[32,16]{1,0:T(8,128)S(1)} %pair_sums.1.refs_0_), channel_id=1, source_target_pairs={{0,8},{8,0},{16,24},{24,16},{1,9},{9,1},{17,25},{25,17},{2,10},{10... | collective-permute-start | bytes 6152 | tf_op jit(solution)/shard_map/ppermute | solution.py:232
  46.4 1.5 %collective-permute-done.9.refs_1_ = f32[32,16]{1,0:T(8,128)S(1)} collective-permute-done((f32[32,16]{1,0:T(8,128)S(1)}, f32[32,16]{1,0:T(8,128)S(1)}, u32[]{:S(2)}, u32[]{:S(2)}) %collective-permute-start.9) | collective-permute-done | bytes 2080 | tf_op jit(solution)/shard_map/ppermute | solution.py:232
  51.1 1.7 %collective-permute-start.17 = (bf16[64,1536]{1,0:T(8,128)(2,1)S(1)}, bf16[64,1536]{1,0:T(8,128)(2,1)S(1)}, u32[]{:S(2)}, u32[]{:S(2)}) collective-permute-start(bf16[64,1536]{1,0:T(8,128)(2,1)S(1)} %get-tuple-element.43), channel_id=1, source_target_pairs={{0,24},{8,16},{16,8},{24,0},{1,25},{9,17},{17,9},{25,1},{2,26},{10... | collective-permute-start | bytes 589832 | tf_op jit(solution)/shard_map/ppermute | solution.py:232
  54.0 1.6 %collective-permute-start.13 = (f32[32,16]{1,0:T(8,128)S(1)}, f32[32,16]{1,0:T(8,128)S(1)}, u32[]{:S(2)}, u32[]{:S(2)}) collective-permute-start(f32[32,16]{1,0:T(8,128)S(1)} %add.21), channel_id=1, source_target_pairs={{0,2},{1,3},{2,0},{3,1},{4,6},{5,7},{6,4},{7,5},{8,10},{9,11},{10,... | collective-permute-start | bytes 6152 | tf_op jit(solution)/shard_map/ppermute | solution.py:244
  55.6 2.2 %collective-permute-done.13 = f32[32,16]{1,0:T(8,128)S(1)} collective-permute-done((f32[32,16]{1,0:T(8,128)S(1)}, f32[32,16]{1,0:T(8,128)S(1)}, u32[]{:S(2)}, u32[]{:S(2)}) %collective-permute-start.13) | collective-permute-done | bytes 2080 | tf_op jit(solution)/shard_map/ppermute | solution.py:244
  57.8 2.6 %collective-permute-start.14 = (f32[32,16]{1,0:T(8,128)S(1)}, f32[32,16]{1,0:T(8,128)S(1)}, u32[]{:S(2)}, u32[]{:S(2)}) collective-permute-start(f32[32,16]{1,0:T(8,128)S(1)} %add.22), channel_id=1, source_target_pairs={{0,4},{1,5},{2,6},{3,7},{4,0},{5,1},{6,2},{7,3},{8,12},{9,13},{10,... | collective-permute-start | bytes 6152 | tf_op jit(solution)/shard_map/ppermute | solution.py:244
  62.9 2.5 %collective-permute-done.16.refs_9_.refs_6_ = bf16[64,2944]{1,0:T(8,128)(2,1)S(1)} collective-permute-done((bf16[64,2944]{1,0:T(8,128)(2,1)S(1)}, bf16[64,2944]{1,0:T(8,128)(2,1)S(1)}, u32[]{:S(2)}, u32[]{:S(2)}) %collective-permute-start.16) | collective-permute-done | bytes 376864 | tf_op jit(solution)/shard_map/ppermute | solution.py:232
  65.4 1.6 %input_gradient_a.1 = (bf16[64,1536]{1,0:T(8,128)(2,1)S(1)}, bf16[64,1536]{1,0:T(8,128)(2,1)S(1)}, bf16[64,1536]{1,0:T(8,128)(2,1)S(1)}, bf16[64,1536]{1,0:T(8,128)(2,1)S(1)}) custom-call(f32[32,16]{1,0:T(8,128)S(1)} %get-tuple-element.38.s_ref, f32[32,16]{1,0:T(8,128)S(1)} %add.23.p_ref, f32[256,256]{1,0:T(8,128)S(1)} %get-tuple-element.29.tile_ref.rest_1_.qk_ref, ...), custom_call_target="tpu_custom_call" | custom-call | flops 805306368 | bytes 2359296 | tf_op jit(solution)/shard_map/input_gradient_a/pallas_call | solution.py:354
  67.1 2.3 %collective-permute-start.20 = (bf16[64,1536]{1,0:T(8,128)(2,1)S(1)}, bf16[64,1536]{1,0:T(8,128)(2,1)S(1)}, u32[]{:S(2)}, u32[]{:S(2)}) collective-permute-start(bf16[64,1536]{1,0:T(8,128)(2,1)S(1)} %get-tuple-element.48), channel_id=1, source_target_pairs={{0,16},{8,24},{16,0},{24,8},{1,17},{9,25},{17,1},{25,9},{2,18},{10... | collective-permute-start | bytes 589832 | tf_op jit(solution)/shard_map/ppermute | solution.py:232
  70.5 1.6 %input_gradient_b.1 = (bf16[64,1408]{1,0:T(8,128)(2,1)S(1)}, bf16[64,1408]{1,0:T(8,128)(2,1)S(1)}, bf16[64,1408]{1,0:T(8,128)(2,1)S(1)}, bf16[64,1408]{1,0:T(8,128)(2,1)S(1)}) custom-call(f32[32,16]{1,0:T(8,128)S(1)} %get-tuple-element.38.s_ref, f32[32,16]{1,0:T(8,128)S(1)} %add.23.p_ref, f32[256,256]{1,0:T(8,128)S(1)} %get-tuple-element.29.tile_ref.rest_1_.qk_ref, ...), custom_call_target="tpu_custom_call" | custom-call | flops 738197504 | bytes 2162688 | tf_op jit(solution)/shard_map/input_gradient_b/pallas_call | solution.py:354
  72.5 2.0 %collective-permute-start.23 = (bf16[64,1408]{1,0:T(8,128)(2,1)S(1)}, bf16[64,1408]{1,0:T(8,128)(2,1)S(1)}, u32[]{:S(2)}, u32[]{:S(2)}) collective-permute-start(bf16[64,1408]{1,0:T(8,128)(2,1)S(1)} %get-tuple-element.52), channel_id=1, source_target_pairs={{0,16},{8,24},{16,0},{24,8},{1,17},{9,25},{17,1},{25,9},{2,18},{10... | collective-permute-start | bytes 540680 | tf_op jit(solution)/shard_map/ppermute | solution.py:232
  74.9 1.7 %collective-permute-start.24 = (bf16[64,1408]{1,0:T(8,128)(2,1)S(1)}, bf16[64,1408]{1,0:T(8,128)(2,1)S(1)}, u32[]{:S(2)}, u32[]{:S(2)}) collective-permute-start(bf16[64,1408]{1,0:T(8,128)(2,1)S(1)} %get-tuple-element.53), channel_id=1, source_target_pairs={{0,24},{8,16},{16,8},{24,0},{1,25},{9,17},{17,9},{25,1},{2,26},{10... | collective-permute-start | bytes 540680 | tf_op jit(solution)/shard_map/ppermute | solution.py:232
  76.6 1.7 %updated.1 = f32[64,11520]{1,0:T(8,128)} custom-call(bf16[64,1536]{1,0:T(8,128)(2,1)S(1)} %collective-permute-done.18.dep_ref.refs_5_, bf16[64,2944]{1,0:T(8,128)(2,1)S(1)} %get-tuple-element.30.refs_0_.refs_4_, bf16[64,2944]{1,0:T(8,128)(2,1)S(1)} %get-tuple-element.31.refs_1_, bf16[64,2944]{1,0:T(8,128)(2,1)S(1)} %get-tuple-element.32.refs_2_, ...), custom_call_target="tpu_custom_call" | custom-call | flops 737280 | bytes 5898240 | tf_op jit(solution)/shard_map/updated/pallas_call | solution.py:374
  78.3 1.7 %collective-permute-done.22.refs_9_ = bf16[64,1408]{1,0:T(8,128)(2,1)S(1)} collective-permute-done((bf16[64,1408]{1,0:T(8,128)(2,1)S(1)}, bf16[64,1408]{1,0:T(8,128)(2,1)S(1)}, u32[]{:S(2)}, u32[]{:S(2)}) %collective-permute-start.22) | collective-permute-done | bytes 180256 | tf_op jit(solution)/shard_map/ppermute | solution.py:232
  81.1 1.9 %collective-permute-done.24.refs_11_ = bf16[64,1408]{1,0:T(8,128)(2,1)S(1)} collective-permute-done((bf16[64,1408]{1,0:T(8,128)(2,1)S(1)}, bf16[64,1408]{1,0:T(8,128)(2,1)S(1)}, u32[]{:S(2)}, u32[]{:S(2)}) %collective-permute-start.24) | collective-permute-done | bytes 180256 | tf_op jit(solution)/shard_map/ppermute | solution.py:232
  83.0 1.7 %ensemble_grad.1 = f32[64,11520]{1,0:T(8,128)} custom-call(bf16[64,1536]{1,0:T(8,128)(2,1)S(1)} %get-tuple-element.47.dep_ref.refs_4_, bf16[64,2944]{1,0:T(8,128)(2,1)S(1)} %get-tuple-element.34.refs_4_.refs_0_, bf16[64,2944]{1,0:T(8,128)(2,1)S(1)} %get-tuple-element.35.refs_1_, bf16[64,2944]{1,0:T(8,128)(2,1)S(1)} %get-tuple-element.36.refs_2_, ...), custom_call_target="tpu_custom_call" | custom-call | flops 737280 | bytes 5898240 | tf_op jit(solution)/shard_map/ensemble_grad/pallas_call | solution.py:374
  (46 shorter events, 18.5 us)
Async XLA Ops:
  0.6 1.4 %copy-start = (bf16[4,16,11520]{2,1,0:T(8,128)(2,1)S(1)}, bf16[4,16,11520]{2,1,0:T(8,128)(2,1)}, u32[]{:S(2)}) copy-start(bf16[4,16,11520]{2,1,0:T(8,128)(2,1)} %param.6) | copy-start | bytes 4423684
  2.2 12.6 %collective-permute-start = (bf16[64,2944]{1,0:T(8,128)(2,1)S(1)}, bf16[64,2944]{1,0:T(8,128)(2,1)S(1)}, u32[]{:S(2)}, u32[]{:S(2)}) collective-permute-start(bf16[64,2944]{1,0:T(8,128)(2,1)S(1)} %get-tuple-element.31.refs_1_), channel_id=1, source_target_pairs={{0,8},{8,0},{16,24},{24,16},{1,9},{9,1},{17,25},{25,17},{2,10},{10... | collective-permute-start | bytes 1130504 | tf_op jit(solution)/shard_map/ppermute | solution.py:232
  5.2 18.7 %collective-permute-start.1 = (bf16[64,2944]{1,0:T(8,128)(2,1)S(1)}, bf16[64,2944]{1,0:T(8,128)(2,1)S(1)}, u32[]{:S(2)}, u32[]{:S(2)}) collective-permute-start(bf16[64,2944]{1,0:T(8,128)(2,1)S(1)} %get-tuple-element.32.refs_2_), channel_id=1, source_target_pairs={{0,16},{8,24},{16,0},{24,8},{1,17},{9,25},{17,1},{25,9},{2,18},{10... | collective-permute-start | bytes 1130504 | tf_op jit(solution)/shard_map/ppermute | solution.py:232
  6.7 17.7 %collective-permute-start.2 = (bf16[64,2944]{1,0:T(8,128)(2,1)S(1)}, bf16[64,2944]{1,0:T(8,128)(2,1)S(1)}, u32[]{:S(2)}, u32[]{:S(2)}) collective-permute-start(bf16[64,2944]{1,0:T(8,128)(2,1)S(1)} %get-tuple-element.33.refs_3_), channel_id=1, source_target_pairs={{0,24},{8,16},{16,8},{24,0},{1,25},{9,17},{17,9},{25,1},{2,26},{10... | collective-permute-start | bytes 1130504 | tf_op jit(solution)/shard_map/ppermute | solution.py:232
  6.7 0.7 copy-start.2
  7.4 0.7 copy-start.3
  8.1 0.7 copy-start.4
  8.8 0.7 copy-start.5
  14.8 1.4 %copy-start.1 = (bf16[4,16,11520]{2,1,0:T(8,128)(2,1)S(1)}, bf16[4,16,11520]{2,1,0:T(8,128)(2,1)}, u32[]{:S(2)}) copy-start(bf16[4,16,11520]{2,1,0:T(8,128)(2,1)} %param.7) | copy-start | bytes 4423684
  16.4 19.0 %collective-permute-start.6 = (bf16[64,2944]{1,0:T(8,128)(2,1)S(1)}, bf16[64,2944]{1,0:T(8,128)(2,1)S(1)}, u32[]{:S(2)}, u32[]{:S(2)}) collective-permute-start(bf16[64,2944]{1,0:T(8,128)(2,1)S(1)} %get-tuple-element.35.refs_1_), channel_id=1, source_target_pairs={{0,8},{8,0},{16,24},{24,16},{1,9},{9,1},{17,25},{25,17},{2,10},{10... | collective-permute-start | bytes 1130504 | tf_op jit(solution)/shard_map/ppermute | solution.py:232
  18.5 21.2 %collective-permute-start.7 = (bf16[64,2944]{1,0:T(8,128)(2,1)S(1)}, bf16[64,2944]{1,0:T(8,128)(2,1)S(1)}, u32[]{:S(2)}, u32[]{:S(2)}) collective-permute-start(bf16[64,2944]{1,0:T(8,128)(2,1)S(1)} %get-tuple-element.36.refs_2_), channel_id=1, source_target_pairs={{0,16},{8,24},{16,0},{24,8},{1,17},{9,25},{17,1},{25,9},{2,18},{10... | collective-permute-start | bytes 1130504 | tf_op jit(solution)/shard_map/ppermute | solution.py:232
  20.0 19.7 %collective-permute-start.8 = (bf16[64,2944]{1,0:T(8,128)(2,1)S(1)}, bf16[64,2944]{1,0:T(8,128)(2,1)S(1)}, u32[]{:S(2)}, u32[]{:S(2)}) collective-permute-start(bf16[64,2944]{1,0:T(8,128)(2,1)S(1)} %get-tuple-element.37.refs_3_), channel_id=1, source_target_pairs={{0,24},{8,16},{16,8},{24,0},{1,25},{9,17},{17,9},{25,1},{2,26},{10... | collective-permute-start | bytes 1130504 | tf_op jit(solution)/shard_map/ppermute | solution.py:232
  25.9 1.2 %collective-permute-start.3 = (f32[16,16]{1,0:T(8,128)S(1)}, f32[16,16]{1,0:T(8,128)S(1)}, u32[]{:S(2)}, u32[]{:S(2)}) collective-permute-start(f32[16,16]{1,0:T(8,128)S(1)} %score_sums.1), channel_id=1, source_target_pairs={{0,1},{1,0},{2,3},{3,2},{4,5},{5,4},{6,7},{7,6},{8,9},{9,8},{10,11... | collective-permute-start | bytes 3080 | tf_op jit(solution)/shard_map/ppermute | solution.py:244
  27.1 3.7 %collective-permute-start.4 = (f32[16,16]{1,0:T(8,128)S(1)}, f32[16,16]{1,0:T(8,128)S(1)}, u32[]{:S(2)}, u32[]{:S(2)}) collective-permute-start(f32[16,16]{1,0:T(8,128)S(1)} %add.18), channel_id=1, source_target_pairs={{0,2},{1,3},{2,0},{3,1},{4,6},{5,7},{6,4},{7,5},{8,10},{9,11},{10,... | collective-permute-start | bytes 3080 | tf_op jit(solution)/shard_map/ppermute | solution.py:244
  30.8 4.5 %collective-permute-start.5 = (f32[16,16]{1,0:T(8,128)S(1)}, f32[16,16]{1,0:T(8,128)S(1)}, u32[]{:S(2)}, u32[]{:S(2)}) collective-permute-start(f32[16,16]{1,0:T(8,128)S(1)} %add.19), channel_id=1, source_target_pairs={{0,4},{1,5},{2,6},{3,7},{4,0},{5,1},{6,2},{7,3},{8,12},{9,13},{10,... | collective-permute-start | bytes 3080 | tf_op jit(solution)/shard_map/ppermute | solution.py:244
  41.1 4.7 %collective-permute-start.11 = (f32[32,16]{1,0:T(8,128)S(1)}, f32[32,16]{1,0:T(8,128)S(1)}, u32[]{:S(2)}, u32[]{:S(2)}) collective-permute-start(f32[32,16]{1,0:T(8,128)S(1)} %pair_sums.1.refs_0_), channel_id=1, source_target_pairs={{0,24},{8,16},{16,8},{24,0},{1,25},{9,17},{17,9},{25,1},{2,26},{10... | collective-permute-start | bytes 6152 | tf_op jit(solution)/shard_map/ppermute | solution.py:232
  42.7 3.7 %collective-permute-start.10 = (f32[32,16]{1,0:T(8,128)S(1)}, f32[32,16]{1,0:T(8,128)S(1)}, u32[]{:S(2)}, u32[]{:S(2)}) collective-permute-start(f32[32,16]{1,0:T(8,128)S(1)} %pair_sums.1.refs_0_), channel_id=1, source_target_pairs={{0,8},{8,0},{16,24},{24,16},{1,9},{9,1},{17,25},{25,17},{2,10},{10... | collective-permute-start | bytes 6152 | tf_op jit(solution)/shard_map/ppermute | solution.py:232
  44.2 3.7 %collective-permute-start.9 = (f32[32,16]{1,0:T(8,128)S(1)}, f32[32,16]{1,0:T(8,128)S(1)}, u32[]{:S(2)}, u32[]{:S(2)}) collective-permute-start(f32[32,16]{1,0:T(8,128)S(1)} %pair_sums.1.refs_0_), channel_id=1, source_target_pairs={{0,16},{8,24},{16,0},{24,8},{1,17},{9,25},{17,1},{25,9},{2,18},{10... | collective-permute-start | bytes 6152 | tf_op jit(solution)/shard_map/ppermute | solution.py:232
  49.3 13.6 %collective-permute-start.15 = (bf16[64,2944]{1,0:T(8,128)(2,1)S(1)}, bf16[64,2944]{1,0:T(8,128)(2,1)S(1)}, u32[]{:S(2)}, u32[]{:S(2)}) collective-permute-start(bf16[64,2944]{1,0:T(8,128)(2,1)S(1)} %get-tuple-element.41), channel_id=1, source_target_pairs={{0,8},{8,0},{16,24},{24,16},{1,9},{9,1},{17,25},{25,17},{2,10},{10... | collective-permute-start | bytes 1130504 | tf_op jit(solution)/shard_map/ppermute | solution.py:232
  49.9 15.5 %collective-permute-start.16 = (bf16[64,2944]{1,0:T(8,128)(2,1)S(1)}, bf16[64,2944]{1,0:T(8,128)(2,1)S(1)}, u32[]{:S(2)}, u32[]{:S(2)}) collective-permute-start(bf16[64,2944]{1,0:T(8,128)(2,1)S(1)} %get-tuple-element.42), channel_id=1, source_target_pairs={{0,16},{8,24},{16,0},{24,8},{1,17},{9,25},{17,1},{25,9},{2,18},{10... | collective-permute-start | bytes 1130504 | tf_op jit(solution)/shard_map/ppermute | solution.py:232
  51.1 11.8 %collective-permute-start.17 = (bf16[64,1536]{1,0:T(8,128)(2,1)S(1)}, bf16[64,1536]{1,0:T(8,128)(2,1)S(1)}, u32[]{:S(2)}, u32[]{:S(2)}) collective-permute-start(bf16[64,1536]{1,0:T(8,128)(2,1)S(1)} %get-tuple-element.43), channel_id=1, source_target_pairs={{0,24},{8,16},{16,8},{24,0},{1,25},{9,17},{17,9},{25,1},{2,26},{10... | collective-permute-start | bytes 589832 | tf_op jit(solution)/shard_map/ppermute | solution.py:232
  52.8 1.2 %collective-permute-start.12 = (f32[32,16]{1,0:T(8,128)S(1)}, f32[32,16]{1,0:T(8,128)S(1)}, u32[]{:S(2)}, u32[]{:S(2)}) collective-permute-start(f32[32,16]{1,0:T(8,128)S(1)} %get-tuple-element.38.s_ref), channel_id=1, source_target_pairs={{0,1},{1,0},{2,3},{3,2},{4,5},{5,4},{6,7},{7,6},{8,9},{9,8},{10,11... | collective-permute-start | bytes 6152 | tf_op jit(solution)/shard_map/ppermute | solution.py:244
  54.0 3.7 %collective-permute-start.13 = (f32[32,16]{1,0:T(8,128)S(1)}, f32[32,16]{1,0:T(8,128)S(1)}, u32[]{:S(2)}, u32[]{:S(2)}) collective-permute-start(f32[32,16]{1,0:T(8,128)S(1)} %add.21), channel_id=1, source_target_pairs={{0,2},{1,3},{2,0},{3,1},{4,6},{5,7},{6,4},{7,5},{8,10},{9,11},{10,... | collective-permute-start | bytes 6152 | tf_op jit(solution)/shard_map/ppermute | solution.py:244
  57.8 4.6 %collective-permute-start.14 = (f32[32,16]{1,0:T(8,128)S(1)}, f32[32,16]{1,0:T(8,128)S(1)}, u32[]{:S(2)}, u32[]{:S(2)}) collective-permute-start(f32[32,16]{1,0:T(8,128)S(1)} %add.22), channel_id=1, source_target_pairs={{0,4},{1,5},{2,6},{3,7},{4,0},{5,1},{6,2},{7,3},{8,12},{9,13},{10,... | collective-permute-start | bytes 6152 | tf_op jit(solution)/shard_map/ppermute | solution.py:244
  60.3 10.2 %collective-permute-start.19 = (bf16[64,1408]{1,0:T(8,128)(2,1)S(1)}, bf16[64,1408]{1,0:T(8,128)(2,1)S(1)}, u32[]{:S(2)}, u32[]{:S(2)}) collective-permute-start(bf16[64,1408]{1,0:T(8,128)(2,1)S(1)} %get-tuple-element.46), channel_id=1, source_target_pairs={{0,24},{8,16},{16,8},{24,0},{1,25},{9,17},{17,9},{25,1},{2,26},{10... | collective-permute-start | bytes 540680 | tf_op jit(solution)/shard_map/ppermute | solution.py:232
  67.0 7.9 %collective-permute-start.18 = (bf16[64,1536]{1,0:T(8,128)(2,1)S(1)}, bf16[64,1536]{1,0:T(8,128)(2,1)S(1)}, u32[]{:S(2)}, u32[]{:S(2)}) collective-permute-start(bf16[64,1536]{1,0:T(8,128)(2,1)S(1)} %get-tuple-element.44), channel_id=1, source_target_pairs={{0,8},{8,0},{16,24},{24,16},{1,9},{9,1},{17,25},{25,17},{2,10},{10... | collective-permute-start | bytes 589832 | tf_op jit(solution)/shard_map/ppermute | solution.py:232
  67.1 16.0 %collective-permute-start.20 = (bf16[64,1536]{1,0:T(8,128)(2,1)S(1)}, bf16[64,1536]{1,0:T(8,128)(2,1)S(1)}, u32[]{:S(2)}, u32[]{:S(2)}) collective-permute-start(bf16[64,1536]{1,0:T(8,128)(2,1)S(1)} %get-tuple-element.48), channel_id=1, source_target_pairs={{0,16},{8,24},{16,0},{24,8},{1,17},{9,25},{17,1},{25,9},{2,18},{10... | collective-permute-start | bytes 589832 | tf_op jit(solution)/shard_map/ppermute | solution.py:232
  69.4 13.7 %collective-permute-start.21 = (bf16[64,1536]{1,0:T(8,128)(2,1)S(1)}, bf16[64,1536]{1,0:T(8,128)(2,1)S(1)}, u32[]{:S(2)}, u32[]{:S(2)}) collective-permute-start(bf16[64,1536]{1,0:T(8,128)(2,1)S(1)} %get-tuple-element.49), channel_id=1, source_target_pairs={{0,24},{8,16},{16,8},{24,0},{1,25},{9,17},{17,9},{25,1},{2,26},{10... | collective-permute-start | bytes 589832 | tf_op jit(solution)/shard_map/ppermute | solution.py:232
  72.2 7.9 %collective-permute-start.22 = (bf16[64,1408]{1,0:T(8,128)(2,1)S(1)}, bf16[64,1408]{1,0:T(8,128)(2,1)S(1)}, u32[]{:S(2)}, u32[]{:S(2)}) collective-permute-start(bf16[64,1408]{1,0:T(8,128)(2,1)S(1)} %get-tuple-element.51), channel_id=1, source_target_pairs={{0,8},{8,0},{16,24},{24,16},{1,9},{9,1},{17,25},{25,17},{2,10},{10... | collective-permute-start | bytes 540680 | tf_op jit(solution)/shard_map/ppermute | solution.py:232
  72.5 8.6 %collective-permute-start.23 = (bf16[64,1408]{1,0:T(8,128)(2,1)S(1)}, bf16[64,1408]{1,0:T(8,128)(2,1)S(1)}, u32[]{:S(2)}, u32[]{:S(2)}) collective-permute-start(bf16[64,1408]{1,0:T(8,128)(2,1)S(1)} %get-tuple-element.52), channel_id=1, source_target_pairs={{0,16},{8,24},{16,0},{24,8},{1,17},{9,25},{17,1},{25,9},{2,18},{10... | collective-permute-start | bytes 540680 | tf_op jit(solution)/shard_map/ppermute | solution.py:232
  74.9 8.2 %collective-permute-start.24 = (bf16[64,1408]{1,0:T(8,128)(2,1)S(1)}, bf16[64,1408]{1,0:T(8,128)(2,1)S(1)}, u32[]{:S(2)}, u32[]{:S(2)}) collective-permute-start(bf16[64,1408]{1,0:T(8,128)(2,1)S(1)} %get-tuple-element.53), channel_id=1, source_target_pairs={{0,24},{8,16},{16,8},{24,0},{1,25},{9,17},{17,9},{25,1},{2,26},{10... | collective-permute-start | bytes 540680 | tf_op jit(solution)/shard_map/ppermute | solution.py:232

commit v3 on v2

--- a/solution.py
+++ b/solution.py
@@ -33,23 +33,6 @@
 
 def half_of(chunk):
     return -(-chunk // (2 * LANES)) * LANES
-
-
-def whole_pieces(count, chunk):
-    return [(s, 0, chunk) for s in range(count)]
-
-
-def last_cut(count, chunk):
-    pieces = whole_pieces(count, chunk)
-    half = half_of(chunk)
-    return pieces[:-1] + [(count - 1, 0, half), (count - 1, half, chunk - half)]
-
-
-def store_pieces(outs, pieces, value, at, width, per):
-    for out, (s, low, size) in zip(outs, pieces):
-        a, b = max(at, low), min(at + width, low + size)
-        if a < b:
-            out[:, a - low:b - low] = value[s * per:(s + 1) * per, a - at:b - at]
 
 
 def member_of_row(me, rows, channels, members, group):
@@ -108,12 +91,14 @@
 def masked_gram(me, count, chunk, length, left, right):
     rows = count * right[0].shape[0]
     skip = me * chunk - chunk_start(me, chunk, length)
+    most = max(0, count * chunk - length)
     total = jnp.zeros((rows, rows), jnp.float32)
     for at, width in lane_tiles(chunk):
         b = gather_tile(right, at, width)
         a = b if left is right else gather_tile(left, at, width)
-        lane = lax.broadcasted_iota(jnp.int32, (rows, width), 1) + at
-        a = jnp.where(lane >= skip, a.astype(jnp.float32), 0.0).astype(jnp.bfloat16)
+        if at < most:
+            lane = lax.broadcasted_iota(jnp.int32, (rows, width), 1) + at
+            a = jnp.where(lane >= skip, a.astype(jnp.float32), 0.0).astype(jnp.bfloat16)
         total = total + mm(a, b, ((1,), (1,)))
     return total
 
@@ -127,14 +112,21 @@
     out_ref[...] = fold(total * tile_ref[...], picks)
 
 
-def pair_kernel(me_of, count, chunk, length, group, channels, members, tile_ref, s_ref, *refs):
+def pair_kernel(me_of, count, chunk, length, group, channels, members, tile_ref, *refs):
     me = me_of()
     fields, grads, out_ref = refs[:count], refs[count:2 * count], refs[-1]
     rows = count * fields[0].shape[0]
     total = masked_gram(me, count, chunk, length, grads, fields)
     picks = member_of_row(me, rows, channels, members, group)
-    out_ref[:members, :] = s_ref[...]
-    out_ref[members:, :] = fold(total * tile_ref[...], picks)
+    out_ref[...] = fold(total * tile_ref[...], picks)
+
+
+def add_up(refs):
+    return functools.reduce(jnp.add, [r[...] for r in refs])
+
+
+def join_kernel(a_ref, b_ref, *refs):
+    refs[-1][...] = a_ref[...] + b_ref[...]
 
 
 def softmax(scores):
@@ -159,37 +151,37 @@
 
 
 def branch_kernel(
-    me_of, count, chunk, group, channels, members, scale, pieces, ov_ref, *refs
+    me_of, count, chunk, group, channels, members, scale, waits, ov_ref, *refs
 ):
     me = me_of()
     sums, fields = refs[:count], refs[count:2 * count]
-    total_ref, outs = refs[2 * count], refs[2 * count + 1:]
+    total_ref, outs = refs[2 * count + waits], refs[2 * count + waits + 1:]
     per = fields[0].shape[0]
     rows = count * per
-    total = sums[0][...]
-    for other in sums[1:]:
-        total = total + other[...]
+    total = add_up(sums)
     total_ref[...] = total
     picks = member_of_row(me, rows, channels, members, group).astype(jnp.bfloat16)
-    weights = softmax(total[:members, :] * scale)
+    weights = softmax(total * scale)
     high, low = two_parts(spread(weights, picks) * ov_ref[...])
     for at, width in lane_tiles(chunk):
         e = gather_tile(fields, at, width)
         b = (mm(high, e, ((1,), (0,))) + mm(low, e, ((1,), (0,)))).astype(jnp.bfloat16)
-        store_pieces(outs, pieces, b, at, width, per)
+        for s in range(count):
+            outs[s][:, at:at + width] = b[s * per:(s + 1) * per]
 
 
 def grad_kernel(
     me_of, count, chunk, group, channels, members, scale, low, size, waits,
-    s_ref, p_ref, qk_ref, qkt_ref, ovt_ref, *refs,
+    s_ref, qk_ref, qkt_ref, ovt_ref, *refs,
 ):
     me = me_of()
-    fields, grads, outs = refs[:count], refs[count:2 * count], refs[2 * count + waits:]
+    fields, grads, sums = refs[:count], refs[count:2 * count], refs[2 * count:3 * count]
+    outs = refs[3 * count + waits:]
     per = fields[0].shape[0]
     rows = count * per
     picks = member_of_row(me, rows, channels, members, group).astype(jnp.bfloat16)
-    weights = softmax(s_ref[:members, :] * scale)
-    pairs = p_ref[members:, :]
+    weights = softmax(s_ref[...] * scale)
+    pairs = add_up(sums)
     slope = weights * (pairs - jnp.sum(weights * pairs, axis=1, keepdims=True)) * scale
     d_high, d_low = two_parts(
         spread(slope, picks) * qk_ref[...] + spread_t(slope, picks) * qkt_ref[...]
@@ -206,36 +198,38 @@
             outs[s][:, at:at + width] = b[s * per:(s + 1) * per]
 
 
-def finish_kernel(me_of, count, chunk, length, pieces, dep_ref, *refs):
-    me = me_of()
-    base, extra = refs[:count], refs[count:count + len(pieces)]
-    out_ref, held, sem = refs[count + len(pieces):]
-    per = base[0].shape[0]
-    rows = 16
-    copies = []
-    for at in range(0, per, rows):
-        for more, (s, low, size) in zip(extra, pieces):
-            start = chunk_start(partner(me, s), chunk, length) + low
-            held[at:at + rows, pl.ds(pl.multiple_of(start, LANES), size)] = base[s][
-                at:at + rows, low:low + size
-            ].astype(jnp.float32) + more[at:at + rows, :].astype(jnp.float32)
-        copy = pltpu.make_async_copy(
-            held.at[at:at + rows], out_ref.at[at:at + rows], sem.at[at // rows]
-        )
-        copy.start()
-        copies.append(copy)
-    for copy in copies:
-        copy.wait()
+def finish_kernel(me_of, count, chunk, length, stages, serial, waits, extras, *refs):
+    me = me_of()
+    base, extra = refs[waits:waits + count], refs[waits + count:waits + count + extras]
+    out_ref, held, sem = refs[waits + count + extras:]
+    slot = 0
+    for stage in stages:
+        copies = []
+        for s, low, size, index, start in stage:
+            held[slot, :, :size] = base[s][:, low:low + size].astype(jnp.float32) + extra[
+                index
+            ][:, start:start + size].astype(jnp.float32)
+            place = pl.multiple_of(chunk_start(partner(me, s), chunk, length) + low, LANES)
+            copy = pltpu.make_async_copy(
+                held.at[slot, :, pl.ds(0, size)], out_ref.at[:, pl.ds(place, size)], sem.at[slot]
+            )
+            copy.start()
+            if serial:
+                copy.wait()
+            copies.append(copy)
+            slot += 1
+        if not serial:
+            for copy in copies:
+                copy.wait()
 
 
 def swap(value, step, count):
     return lax.ppermute(value, "mem", [(i, i ^ step) for i in range(count)])
 
 
-def exchange(parts, pieces, count):
-    return [
-        part if s == 0 else swap(part, s, count) for part, (s, _, _) in zip(parts, pieces)
-    ]
+def exchange(parts):
+    count = len(parts)
+    return [part if s == 0 else swap(part, s, count) for s, part in enumerate(parts)]
 
 
 def sum_steps(value, name, steps):
@@ -266,7 +260,7 @@
     whole = pl.BlockSpec(memory_space=VMEM)
     anywhere = pl.BlockSpec(memory_space=pl.ANY)
     in_hbm = pl.BlockSpec(memory_space=pltpu.MemorySpace.HBM)
-    params = pltpu.CompilerParams(vmem_limit_bytes=40 * 1024 * 1024)
+    params = pltpu.CompilerParams(vmem_limit_bytes=16 * 1024 * 1024 + 24 * rows * rows)
     part = jax.ShapeDtypeStruct((per, chunk), bf)
     square = jax.ShapeDtypeStruct((rows, rows), f32)
     pair = jax.ShapeDtypeStruct((members, members), f32)
@@ -277,11 +271,6 @@
         return pl.CostEstimate(flops=flops, bytes_accessed=moved, transcendentals=0)
 
     first = min(1, count - 1)
-    plain = whole_pieces(count, chunk)
-    cut = last_cut(count, chunk)
-
-    def shapes(pieces):
-        return [jax.ShapeDtypeStruct((per, size), bf) for _, _, size in pieces]
 
     def split(operands, name):
         return pl.pallas_call(
@@ -295,7 +284,7 @@
         )(*operands)
 
     e_mine = split([fields], "split_fields")
-    e_cells = exchange(e_mine, plain, count)
+    e_cells = exchange(e_mine)
     qk, qkt, ov, ovt = pl.pallas_call(
         functools.partial(tiles_kernel, rows, channels),
         out_shape=[square] * 4,
@@ -306,8 +295,21 @@
         name="weight_tiles",
     )(w_query, w_key, w_value, w_out)
     c_mine = split([grads, e_cells[first], qk], "split_grads")
-    c_cells = exchange(c_mine, plain, count)
+    c_cells = exchange(c_mine)
     space_steps = doubling(lax.axis_size("space"))
+
+    def join(value, name, step, waited):
+        size = lax.axis_size(name)
+        other = lax.ppermute(value, name, [(i, i ^ step) for i in range(size)])
+        return pl.pallas_call(
+            join_kernel,
+            out_shape=pair,
+            in_specs=[whole] * 2 + [anywhere] * len(waited),
+            out_specs=whole,
+            compiler_params=params,
+            cost_estimate=cost(members * members, 12 * members * members),
+            name="join_sums",
+        )(value, other, *waited)
 
     scores = pl.pallas_call(
         functools.partial(
@@ -320,35 +322,39 @@
         cost_estimate=cost(2 * rows * rows * chunk, 2 * rows * chunk),
         name="score_sums",
     )(qk, *e_cells)
-    scores = sum_steps(scores, "space", space_steps)
-    both = pl.pallas_call(
+    scores = sum_steps(scores, "space", space_steps[:-1])
+    scores = join(scores, "space", space_steps[-1], c_cells[first:first + 1])
+    order = sorted(range(1, count), key=lambda s: (s & (s - 1) != 0, -s))
+    score_parts = [scores] + [swap(scores, s, count) for s in order]
+    waited = score_parts[:1]
+    pairs = pl.pallas_call(
         functools.partial(
             pair_kernel, me_of, count, chunk, length, group, channels, members
         ),
-        out_shape=jax.ShapeDtypeStruct((2 * members, members), f32),
-        in_specs=[whole] * (2 * count + 2),
+        out_shape=pair,
+        in_specs=[whole] * (2 * count + 1) + [anywhere] * len(waited),
         out_specs=whole,
         compiler_params=params,
         cost_estimate=cost(2 * rows * rows * chunk, 4 * rows * chunk),
         name="pair_sums",
-    )(ov, scores, *e_cells, *c_cells)
-    order = sorted(range(1, count), key=lambda s: (s & (s - 1) != 0, -s))
-    sums = [both] + [swap(both, s, count) for s in order]
-
+    )(ov, *e_cells, *c_cells, *waited)
+    ahead = [pairs]
     outcome = pl.pallas_call(
         functools.partial(
-            branch_kernel, me_of, count, chunk, group, channels, members, scale, cut
+            branch_kernel, me_of, count, chunk, group, channels, members, scale, len(ahead),
         ),
-        out_shape=[jax.ShapeDtypeStruct((2 * members, members), f32)] + shapes(cut),
-        in_specs=[whole] * (2 * count + 1),
-        out_specs=[whole] * (len(cut) + 1),
+        out_shape=[pair] + [part] * count,
+        in_specs=[whole] * (2 * count + 1) + [anywhere] * len(ahead),
+        out_specs=[whole] * (count + 1),
         compiler_params=params,
         cost_estimate=cost(4 * rows * rows * chunk, 4 * rows * chunk),
         name="branch",
-    )(ov, *sums, *e_cells)
-    mem_sums, branch = outcome[0], outcome[1:]
-    pairs = sum_steps(mem_sums, "space", space_steps)
-    branch_home = exchange(branch, cut, count)
+    )(ov, *score_parts, *e_cells, *ahead)
+    scores, branch = outcome[0], outcome[1:]
+    branch_home = exchange(branch)
+    pairs = sum_steps(pairs, "space", space_steps[:-1])
+    pairs = join(pairs, "space", space_steps[-1], branch_home[first:first + 1])
+    pair_parts = [pairs] + [swap(pairs, s, count) for s in order]
 
     def gradient(low, size, awaited, name):
         parts = pl.pallas_call(
@@ -357,39 +363,60 @@
                 size, len(awaited),
             ),
             out_shape=[jax.ShapeDtypeStruct((per, size), bf)] * count,
-            in_specs=[whole] * (2 * count + 5) + [anywhere] * len(awaited),
+            in_specs=[whole] * (3 * count + 4) + [anywhere] * len(awaited),
             out_specs=[whole] * count,
             compiler_params=params,
             cost_estimate=cost(8 * rows * rows * size, 6 * rows * size),
             name=name,
-        )(mem_sums, pairs, qk, qkt, ovt, *e_cells, *c_cells, *awaited)
-        pieces = [(s, low, size) for s in range(count)]
-        return pieces, exchange(parts, pieces, count)
+        )(scores, qk, qkt, ovt, *e_cells, *c_cells, *pair_parts, *awaited)
+        return exchange(parts)
 
     half = half_of(chunk)
-    pieces_a, grad_a = gradient(0, half, branch_home[1:-1], "input_gradient_a")
-    pieces_b, grad_b = gradient(half, chunk - half, branch_home[-1:], "input_gradient_b")
-
-    def finish(base, extra, pieces, after, name):
+    grad_a = gradient(0, half, branch_home[1:], "input_gradient_a")
+    grad_b = gradient(half, chunk - half, branch_home[1:], "input_gradient_b")
+
+    rest = chunk - half
+    serial = count * chunk - length > rest
+
+    def finish(base, extra, stages, before, after, name):
+        slots = sum(len(stage) for stage in stages)
+        waited = list(before) + list(after)
         return pl.pallas_call(
-            functools.partial(finish_kernel, me_of, count, chunk, length, pieces),
+            functools.partial(
+                finish_kernel, me_of, count, chunk, length, stages, serial, len(waited),
+                len(extra),
+            ),
             out_shape=jax.ShapeDtypeStruct((per, length), f32),
-            in_specs=[anywhere] + [whole] * (count + len(pieces)),
+            in_specs=[anywhere] * len(waited) + [whole] * (count + len(extra)),
             out_specs=in_hbm,
             scratch_shapes=[
-                pltpu.VMEM((per, length), f32),
-                pltpu.SemaphoreType.DMA((per // 16,)),
+                pltpu.VMEM((slots, per, half), f32),
+                pltpu.SemaphoreType.DMA((slots,)),
             ],
+            input_output_aliases={0: 0} if before else {},
             compiler_params=params,
             cost_estimate=cost(per * length, 8 * per * length),
             name=name,
-        )(after, *base, *extra).reshape(group, channels, length)
-
-    updated = finish(e_mine, branch_home, cut, grad_a[first], "updated")
+        )(*waited, *base, *extra)
+
+    steps = list(range(count))
+    updated = finish(
+        e_mine, branch_home,
+        [[(s, 0, half, s, 0) for s in steps], [(s, half, rest, s, half) for s in steps]],
+        [], [grad_a[first]], "updated",
+    )
     ensemble_grad = finish(
-        c_mine, grad_a + grad_b, pieces_a + pieces_b, grad_a[0], "ensemble_grad"
+        c_mine, grad_a + grad_b[:1],
+        [[(s, 0, half, s, 0) for s in steps], [(0, half, rest, count, 0)]],
+        [], [], "ensemble_grad_early",
     )
-    return (updated, ensemble_grad)
+    if count > 1:
+        ensemble_grad = finish(
+            c_mine, grad_b[1:], [[(s, half, rest, s - 1, 0) for s in steps[1:]]],
+            [ensemble_grad], [], "ensemble_grad_late",
+        )
+    shape = (group, channels, length)
+    return (updated.reshape(shape), ensemble_grad.reshape(shape))
 
 
 def solution(mesh):

time: 85.1 us -> 83.9 us (0.986)
  waiting for transfers between devices: 33.3 us -> 29.5 us
  Pallas kernels: 12.6 us -> 14.6 us
    ppermute x6 -> x4, starting transfers between devices: 8.4 us -> 2.98 us  [sum_steps(): lax.ppermute(value, name, [(i, i ^ step) for i in range(size)])]
    ppermute x19 -> x21, waiting for transfers between devices: 24 us -> 18.6 us  [swap(): return lax.ppermute(value, 'mem', [(i, i ^ step) for i in range(count)])]
    ppermute x0 -> x2, starting transfers between devices: none -> 4.93 us  [join(): other = lax.ppermute(value, name, [(i, i ^ step) for i in range(size)])]
    ppermute x0 -> x2, waiting for transfers between devices: none -> 4.17 us  [join(): other = lax.ppermute(value, name, [(i, i ^ step) for i in range(size)])]
    ppermute x6 -> x4, waiting for transfers between devices: 9.37 us -> 6.72 us  [sum_steps(): lax.ppermute(value, name, [(i, i ^ step) for i in range(size)])]
    pallas_call x2 -> x3, Pallas kernels: 3.4 us -> 5.4 us  [finish(): pl.pallas_call(functools.partial(finish_kernel, me_of, count, chunk, leng...]
    ppermute x19 -> x21, starting transfers between devices: 24.2 us -> 25.4 us  [swap(): return lax.ppermute(value, 'mem', [(i, i ^ step) for i in range(count)])]
  transfers between devices with their start and end apart: 25 -> 27, of which waited for: 19 -> 18; matrix products, arithmetic and copies ran while one was open for 0% -> 0% of each run, Pallas kernels for 9% -> 12%
where the time goes in v3:
time: 83.9 us; the launch traced here: 83.6 us
  starting transfers between devices  33.3 us (40%)
  waiting for transfers between devices  29.5 us (35%)
  Pallas kernels  14.6 us (17%)
  local copies, waits for them, and re-layouts  5.48 us (7%)
    ppermute x21, starting transfers between devices, swap(): return lax.ppermute(value, 'mem', [(i, i ^ step) for i in range(count)])  25.4 us
    ppermute x21, waiting for transfers between devices, swap(): return lax.ppermute(value, 'mem', [(i, i ^ step) for i in range(count)])  18.6 us
    ppermute x4, waiting for transfers between devices, sum_steps(): lax.ppermute(value, name, [(i, i ^ step) for i in range(size)])  6.72 us
    unnamed x12, local copies, waits for them, and re-layouts  5.48 us
    pallas_call x3, Pallas kernels, finish(): pl.pallas_call(functools.partial(finish_kernel, me_of, count, chunk, leng...  5.4 us
    ppermute x2, starting transfers between devices, join(): other = lax.ppermute(value, name, [(i, i ^ step) for i in range(size)])  4.93 us
    ppermute x2, waiting for transfers between devices, join(): other = lax.ppermute(value, name, [(i, i ^ step) for i in range(size)])  4.17 us
    pallas_call x2, Pallas kernels, gradient(): pl.pallas_call(functools.partial(grad_kernel, me_of, count, chunk, group,...  3.23 us
  transfers between devices with their start and end apart: 27, of which 18 were waited for; matrix products, arithmetic and copies ran while one was open for 0% of the time, Pallas kernels for 12%

profile of v3, /device:TPU:0, one launch (start us, length us, event | category | flops | bytes accessed | tf_op | source)
XLA Modules:
  0.0 83.6 jit_solution(5581601347705669632)
XLA Ops:
  0.6 1.4 %copy-done = bf16[4,16,11520]{2,1,0:T(8,128)(2,1)S(1)} copy-done((bf16[4,16,11520]{2,1,0:T(8,128)(2,1)S(1)}, bf16[4,16,11520]{2,1,0:T(8,128)(2,1)}, u32[]{:S(2)}) %copy-start) | copy-done | bytes 1474584
  2.2 3.0 %collective-permute-start = (bf16[64,2944]{1,0:T(8,128)(2,1)S(1)}, bf16[64,2944]{1,0:T(8,128)(2,1)S(1)}, u32[]{:S(2)}, u32[]{:S(2)}) collective-permute-start(bf16[64,2944]{1,0:T(8,128)(2,1)S(1)} %get-tuple-element.30.refs_2_), channel_id=1, source_target_pairs={{0,8},{8,0},{16,24},{24,16},{1,9},{9,1},{17,25},{25,17},{2,10},{10... | collective-permute-start | bytes 1130504 | tf_op jit(solution)/shard_map/ppermute | solution.py:227
  5.2 1.5 %collective-permute-start.1 = (bf16[64,2944]{1,0:T(8,128)(2,1)S(1)}, bf16[64,2944]{1,0:T(8,128)(2,1)S(1)}, u32[]{:S(2)}, u32[]{:S(2)}) collective-permute-start(bf16[64,2944]{1,0:T(8,128)(2,1)S(1)} %get-tuple-element.31.refs_3_), channel_id=1, source_target_pairs={{0,16},{8,24},{16,0},{24,8},{1,17},{9,25},{17,1},{25,9},{2,18},{10... | collective-permute-start | bytes 1130504 | tf_op jit(solution)/shard_map/ppermute | solution.py:227
  10.8 4.0 %collective-permute-done.refs_1_.rest_0_.refs_5_ = bf16[64,2944]{1,0:T(8,128)(2,1)S(1)} collective-permute-done((bf16[64,2944]{1,0:T(8,128)(2,1)S(1)}, bf16[64,2944]{1,0:T(8,128)(2,1)S(1)}, u32[]{:S(2)}, u32[]{:S(2)}) %collective-permute-start) | collective-permute-done | bytes 376864 | tf_op jit(solution)/shard_map/ppermute | solution.py:227
  14.8 1.4 %copy-done.1 = bf16[4,16,11520]{2,1,0:T(8,128)(2,1)S(1)} copy-done((bf16[4,16,11520]{2,1,0:T(8,128)(2,1)S(1)}, bf16[4,16,11520]{2,1,0:T(8,128)(2,1)}, u32[]{:S(2)}) %copy-start.1) | copy-done | bytes 1474584
  16.4 2.1 %collective-permute-start.6 = (bf16[64,2944]{1,0:T(8,128)(2,1)S(1)}, bf16[64,2944]{1,0:T(8,128)(2,1)S(1)}, u32[]{:S(2)}, u32[]{:S(2)}) collective-permute-start(bf16[64,2944]{1,0:T(8,128)(2,1)S(1)} %get-tuple-element.33.refs_1_.refs_2_), channel_id=1, source_target_pairs={{0,8},{8,0},{16,24},{24,16},{1,9},{9,1},{17,25},{25,17},{2,10},{10... | collective-permute-start | bytes 1130504 | tf_op jit(solution)/shard_map/ppermute | solution.py:227
  18.5 1.5 %collective-permute-start.10 = (bf16[64,2944]{1,0:T(8,128)(2,1)S(1)}, bf16[64,2944]{1,0:T(8,128)(2,1)S(1)}, u32[]{:S(2)}, u32[]{:S(2)}) collective-permute-start(bf16[64,2944]{1,0:T(8,128)(2,1)S(1)} %get-tuple-element.35.refs_2_.refs_3_), channel_id=1, source_target_pairs={{0,16},{8,24},{16,0},{24,8},{1,17},{9,25},{17,1},{25,9},{2,18},{10... | collective-permute-start | bytes 1130504 | tf_op jit(solution)/shard_map/ppermute | solution.py:227
  20.0 3.9 %collective-permute-done.1.refs_2_.refs_6_ = bf16[64,2944]{1,0:T(8,128)(2,1)S(1)} collective-permute-done((bf16[64,2944]{1,0:T(8,128)(2,1)S(1)}, bf16[64,2944]{1,0:T(8,128)(2,1)S(1)}, u32[]{:S(2)}, u32[]{:S(2)}) %collective-permute-start.1) | collective-permute-done | bytes 376864 | tf_op jit(solution)/shard_map/ppermute | solution.py:227
  24.4 1.5 %score_sums.1 = f32[16,16]{1,0:T(8,128)S(1)} custom-call(f32[256,256]{1,0:T(8,128)S(1)} %get-tuple-element.28.tile_ref.rest_1_.qk_ref, bf16[64,2944]{1,0:T(8,128)(2,1)S(1)} %get-tuple-element.29.refs_0_.refs_4_.refs_1_, bf16[64,2944]{1,0:T(8,128)(2,1)S(1)} %collective-permute-done.refs_1_.rest_0_.refs_5_, ...), custom_call_target="tpu_custom_call" | custom-call | flops 385875968 | bytes 1507328 | tf_op jit(solution)/shard_map/score_sums/pallas_call | solution.py:314
  27.1 1.6 %collective-permute-start.4 = (f32[16,16]{1,0:T(8,128)S(1)}, f32[16,16]{1,0:T(8,128)S(1)}, u32[]{:S(2)}, u32[]{:S(2)}) collective-permute-start(f32[16,16]{1,0:T(8,128)S(1)} %add.12), channel_id=1, source_target_pairs={{0,2},{1,3},{2,0},{3,1},{4,6},{5,7},{6,4},{7,5},{8,10},{9,11},{10,... | collective-permute-start | bytes 3080 | tf_op jit(solution)/shard_map/ppermute | solution.py:238
  28.7 2.1 %collective-permute-done.4 = f32[16,16]{1,0:T(8,128)S(1)} collective-permute-done((f32[16,16]{1,0:T(8,128)S(1)}, f32[16,16]{1,0:T(8,128)S(1)}, u32[]{:S(2)}, u32[]{:S(2)}) %collective-permute-start.4) | collective-permute-done | bytes 1056 | tf_op jit(solution)/shard_map/ppermute | solution.py:238
  30.8 2.6 %collective-permute-start.5 = (f32[16,16]{1,0:T(8,128)S(1)}, f32[16,16]{1,0:T(8,128)S(1)}, u32[]{:S(2)}, u32[]{:S(2)}) collective-permute-start(f32[16,16]{1,0:T(8,128)S(1)} %add.13.a_ref), channel_id=1, source_target_pairs={{0,4},{1,5},{2,6},{3,7},{4,0},{5,1},{6,2},{7,3},{8,12},{9,13},{10,... | collective-permute-start | bytes 3080 | tf_op jit(solution)/shard_map/ppermute | solution.py:303
  33.4 2.0 %collective-permute-done.5.b_ref = f32[16,16]{1,0:T(8,128)S(1)} collective-permute-done((f32[16,16]{1,0:T(8,128)S(1)}, f32[16,16]{1,0:T(8,128)S(1)}, u32[]{:S(2)}, u32[]{:S(2)}) %collective-permute-start.5) | collective-permute-done | bytes 1056 | tf_op jit(solution)/shard_map/ppermute | solution.py:303
  35.4 1.4 %collective-permute-start.9 = (f32[16,16]{1,0:T(8,128)S(1)}, f32[16,16]{1,0:T(8,128)S(1)}, u32[]{:S(2)}, u32[]{:S(2)}) collective-permute-start(f32[16,16]{1,0:T(8,128)S(1)} %join_sums.2.refs_8_.refs_0_), channel_id=1, source_target_pairs={{0,24},{8,16},{16,8},{24,0},{1,25},{9,17},{17,9},{25,1},{2,26},{10... | collective-permute-start | bytes 3080 | tf_op jit(solution)/shard_map/ppermute | solution.py:227
  36.8 2.0 %collective-permute-start.8 = (f32[16,16]{1,0:T(8,128)S(1)}, f32[16,16]{1,0:T(8,128)S(1)}, u32[]{:S(2)}, u32[]{:S(2)}) collective-permute-start(f32[16,16]{1,0:T(8,128)S(1)} %join_sums.2.refs_8_.refs_0_), channel_id=1, source_target_pairs={{0,8},{8,0},{16,24},{24,16},{1,9},{9,1},{17,25},{25,17},{2,10},{10... | collective-permute-start | bytes 3080 | tf_op jit(solution)/shard_map/ppermute | solution.py:227
  39.7 1.5 %pair_sums.1.refs_8_ = f32[16,16]{1,0:T(8,128)S(1)} custom-call(f32[256,256]{1,0:T(8,128)S(1)} %get-tuple-element.27.tile_ref.ov_ref, bf16[64,2944]{1,0:T(8,128)(2,1)S(1)} %get-tuple-element.29.refs_0_.refs_4_.refs_1_, bf16[64,2944]{1,0:T(8,128)(2,1)S(1)} %collective-permute-done.refs_1_.rest_0_.refs_5_, ...), custom_call_target="tpu_custom_call" | custom-call | flops 385875968 | bytes 3014656 | tf_op jit(solution)/shard_map/pair_sums/pallas_call | solution.py:330
  42.4 1.4 %branch.1 = (f32[16,16]{1,0:T(8,128)S(1)}, bf16[64,2944]{1,0:T(8,128)(2,1)S(1)}, bf16[64,2944]{1,0:T(8,128)(2,1)S(1)}, bf16[64,2944]{1,0:T(8,128)(2,1)S(1)}, bf16[64,2944]{1,0:T(8,128)(2,1)S(1)}) custom-call(f32[256,256]{1,0:T(8,128)S(1)} %get-tuple-element.27.tile_ref.ov_ref, f32[16,16]{1,0:T(8,128)S(1)} %join_sums.2.refs_8_.refs_0_, ...), custom_call_target="tpu_custom_call" | custom-call | flops 771751936 | bytes 3014656 | tf_op jit(solution)/shard_map/branch/pallas_call | solution.py:342
  44.1 1.4 %collective-permute-start.19 = (bf16[64,2944]{1,0:T(8,128)(2,1)S(1)}, bf16[64,2944]{1,0:T(8,128)(2,1)S(1)}, u32[]{:S(2)}, u32[]{:S(2)}) collective-permute-start(bf16[64,2944]{1,0:T(8,128)(2,1)S(1)} %get-tuple-element.41), channel_id=1, source_target_pairs={{0,16},{8,24},{16,0},{24,8},{1,17},{9,25},{17,1},{25,9},{2,18},{10... | collective-permute-start | bytes 1130504 | tf_op jit(solution)/shard_map/ppermute | solution.py:227
  45.4 1.9 %collective-permute-start.20 = (bf16[64,2944]{1,0:T(8,128)(2,1)S(1)}, bf16[64,2944]{1,0:T(8,128)(2,1)S(1)}, u32[]{:S(2)}, u32[]{:S(2)}) collective-permute-start(bf16[64,2944]{1,0:T(8,128)(2,1)S(1)} %get-tuple-element.42), channel_id=1, source_target_pairs={{0,24},{8,16},{16,8},{24,0},{1,25},{9,17},{17,9},{25,1},{2,26},{10... | collective-permute-start | bytes 1130504 | tf_op jit(solution)/shard_map/ppermute | solution.py:227
  48.5 1.3 %collective-permute-start.13 = (f32[16,16]{1,0:T(8,128)S(1)}, f32[16,16]{1,0:T(8,128)S(1)}, u32[]{:S(2)}, u32[]{:S(2)}) collective-permute-start(f32[16,16]{1,0:T(8,128)S(1)} %add.14), channel_id=1, source_target_pairs={{0,2},{1,3},{2,0},{3,1},{4,6},{5,7},{6,4},{7,5},{8,10},{9,11},{10,... | collective-permute-start | bytes 3080 | tf_op jit(solution)/shard_map/ppermute | solution.py:238
  49.8 2.3 %collective-permute-done.13 = f32[16,16]{1,0:T(8,128)S(1)} collective-permute-done((f32[16,16]{1,0:T(8,128)S(1)}, f32[16,16]{1,0:T(8,128)S(1)}, u32[]{:S(2)}, u32[]{:S(2)}) %collective-permute-start.13) | collective-permute-done | bytes 1056 | tf_op jit(solution)/shard_map/ppermute | solution.py:238
  52.2 2.3 %collective-permute-start.14 = (f32[16,16]{1,0:T(8,128)S(1)}, f32[16,16]{1,0:T(8,128)S(1)}, u32[]{:S(2)}, u32[]{:S(2)}) collective-permute-start(f32[16,16]{1,0:T(8,128)S(1)} %add.15.a_ref), channel_id=1, source_target_pairs={{0,4},{1,5},{2,6},{3,7},{4,0},{5,1},{6,2},{7,3},{8,12},{9,13},{10,... | collective-permute-start | bytes 3080 | tf_op jit(solution)/shard_map/ppermute | solution.py:303
  54.5 2.2 %collective-permute-done.14.b_ref = f32[16,16]{1,0:T(8,128)S(1)} collective-permute-done((f32[16,16]{1,0:T(8,128)S(1)}, f32[16,16]{1,0:T(8,128)S(1)}, u32[]{:S(2)}, u32[]{:S(2)}) %collective-permute-start.14) | collective-permute-done | bytes 1056 | tf_op jit(solution)/shard_map/ppermute | solution.py:303
  58.6 1.6 %collective-permute-start.16 = (f32[16,16]{1,0:T(8,128)S(1)}, f32[16,16]{1,0:T(8,128)S(1)}, u32[]{:S(2)}, u32[]{:S(2)}) collective-permute-start(f32[16,16]{1,0:T(8,128)S(1)} %join_sums.3.refs_8_), channel_id=1, source_target_pairs={{0,16},{8,24},{16,0},{24,8},{1,17},{9,25},{17,1},{25,9},{2,18},{10... | collective-permute-start | bytes 3080 | tf_op jit(solution)/shard_map/ppermute | solution.py:227
  60.2 1.4 %collective-permute-done.19.refs_13_.refs_7_ = bf16[64,2944]{1,0:T(8,128)(2,1)S(1)} collective-permute-done((bf16[64,2944]{1,0:T(8,128)(2,1)S(1)}, bf16[64,2944]{1,0:T(8,128)(2,1)S(1)}, u32[]{:S(2)}, u32[]{:S(2)}) %collective-permute-start.19) | collective-permute-done | bytes 376864 | tf_op jit(solution)/shard_map/ppermute | solution.py:227
  62.3 1.6 %input_gradient_a.1 = (bf16[64,1536]{1,0:T(8,128)(2,1)S(1)}, bf16[64,1536]{1,0:T(8,128)(2,1)S(1)}, bf16[64,1536]{1,0:T(8,128)(2,1)S(1)}, bf16[64,1536]{1,0:T(8,128)(2,1)S(1)}) custom-call(f32[16,16]{1,0:T(8,128)S(1)} %get-tuple-element.37.s_ref, f32[256,256]{1,0:T(8,128)S(1)} %get-tuple-element.28.tile_ref.rest_1_.qk_ref, ...), custom_call_target="tpu_custom_call" | custom-call | flops 805306368 | bytes 2359296 | tf_op jit(solution)/shard_map/input_gradient_a/pallas_call | solution.py:360
  65.8 1.7 %collective-permute-start.23 = (bf16[64,1536]{1,0:T(8,128)(2,1)S(1)}, bf16[64,1536]{1,0:T(8,128)(2,1)S(1)}, u32[]{:S(2)}, u32[]{:S(2)}) collective-permute-start(bf16[64,1536]{1,0:T(8,128)(2,1)S(1)} %get-tuple-element.47), channel_id=1, source_target_pairs={{0,24},{8,16},{16,8},{24,0},{1,25},{9,17},{17,9},{25,1},{2,26},{10... | collective-permute-start | bytes 589832 | tf_op jit(solution)/shard_map/ppermute | solution.py:227
  67.5 1.6 %input_gradient_b.1 = (bf16[64,1408]{1,0:T(8,128)(2,1)S(1)}, bf16[64,1408]{1,0:T(8,128)(2,1)S(1)}, bf16[64,1408]{1,0:T(8,128)(2,1)S(1)}, bf16[64,1408]{1,0:T(8,128)(2,1)S(1)}) custom-call(f32[16,16]{1,0:T(8,128)S(1)} %get-tuple-element.37.s_ref, f32[256,256]{1,0:T(8,128)S(1)} %get-tuple-element.28.tile_ref.rest_1_.qk_ref, ...), custom_call_target="tpu_custom_call" | custom-call | flops 738197504 | bytes 2162688 | tf_op jit(solution)/shard_map/input_gradient_b/pallas_call | solution.py:360
  73.0 2.4 %updated.1 = f32[64,11520]{1,0:T(8,128)} custom-call(bf16[64,1536]{1,0:T(8,128)(2,1)S(1)} %collective-permute-done.21.refs_0_.refs_5_, bf16[64,2944]{1,0:T(8,128)(2,1)S(1)} %get-tuple-element.29.refs_0_.refs_4_.refs_1_, bf16[64,2944]{1,0:T(8,128)(2,1)S(1)} %get-tuple-element.30.refs_2_, bf16[64,2944]{1,0:T(8,128)(2,1)S(1)} %get-tuple-element.31.refs_3_, ...), custom_call_target="tpu_custom_call" | custom-call | flops 737280 | bytes 5898240 | tf_op jit(solution)/shard_map/updated/pallas_call | solution.py:384
  75.4 1.7 %collective-permute-done.23.refs_7_ = bf16[64,1536]{1,0:T(8,128)(2,1)S(1)} collective-permute-done((bf16[64,1536]{1,0:T(8,128)(2,1)S(1)}, bf16[64,1536]{1,0:T(8,128)(2,1)S(1)}, u32[]{:S(2)}, u32[]{:S(2)}) %collective-permute-start.23) | collective-permute-done | bytes 196640 | tf_op jit(solution)/shard_map/ppermute | solution.py:227
  77.1 2.0 %ensemble_grad_early.1.refs_0_ = f32[64,11520]{1,0:T(8,128)} custom-call(bf16[64,2944]{1,0:T(8,128)(2,1)S(1)} %get-tuple-element.34.refs_4_.refs_0_.refs_1_, bf16[64,2944]{1,0:T(8,128)(2,1)S(1)} %get-tuple-element.33.refs_1_.refs_2_, bf16[64,2944]{1,0:T(8,128)(2,1)S(1)} %get-tuple-element.35.refs_2_.refs_3_, ...), custom_call_target="tpu_custom_call" | custom-call | flops 737280 | bytes 5898240 | tf_op jit(solution)/shard_map/ensemble_grad_early/pallas_call | solution.py:384
  80.9 1.7 %collective-permute-done.26.refs_7_ = bf16[64,1408]{1,0:T(8,128)(2,1)S(1)} collective-permute-done((bf16[64,1408]{1,0:T(8,128)(2,1)S(1)}, bf16[64,1408]{1,0:T(8,128)(2,1)S(1)}, u32[]{:S(2)}, u32[]{:S(2)}) %collective-permute-start.26) | collective-permute-done | bytes 180256 | tf_op jit(solution)/shard_map/ppermute | solution.py:227
  (51 shorter events, 21.1 us)
Async XLA Ops:
  0.6 1.4 %copy-start = (bf16[4,16,11520]{2,1,0:T(8,128)(2,1)S(1)}, bf16[4,16,11520]{2,1,0:T(8,128)(2,1)}, u32[]{:S(2)}) copy-start(bf16[4,16,11520]{2,1,0:T(8,128)(2,1)} %param.6) | copy-start | bytes 4423684
  2.2 12.6 %collective-permute-start = (bf16[64,2944]{1,0:T(8,128)(2,1)S(1)}, bf16[64,2944]{1,0:T(8,128)(2,1)S(1)}, u32[]{:S(2)}, u32[]{:S(2)}) collective-permute-start(bf16[64,2944]{1,0:T(8,128)(2,1)S(1)} %get-tuple-element.30.refs_2_), channel_id=1, source_target_pairs={{0,8},{8,0},{16,24},{24,16},{1,9},{9,1},{17,25},{25,17},{2,10},{10... | collective-permute-start | bytes 1130504 | tf_op jit(solution)/shard_map/ppermute | solution.py:227
  5.2 18.7 %collective-permute-start.1 = (bf16[64,2944]{1,0:T(8,128)(2,1)S(1)}, bf16[64,2944]{1,0:T(8,128)(2,1)S(1)}, u32[]{:S(2)}, u32[]{:S(2)}) collective-permute-start(bf16[64,2944]{1,0:T(8,128)(2,1)S(1)} %get-tuple-element.31.refs_3_), channel_id=1, source_target_pairs={{0,16},{8,24},{16,0},{24,8},{1,17},{9,25},{17,1},{25,9},{2,18},{10... | collective-permute-start | bytes 1130504 | tf_op jit(solution)/shard_map/ppermute | solution.py:227
  6.7 17.7 %collective-permute-start.2 = (bf16[64,2944]{1,0:T(8,128)(2,1)S(1)}, bf16[64,2944]{1,0:T(8,128)(2,1)S(1)}, u32[]{:S(2)}, u32[]{:S(2)}) collective-permute-start(bf16[64,2944]{1,0:T(8,128)(2,1)S(1)} %get-tuple-element.32.refs_4_), channel_id=1, source_target_pairs={{0,24},{8,16},{16,8},{24,0},{1,25},{9,17},{17,9},{25,1},{2,26},{10... | collective-permute-start | bytes 1130504 | tf_op jit(solution)/shard_map/ppermute | solution.py:227
  6.7 0.7 copy-start.2
  7.4 0.7 copy-start.3
  8.1 0.7 copy-start.4
  14.8 1.4 %copy-start.1 = (bf16[4,16,11520]{2,1,0:T(8,128)(2,1)S(1)}, bf16[4,16,11520]{2,1,0:T(8,128)(2,1)}, u32[]{:S(2)}) copy-start(bf16[4,16,11520]{2,1,0:T(8,128)(2,1)} %param.7) | copy-start | bytes 4423684
  16.4 19.0 %collective-permute-start.6 = (bf16[64,2944]{1,0:T(8,128)(2,1)S(1)}, bf16[64,2944]{1,0:T(8,128)(2,1)S(1)}, u32[]{:S(2)}, u32[]{:S(2)}) collective-permute-start(bf16[64,2944]{1,0:T(8,128)(2,1)S(1)} %get-tuple-element.33.refs_1_.refs_2_), channel_id=1, source_target_pairs={{0,8},{8,0},{16,24},{24,16},{1,9},{9,1},{17,25},{25,17},{2,10},{10... | collective-permute-start | bytes 1130504 | tf_op jit(solution)/shard_map/ppermute | solution.py:227
  18.5 21.3 %collective-permute-start.10 = (bf16[64,2944]{1,0:T(8,128)(2,1)S(1)}, bf16[64,2944]{1,0:T(8,128)(2,1)S(1)}, u32[]{:S(2)}, u32[]{:S(2)}) collective-permute-start(bf16[64,2944]{1,0:T(8,128)(2,1)S(1)} %get-tuple-element.35.refs_2_.refs_3_), channel_id=1, source_target_pairs={{0,16},{8,24},{16,0},{24,8},{1,17},{9,25},{17,1},{25,9},{2,18},{10... | collective-permute-start | bytes 1130504 | tf_op jit(solution)/shard_map/ppermute | solution.py:227
  20.0 19.7 %collective-permute-start.11 = (bf16[64,2944]{1,0:T(8,128)(2,1)S(1)}, bf16[64,2944]{1,0:T(8,128)(2,1)S(1)}, u32[]{:S(2)}, u32[]{:S(2)}) collective-permute-start(bf16[64,2944]{1,0:T(8,128)(2,1)S(1)} %get-tuple-element.36.refs_3_.refs_4_), channel_id=1, source_target_pairs={{0,24},{8,16},{16,8},{24,0},{1,25},{9,17},{17,9},{25,1},{2,26},{10... | collective-permute-start | bytes 1130504 | tf_op jit(solution)/shard_map/ppermute | solution.py:227
  25.9 1.2 %collective-permute-start.3 = (f32[16,16]{1,0:T(8,128)S(1)}, f32[16,16]{1,0:T(8,128)S(1)}, u32[]{:S(2)}, u32[]{:S(2)}) collective-permute-start(f32[16,16]{1,0:T(8,128)S(1)} %score_sums.1), channel_id=1, source_target_pairs={{0,1},{1,0},{2,3},{3,2},{4,5},{5,4},{6,7},{7,6},{8,9},{9,8},{10,11... | collective-permute-start | bytes 3080 | tf_op jit(solution)/shard_map/ppermute | solution.py:238
  27.1 3.7 %collective-permute-start.4 = (f32[16,16]{1,0:T(8,128)S(1)}, f32[16,16]{1,0:T(8,128)S(1)}, u32[]{:S(2)}, u32[]{:S(2)}) collective-permute-start(f32[16,16]{1,0:T(8,128)S(1)} %add.12), channel_id=1, source_target_pairs={{0,2},{1,3},{2,0},{3,1},{4,6},{5,7},{6,4},{7,5},{8,10},{9,11},{10,... | collective-permute-start | bytes 3080 | tf_op jit(solution)/shard_map/ppermute | solution.py:238
  30.8 4.5 %collective-permute-start.5 = (f32[16,16]{1,0:T(8,128)S(1)}, f32[16,16]{1,0:T(8,128)S(1)}, u32[]{:S(2)}, u32[]{:S(2)}) collective-permute-start(f32[16,16]{1,0:T(8,128)S(1)} %add.13.a_ref), channel_id=1, source_target_pairs={{0,4},{1,5},{2,6},{3,7},{4,0},{5,1},{6,2},{7,3},{8,12},{9,13},{10,... | collective-permute-start | bytes 3080 | tf_op jit(solution)/shard_map/ppermute | solution.py:303
  35.4 5.9 %collective-permute-start.9 = (f32[16,16]{1,0:T(8,128)S(1)}, f32[16,16]{1,0:T(8,128)S(1)}, u32[]{:S(2)}, u32[]{:S(2)}) collective-permute-start(f32[16,16]{1,0:T(8,128)S(1)} %join_sums.2.refs_8_.refs_0_), channel_id=1, source_target_pairs={{0,24},{8,16},{16,8},{24,0},{1,25},{9,17},{17,9},{25,1},{2,26},{10... | collective-permute-start | bytes 3080 | tf_op jit(solution)/shard_map/ppermute | solution.py:227
  36.8 4.4 %collective-permute-start.8 = (f32[16,16]{1,0:T(8,128)S(1)}, f32[16,16]{1,0:T(8,128)S(1)}, u32[]{:S(2)}, u32[]{:S(2)}) collective-permute-start(f32[16,16]{1,0:T(8,128)S(1)} %join_sums.2.refs_8_.refs_0_), channel_id=1, source_target_pairs={{0,8},{8,0},{16,24},{24,16},{1,9},{9,1},{17,25},{25,17},{2,10},{10... | collective-permute-start | bytes 3080 | tf_op jit(solution)/shard_map/ppermute | solution.py:227
  38.8 3.7 %collective-permute-start.7 = (f32[16,16]{1,0:T(8,128)S(1)}, f32[16,16]{1,0:T(8,128)S(1)}, u32[]{:S(2)}, u32[]{:S(2)}) collective-permute-start(f32[16,16]{1,0:T(8,128)S(1)} %join_sums.2.refs_8_.refs_0_), channel_id=1, source_target_pairs={{0,16},{8,24},{16,0},{24,8},{1,17},{9,25},{17,1},{25,9},{2,18},{10... | collective-permute-start | bytes 3080 | tf_op jit(solution)/shard_map/ppermute | solution.py:227
  43.8 12.9 %collective-permute-start.15 = (bf16[64,2944]{1,0:T(8,128)(2,1)S(1)}, bf16[64,2944]{1,0:T(8,128)(2,1)S(1)}, u32[]{:S(2)}, u32[]{:S(2)}) collective-permute-start(bf16[64,2944]{1,0:T(8,128)(2,1)S(1)} %get-tuple-element.40), channel_id=1, source_target_pairs={{0,8},{8,0},{16,24},{24,16},{1,9},{9,1},{17,25},{25,17},{2,10},{10... | collective-permute-start | bytes 1130504 | tf_op jit(solution)/shard_map/ppermute | solution.py:227
  44.1 17.5 %collective-permute-start.19 = (bf16[64,2944]{1,0:T(8,128)(2,1)S(1)}, bf16[64,2944]{1,0:T(8,128)(2,1)S(1)}, u32[]{:S(2)}, u32[]{:S(2)}) collective-permute-start(bf16[64,2944]{1,0:T(8,128)(2,1)S(1)} %get-tuple-element.41), channel_id=1, source_target_pairs={{0,16},{8,24},{16,0},{24,8},{1,17},{9,25},{17,1},{25,9},{2,18},{10... | collective-permute-start | bytes 1130504 | tf_op jit(solution)/shard_map/ppermute | solution.py:227
  45.4 16.1 %collective-permute-start.20 = (bf16[64,2944]{1,0:T(8,128)(2,1)S(1)}, bf16[64,2944]{1,0:T(8,128)(2,1)S(1)}, u32[]{:S(2)}, u32[]{:S(2)}) collective-permute-start(bf16[64,2944]{1,0:T(8,128)(2,1)S(1)} %get-tuple-element.42), channel_id=1, source_target_pairs={{0,24},{8,16},{16,8},{24,0},{1,25},{9,17},{17,9},{25,1},{2,26},{10... | collective-permute-start | bytes 1130504 | tf_op jit(solution)/shard_map/ppermute | solution.py:227
  47.3 1.2 %collective-permute-start.12 = (f32[16,16]{1,0:T(8,128)S(1)}, f32[16,16]{1,0:T(8,128)S(1)}, u32[]{:S(2)}, u32[]{:S(2)}) collective-permute-start(f32[16,16]{1,0:T(8,128)S(1)} %pair_sums.1.refs_8_), channel_id=1, source_target_pairs={{0,1},{1,0},{2,3},{3,2},{4,5},{5,4},{6,7},{7,6},{8,9},{9,8},{10,11... | collective-permute-start | bytes 3080 | tf_op jit(solution)/shard_map/ppermute | solution.py:238
  48.5 3.7 %collective-permute-start.13 = (f32[16,16]{1,0:T(8,128)S(1)}, f32[16,16]{1,0:T(8,128)S(1)}, u32[]{:S(2)}, u32[]{:S(2)}) collective-permute-start(f32[16,16]{1,0:T(8,128)S(1)} %add.14), channel_id=1, source_target_pairs={{0,2},{1,3},{2,0},{3,1},{4,6},{5,7},{6,4},{7,5},{8,10},{9,11},{10,... | collective-permute-start | bytes 3080 | tf_op jit(solution)/shard_map/ppermute | solution.py:238
  52.2 4.5 %collective-permute-start.14 = (f32[16,16]{1,0:T(8,128)S(1)}, f32[16,16]{1,0:T(8,128)S(1)}, u32[]{:S(2)}, u32[]{:S(2)}) collective-permute-start(f32[16,16]{1,0:T(8,128)S(1)} %add.15.a_ref), channel_id=1, source_target_pairs={{0,4},{1,5},{2,6},{3,7},{4,0},{5,1},{6,2},{7,3},{8,12},{9,13},{10,... | collective-permute-start | bytes 3080 | tf_op jit(solution)/shard_map/ppermute | solution.py:303
  56.7 4.8 %collective-permute-start.18 = (f32[16,16]{1,0:T(8,128)S(1)}, f32[16,16]{1,0:T(8,128)S(1)}, u32[]{:S(2)}, u32[]{:S(2)}) collective-permute-start(f32[16,16]{1,0:T(8,128)S(1)} %join_sums.3.refs_8_), channel_id=1, source_target_pairs={{0,24},{8,16},{16,8},{24,0},{1,25},{9,17},{17,9},{25,1},{2,26},{10... | collective-permute-start | bytes 3080 | tf_op jit(solution)/shard_map/ppermute | solution.py:227
  57.7 3.8 %collective-permute-start.17 = (f32[16,16]{1,0:T(8,128)S(1)}, f32[16,16]{1,0:T(8,128)S(1)}, u32[]{:S(2)}, u32[]{:S(2)}) collective-permute-start(f32[16,16]{1,0:T(8,128)S(1)} %join_sums.3.refs_8_), channel_id=1, source_target_pairs={{0,8},{8,0},{16,24},{24,16},{1,9},{9,1},{17,25},{25,17},{2,10},{10... | collective-permute-start | bytes 3080 | tf_op jit(solution)/shard_map/ppermute | solution.py:227
  58.6 3.7 %collective-permute-start.16 = (f32[16,16]{1,0:T(8,128)S(1)}, f32[16,16]{1,0:T(8,128)S(1)}, u32[]{:S(2)}, u32[]{:S(2)}) collective-permute-start(f32[16,16]{1,0:T(8,128)S(1)} %join_sums.3.refs_8_), channel_id=1, source_target_pairs={{0,16},{8,24},{16,0},{24,8},{1,17},{9,25},{17,1},{25,9},{2,18},{10... | collective-permute-start | bytes 3080 | tf_op jit(solution)/shard_map/ppermute | solution.py:227
  63.9 7.9 %collective-permute-start.21 = (bf16[64,1536]{1,0:T(8,128)(2,1)S(1)}, bf16[64,1536]{1,0:T(8,128)(2,1)S(1)}, u32[]{:S(2)}, u32[]{:S(2)}) collective-permute-start(bf16[64,1536]{1,0:T(8,128)(2,1)S(1)} %get-tuple-element.43), channel_id=1, source_target_pairs={{0,8},{8,0},{16,24},{24,16},{1,9},{9,1},{17,25},{25,17},{2,10},{10... | collective-permute-start | bytes 589832 | tf_op jit(solution)/shard_map/ppermute | solution.py:227
  65.1 10.3 %collective-permute-start.22 = (bf16[64,1536]{1,0:T(8,128)(2,1)S(1)}, bf16[64,1536]{1,0:T(8,128)(2,1)S(1)}, u32[]{:S(2)}, u32[]{:S(2)}) collective-permute-start(bf16[64,1536]{1,0:T(8,128)(2,1)S(1)} %get-tuple-element.46), channel_id=1, source_target_pairs={{0,16},{8,24},{16,0},{24,8},{1,17},{9,25},{17,1},{25,9},{2,18},{10... | collective-permute-start | bytes 589832 | tf_op jit(solution)/shard_map/ppermute | solution.py:227
  65.8 11.4 %collective-permute-start.23 = (bf16[64,1536]{1,0:T(8,128)(2,1)S(1)}, bf16[64,1536]{1,0:T(8,128)(2,1)S(1)}, u32[]{:S(2)}, u32[]{:S(2)}) collective-permute-start(bf16[64,1536]{1,0:T(8,128)(2,1)S(1)} %get-tuple-element.47), channel_id=1, source_target_pairs={{0,24},{8,16},{16,8},{24,0},{1,25},{9,17},{17,9},{25,1},{2,26},{10... | collective-permute-start | bytes 589832 | tf_op jit(solution)/shard_map/ppermute | solution.py:227
  69.1 10.8 %collective-permute-start.24 = (bf16[64,1408]{1,0:T(8,128)(2,1)S(1)}, bf16[64,1408]{1,0:T(8,128)(2,1)S(1)}, u32[]{:S(2)}, u32[]{:S(2)}) collective-permute-start(bf16[64,1408]{1,0:T(8,128)(2,1)S(1)} %get-tuple-element.49), channel_id=1, source_target_pairs={{0,8},{8,0},{16,24},{24,16},{1,9},{9,1},{17,25},{25,17},{2,10},{10... | collective-permute-start | bytes 540680 | tf_op jit(solution)/shard_map/ppermute | solution.py:227
  70.3 10.6 %collective-permute-start.25 = (bf16[64,1408]{1,0:T(8,128)(2,1)S(1)}, bf16[64,1408]{1,0:T(8,128)(2,1)S(1)}, u32[]{:S(2)}, u32[]{:S(2)}) collective-permute-start(bf16[64,1408]{1,0:T(8,128)(2,1)S(1)} %get-tuple-element.50), channel_id=1, source_target_pairs={{0,16},{8,24},{16,0},{24,8},{1,17},{9,25},{17,1},{25,9},{2,18},{10... | collective-permute-start | bytes 540680 | tf_op jit(solution)/shard_map/ppermute | solution.py:227
  71.8 10.8 %collective-permute-start.26 = (bf16[64,1408]{1,0:T(8,128)(2,1)S(1)}, bf16[64,1408]{1,0:T(8,128)(2,1)S(1)}, u32[]{:S(2)}, u32[]{:S(2)}) collective-permute-start(bf16[64,1408]{1,0:T(8,128)(2,1)S(1)} %get-tuple-element.51), channel_id=1, source_target_pairs={{0,24},{8,16},{16,8},{24,0},{1,25},{9,17},{17,9},{25,1},{2,26},{10... | collective-permute-start | bytes 540680 | tf_op jit(solution)/shard_map/ppermute | solution.py:227
  (1 other events, 0.7 us)

commit v4 on v3

--- a/solution.py
+++ b/solution.py
@@ -83,9 +83,23 @@
     return jnp.concatenate([r[:, at:at + width] for r in refs], axis=0)
 
 
-def fold(weighted, picks):
-    half = mm(weighted, picks, ((1,), (0,)), HIGH)
-    return mm(picks, half, ((0,), (0,)), HIGH)
+def three_parts(value):
+    parts = []
+    for _ in range(3):
+        parts.append(value.astype(jnp.bfloat16))
+        value = value - parts[-1].astype(jnp.float32)
+    return parts
+
+
+def fold(me, weighted, channels, members, group):
+    rows = weighted.shape[0]
+    half = jnp.sum(weighted.reshape(members, channels, rows), axis=1)
+    picks = member_of_row(me, rows, channels, members, group).astype(jnp.bfloat16)
+    half = sum(mm(part, picks, ((1,), (0,))) for part in three_parts(half))
+    local = lax.broadcasted_iota(jnp.int32, (members, members), 1)
+    member = lax.broadcasted_iota(jnp.int32, (members, members), 0)
+    order = (((local // group) ^ me) * group + local % group == member).astype(jnp.bfloat16)
+    return sum(mm(order, part, ((1,), (0,))) for part in three_parts(half))
 
 
 def masked_gram(me, count, chunk, length, left, right):
@@ -106,19 +120,15 @@
 def score_kernel(me_of, count, chunk, length, group, channels, members, tile_ref, *refs):
     me = me_of()
     fields, out_ref = refs[:count], refs[-1]
-    rows = count * fields[0].shape[0]
     total = masked_gram(me, count, chunk, length, fields, fields)
-    picks = member_of_row(me, rows, channels, members, group)
-    out_ref[...] = fold(total * tile_ref[...], picks)
+    out_ref[...] = fold(me, total * tile_ref[...], channels, members, group)
 
 
 def pair_kernel(me_of, count, chunk, length, group, channels, members, tile_ref, *refs):
     me = me_of()
     fields, grads, out_ref = refs[:count], refs[count:2 * count], refs[-1]
-    rows = count * fields[0].shape[0]
     total = masked_gram(me, count, chunk, length, grads, fields)
-    picks = member_of_row(me, rows, channels, members, group)
-    out_ref[...] = fold(total * tile_ref[...], picks)
+    out_ref[...] = fold(me, total * tile_ref[...], channels, members, group)
 
 
 def add_up(refs):
@@ -170,9 +180,19 @@
             outs[s][:, at:at + width] = b[s * per:(s + 1) * per]
 
 
+def transposed_weights_kernel(
+    me_of, channels, members, group, scale, s_ref, ovt_ref, w_ref, high_ref, low_ref
+):
+    rows = ovt_ref.shape[0]
+    picks = member_of_row(me_of(), rows, channels, members, group).astype(jnp.bfloat16)
+    weights = softmax(s_ref[...] * scale)
+    w_ref[...] = weights
+    high_ref[...], low_ref[...] = two_parts(spread_t(weights, picks) * ovt_ref[...])
+
+
 def grad_kernel(
     me_of, count, chunk, group, channels, members, scale, low, size, waits,
-    s_ref, qk_ref, qkt_ref, ovt_ref, *refs,
+    w_ref, qk_ref, qkt_ref, a_high_ref, a_low_ref, *refs,
 ):
     me = me_of()
     fields, grads, sums = refs[:count], refs[count:2 * count], refs[2 * count:3 * count]
@@ -180,13 +200,13 @@
     per = fields[0].shape[0]
     rows = count * per
     picks = member_of_row(me, rows, channels, members, group).astype(jnp.bfloat16)
-    weights = softmax(s_ref[...] * scale)
+    weights = w_ref[...]
     pairs = add_up(sums)
     slope = weights * (pairs - jnp.sum(weights * pairs, axis=1, keepdims=True)) * scale
     d_high, d_low = two_parts(
         spread(slope, picks) * qk_ref[...] + spread_t(slope, picks) * qkt_ref[...]
     )
-    a_high, a_low = two_parts(spread_t(weights, picks) * ovt_ref[...])
+    a_high, a_low = a_high_ref[...], a_low_ref[...]
     for at, width in lane_tiles(size):
         e = gather_tile(fields, low + at, width)
         c = gather_tile(grads, low + at, width)
@@ -324,7 +344,7 @@
     )(qk, *e_cells)
     scores = sum_steps(scores, "space", space_steps[:-1])
     scores = join(scores, "space", space_steps[-1], c_cells[first:first + 1])
-    order = sorted(range(1, count), key=lambda s: (s & (s - 1) != 0, -s))
+    order = sorted(range(1, count), key=lambda s: (s & (s - 1) == 0, s))
     score_parts = [scores] + [swap(scores, s, count) for s in order]
     waited = score_parts[:1]
     pairs = pl.pallas_call(
@@ -356,6 +376,18 @@
     pairs = join(pairs, "space", space_steps[-1], branch_home[first:first + 1])
     pair_parts = [pairs] + [swap(pairs, s, count) for s in order]
 
+    weights, a_high, a_low = pl.pallas_call(
+        functools.partial(
+            transposed_weights_kernel, me_of, channels, members, group, scale
+        ),
+        out_shape=[pair] + [jax.ShapeDtypeStruct((rows, rows), bf)] * 2,
+        in_specs=[whole] * 2,
+        out_specs=[whole] * 3,
+        compiler_params=params,
+        cost_estimate=cost(10**8, 8 * rows * rows),
+        name="transposed_weights",
+    )(scores, ovt)
+
     def gradient(low, size, awaited, name):
         parts = pl.pallas_call(
             functools.partial(
@@ -363,12 +395,12 @@
                 size, len(awaited),
             ),
             out_shape=[jax.ShapeDtypeStruct((per, size), bf)] * count,
-            in_specs=[whole] * (3 * count + 4) + [anywhere] * len(awaited),
+            in_specs=[whole] * (3 * count + 5) + [anywhere] * len(awaited),
             out_specs=[whole] * count,
             compiler_params=params,
             cost_estimate=cost(8 * rows * rows * size, 6 * rows * size),
             name=name,
-        )(scores, qk, qkt, ovt, *e_cells, *c_cells, *pair_parts, *awaited)
+        )(weights, qk, qkt, a_high, a_low, *e_cells, *c_cells, *pair_parts, *awaited)
         return exchange(parts)
 
     half = half_of(chunk)

time: 83.9 us -> 83.3 us (level)
  Pallas kernels: 14.6 us -> 13.5 us
  starting transfers between devices: 33.3 us -> 34.2 us
  transfers between devices with their start and end apart: 27 -> 27, of which waited for: 18 -> 17; matrix products, arithmetic and copies ran while one was open for 0% -> 0% of each run, Pallas kernels for 12% -> 12%
where the time goes in v4:
time: 83.3 us; the launch traced here: 83 us
  starting transfers between devices  34.2 us (41%)
  waiting for transfers between devices  29.1 us (35%)
  Pallas kernels  13.5 us (16%)
  local copies, waits for them, and re-layouts  5.48 us (7%)
    ppermute x21, starting transfers between devices, swap(): return lax.ppermute(value, 'mem', [(i, i ^ step) for i in range(count)])  25.8 us
    ppermute x21, waiting for transfers between devices, swap(): return lax.ppermute(value, 'mem', [(i, i ^ step) for i in range(count)])  18.6 us
    ppermute x4, waiting for transfers between devices, sum_steps(): lax.ppermute(value, name, [(i, i ^ step) for i in range(size)])  6.53 us
    unnamed x12, local copies, waits for them, and re-layouts  5.48 us
    pallas_call x3, Pallas kernels, finish(): pl.pallas_call(functools.partial(finish_kernel, me_of, count, chunk, leng...  5.4 us
    ppermute x2, starting transfers between devices, join(): other = lax.ppermute(value, name, [(i, i ^ step) for i in range(size)])  5.16 us
    ppermute x2, waiting for transfers between devices, join(): other = lax.ppermute(value, name, [(i, i ^ step) for i in range(size)])  3.93 us
    ppermute x4, starting transfers between devices, sum_steps(): lax.ppermute(value, name, [(i, i ^ step) for i in range(size)])  3.14 us
  transfers between devices with their start and end apart: 27, of which 17 were waited for; matrix products, arithmetic and copies ran while one was open for 0% of the time, Pallas kernels for 12%

profile of v4, /device:TPU:0, one launch (start us, length us, event | category | flops | bytes accessed | tf_op | source)
XLA Modules:
  0.0 83.0 jit_solution(1991018046891211704)
XLA Ops:
  0.6 1.4 %copy-done = bf16[4,16,11520]{2,1,0:T(8,128)(2,1)S(1)} copy-done((bf16[4,16,11520]{2,1,0:T(8,128)(2,1)S(1)}, bf16[4,16,11520]{2,1,0:T(8,128)(2,1)}, u32[]{:S(2)}) %copy-start) | copy-done | bytes 1474584
  2.2 3.0 %collective-permute-start = (bf16[64,2944]{1,0:T(8,128)(2,1)S(1)}, bf16[64,2944]{1,0:T(8,128)(2,1)S(1)}, u32[]{:S(2)}, u32[]{:S(2)}) collective-permute-start(bf16[64,2944]{1,0:T(8,128)(2,1)S(1)} %get-tuple-element.33.refs_2_), channel_id=1, source_target_pairs={{0,8},{8,0},{16,24},{24,16},{1,9},{9,1},{17,25},{25,17},{2,10},{10... | collective-permute-start | bytes 1130504 | tf_op jit(solution)/shard_map/ppermute | solution.py:247
  5.2 1.5 %collective-permute-start.1 = (bf16[64,2944]{1,0:T(8,128)(2,1)S(1)}, bf16[64,2944]{1,0:T(8,128)(2,1)S(1)}, u32[]{:S(2)}, u32[]{:S(2)}) collective-permute-start(bf16[64,2944]{1,0:T(8,128)(2,1)S(1)} %get-tuple-element.34.refs_3_), channel_id=1, source_target_pairs={{0,16},{8,24},{16,0},{24,8},{1,17},{9,25},{17,1},{25,9},{2,18},{10... | collective-permute-start | bytes 1130504 | tf_op jit(solution)/shard_map/ppermute | solution.py:247
  10.8 4.0 %collective-permute-done.refs_1_.rest_0_.refs_5_ = bf16[64,2944]{1,0:T(8,128)(2,1)S(1)} collective-permute-done((bf16[64,2944]{1,0:T(8,128)(2,1)S(1)}, bf16[64,2944]{1,0:T(8,128)(2,1)S(1)}, u32[]{:S(2)}, u32[]{:S(2)}) %collective-permute-start) | collective-permute-done | bytes 376864 | tf_op jit(solution)/shard_map/ppermute | solution.py:247
  14.8 1.4 %copy-done.1 = bf16[4,16,11520]{2,1,0:T(8,128)(2,1)S(1)} copy-done((bf16[4,16,11520]{2,1,0:T(8,128)(2,1)S(1)}, bf16[4,16,11520]{2,1,0:T(8,128)(2,1)}, u32[]{:S(2)}) %copy-start.1) | copy-done | bytes 1474584
  16.4 2.1 %collective-permute-start.6 = (bf16[64,2944]{1,0:T(8,128)(2,1)S(1)}, bf16[64,2944]{1,0:T(8,128)(2,1)S(1)}, u32[]{:S(2)}, u32[]{:S(2)}) collective-permute-start(bf16[64,2944]{1,0:T(8,128)(2,1)S(1)} %get-tuple-element.36.refs_1_.refs_2_), channel_id=1, source_target_pairs={{0,8},{8,0},{16,24},{24,16},{1,9},{9,1},{17,25},{25,17},{2,10},{10... | collective-permute-start | bytes 1130504 | tf_op jit(solution)/shard_map/ppermute | solution.py:247
  18.5 1.5 %collective-permute-start.10 = (bf16[64,2944]{1,0:T(8,128)(2,1)S(1)}, bf16[64,2944]{1,0:T(8,128)(2,1)S(1)}, u32[]{:S(2)}, u32[]{:S(2)}) collective-permute-start(bf16[64,2944]{1,0:T(8,128)(2,1)S(1)} %get-tuple-element.38.refs_2_.refs_3_), channel_id=1, source_target_pairs={{0,16},{8,24},{16,0},{24,8},{1,17},{9,25},{17,1},{25,9},{2,18},{10... | collective-permute-start | bytes 1130504 | tf_op jit(solution)/shard_map/ppermute | solution.py:247
  20.0 3.9 %collective-permute-done.1.refs_2_.refs_6_ = bf16[64,2944]{1,0:T(8,128)(2,1)S(1)} collective-permute-done((bf16[64,2944]{1,0:T(8,128)(2,1)S(1)}, bf16[64,2944]{1,0:T(8,128)(2,1)S(1)}, u32[]{:S(2)}, u32[]{:S(2)}) %collective-permute-start.1) | collective-permute-done | bytes 376864 | tf_op jit(solution)/shard_map/ppermute | solution.py:247
  26.6 1.6 %collective-permute-start.4 = (f32[16,16]{1,0:T(8,128)S(1)}, f32[16,16]{1,0:T(8,128)S(1)}, u32[]{:S(2)}, u32[]{:S(2)}) collective-permute-start(f32[16,16]{1,0:T(8,128)S(1)} %add.12), channel_id=1, source_target_pairs={{0,2},{1,3},{2,0},{3,1},{4,6},{5,7},{6,4},{7,5},{8,10},{9,11},{10,... | collective-permute-start | bytes 3080 | tf_op jit(solution)/shard_map/ppermute | solution.py:258
  28.2 2.1 %collective-permute-done.4 = f32[16,16]{1,0:T(8,128)S(1)} collective-permute-done((f32[16,16]{1,0:T(8,128)S(1)}, f32[16,16]{1,0:T(8,128)S(1)}, u32[]{:S(2)}, u32[]{:S(2)}) %collective-permute-start.4) | collective-permute-done | bytes 1056 | tf_op jit(solution)/shard_map/ppermute | solution.py:258
  30.3 2.6 %collective-permute-start.5 = (f32[16,16]{1,0:T(8,128)S(1)}, f32[16,16]{1,0:T(8,128)S(1)}, u32[]{:S(2)}, u32[]{:S(2)}) collective-permute-start(f32[16,16]{1,0:T(8,128)S(1)} %add.13.a_ref), channel_id=1, source_target_pairs={{0,4},{1,5},{2,6},{3,7},{4,0},{5,1},{6,2},{7,3},{8,12},{9,13},{10,... | collective-permute-start | bytes 3080 | tf_op jit(solution)/shard_map/ppermute | solution.py:323
  32.9 2.0 %collective-permute-done.5.b_ref = f32[16,16]{1,0:T(8,128)S(1)} collective-permute-done((f32[16,16]{1,0:T(8,128)S(1)}, f32[16,16]{1,0:T(8,128)S(1)}, u32[]{:S(2)}, u32[]{:S(2)}) %collective-permute-start.5) | collective-permute-done | bytes 1056 | tf_op jit(solution)/shard_map/ppermute | solution.py:323
  34.8 1.9 %collective-permute-start.9 = (f32[16,16]{1,0:T(8,128)S(1)}, f32[16,16]{1,0:T(8,128)S(1)}, u32[]{:S(2)}, u32[]{:S(2)}) collective-permute-start(f32[16,16]{1,0:T(8,128)S(1)} %join_sums.2.refs_8_.refs_0_), channel_id=1, source_target_pairs={{0,16},{8,24},{16,0},{24,8},{1,17},{9,25},{17,1},{25,9},{2,18},{10... | collective-permute-start | bytes 3080 | tf_op jit(solution)/shard_map/ppermute | solution.py:247
  36.8 1.5 %collective-permute-start.7 = (f32[16,16]{1,0:T(8,128)S(1)}, f32[16,16]{1,0:T(8,128)S(1)}, u32[]{:S(2)}, u32[]{:S(2)}) collective-permute-start(f32[16,16]{1,0:T(8,128)S(1)} %join_sums.2.refs_8_.refs_0_), channel_id=1, source_target_pairs={{0,24},{8,16},{16,8},{24,0},{1,25},{9,17},{17,9},{25,1},{2,26},{10... | collective-permute-start | bytes 3080 | tf_op jit(solution)/shard_map/ppermute | solution.py:247
  38.3 1.5 %collective-permute-done.10.refs_6_ = bf16[64,2944]{1,0:T(8,128)(2,1)S(1)} collective-permute-done((bf16[64,2944]{1,0:T(8,128)(2,1)S(1)}, bf16[64,2944]{1,0:T(8,128)(2,1)S(1)}, u32[]{:S(2)}, u32[]{:S(2)}) %collective-permute-start.10) | collective-permute-done | bytes 376864 | tf_op jit(solution)/shard_map/ppermute | solution.py:247
  41.4 1.4 %branch.1 = (f32[16,16]{1,0:T(8,128)S(1)}, bf16[64,2944]{1,0:T(8,128)(2,1)S(1)}, bf16[64,2944]{1,0:T(8,128)(2,1)S(1)}, bf16[64,2944]{1,0:T(8,128)(2,1)S(1)}, bf16[64,2944]{1,0:T(8,128)(2,1)S(1)}) custom-call(f32[256,256]{1,0:T(8,128)S(1)} %get-tuple-element.30.tile_ref.ov_ref, f32[16,16]{1,0:T(8,128)S(1)} %join_sums.2.refs_8_.refs_0_, ...), custom_call_target="tpu_custom_call" | custom-call | flops 771751936 | bytes 3014656 | tf_op jit(solution)/shard_map/branch/pallas_call | solution.py:362
  42.7 2.0 %collective-permute-start.15 = (bf16[64,2944]{1,0:T(8,128)(2,1)S(1)}, bf16[64,2944]{1,0:T(8,128)(2,1)S(1)}, u32[]{:S(2)}, u32[]{:S(2)}) collective-permute-start(bf16[64,2944]{1,0:T(8,128)(2,1)S(1)} %get-tuple-element.46), channel_id=1, source_target_pairs={{0,8},{8,0},{16,24},{24,16},{1,9},{9,1},{17,25},{25,17},{2,10},{10... | collective-permute-start | bytes 1130504 | tf_op jit(solution)/shard_map/ppermute | solution.py:247
  44.9 1.5 %collective-permute-start.20 = (bf16[64,2944]{1,0:T(8,128)(2,1)S(1)}, bf16[64,2944]{1,0:T(8,128)(2,1)S(1)}, u32[]{:S(2)}, u32[]{:S(2)}) collective-permute-start(bf16[64,2944]{1,0:T(8,128)(2,1)S(1)} %get-tuple-element.48), channel_id=1, source_target_pairs={{0,24},{8,16},{16,8},{24,0},{1,25},{9,17},{17,9},{25,1},{2,26},{10... | collective-permute-start | bytes 1130504 | tf_op jit(solution)/shard_map/ppermute | solution.py:247
  47.5 1.6 %collective-permute-start.13 = (f32[16,16]{1,0:T(8,128)S(1)}, f32[16,16]{1,0:T(8,128)S(1)}, u32[]{:S(2)}, u32[]{:S(2)}) collective-permute-start(f32[16,16]{1,0:T(8,128)S(1)} %add.14), channel_id=1, source_target_pairs={{0,2},{1,3},{2,0},{3,1},{4,6},{5,7},{6,4},{7,5},{8,10},{9,11},{10,... | collective-permute-start | bytes 3080 | tf_op jit(solution)/shard_map/ppermute | solution.py:258
  49.1 2.1 %collective-permute-done.13 = f32[16,16]{1,0:T(8,128)S(1)} collective-permute-done((f32[16,16]{1,0:T(8,128)S(1)}, f32[16,16]{1,0:T(8,128)S(1)}, u32[]{:S(2)}, u32[]{:S(2)}) %collective-permute-start.13) | collective-permute-done | bytes 1056 | tf_op jit(solution)/shard_map/ppermute | solution.py:258
  51.2 2.6 %collective-permute-start.14 = (f32[16,16]{1,0:T(8,128)S(1)}, f32[16,16]{1,0:T(8,128)S(1)}, u32[]{:S(2)}, u32[]{:S(2)}) collective-permute-start(f32[16,16]{1,0:T(8,128)S(1)} %add.15.a_ref), channel_id=1, source_target_pairs={{0,4},{1,5},{2,6},{3,7},{4,0},{5,1},{6,2},{7,3},{8,12},{9,13},{10,... | collective-permute-start | bytes 3080 | tf_op jit(solution)/shard_map/ppermute | solution.py:323
  53.7 2.0 %collective-permute-done.14.b_ref = f32[16,16]{1,0:T(8,128)S(1)} collective-permute-done((f32[16,16]{1,0:T(8,128)S(1)}, f32[16,16]{1,0:T(8,128)S(1)}, u32[]{:S(2)}, u32[]{:S(2)}) %collective-permute-start.14) | collective-permute-done | bytes 1056 | tf_op jit(solution)/shard_map/ppermute | solution.py:323
  55.7 1.5 %collective-permute-start.18 = (f32[16,16]{1,0:T(8,128)S(1)}, f32[16,16]{1,0:T(8,128)S(1)}, u32[]{:S(2)}, u32[]{:S(2)}) collective-permute-start(f32[16,16]{1,0:T(8,128)S(1)} %join_sums.3.refs_8_), channel_id=1, source_target_pairs={{0,16},{8,24},{16,0},{24,8},{1,17},{9,25},{17,1},{25,9},{2,18},{10... | collective-permute-start | bytes 3080 | tf_op jit(solution)/shard_map/ppermute | solution.py:247
  57.8 1.5 %collective-permute-start.16 = (f32[16,16]{1,0:T(8,128)S(1)}, f32[16,16]{1,0:T(8,128)S(1)}, u32[]{:S(2)}, u32[]{:S(2)}) collective-permute-start(f32[16,16]{1,0:T(8,128)S(1)} %join_sums.3.refs_8_), channel_id=1, source_target_pairs={{0,24},{8,16},{16,8},{24,0},{1,25},{9,17},{17,9},{25,1},{2,26},{10... | collective-permute-start | bytes 3080 | tf_op jit(solution)/shard_map/ppermute | solution.py:247
  63.6 1.6 %collective-permute-start.21 = (bf16[64,1536]{1,0:T(8,128)(2,1)S(1)}, bf16[64,1536]{1,0:T(8,128)(2,1)S(1)}, u32[]{:S(2)}, u32[]{:S(2)}) collective-permute-start(bf16[64,1536]{1,0:T(8,128)(2,1)S(1)} %get-tuple-element.49), channel_id=1, source_target_pairs={{0,8},{8,0},{16,24},{24,16},{1,9},{9,1},{17,25},{25,17},{2,10},{10... | collective-permute-start | bytes 589832 | tf_op jit(solution)/shard_map/ppermute | solution.py:247
  65.7 1.5 %collective-permute-start.23 = (bf16[64,1536]{1,0:T(8,128)(2,1)S(1)}, bf16[64,1536]{1,0:T(8,128)(2,1)S(1)}, u32[]{:S(2)}, u32[]{:S(2)}) collective-permute-start(bf16[64,1536]{1,0:T(8,128)(2,1)S(1)} %get-tuple-element.53), channel_id=1, source_target_pairs={{0,24},{8,16},{16,8},{24,0},{1,25},{9,17},{17,9},{25,1},{2,26},{10... | collective-permute-start | bytes 589832 | tf_op jit(solution)/shard_map/ppermute | solution.py:247
  68.5 1.6 %collective-permute-start.24 = (bf16[64,1408]{1,0:T(8,128)(2,1)S(1)}, bf16[64,1408]{1,0:T(8,128)(2,1)S(1)}, u32[]{:S(2)}, u32[]{:S(2)}) collective-permute-start(bf16[64,1408]{1,0:T(8,128)(2,1)S(1)} %get-tuple-element.55), channel_id=1, source_target_pairs={{0,8},{8,0},{16,24},{24,16},{1,9},{9,1},{17,25},{25,17},{2,10},{10... | collective-permute-start | bytes 540680 | tf_op jit(solution)/shard_map/ppermute | solution.py:247
  71.4 1.5 %collective-permute-start.26 = (bf16[64,1408]{1,0:T(8,128)(2,1)S(1)}, bf16[64,1408]{1,0:T(8,128)(2,1)S(1)}, u32[]{:S(2)}, u32[]{:S(2)}) collective-permute-start(bf16[64,1408]{1,0:T(8,128)(2,1)S(1)} %get-tuple-element.57), channel_id=1, source_target_pairs={{0,24},{8,16},{16,8},{24,0},{1,25},{9,17},{17,9},{25,1},{2,26},{10... | collective-permute-start | bytes 540680 | tf_op jit(solution)/shard_map/ppermute | solution.py:247
  72.9 2.4 %updated.1 = f32[64,11520]{1,0:T(8,128)} custom-call(bf16[64,1536]{1,0:T(8,128)(2,1)S(1)} %collective-permute-done.21.refs_0_.refs_5_, bf16[64,2944]{1,0:T(8,128)(2,1)S(1)} %get-tuple-element.32.refs_0_.refs_4_.refs_1_, bf16[64,2944]{1,0:T(8,128)(2,1)S(1)} %get-tuple-element.33.refs_2_, bf16[64,2944]{1,0:T(8,128)(2,1)S(1)} %get-tuple-element.34.refs_3_, ...), custom_call_target="tpu_custom_call" | custom-call | flops 737280 | bytes 5898240 | tf_op jit(solution)/shard_map/updated/pallas_call | solution.py:416
  75.3 2.0 %collective-permute-done.23.refs_7_ = bf16[64,1536]{1,0:T(8,128)(2,1)S(1)} collective-permute-done((bf16[64,1536]{1,0:T(8,128)(2,1)S(1)}, bf16[64,1536]{1,0:T(8,128)(2,1)S(1)}, u32[]{:S(2)}, u32[]{:S(2)}) %collective-permute-start.23) | collective-permute-done | bytes 196640 | tf_op jit(solution)/shard_map/ppermute | solution.py:247
  77.2 2.0 %ensemble_grad_early.1.refs_0_ = f32[64,11520]{1,0:T(8,128)} custom-call(bf16[64,2944]{1,0:T(8,128)(2,1)S(1)} %get-tuple-element.37.refs_4_.refs_0_.refs_1_, bf16[64,2944]{1,0:T(8,128)(2,1)S(1)} %get-tuple-element.36.refs_1_.refs_2_, bf16[64,2944]{1,0:T(8,128)(2,1)S(1)} %get-tuple-element.38.refs_2_.refs_3_, ...), custom_call_target="tpu_custom_call" | custom-call | flops 737280 | bytes 5898240 | tf_op jit(solution)/shard_map/ensemble_grad_early/pallas_call | solution.py:416
  79.3 2.7 %collective-permute-done.25.refs_6_ = bf16[64,1408]{1,0:T(8,128)(2,1)S(1)} collective-permute-done((bf16[64,1408]{1,0:T(8,128)(2,1)S(1)}, bf16[64,1408]{1,0:T(8,128)(2,1)S(1)}, u32[]{:S(2)}, u32[]{:S(2)}) %collective-permute-start.25) | collective-permute-done | bytes 180256 | tf_op jit(solution)/shard_map/ppermute | solution.py:247
  (52 shorter events, 19.3 us)
Async XLA Ops:
  0.6 1.4 %copy-start = (bf16[4,16,11520]{2,1,0:T(8,128)(2,1)S(1)}, bf16[4,16,11520]{2,1,0:T(8,128)(2,1)}, u32[]{:S(2)}) copy-start(bf16[4,16,11520]{2,1,0:T(8,128)(2,1)} %param.6) | copy-start | bytes 4423684
  2.2 12.6 %collective-permute-start = (bf16[64,2944]{1,0:T(8,128)(2,1)S(1)}, bf16[64,2944]{1,0:T(8,128)(2,1)S(1)}, u32[]{:S(2)}, u32[]{:S(2)}) collective-permute-start(bf16[64,2944]{1,0:T(8,128)(2,1)S(1)} %get-tuple-element.33.refs_2_), channel_id=1, source_target_pairs={{0,8},{8,0},{16,24},{24,16},{1,9},{9,1},{17,25},{25,17},{2,10},{10... | collective-permute-start | bytes 1130504 | tf_op jit(solution)/shard_map/ppermute | solution.py:247
  5.2 18.7 %collective-permute-start.1 = (bf16[64,2944]{1,0:T(8,128)(2,1)S(1)}, bf16[64,2944]{1,0:T(8,128)(2,1)S(1)}, u32[]{:S(2)}, u32[]{:S(2)}) collective-permute-start(bf16[64,2944]{1,0:T(8,128)(2,1)S(1)} %get-tuple-element.34.refs_3_), channel_id=1, source_target_pairs={{0,16},{8,24},{16,0},{24,8},{1,17},{9,25},{17,1},{25,9},{2,18},{10... | collective-permute-start | bytes 1130504 | tf_op jit(solution)/shard_map/ppermute | solution.py:247
  6.7 17.7 %collective-permute-start.2 = (bf16[64,2944]{1,0:T(8,128)(2,1)S(1)}, bf16[64,2944]{1,0:T(8,128)(2,1)S(1)}, u32[]{:S(2)}, u32[]{:S(2)}) collective-permute-start(bf16[64,2944]{1,0:T(8,128)(2,1)S(1)} %get-tuple-element.35.refs_4_), channel_id=1, source_target_pairs={{0,24},{8,16},{16,8},{24,0},{1,25},{9,17},{17,9},{25,1},{2,26},{10... | collective-permute-start | bytes 1130504 | tf_op jit(solution)/shard_map/ppermute | solution.py:247
  6.7 0.7 copy-start.2
  7.4 0.7 copy-start.3
  8.8 0.7 copy-start.5
  14.8 1.4 %copy-start.1 = (bf16[4,16,11520]{2,1,0:T(8,128)(2,1)S(1)}, bf16[4,16,11520]{2,1,0:T(8,128)(2,1)}, u32[]{:S(2)}) copy-start(bf16[4,16,11520]{2,1,0:T(8,128)(2,1)} %param.7) | copy-start | bytes 4423684
  16.4 18.5 %collective-permute-start.6 = (bf16[64,2944]{1,0:T(8,128)(2,1)S(1)}, bf16[64,2944]{1,0:T(8,128)(2,1)S(1)}, u32[]{:S(2)}, u32[]{:S(2)}) collective-permute-start(bf16[64,2944]{1,0:T(8,128)(2,1)S(1)} %get-tuple-element.36.refs_1_.refs_2_), channel_id=1, source_target_pairs={{0,8},{8,0},{16,24},{24,16},{1,9},{9,1},{17,25},{25,17},{2,10},{10... | collective-permute-start | bytes 1130504 | tf_op jit(solution)/shard_map/ppermute | solution.py:247
  18.5 21.3 %collective-permute-start.10 = (bf16[64,2944]{1,0:T(8,128)(2,1)S(1)}, bf16[64,2944]{1,0:T(8,128)(2,1)S(1)}, u32[]{:S(2)}, u32[]{:S(2)}) collective-permute-start(bf16[64,2944]{1,0:T(8,128)(2,1)S(1)} %get-tuple-element.38.refs_2_.refs_3_), channel_id=1, source_target_pairs={{0,16},{8,24},{16,0},{24,8},{1,17},{9,25},{17,1},{25,9},{2,18},{10... | collective-permute-start | bytes 1130504 | tf_op jit(solution)/shard_map/ppermute | solution.py:247
  20.0 19.8 %collective-permute-start.11 = (bf16[64,2944]{1,0:T(8,128)(2,1)S(1)}, bf16[64,2944]{1,0:T(8,128)(2,1)S(1)}, u32[]{:S(2)}, u32[]{:S(2)}) collective-permute-start(bf16[64,2944]{1,0:T(8,128)(2,1)S(1)} %get-tuple-element.39.refs_3_.refs_4_), channel_id=1, source_target_pairs={{0,24},{8,16},{16,8},{24,0},{1,25},{9,17},{17,9},{25,1},{2,26},{10... | collective-permute-start | bytes 1130504 | tf_op jit(solution)/shard_map/ppermute | solution.py:247
  25.4 1.2 %collective-permute-start.3 = (f32[16,16]{1,0:T(8,128)S(1)}, f32[16,16]{1,0:T(8,128)S(1)}, u32[]{:S(2)}, u32[]{:S(2)}) collective-permute-start(f32[16,16]{1,0:T(8,128)S(1)} %score_sums.1), channel_id=1, source_target_pairs={{0,1},{1,0},{2,3},{3,2},{4,5},{5,4},{6,7},{7,6},{8,9},{9,8},{10,11... | collective-permute-start | bytes 3080 | tf_op jit(solution)/shard_map/ppermute | solution.py:258
  26.6 3.7 %collective-permute-start.4 = (f32[16,16]{1,0:T(8,128)S(1)}, f32[16,16]{1,0:T(8,128)S(1)}, u32[]{:S(2)}, u32[]{:S(2)}) collective-permute-start(f32[16,16]{1,0:T(8,128)S(1)} %add.12), channel_id=1, source_target_pairs={{0,2},{1,3},{2,0},{3,1},{4,6},{5,7},{6,4},{7,5},{8,10},{9,11},{10,... | collective-permute-start | bytes 3080 | tf_op jit(solution)/shard_map/ppermute | solution.py:258
  30.3 4.5 %collective-permute-start.5 = (f32[16,16]{1,0:T(8,128)S(1)}, f32[16,16]{1,0:T(8,128)S(1)}, u32[]{:S(2)}, u32[]{:S(2)}) collective-permute-start(f32[16,16]{1,0:T(8,128)S(1)} %add.13.a_ref), channel_id=1, source_target_pairs={{0,4},{1,5},{2,6},{3,7},{4,0},{5,1},{6,2},{7,3},{8,12},{9,13},{10,... | collective-permute-start | bytes 3080 | tf_op jit(solution)/shard_map/ppermute | solution.py:323
  34.8 6.0 %collective-permute-start.9 = (f32[16,16]{1,0:T(8,128)S(1)}, f32[16,16]{1,0:T(8,128)S(1)}, u32[]{:S(2)}, u32[]{:S(2)}) collective-permute-start(f32[16,16]{1,0:T(8,128)S(1)} %join_sums.2.refs_8_.refs_0_), channel_id=1, source_target_pairs={{0,16},{8,24},{16,0},{24,8},{1,17},{9,25},{17,1},{25,9},{2,18},{10... | collective-permute-start | bytes 3080 | tf_op jit(solution)/shard_map/ppermute | solution.py:247
  36.8 4.0 %collective-permute-start.8 = (f32[16,16]{1,0:T(8,128)S(1)}, f32[16,16]{1,0:T(8,128)S(1)}, u32[]{:S(2)}, u32[]{:S(2)}) collective-permute-start(f32[16,16]{1,0:T(8,128)S(1)} %join_sums.2.refs_8_.refs_0_), channel_id=1, source_target_pairs={{0,8},{8,0},{16,24},{24,16},{1,9},{9,1},{17,25},{25,17},{2,10},{10... | collective-permute-start | bytes 3080 | tf_op jit(solution)/shard_map/ppermute | solution.py:247
  36.8 4.5 %collective-permute-start.7 = (f32[16,16]{1,0:T(8,128)S(1)}, f32[16,16]{1,0:T(8,128)S(1)}, u32[]{:S(2)}, u32[]{:S(2)}) collective-permute-start(f32[16,16]{1,0:T(8,128)S(1)} %join_sums.2.refs_8_.refs_0_), channel_id=1, source_target_pairs={{0,24},{8,16},{16,8},{24,0},{1,25},{9,17},{17,9},{25,1},{2,26},{10... | collective-permute-start | bytes 3080 | tf_op jit(solution)/shard_map/ppermute | solution.py:247
  42.7 13.0 %collective-permute-start.15 = (bf16[64,2944]{1,0:T(8,128)(2,1)S(1)}, bf16[64,2944]{1,0:T(8,128)(2,1)S(1)}, u32[]{:S(2)}, u32[]{:S(2)}) collective-permute-start(bf16[64,2944]{1,0:T(8,128)(2,1)S(1)} %get-tuple-element.46), channel_id=1, source_target_pairs={{0,8},{8,0},{16,24},{24,16},{1,9},{9,1},{17,25},{25,17},{2,10},{10... | collective-permute-start | bytes 1130504 | tf_op jit(solution)/shard_map/ppermute | solution.py:247
  44.8 16.2 %collective-permute-start.19 = (bf16[64,2944]{1,0:T(8,128)(2,1)S(1)}, bf16[64,2944]{1,0:T(8,128)(2,1)S(1)}, u32[]{:S(2)}, u32[]{:S(2)}) collective-permute-start(bf16[64,2944]{1,0:T(8,128)(2,1)S(1)} %get-tuple-element.47), channel_id=1, source_target_pairs={{0,16},{8,24},{16,0},{24,8},{1,17},{9,25},{17,1},{25,9},{2,18},{10... | collective-permute-start | bytes 1130504 | tf_op jit(solution)/shard_map/ppermute | solution.py:247
  44.9 16.2 %collective-permute-start.20 = (bf16[64,2944]{1,0:T(8,128)(2,1)S(1)}, bf16[64,2944]{1,0:T(8,128)(2,1)S(1)}, u32[]{:S(2)}, u32[]{:S(2)}) collective-permute-start(bf16[64,2944]{1,0:T(8,128)(2,1)S(1)} %get-tuple-element.48), channel_id=1, source_target_pairs={{0,24},{8,16},{16,8},{24,0},{1,25},{9,17},{17,9},{25,1},{2,26},{10... | collective-permute-start | bytes 1130504 | tf_op jit(solution)/shard_map/ppermute | solution.py:247
  46.3 1.2 %collective-permute-start.12 = (f32[16,16]{1,0:T(8,128)S(1)}, f32[16,16]{1,0:T(8,128)S(1)}, u32[]{:S(2)}, u32[]{:S(2)}) collective-permute-start(f32[16,16]{1,0:T(8,128)S(1)} %pair_sums.1.refs_8_), channel_id=1, source_target_pairs={{0,1},{1,0},{2,3},{3,2},{4,5},{5,4},{6,7},{7,6},{8,9},{9,8},{10,11... | collective-permute-start | bytes 3080 | tf_op jit(solution)/shard_map/ppermute | solution.py:258
  47.5 3.7 %collective-permute-start.13 = (f32[16,16]{1,0:T(8,128)S(1)}, f32[16,16]{1,0:T(8,128)S(1)}, u32[]{:S(2)}, u32[]{:S(2)}) collective-permute-start(f32[16,16]{1,0:T(8,128)S(1)} %add.14), channel_id=1, source_target_pairs={{0,2},{1,3},{2,0},{3,1},{4,6},{5,7},{6,4},{7,5},{8,10},{9,11},{10,... | collective-permute-start | bytes 3080 | tf_op jit(solution)/shard_map/ppermute | solution.py:258
  51.2 4.5 %collective-permute-start.14 = (f32[16,16]{1,0:T(8,128)S(1)}, f32[16,16]{1,0:T(8,128)S(1)}, u32[]{:S(2)}, u32[]{:S(2)}) collective-permute-start(f32[16,16]{1,0:T(8,128)S(1)} %add.15.a_ref), channel_id=1, source_target_pairs={{0,4},{1,5},{2,6},{3,7},{4,0},{5,1},{6,2},{7,3},{8,12},{9,13},{10,... | collective-permute-start | bytes 3080 | tf_op jit(solution)/shard_map/ppermute | solution.py:323
  55.7 5.4 %collective-permute-start.18 = (f32[16,16]{1,0:T(8,128)S(1)}, f32[16,16]{1,0:T(8,128)S(1)}, u32[]{:S(2)}, u32[]{:S(2)}) collective-permute-start(f32[16,16]{1,0:T(8,128)S(1)} %join_sums.3.refs_8_), channel_id=1, source_target_pairs={{0,16},{8,24},{16,0},{24,8},{1,17},{9,25},{17,1},{25,9},{2,18},{10... | collective-permute-start | bytes 3080 | tf_op jit(solution)/shard_map/ppermute | solution.py:247
  57.2 3.9 %collective-permute-start.17 = (f32[16,16]{1,0:T(8,128)S(1)}, f32[16,16]{1,0:T(8,128)S(1)}, u32[]{:S(2)}, u32[]{:S(2)}) collective-permute-start(f32[16,16]{1,0:T(8,128)S(1)} %join_sums.3.refs_8_), channel_id=1, source_target_pairs={{0,8},{8,0},{16,24},{24,16},{1,9},{9,1},{17,25},{25,17},{2,10},{10... | collective-permute-start | bytes 3080 | tf_op jit(solution)/shard_map/ppermute | solution.py:247
  57.8 4.5 %collective-permute-start.16 = (f32[16,16]{1,0:T(8,128)S(1)}, f32[16,16]{1,0:T(8,128)S(1)}, u32[]{:S(2)}, u32[]{:S(2)}) collective-permute-start(f32[16,16]{1,0:T(8,128)S(1)} %join_sums.3.refs_8_), channel_id=1, source_target_pairs={{0,24},{8,16},{16,8},{24,0},{1,25},{9,17},{17,9},{25,1},{2,26},{10... | collective-permute-start | bytes 3080 | tf_op jit(solution)/shard_map/ppermute | solution.py:247
  63.6 7.8 %collective-permute-start.21 = (bf16[64,1536]{1,0:T(8,128)(2,1)S(1)}, bf16[64,1536]{1,0:T(8,128)(2,1)S(1)}, u32[]{:S(2)}, u32[]{:S(2)}) collective-permute-start(bf16[64,1536]{1,0:T(8,128)(2,1)S(1)} %get-tuple-element.49), channel_id=1, source_target_pairs={{0,8},{8,0},{16,24},{24,16},{1,9},{9,1},{17,25},{25,17},{2,10},{10... | collective-permute-start | bytes 589832 | tf_op jit(solution)/shard_map/ppermute | solution.py:247
  65.2 10.1 %collective-permute-start.22 = (bf16[64,1536]{1,0:T(8,128)(2,1)S(1)}, bf16[64,1536]{1,0:T(8,128)(2,1)S(1)}, u32[]{:S(2)}, u32[]{:S(2)}) collective-permute-start(bf16[64,1536]{1,0:T(8,128)(2,1)S(1)} %get-tuple-element.52), channel_id=1, source_target_pairs={{0,16},{8,24},{16,0},{24,8},{1,17},{9,25},{17,1},{25,9},{2,18},{10... | collective-permute-start | bytes 589832 | tf_op jit(solution)/shard_map/ppermute | solution.py:247
  65.7 11.5 %collective-permute-start.23 = (bf16[64,1536]{1,0:T(8,128)(2,1)S(1)}, bf16[64,1536]{1,0:T(8,128)(2,1)S(1)}, u32[]{:S(2)}, u32[]{:S(2)}) collective-permute-start(bf16[64,1536]{1,0:T(8,128)(2,1)S(1)} %get-tuple-element.53), channel_id=1, source_target_pairs={{0,24},{8,16},{16,8},{24,0},{1,25},{9,17},{17,9},{25,1},{2,26},{10... | collective-permute-start | bytes 589832 | tf_op jit(solution)/shard_map/ppermute | solution.py:247
  68.5 10.8 %collective-permute-start.24 = (bf16[64,1408]{1,0:T(8,128)(2,1)S(1)}, bf16[64,1408]{1,0:T(8,128)(2,1)S(1)}, u32[]{:S(2)}, u32[]{:S(2)}) collective-permute-start(bf16[64,1408]{1,0:T(8,128)(2,1)S(1)} %get-tuple-element.55), channel_id=1, source_target_pairs={{0,8},{8,0},{16,24},{24,16},{1,9},{9,1},{17,25},{25,17},{2,10},{10... | collective-permute-start | bytes 540680 | tf_op jit(solution)/shard_map/ppermute | solution.py:247
  70.0 11.9 %collective-permute-start.25 = (bf16[64,1408]{1,0:T(8,128)(2,1)S(1)}, bf16[64,1408]{1,0:T(8,128)(2,1)S(1)}, u32[]{:S(2)}, u32[]{:S(2)}) collective-permute-start(bf16[64,1408]{1,0:T(8,128)(2,1)S(1)} %get-tuple-element.56), channel_id=1, source_target_pairs={{0,16},{8,24},{16,0},{24,8},{1,17},{9,25},{17,1},{25,9},{2,18},{10... | collective-permute-start | bytes 540680 | tf_op jit(solution)/shard_map/ppermute | solution.py:247
  71.4 10.5 %collective-permute-start.26 = (bf16[64,1408]{1,0:T(8,128)(2,1)S(1)}, bf16[64,1408]{1,0:T(8,128)(2,1)S(1)}, u32[]{:S(2)}, u32[]{:S(2)}) collective-permute-start(bf16[64,1408]{1,0:T(8,128)(2,1)S(1)} %get-tuple-element.57), channel_id=1, source_target_pairs={{0,24},{8,16},{16,8},{24,0},{1,25},{9,17},{17,9},{25,1},{2,26},{10... | collective-permute-start | bytes 540680 | tf_op jit(solution)/shard_map/ppermute | solution.py:247
  (1 other events, 0.7 us)

commit v5 on v4

--- a/solution.py
+++ b/solution.py
@@ -27,12 +27,63 @@
     return me ^ step
 
 
-def lane_tiles(width, step=512):
-    return [(at, min(step, width - at)) for at in range(0, width, step)]
-
-
-def half_of(chunk):
-    return -(-chunk // (2 * LANES)) * LANES
+def tile_layout(length, count):
+    main, left = divmod(length // LANES, count)
+    if left and 2 * left == count:
+        return main, 1
+    return main + (left > 0), 0
+
+
+def tile_groups(first, last, half, most=4):
+    tiles = list(range(first, last)) + [None] * half
+    return [tiles[at:at + most] for at in range(0, len(tiles), most)]
+
+
+def swap_halves(value):
+    return pltpu.roll(value, LANES // 2, 1)
+
+
+def left_half(shape):
+    return lax.broadcasted_iota(jnp.int32, shape, 1) < LANES // 2
+
+
+def pack(tile, odd=None):
+    half = tile.shape[0] // 2
+    top, low = tile[:half], tile[half:]
+    left, right = top, swap_halves(low)
+    if odd is not None:
+        second = lax.broadcasted_iota(jnp.int32, top.shape, 1) * 0 + odd == 1
+        left, right = jnp.where(second, swap_halves(top), top), jnp.where(second, low, right)
+    return jnp.where(left_half(top.shape), left, right)
+
+
+def tile_of(ref, tile, per, main):
+    if tile is not None:
+        return ref[tile * per:(tile + 1) * per, :]
+    packed = ref[main * per:, :].astype(jnp.float32)
+    return jnp.concatenate([packed, swap_halves(packed)], axis=0).astype(jnp.bfloat16)
+
+
+def gather_tiles(refs, group, per, main):
+    return jnp.concatenate(
+        [
+            jnp.concatenate([tile_of(ref, tile, per, main) for tile in group], axis=1)
+            for ref in refs
+        ],
+        axis=0,
+    )
+
+
+def store_tiles(outs, value, group, per, first, last):
+    for at, tile in enumerate(group):
+        for s, out in enumerate(outs):
+            rows = value[s * per:(s + 1) * per, at * LANES:(at + 1) * LANES]
+            if tile is None:
+                out[(last - first) * per:, :] = pack(rows).astype(jnp.bfloat16)
+            else:
+                out[(tile - first) * per:(tile - first + 1) * per, :] = rows.astype(
+                    jnp.bfloat16
+                )
 
 
 def member_of_row(me, rows, channels, members, group):
@@ -44,21 +95,20 @@
     return (member == col).astype(jnp.float32)
 
 
-def split_kernel(me_of, count, chunk, length, x_ref, *rest):
-    outs, sem = rest[-count - 1:-1], rest[-1]
+def split_kernel(me_of, count, main, half, length, x_ref, *rest):
+    outs = rest[-count:]
     me = me_of()
-    copies = [
-        pltpu.make_async_copy(
-            x_ref.at[:, pl.ds(chunk_start(partner(me, s), chunk, length), chunk)],
-            outs[s],
-            sem.at[s],
-        )
-        for s in range(count)
-    ]
-    for copy in copies:
-        copy.start()
-    for copy in copies:
-        copy.wait()
+    per = x_ref.shape[0]
+    for s in range(count):
+        owner = partner(me, s)
+        start = chunk_start(owner, main * LANES, length)
+        for tile in range(main):
+            place = pl.multiple_of(start + tile * LANES, LANES)
+            outs[s][tile * per:(tile + 1) * per, :] = x_ref[:, pl.ds(place, LANES)]
+        if half:
+            place = pl.multiple_of((main * count + owner // 2) * LANES, LANES)
+            shared = x_ref[:, pl.ds(place, LANES)].astype(jnp.float32)
+            outs[s][main * per:, :] = pack(shared, owner % 2).astype(jnp.bfloat16)
 
 
 def tiled(small, rows, channels):
@@ -77,10 +127,6 @@
     qkt_ref[...] = tiled(mm(wkt, wq, ((1,), (0,)), HIGH), rows, channels)
     ov_ref[...] = tiled(mm(wo, wv, ((1,), (0,)), HIGH), rows, channels)
     ovt_ref[...] = tiled(mm(wvt, wot, ((1,), (0,)), HIGH), rows, channels)
-
-
-def gather_tile(refs, at, width):
-    return jnp.concatenate([r[:, at:at + width] for r in refs], axis=0)
 
 
 def three_parts(value):
@@ -102,32 +148,36 @@
     return sum(mm(order, part, ((1,), (0,))) for part in three_parts(half))
 
 
-def masked_gram(me, count, chunk, length, left, right):
-    rows = count * right[0].shape[0]
+def masked_gram(me, count, main, half, per, length, left, right):
+    rows = count * per
+    chunk = main * LANES
     skip = me * chunk - chunk_start(me, chunk, length)
     most = max(0, count * chunk - length)
     total = jnp.zeros((rows, rows), jnp.float32)
-    for at, width in lane_tiles(chunk):
-        b = gather_tile(right, at, width)
-        a = b if left is right else gather_tile(left, at, width)
-        if at < most:
-            lane = lax.broadcasted_iota(jnp.int32, (rows, width), 1) + at
-            a = jnp.where(lane >= skip, a.astype(jnp.float32), 0.0).astype(jnp.bfloat16)
+    at = 0
+    for group in tile_groups(0, main, half):
+        b = gather_tiles(right, group, per, main)
+        a = b if left is right else gather_tiles(left, group, per, main)
+        if at < most or None in group:
+            lane = lax.broadcasted_iota(jnp.int32, a.shape, 1) + at
+            valid = (lane >= skip) & (lane < chunk + LANES // 2)
+            a = jnp.where(valid, a.astype(jnp.float32), 0.0).astype(jnp.bfloat16)
         total = total + mm(a, b, ((1,), (1,)))
+        at += len(group) * LANES
     return total
 
 
-def score_kernel(me_of, count, chunk, length, group, channels, members, tile_ref, *refs):
+def score_kernel(me_of, count, main, half, per, length, group, channels, members, tile_ref, *refs):
     me = me_of()
     fields, out_ref = refs[:count], refs[-1]
-    total = masked_gram(me, count, chunk, length, fields, fields)
+    total = masked_gram(me, count, main, half, per, length, fields, fields)
     out_ref[...] = fold(me, total * tile_ref[...], channels, members, group)
 
 
-def pair_kernel(me_of, count, chunk, length, group, channels, members, tile_ref, *refs):
+def pair_kernel(me_of, count, main, half, per, length, group, channels, members, tile_ref, *refs):
     me = me_of()
     fields, grads, out_ref = refs[:count], refs[count:2 * count], refs[-1]
-    total = masked_gram(me, count, chunk, length, grads, fields)
+    total = masked_gram(me, count, main, half, per, length, grads, fields)
     out_ref[...] = fold(me, total * tile_ref[...], channels, members, group)
 
 
@@ -161,23 +211,21 @@
 
 
 def branch_kernel(
-    me_of, count, chunk, group, channels, members, scale, waits, ov_ref, *refs
+    me_of, count, main, half, per, group, channels, members, scale, waits, ov_ref, *refs
 ):
     me = me_of()
     sums, fields = refs[:count], refs[count:2 * count]
     total_ref, outs = refs[2 * count + waits], refs[2 * count + waits + 1:]
-    per = fields[0].shape[0]
     rows = count * per
     total = add_up(sums)
     total_ref[...] = total
     picks = member_of_row(me, rows, channels, members, group).astype(jnp.bfloat16)
     weights = softmax(total * scale)
     high, low = two_parts(spread(weights, picks) * ov_ref[...])
-    for at, width in lane_tiles(chunk):
-        e = gather_tile(fields, at, width)
-        b = (mm(high, e, ((1,), (0,))) + mm(low, e, ((1,), (0,)))).astype(jnp.bfloat16)
-        for s in range(count):
-            outs[s][:, at:at + width] = b[s * per:(s + 1) * per]
+    for tiles in tile_groups(0, main, half):
+        e = gather_tiles(fields, tiles, per, main)
+        value = mm(high, e, ((1,), (0,))) + mm(low, e, ((1,), (0,)))
+        store_tiles(outs, value, tiles, per, 0, main)
 
 
 def transposed_weights_kernel(
@@ -191,13 +239,12 @@
 
 
 def grad_kernel(
-    me_of, count, chunk, group, channels, members, scale, low, size, waits,
+    me_of, count, main, half, per, group, channels, members, scale, first, last, waits,
     w_ref, qk_ref, qkt_ref, a_high_ref, a_low_ref, *refs,
 ):
     me = me_of()
     fields, grads, sums = refs[:count], refs[count:2 * count], refs[2 * count:3 * count]
     outs = refs[3 * count + waits:]
-    per = fields[0].shape[0]
     rows = count * per
     picks = member_of_row(me, rows, channels, members, group).astype(jnp.bfloat16)
     weights = w_ref[...]
@@ -207,37 +254,67 @@
         spread(slope, picks) * qk_ref[...] + spread_t(slope, picks) * qkt_ref[...]
     )
     a_high, a_low = a_high_ref[...], a_low_ref[...]
-    for at, width in lane_tiles(size):
-        e = gather_tile(fields, low + at, width)
-        c = gather_tile(grads, low + at, width)
-        b = (
+    for tiles in tile_groups(first, last, half):
+        e = gather_tiles(fields, tiles, per, main)
+        c = gather_tiles(grads, tiles, per, main)
+        value = (
             mm(d_high, e, ((1,), (0,))) + mm(d_low, e, ((1,), (0,)))
             + mm(a_high, c, ((1,), (0,))) + mm(a_low, c, ((1,), (0,)))
-        ).astype(jnp.bfloat16)
-        for s in range(count):
-            outs[s][:, at:at + width] = b[s * per:(s + 1) * per]
-
-
-def finish_kernel(me_of, count, chunk, length, stages, serial, waits, extras, *refs):
+        )
+        store_tiles(outs, value, tiles, per, first, last)
+
+
+def finish_kernel(
+    me_of, count, main, per, length, stages, halves, serial, waits, extras, *refs
+):
     me = me_of()
     base, extra = refs[waits:waits + count], refs[waits + count:waits + count + extras]
     out_ref, held, sem = refs[waits + count + extras:]
+
+    def send(slot, size, place):
+        place = pl.multiple_of(place, LANES)
+        copy = pltpu.make_async_copy(
+            held.at[slot, :, pl.ds(0, size)], out_ref.at[:, pl.ds(place, size)], sem.at[slot]
+        )
+        copy.start()
+        if serial:
+            copy.wait()
+        return copy
+
     slot = 0
-    for stage in stages:
+    for number, stage in enumerate(stages):
         copies = []
-        for s, low, size, index, start in stage:
-            held[slot, :, :size] = base[s][:, low:low + size].astype(jnp.float32) + extra[
-                index
-            ][:, start:start + size].astype(jnp.float32)
-            place = pl.multiple_of(chunk_start(partner(me, s), chunk, length) + low, LANES)
-            copy = pltpu.make_async_copy(
-                held.at[slot, :, pl.ds(0, size)], out_ref.at[:, pl.ds(place, size)], sem.at[slot]
-            )
-            copy.start()
-            if serial:
-                copy.wait()
-            copies.append(copy)
+        for s, begin, end, index, origin in stage:
+            for tile in range(begin, end):
+                mine = base[s][tile * per:(tile + 1) * per, :].astype(jnp.float32)
+                more = extra[index][(tile - origin) * per:(tile - origin + 1) * per, :]
+                held[slot, :, (tile - begin) * LANES:(tile - begin + 1) * LANES] = (
+                    mine + more.astype(jnp.float32)
+                )
+            start = chunk_start(partner(me, s), main * LANES, length)
+            copies.append(send(slot, (end - begin) * LANES, start + begin * LANES))
             slot += 1
+        if halves and number == len(stages) - 1:
+            packed = [
+                base[s][main * per:, :].astype(jnp.float32)
+                + extra[index][row:, :].astype(jnp.float32)
+                for s, (index, row) in enumerate(halves)
+            ]
+            shape = packed[0].shape
+            odd = lax.broadcasted_iota(jnp.int32, shape, 1) * 0 + me % 2 == 1
+            for s in range(0, count, 2):
+                even_part = jnp.where(odd, packed[s + 1], packed[s])
+                odd_part = jnp.where(odd, packed[s], packed[s + 1])
+                left = left_half(shape)
+                held[slot, :per // 2, :LANES] = jnp.where(
+                    left, even_part, swap_halves(odd_part)
+                )
+                held[slot, per // 2:, :LANES] = jnp.where(
+                    left, swap_halves(even_part), odd_part
+                )
+                place = (main * count + partner(me, s) // 2) * LANES
+                copies.append(send(slot, LANES, place))
+                slot += 1
         if not serial:
             for copy in copies:
                 copy.wait()
@@ -273,7 +350,8 @@
     members = group * count
     per = group * channels
     rows = per * count
-    chunk = -(-length // (LANES * count)) * LANES
+    main, half = tile_layout(length, count)
+    chunk = main * LANES + half * LANES // 2
     scale = 1.0 / (length * lax.axis_size("space") * math.sqrt(channels))
     me_of = lambda: lax.axis_index("mem")
     bf, f32 = jnp.bfloat16, jnp.float32
@@ -281,7 +359,11 @@
     anywhere = pl.BlockSpec(memory_space=pl.ANY)
     in_hbm = pl.BlockSpec(memory_space=pltpu.MemorySpace.HBM)
     params = pltpu.CompilerParams(vmem_limit_bytes=16 * 1024 * 1024 + 24 * rows * rows)
-    part = jax.ShapeDtypeStruct((per, chunk), bf)
+
+    def packed(tiles, with_half):
+        return jax.ShapeDtypeStruct((tiles * per + with_half * per // 2, LANES), bf)
+
+    part = packed(main, half)
     square = jax.ShapeDtypeStruct((rows, rows), f32)
     pair = jax.ShapeDtypeStruct((members, members), f32)
     fields = ensemble.reshape(per, length)
@@ -294,11 +376,10 @@
 
     def split(operands, name):
         return pl.pallas_call(
-            functools.partial(split_kernel, me_of, count, chunk, length),
+            functools.partial(split_kernel, me_of, count, main, half, length),
             out_shape=[part] * count,
-            in_specs=[anywhere] * len(operands),
-            out_specs=[anywhere] * count,
-            scratch_shapes=[pltpu.SemaphoreType.DMA((count,))],
+            in_specs=[whole] + [anywhere] * (len(operands) - 1),
+            out_specs=[whole] * count,
             compiler_params=params,
             name=name,
         )(*operands)
@@ -333,7 +414,7 @@
 
     scores = pl.pallas_call(
         functools.partial(
-            score_kernel, me_of, count, chunk, length, group, channels, members
+            score_kernel, me_of, count, main, half, per, length, group, channels, members
         ),
         out_shape=pair,
         in_specs=[whole] * (count + 1),
@@ -349,7 +430,7 @@
     waited = score_parts[:1]
     pairs = pl.pallas_call(
         functools.partial(
-            pair_kernel, me_of, count, chunk, length, group, channels, members
+            pair_kernel, me_of, count, main, half, per, length, group, channels, members
         ),
         out_shape=pair,
         in_specs=[whole] * (2 * count + 1) + [anywhere] * len(waited),
@@ -361,7 +442,7 @@
     ahead = [pairs]
     outcome = pl.pallas_call(
         functools.partial(
-            branch_kernel, me_of, count, chunk, group, channels, members, scale, len(ahead),
+            branch_kernel, me_of, count, main, half, per, group, channels, members, scale, len(ahead),
         ),
         out_shape=[pair] + [part] * count,
         in_specs=[whole] * (2 * count + 1) + [anywhere] * len(ahead),
@@ -388,13 +469,14 @@
         name="transposed_weights",
     )(scores, ovt)
 
-    def gradient(low, size, awaited, name):
+    def gradient(begin, end, with_half, awaited, name):
+        size = (end - begin) * LANES
         parts = pl.pallas_call(
             functools.partial(
-                grad_kernel, me_of, count, chunk, group, channels, members, scale, low,
-                size, len(awaited),
+                grad_kernel, me_of, count, main, with_half, per, group, channels, members, scale,
+                begin, end, len(awaited),
             ),
-            out_shape=[jax.ShapeDtypeStruct((per, size), bf)] * count,
+            out_shape=[packed(end - begin, with_half)] * count,
             in_specs=[whole] * (3 * count + 5) + [anywhere] * len(awaited),
             out_specs=[whole] * count,
             compiler_params=params,
@@ -403,26 +485,24 @@
         )(weights, qk, qkt, a_high, a_low, *e_cells, *c_cells, *pair_parts, *awaited)
         return exchange(parts)
 
-    half = half_of(chunk)
-    grad_a = gradient(0, half, branch_home[1:], "input_gradient_a")
-    grad_b = gradient(half, chunk - half, branch_home[1:], "input_gradient_b")
-
-    rest = chunk - half
-    serial = count * chunk - length > rest
-
-    def finish(base, extra, stages, before, after, name):
-        slots = sum(len(stage) for stage in stages)
+    mid = (main + 1 + half) // 2
+    grad_a = gradient(0, mid, 0, branch_home[1:], "input_gradient_a")
+    grad_b = gradient(mid, main, half, branch_home[1:], "input_gradient_b")
+    serial = count * main - length // LANES > main - mid
+
+    def finish(base, extra, stages, halves, before, after, name):
+        slots = sum(len(stage) for stage in stages) + (count // 2 if halves else 0)
         waited = list(before) + list(after)
         return pl.pallas_call(
             functools.partial(
-                finish_kernel, me_of, count, chunk, length, stages, serial, len(waited),
-                len(extra),
+                finish_kernel, me_of, count, main, per, length, stages, halves, serial,
+                len(waited), len(extra),
             ),
             out_shape=jax.ShapeDtypeStruct((per, length), f32),
             in_specs=[anywhere] * len(waited) + [whole] * (count + len(extra)),
             out_specs=in_hbm,
             scratch_shapes=[
-                pltpu.VMEM((slots, per, half), f32),
+                pltpu.VMEM((slots, per, mid * LANES), f32),
                 pltpu.SemaphoreType.DMA((slots,)),
             ],
             input_output_aliases={0: 0} if before else {},
@@ -432,19 +512,19 @@
         )(*waited, *base, *extra)
 
     steps = list(range(count))
+    first_part = [(s, 0, mid, s, 0) for s in steps]
     updated = finish(
-        e_mine, branch_home,
-        [[(s, 0, half, s, 0) for s in steps], [(s, half, rest, s, half) for s in steps]],
-        [], [grad_a[first]], "updated",
+        e_mine, branch_home, [first_part, [(s, mid, main, s, 0) for s in steps]],
+        [(s, main * per) for s in steps] if half else [], [], [grad_a[first]], "updated",
     )
     ensemble_grad = finish(
-        c_mine, grad_a + grad_b[:1],
-        [[(s, 0, half, s, 0) for s in steps], [(0, half, rest, count, 0)]],
-        [], [], "ensemble_grad_early",
+        c_mine, grad_a + grad_b[:1], [first_part, [(0, mid, main, count, mid)]],
+        [], [], [], "ensemble_grad_early",
     )
     if count > 1:
         ensemble_grad = finish(
-            c_mine, grad_b[1:], [[(s, half, rest, s - 1, 0) for s in steps[1:]]],
+            c_mine, grad_b, [[(s, mid, main, s, mid) for s in steps[1:]]],
+            [(s, (main - mid) * per) for s in steps] if half else [],
             [ensemble_grad], [], "ensemble_grad_late",
         )
     shape = (group, channels, length)

time: 83.3 us -> 82.1 us (0.986)
  waiting for transfers between devices: 29.1 us -> 27.6 us
    ppermute x21, waiting for transfers between devices: 18.6 us -> 17.1 us  [swap(): return lax.ppermute(value, 'mem', [(i, i ^ step) for i in range(count)])]
  transfers between devices with their start and end apart: 27 -> 27, of which waited for: 17 -> 18; matrix products, arithmetic and copies ran while one was open for 0% -> 0% of each run, Pallas kernels for 12% -> 12%
where the time goes in v5:
time: 82.1 us; the launch traced here: 81.8 us
  starting transfers between devices  34.1 us (42%)
  waiting for transfers between devices  27.6 us (34%)
  Pallas kernels  13.8 us (17%)
  local copies, waits for them, and re-layouts  5.48 us (7%)
    ppermute x21, starting transfers between devices, swap(): return lax.ppermute(value, 'mem', [(i, i ^ step) for i in range(count)])  25.8 us
    ppermute x21, waiting for transfers between devices, swap(): return lax.ppermute(value, 'mem', [(i, i ^ step) for i in range(count)])  17.1 us
    ppermute x4, waiting for transfers between devices, sum_steps(): lax.ppermute(value, name, [(i, i ^ step) for i in range(size)])  6.52 us
    unnamed x12, local copies, waits for them, and re-layouts  5.48 us
    pallas_call x3, Pallas kernels, finish(): pl.pallas_call(functools.partial(finish_kernel, me_of, count, main, per,...  5.37 us
    ppermute x2, starting transfers between devices, join(): other = lax.ppermute(value, name, [(i, i ^ step) for i in range(size)])  5.16 us
    ppermute x2, waiting for transfers between devices, join(): other = lax.ppermute(value, name, [(i, i ^ step) for i in range(size)])  3.93 us
    ppermute x4, starting transfers between devices, sum_steps(): lax.ppermute(value, name, [(i, i ^ step) for i in range(size)])  3.15 us
  transfers between devices with their start and end apart: 27, of which 18 were waited for; matrix products, arithmetic and copies ran while one was open for 0% of the time, Pallas kernels for 12%

profile of v5, /device:TPU:0, one launch (start us, length us, event | category | flops | bytes accessed | tf_op | source)
XLA Modules:
  0.0 81.8 jit_solution(13734024217723276782)
XLA Ops:
  2.3 3.0 %collective-permute-start = (bf16[1440,128]{1,0:T(8,128)(2,1)S(1)}, bf16[1440,128]{1,0:T(8,128)(2,1)S(1)}, u32[]{:S(2)}, u32[]{:S(2)}) collective-permute-start(bf16[1440,128]{1,0:T(8,128)(2,1)S(1)} %get-tuple-element.33.refs_2_), channel_id=1, source_target_pairs={{0,8},{8,0},{16,24},{24,16},{1,9},{9,1},{17,25},{25,17},{2,10},{10... | collective-permute-start | bytes 1105928 | tf_op jit(solution)/shard_map/ppermute | solution.py:324
  5.3 1.5 %collective-permute-start.1 = (bf16[1440,128]{1,0:T(8,128)(2,1)S(1)}, bf16[1440,128]{1,0:T(8,128)(2,1)S(1)}, u32[]{:S(2)}, u32[]{:S(2)}) collective-permute-start(bf16[1440,128]{1,0:T(8,128)(2,1)S(1)} %get-tuple-element.34.refs_3_), channel_id=1, source_target_pairs={{0,16},{8,24},{16,0},{24,8},{1,17},{9,25},{17,1},{25,9},{2,18},{10... | collective-permute-start | bytes 1105928 | tf_op jit(solution)/shard_map/ppermute | solution.py:324
  10.9 3.8 %collective-permute-done.refs_1_.rest_0_.refs_5_ = bf16[1440,128]{1,0:T(8,128)(2,1)S(1)} collective-permute-done((bf16[1440,128]{1,0:T(8,128)(2,1)S(1)}, bf16[1440,128]{1,0:T(8,128)(2,1)S(1)}, u32[]{:S(2)}, u32[]{:S(2)}) %collective-permute-start) | collective-permute-done | bytes 368672 | tf_op jit(solution)/shard_map/ppermute | solution.py:324
  14.7 1.4 %copy-done.1 = bf16[4,16,11520]{2,1,0:T(8,128)(2,1)S(1)} copy-done((bf16[4,16,11520]{2,1,0:T(8,128)(2,1)S(1)}, bf16[4,16,11520]{2,1,0:T(8,128)(2,1)}, u32[]{:S(2)}) %copy-start.1) | copy-done | bytes 1474584
  16.4 2.1 %collective-permute-start.6 = (bf16[1440,128]{1,0:T(8,128)(2,1)S(1)}, bf16[1440,128]{1,0:T(8,128)(2,1)S(1)}, u32[]{:S(2)}, u32[]{:S(2)}) collective-permute-start(bf16[1440,128]{1,0:T(8,128)(2,1)S(1)} %get-tuple-element.36.refs_1_.refs_2_), channel_id=1, source_target_pairs={{0,8},{8,0},{16,24},{24,16},{1,9},{9,1},{17,25},{25,17},{2,10},{10... | collective-permute-start | bytes 1105928 | tf_op jit(solution)/shard_map/ppermute | solution.py:324
  18.5 1.5 %collective-permute-start.10 = (bf16[1440,128]{1,0:T(8,128)(2,1)S(1)}, bf16[1440,128]{1,0:T(8,128)(2,1)S(1)}, u32[]{:S(2)}, u32[]{:S(2)}) collective-permute-start(bf16[1440,128]{1,0:T(8,128)(2,1)S(1)} %get-tuple-element.38.refs_2_.refs_3_), channel_id=1, source_target_pairs={{0,16},{8,24},{16,0},{24,8},{1,17},{9,25},{17,1},{25,9},{2,18},{10... | collective-permute-start | bytes 1105928 | tf_op jit(solution)/shard_map/ppermute | solution.py:324
  20.1 3.6 %collective-permute-done.1.refs_2_.refs_6_ = bf16[1440,128]{1,0:T(8,128)(2,1)S(1)} collective-permute-done((bf16[1440,128]{1,0:T(8,128)(2,1)S(1)}, bf16[1440,128]{1,0:T(8,128)(2,1)S(1)}, u32[]{:S(2)}, u32[]{:S(2)}) %collective-permute-start.1) | collective-permute-done | bytes 368672 | tf_op jit(solution)/shard_map/ppermute | solution.py:324
  26.4 1.6 %collective-permute-start.4 = (f32[16,16]{1,0:T(8,128)S(1)}, f32[16,16]{1,0:T(8,128)S(1)}, u32[]{:S(2)}, u32[]{:S(2)}) collective-permute-start(f32[16,16]{1,0:T(8,128)S(1)} %add.12), channel_id=1, source_target_pairs={{0,2},{1,3},{2,0},{3,1},{4,6},{5,7},{6,4},{7,5},{8,10},{9,11},{10,... | collective-permute-start | bytes 3080 | tf_op jit(solution)/shard_map/ppermute | solution.py:335
  28.0 2.1 %collective-permute-done.4 = f32[16,16]{1,0:T(8,128)S(1)} collective-permute-done((f32[16,16]{1,0:T(8,128)S(1)}, f32[16,16]{1,0:T(8,128)S(1)}, u32[]{:S(2)}, u32[]{:S(2)}) %collective-permute-start.4) | collective-permute-done | bytes 1056 | tf_op jit(solution)/shard_map/ppermute | solution.py:335
  30.0 2.6 %collective-permute-start.5 = (f32[16,16]{1,0:T(8,128)S(1)}, f32[16,16]{1,0:T(8,128)S(1)}, u32[]{:S(2)}, u32[]{:S(2)}) collective-permute-start(f32[16,16]{1,0:T(8,128)S(1)} %add.13.a_ref), channel_id=1, source_target_pairs={{0,4},{1,5},{2,6},{3,7},{4,0},{5,1},{6,2},{7,3},{8,12},{9,13},{10,... | collective-permute-start | bytes 3080 | tf_op jit(solution)/shard_map/ppermute | solution.py:404
  32.6 2.0 %collective-permute-done.5.b_ref = f32[16,16]{1,0:T(8,128)S(1)} collective-permute-done((f32[16,16]{1,0:T(8,128)S(1)}, f32[16,16]{1,0:T(8,128)S(1)}, u32[]{:S(2)}, u32[]{:S(2)}) %collective-permute-start.5) | collective-permute-done | bytes 1056 | tf_op jit(solution)/shard_map/ppermute | solution.py:404
  34.6 1.9 %collective-permute-start.9 = (f32[16,16]{1,0:T(8,128)S(1)}, f32[16,16]{1,0:T(8,128)S(1)}, u32[]{:S(2)}, u32[]{:S(2)}) collective-permute-start(f32[16,16]{1,0:T(8,128)S(1)} %join_sums.2.refs_8_.refs_0_), channel_id=1, source_target_pairs={{0,16},{8,24},{16,0},{24,8},{1,17},{9,25},{17,1},{25,9},{2,18},{10... | collective-permute-start | bytes 3080 | tf_op jit(solution)/shard_map/ppermute | solution.py:324
  36.6 1.5 %collective-permute-start.7 = (f32[16,16]{1,0:T(8,128)S(1)}, f32[16,16]{1,0:T(8,128)S(1)}, u32[]{:S(2)}, u32[]{:S(2)}) collective-permute-start(f32[16,16]{1,0:T(8,128)S(1)} %join_sums.2.refs_8_.refs_0_), channel_id=1, source_target_pairs={{0,24},{8,16},{16,8},{24,0},{1,25},{9,17},{17,9},{25,1},{2,26},{10... | collective-permute-start | bytes 3080 | tf_op jit(solution)/shard_map/ppermute | solution.py:324
  41.1 1.4 %branch.1 = (f32[16,16]{1,0:T(8,128)S(1)}, bf16[1440,128]{1,0:T(8,128)(2,1)S(1)}, bf16[1440,128]{1,0:T(8,128)(2,1)S(1)}, bf16[1440,128]{1,0:T(8,128)(2,1)S(1)}, bf16[1440,128]{1,0:T(8,128)(2,1)S(1)}) custom-call(f32[256,256]{1,0:T(8,128)S(1)} %get-tuple-element.30.tile_ref.ov_ref, f32[16,16]{1,0:T(8,128)S(1)} %join_sums.2.refs_8_.refs_0_, ...), custom_call_target="tpu_custom_call" | custom-call | flops 754974720 | bytes 2949120 | tf_op jit(solution)/shard_map/branch/pallas_call | solution.py:443
  42.6 2.0 %collective-permute-start.15 = (bf16[1440,128]{1,0:T(8,128)(2,1)S(1)}, bf16[1440,128]{1,0:T(8,128)(2,1)S(1)}, u32[]{:S(2)}, u32[]{:S(2)}) collective-permute-start(bf16[1440,128]{1,0:T(8,128)(2,1)S(1)} %get-tuple-element.46), channel_id=1, source_target_pairs={{0,8},{8,0},{16,24},{24,16},{1,9},{9,1},{17,25},{25,17},{2,10},{10... | collective-permute-start | bytes 1105928 | tf_op jit(solution)/shard_map/ppermute | solution.py:324
  44.7 1.4 %collective-permute-start.20 = (bf16[1440,128]{1,0:T(8,128)(2,1)S(1)}, bf16[1440,128]{1,0:T(8,128)(2,1)S(1)}, u32[]{:S(2)}, u32[]{:S(2)}) collective-permute-start(bf16[1440,128]{1,0:T(8,128)(2,1)S(1)} %get-tuple-element.48), channel_id=1, source_target_pairs={{0,24},{8,16},{16,8},{24,0},{1,25},{9,17},{17,9},{25,1},{2,26},{10... | collective-permute-start | bytes 1105928 | tf_op jit(solution)/shard_map/ppermute | solution.py:324
  47.3 1.6 %collective-permute-start.13 = (f32[16,16]{1,0:T(8,128)S(1)}, f32[16,16]{1,0:T(8,128)S(1)}, u32[]{:S(2)}, u32[]{:S(2)}) collective-permute-start(f32[16,16]{1,0:T(8,128)S(1)} %add.14), channel_id=1, source_target_pairs={{0,2},{1,3},{2,0},{3,1},{4,6},{5,7},{6,4},{7,5},{8,10},{9,11},{10,... | collective-permute-start | bytes 3080 | tf_op jit(solution)/shard_map/ppermute | solution.py:335
  48.9 2.1 %collective-permute-done.13 = f32[16,16]{1,0:T(8,128)S(1)} collective-permute-done((f32[16,16]{1,0:T(8,128)S(1)}, f32[16,16]{1,0:T(8,128)S(1)}, u32[]{:S(2)}, u32[]{:S(2)}) %collective-permute-start.13) | collective-permute-done | bytes 1056 | tf_op jit(solution)/shard_map/ppermute | solution.py:335
  51.0 2.6 %collective-permute-start.14 = (f32[16,16]{1,0:T(8,128)S(1)}, f32[16,16]{1,0:T(8,128)S(1)}, u32[]{:S(2)}, u32[]{:S(2)}) collective-permute-start(f32[16,16]{1,0:T(8,128)S(1)} %add.15.a_ref), channel_id=1, source_target_pairs={{0,4},{1,5},{2,6},{3,7},{4,0},{5,1},{6,2},{7,3},{8,12},{9,13},{10,... | collective-permute-start | bytes 3080 | tf_op jit(solution)/shard_map/ppermute | solution.py:404
  53.6 2.0 %collective-permute-done.14.b_ref = f32[16,16]{1,0:T(8,128)S(1)} collective-permute-done((f32[16,16]{1,0:T(8,128)S(1)}, f32[16,16]{1,0:T(8,128)S(1)}, u32[]{:S(2)}, u32[]{:S(2)}) %collective-permute-start.14) | collective-permute-done | bytes 1056 | tf_op jit(solution)/shard_map/ppermute | solution.py:404
  55.5 1.5 %collective-permute-start.18 = (f32[16,16]{1,0:T(8,128)S(1)}, f32[16,16]{1,0:T(8,128)S(1)}, u32[]{:S(2)}, u32[]{:S(2)}) collective-permute-start(f32[16,16]{1,0:T(8,128)S(1)} %join_sums.3.refs_8_), channel_id=1, source_target_pairs={{0,16},{8,24},{16,0},{24,8},{1,17},{9,25},{17,1},{25,9},{2,18},{10... | collective-permute-start | bytes 3080 | tf_op jit(solution)/shard_map/ppermute | solution.py:324
  57.6 1.4 %collective-permute-start.16 = (f32[16,16]{1,0:T(8,128)S(1)}, f32[16,16]{1,0:T(8,128)S(1)}, u32[]{:S(2)}, u32[]{:S(2)}) collective-permute-start(f32[16,16]{1,0:T(8,128)S(1)} %join_sums.3.refs_8_), channel_id=1, source_target_pairs={{0,24},{8,16},{16,8},{24,0},{1,25},{9,17},{17,9},{25,1},{2,26},{10... | collective-permute-start | bytes 3080 | tf_op jit(solution)/shard_map/ppermute | solution.py:324
  60.7 1.4 %collective-permute-done.16.refs_9_ = f32[16,16]{1,0:T(8,128)S(1)} collective-permute-done((f32[16,16]{1,0:T(8,128)S(1)}, f32[16,16]{1,0:T(8,128)S(1)}, u32[]{:S(2)}, u32[]{:S(2)}) %collective-permute-start.16) | collective-permute-done | bytes 1056 | tf_op jit(solution)/shard_map/ppermute | solution.py:324
  63.4 1.6 %collective-permute-start.21 = (bf16[768,128]{1,0:T(8,128)(2,1)S(1)}, bf16[768,128]{1,0:T(8,128)(2,1)S(1)}, u32[]{:S(2)}, u32[]{:S(2)}) collective-permute-start(bf16[768,128]{1,0:T(8,128)(2,1)S(1)} %get-tuple-element.49), channel_id=1, source_target_pairs={{0,8},{8,0},{16,24},{24,16},{1,9},{9,1},{17,25},{25,17},{2,10},{10... | collective-permute-start | bytes 589832 | tf_op jit(solution)/shard_map/ppermute | solution.py:324
  65.5 1.5 %collective-permute-start.23 = (bf16[768,128]{1,0:T(8,128)(2,1)S(1)}, bf16[768,128]{1,0:T(8,128)(2,1)S(1)}, u32[]{:S(2)}, u32[]{:S(2)}) collective-permute-start(bf16[768,128]{1,0:T(8,128)(2,1)S(1)} %get-tuple-element.53), channel_id=1, source_target_pairs={{0,24},{8,16},{16,8},{24,0},{1,25},{9,17},{17,9},{25,1},{2,26},{10... | collective-permute-start | bytes 589832 | tf_op jit(solution)/shard_map/ppermute | solution.py:324
  67.0 1.4 %input_gradient_b.1 = (bf16[672,128]{1,0:T(8,128)(2,1)S(1)}, bf16[672,128]{1,0:T(8,128)(2,1)S(1)}, bf16[672,128]{1,0:T(8,128)(2,1)S(1)}, bf16[672,128]{1,0:T(8,128)(2,1)S(1)}) custom-call(f32[16,16]{1,0:T(8,128)S(1)} %get-tuple-element.42.w_ref, f32[256,256]{1,0:T(8,128)S(1)} %get-tuple-element.31.tile_ref.rest_1_.qk_ref, ...), custom_call_target="tpu_custom_call" | custom-call | flops 671088640 | bytes 1966080 | tf_op jit(solution)/shard_map/input_gradient_b/pallas_call | solution.py:474
  68.4 1.5 %collective-permute-start.24 = (bf16[672,128]{1,0:T(8,128)(2,1)S(1)}, bf16[672,128]{1,0:T(8,128)(2,1)S(1)}, u32[]{:S(2)}, u32[]{:S(2)}) collective-permute-start(bf16[672,128]{1,0:T(8,128)(2,1)S(1)} %get-tuple-element.55), channel_id=1, source_target_pairs={{0,8},{8,0},{16,24},{24,16},{1,9},{9,1},{17,25},{25,17},{2,10},{10... | collective-permute-start | bytes 516104 | tf_op jit(solution)/shard_map/ppermute | solution.py:324
  71.3 1.4 %collective-permute-start.26 = (bf16[672,128]{1,0:T(8,128)(2,1)S(1)}, bf16[672,128]{1,0:T(8,128)(2,1)S(1)}, u32[]{:S(2)}, u32[]{:S(2)}) collective-permute-start(bf16[672,128]{1,0:T(8,128)(2,1)S(1)} %get-tuple-element.57), channel_id=1, source_target_pairs={{0,24},{8,16},{16,8},{24,0},{1,25},{9,17},{17,9},{25,1},{2,26},{10... | collective-permute-start | bytes 516104 | tf_op jit(solution)/shard_map/ppermute | solution.py:324
  72.7 2.4 %updated.1 = f32[64,11520]{1,0:T(8,128)} custom-call(bf16[768,128]{1,0:T(8,128)(2,1)S(1)} %collective-permute-done.21.refs_0_.refs_5_, bf16[1440,128]{1,0:T(8,128)(2,1)S(1)} %get-tuple-element.32.refs_0_.refs_4_.refs_1_, bf16[1440,128]{1,0:T(8,128)(2,1)S(1)} %get-tuple-element.33.refs_2_, bf16[1440,128]{1,0:T(8,128)(2,1)S(1)} %get-tuple-element.34.refs_3_, ...), custom_call_target="tpu_custom_call" | custom-call | flops 737280 | bytes 5898240 | tf_op jit(solution)/shard_map/updated/pallas_call | solution.py:496
  75.1 2.0 %collective-permute-done.22.refs_6_ = bf16[768,128]{1,0:T(8,128)(2,1)S(1)} collective-permute-done((bf16[768,128]{1,0:T(8,128)(2,1)S(1)}, bf16[768,128]{1,0:T(8,128)(2,1)S(1)}, u32[]{:S(2)}, u32[]{:S(2)}) %collective-permute-start.22) | collective-permute-done | bytes 196640 | tf_op jit(solution)/shard_map/ppermute | solution.py:324
  77.0 2.0 %ensemble_grad_early.1.refs_0_ = f32[64,11520]{1,0:T(8,128)} custom-call(bf16[1440,128]{1,0:T(8,128)(2,1)S(1)} %get-tuple-element.37.refs_4_.refs_0_.refs_1_, bf16[1440,128]{1,0:T(8,128)(2,1)S(1)} %get-tuple-element.36.refs_1_.refs_2_, bf16[1440,128]{1,0:T(8,128)(2,1)S(1)} %get-tuple-element.38.refs_2_.refs_3_, ...), custom_call_target="tpu_custom_call" | custom-call | flops 737280 | bytes 5898240 | tf_op jit(solution)/shard_map/ensemble_grad_early/pallas_call | solution.py:496
  79.0 1.7 %collective-permute-done.25.refs_7_ = bf16[672,128]{1,0:T(8,128)(2,1)S(1)} collective-permute-done((bf16[672,128]{1,0:T(8,128)(2,1)S(1)}, bf16[672,128]{1,0:T(8,128)(2,1)S(1)}, u32[]{:S(2)}, u32[]{:S(2)}) %collective-permute-start.25) | collective-permute-done | bytes 172064 | tf_op jit(solution)/shard_map/ppermute | solution.py:324
  (52 shorter events, 19.6 us)
Async XLA Ops:
  0.6 1.4 %copy-start = (bf16[4,16,11520]{2,1,0:T(8,128)(2,1)S(1)}, bf16[4,16,11520]{2,1,0:T(8,128)(2,1)}, u32[]{:S(2)}) copy-start(bf16[4,16,11520]{2,1,0:T(8,128)(2,1)} %param.6) | copy-start | bytes 4423684
  2.3 12.4 %collective-permute-start = (bf16[1440,128]{1,0:T(8,128)(2,1)S(1)}, bf16[1440,128]{1,0:T(8,128)(2,1)S(1)}, u32[]{:S(2)}, u32[]{:S(2)}) collective-permute-start(bf16[1440,128]{1,0:T(8,128)(2,1)S(1)} %get-tuple-element.33.refs_2_), channel_id=1, source_target_pairs={{0,8},{8,0},{16,24},{24,16},{1,9},{9,1},{17,25},{25,17},{2,10},{10... | collective-permute-start | bytes 1105928 | tf_op jit(solution)/shard_map/ppermute | solution.py:324
  5.3 18.3 %collective-permute-start.1 = (bf16[1440,128]{1,0:T(8,128)(2,1)S(1)}, bf16[1440,128]{1,0:T(8,128)(2,1)S(1)}, u32[]{:S(2)}, u32[]{:S(2)}) collective-permute-start(bf16[1440,128]{1,0:T(8,128)(2,1)S(1)} %get-tuple-element.34.refs_3_), channel_id=1, source_target_pairs={{0,16},{8,24},{16,0},{24,8},{1,17},{9,25},{17,1},{25,9},{2,18},{10... | collective-permute-start | bytes 1105928 | tf_op jit(solution)/shard_map/ppermute | solution.py:324
  6.8 17.4 %collective-permute-start.2 = (bf16[1440,128]{1,0:T(8,128)(2,1)S(1)}, bf16[1440,128]{1,0:T(8,128)(2,1)S(1)}, u32[]{:S(2)}, u32[]{:S(2)}) collective-permute-start(bf16[1440,128]{1,0:T(8,128)(2,1)S(1)} %get-tuple-element.35.refs_4_), channel_id=1, source_target_pairs={{0,24},{8,16},{16,8},{24,0},{1,25},{9,17},{17,9},{25,1},{2,26},{10... | collective-permute-start | bytes 1105928 | tf_op jit(solution)/shard_map/ppermute | solution.py:324
  6.9 0.7 copy-start.2
  7.5 0.7 copy-start.3
  8.2 0.7 copy-start.4
  14.7 1.4 %copy-start.1 = (bf16[4,16,11520]{2,1,0:T(8,128)(2,1)S(1)}, bf16[4,16,11520]{2,1,0:T(8,128)(2,1)}, u32[]{:S(2)}) copy-start(bf16[4,16,11520]{2,1,0:T(8,128)(2,1)} %param.7) | copy-start | bytes 4423684
  16.4 18.2 %collective-permute-start.6 = (bf16[1440,128]{1,0:T(8,128)(2,1)S(1)}, bf16[1440,128]{1,0:T(8,128)(2,1)S(1)}, u32[]{:S(2)}, u32[]{:S(2)}) collective-permute-start(bf16[1440,128]{1,0:T(8,128)(2,1)S(1)} %get-tuple-element.36.refs_1_.refs_2_), channel_id=1, source_target_pairs={{0,8},{8,0},{16,24},{24,16},{1,9},{9,1},{17,25},{25,17},{2,10},{10... | collective-permute-start | bytes 1105928 | tf_op jit(solution)/shard_map/ppermute | solution.py:324
  18.5 20.7 %collective-permute-start.10 = (bf16[1440,128]{1,0:T(8,128)(2,1)S(1)}, bf16[1440,128]{1,0:T(8,128)(2,1)S(1)}, u32[]{:S(2)}, u32[]{:S(2)}) collective-permute-start(bf16[1440,128]{1,0:T(8,128)(2,1)S(1)} %get-tuple-element.38.refs_2_.refs_3_), channel_id=1, source_target_pairs={{0,16},{8,24},{16,0},{24,8},{1,17},{9,25},{17,1},{25,9},{2,18},{10... | collective-permute-start | bytes 1105928 | tf_op jit(solution)/shard_map/ppermute | solution.py:324
  20.1 19.2 %collective-permute-start.11 = (bf16[1440,128]{1,0:T(8,128)(2,1)S(1)}, bf16[1440,128]{1,0:T(8,128)(2,1)S(1)}, u32[]{:S(2)}, u32[]{:S(2)}) collective-permute-start(bf16[1440,128]{1,0:T(8,128)(2,1)S(1)} %get-tuple-element.39.refs_3_.refs_4_), channel_id=1, source_target_pairs={{0,24},{8,16},{16,8},{24,0},{1,25},{9,17},{17,9},{25,1},{2,26},{10... | collective-permute-start | bytes 1105928 | tf_op jit(solution)/shard_map/ppermute | solution.py:324
  25.2 1.2 %collective-permute-start.3 = (f32[16,16]{1,0:T(8,128)S(1)}, f32[16,16]{1,0:T(8,128)S(1)}, u32[]{:S(2)}, u32[]{:S(2)}) collective-permute-start(f32[16,16]{1,0:T(8,128)S(1)} %score_sums.1), channel_id=1, source_target_pairs={{0,1},{1,0},{2,3},{3,2},{4,5},{5,4},{6,7},{7,6},{8,9},{9,8},{10,11... | collective-permute-start | bytes 3080 | tf_op jit(solution)/shard_map/ppermute | solution.py:335
  26.4 3.7 %collective-permute-start.4 = (f32[16,16]{1,0:T(8,128)S(1)}, f32[16,16]{1,0:T(8,128)S(1)}, u32[]{:S(2)}, u32[]{:S(2)}) collective-permute-start(f32[16,16]{1,0:T(8,128)S(1)} %add.12), channel_id=1, source_target_pairs={{0,2},{1,3},{2,0},{3,1},{4,6},{5,7},{6,4},{7,5},{8,10},{9,11},{10,... | collective-permute-start | bytes 3080 | tf_op jit(solution)/shard_map/ppermute | solution.py:335
  30.0 4.5 %collective-permute-start.5 = (f32[16,16]{1,0:T(8,128)S(1)}, f32[16,16]{1,0:T(8,128)S(1)}, u32[]{:S(2)}, u32[]{:S(2)}) collective-permute-start(f32[16,16]{1,0:T(8,128)S(1)} %add.13.a_ref), channel_id=1, source_target_pairs={{0,4},{1,5},{2,6},{3,7},{4,0},{5,1},{6,2},{7,3},{8,12},{9,13},{10,... | collective-permute-start | bytes 3080 | tf_op jit(solution)/shard_map/ppermute | solution.py:404
  34.6 5.6 %collective-permute-start.9 = (f32[16,16]{1,0:T(8,128)S(1)}, f32[16,16]{1,0:T(8,128)S(1)}, u32[]{:S(2)}, u32[]{:S(2)}) collective-permute-start(f32[16,16]{1,0:T(8,128)S(1)} %join_sums.2.refs_8_.refs_0_), channel_id=1, source_target_pairs={{0,16},{8,24},{16,0},{24,8},{1,17},{9,25},{17,1},{25,9},{2,18},{10... | collective-permute-start | bytes 3080 | tf_op jit(solution)/shard_map/ppermute | solution.py:324
  36.5 3.7 %collective-permute-start.8 = (f32[16,16]{1,0:T(8,128)S(1)}, f32[16,16]{1,0:T(8,128)S(1)}, u32[]{:S(2)}, u32[]{:S(2)}) collective-permute-start(f32[16,16]{1,0:T(8,128)S(1)} %join_sums.2.refs_8_.refs_0_), channel_id=1, source_target_pairs={{0,8},{8,0},{16,24},{24,16},{1,9},{9,1},{17,25},{25,17},{2,10},{10... | collective-permute-start | bytes 3080 | tf_op jit(solution)/shard_map/ppermute | solution.py:324
  36.6 4.5 %collective-permute-start.7 = (f32[16,16]{1,0:T(8,128)S(1)}, f32[16,16]{1,0:T(8,128)S(1)}, u32[]{:S(2)}, u32[]{:S(2)}) collective-permute-start(f32[16,16]{1,0:T(8,128)S(1)} %join_sums.2.refs_8_.refs_0_), channel_id=1, source_target_pairs={{0,24},{8,16},{16,8},{24,0},{1,25},{9,17},{17,9},{25,1},{2,26},{10... | collective-permute-start | bytes 3080 | tf_op jit(solution)/shard_map/ppermute | solution.py:324
  42.6 12.9 %collective-permute-start.15 = (bf16[1440,128]{1,0:T(8,128)(2,1)S(1)}, bf16[1440,128]{1,0:T(8,128)(2,1)S(1)}, u32[]{:S(2)}, u32[]{:S(2)}) collective-permute-start(bf16[1440,128]{1,0:T(8,128)(2,1)S(1)} %get-tuple-element.46), channel_id=1, source_target_pairs={{0,8},{8,0},{16,24},{24,16},{1,9},{9,1},{17,25},{25,17},{2,10},{10... | collective-permute-start | bytes 1105928 | tf_op jit(solution)/shard_map/ppermute | solution.py:324
  44.6 15.5 %collective-permute-start.19 = (bf16[1440,128]{1,0:T(8,128)(2,1)S(1)}, bf16[1440,128]{1,0:T(8,128)(2,1)S(1)}, u32[]{:S(2)}, u32[]{:S(2)}) collective-permute-start(bf16[1440,128]{1,0:T(8,128)(2,1)S(1)} %get-tuple-element.47), channel_id=1, source_target_pairs={{0,16},{8,24},{16,0},{24,8},{1,17},{9,25},{17,1},{25,9},{2,18},{10... | collective-permute-start | bytes 1105928 | tf_op jit(solution)/shard_map/ppermute | solution.py:324
  44.7 15.4 %collective-permute-start.20 = (bf16[1440,128]{1,0:T(8,128)(2,1)S(1)}, bf16[1440,128]{1,0:T(8,128)(2,1)S(1)}, u32[]{:S(2)}, u32[]{:S(2)}) collective-permute-start(bf16[1440,128]{1,0:T(8,128)(2,1)S(1)} %get-tuple-element.48), channel_id=1, source_target_pairs={{0,24},{8,16},{16,8},{24,0},{1,25},{9,17},{17,9},{25,1},{2,26},{10... | collective-permute-start | bytes 1105928 | tf_op jit(solution)/shard_map/ppermute | solution.py:324
  46.1 1.2 %collective-permute-start.12 = (f32[16,16]{1,0:T(8,128)S(1)}, f32[16,16]{1,0:T(8,128)S(1)}, u32[]{:S(2)}, u32[]{:S(2)}) collective-permute-start(f32[16,16]{1,0:T(8,128)S(1)} %pair_sums.1.refs_8_), channel_id=1, source_target_pairs={{0,1},{1,0},{2,3},{3,2},{4,5},{5,4},{6,7},{7,6},{8,9},{9,8},{10,11... | collective-permute-start | bytes 3080 | tf_op jit(solution)/shard_map/ppermute | solution.py:335
  47.3 3.7 %collective-permute-start.13 = (f32[16,16]{1,0:T(8,128)S(1)}, f32[16,16]{1,0:T(8,128)S(1)}, u32[]{:S(2)}, u32[]{:S(2)}) collective-permute-start(f32[16,16]{1,0:T(8,128)S(1)} %add.14), channel_id=1, source_target_pairs={{0,2},{1,3},{2,0},{3,1},{4,6},{5,7},{6,4},{7,5},{8,10},{9,11},{10,... | collective-permute-start | bytes 3080 | tf_op jit(solution)/shard_map/ppermute | solution.py:335
  51.0 4.5 %collective-permute-start.14 = (f32[16,16]{1,0:T(8,128)S(1)}, f32[16,16]{1,0:T(8,128)S(1)}, u32[]{:S(2)}, u32[]{:S(2)}) collective-permute-start(f32[16,16]{1,0:T(8,128)S(1)} %add.15.a_ref), channel_id=1, source_target_pairs={{0,4},{1,5},{2,6},{3,7},{4,0},{5,1},{6,2},{7,3},{8,12},{9,13},{10,... | collective-permute-start | bytes 3080 | tf_op jit(solution)/shard_map/ppermute | solution.py:404
  55.5 4.7 %collective-permute-start.18 = (f32[16,16]{1,0:T(8,128)S(1)}, f32[16,16]{1,0:T(8,128)S(1)}, u32[]{:S(2)}, u32[]{:S(2)}) collective-permute-start(f32[16,16]{1,0:T(8,128)S(1)} %join_sums.3.refs_8_), channel_id=1, source_target_pairs={{0,16},{8,24},{16,0},{24,8},{1,17},{9,25},{17,1},{25,9},{2,18},{10... | collective-permute-start | bytes 3080 | tf_op jit(solution)/shard_map/ppermute | solution.py:324
  57.0 3.7 %collective-permute-start.17 = (f32[16,16]{1,0:T(8,128)S(1)}, f32[16,16]{1,0:T(8,128)S(1)}, u32[]{:S(2)}, u32[]{:S(2)}) collective-permute-start(f32[16,16]{1,0:T(8,128)S(1)} %join_sums.3.refs_8_), channel_id=1, source_target_pairs={{0,8},{8,0},{16,24},{24,16},{1,9},{9,1},{17,25},{25,17},{2,10},{10... | collective-permute-start | bytes 3080 | tf_op jit(solution)/shard_map/ppermute | solution.py:324
  57.6 4.5 %collective-permute-start.16 = (f32[16,16]{1,0:T(8,128)S(1)}, f32[16,16]{1,0:T(8,128)S(1)}, u32[]{:S(2)}, u32[]{:S(2)}) collective-permute-start(f32[16,16]{1,0:T(8,128)S(1)} %join_sums.3.refs_8_), channel_id=1, source_target_pairs={{0,24},{8,16},{16,8},{24,0},{1,25},{9,17},{17,9},{25,1},{2,26},{10... | collective-permute-start | bytes 3080 | tf_op jit(solution)/shard_map/ppermute | solution.py:324
  63.4 7.8 %collective-permute-start.21 = (bf16[768,128]{1,0:T(8,128)(2,1)S(1)}, bf16[768,128]{1,0:T(8,128)(2,1)S(1)}, u32[]{:S(2)}, u32[]{:S(2)}) collective-permute-start(bf16[768,128]{1,0:T(8,128)(2,1)S(1)} %get-tuple-element.49), channel_id=1, source_target_pairs={{0,8},{8,0},{16,24},{24,16},{1,9},{9,1},{17,25},{25,17},{2,10},{10... | collective-permute-start | bytes 589832 | tf_op jit(solution)/shard_map/ppermute | solution.py:324
  65.0 12.1 %collective-permute-start.22 = (bf16[768,128]{1,0:T(8,128)(2,1)S(1)}, bf16[768,128]{1,0:T(8,128)(2,1)S(1)}, u32[]{:S(2)}, u32[]{:S(2)}) collective-permute-start(bf16[768,128]{1,0:T(8,128)(2,1)S(1)} %get-tuple-element.52), channel_id=1, source_target_pairs={{0,16},{8,24},{16,0},{24,8},{1,17},{9,25},{17,1},{25,9},{2,18},{10... | collective-permute-start | bytes 589832 | tf_op jit(solution)/shard_map/ppermute | solution.py:324
  65.5 11.5 %collective-permute-start.23 = (bf16[768,128]{1,0:T(8,128)(2,1)S(1)}, bf16[768,128]{1,0:T(8,128)(2,1)S(1)}, u32[]{:S(2)}, u32[]{:S(2)}) collective-permute-start(bf16[768,128]{1,0:T(8,128)(2,1)S(1)} %get-tuple-element.53), channel_id=1, source_target_pairs={{0,24},{8,16},{16,8},{24,0},{1,25},{9,17},{17,9},{25,1},{2,26},{10... | collective-permute-start | bytes 589832 | tf_op jit(solution)/shard_map/ppermute | solution.py:324
  68.4 10.7 %collective-permute-start.24 = (bf16[672,128]{1,0:T(8,128)(2,1)S(1)}, bf16[672,128]{1,0:T(8,128)(2,1)S(1)}, u32[]{:S(2)}, u32[]{:S(2)}) collective-permute-start(bf16[672,128]{1,0:T(8,128)(2,1)S(1)} %get-tuple-element.55), channel_id=1, source_target_pairs={{0,8},{8,0},{16,24},{24,16},{1,9},{9,1},{17,25},{25,17},{2,10},{10... | collective-permute-start | bytes 516104 | tf_op jit(solution)/shard_map/ppermute | solution.py:324
  69.9 10.8 %collective-permute-start.25 = (bf16[672,128]{1,0:T(8,128)(2,1)S(1)}, bf16[672,128]{1,0:T(8,128)(2,1)S(1)}, u32[]{:S(2)}, u32[]{:S(2)}) collective-permute-start(bf16[672,128]{1,0:T(8,128)(2,1)S(1)} %get-tuple-element.56), channel_id=1, source_target_pairs={{0,16},{8,24},{16,0},{24,8},{1,17},{9,25},{17,1},{25,9},{2,18},{10... | collective-permute-start | bytes 516104 | tf_op jit(solution)/shard_map/ppermute | solution.py:324
  71.3 9.5 %collective-permute-start.26 = (bf16[672,128]{1,0:T(8,128)(2,1)S(1)}, bf16[672,128]{1,0:T(8,128)(2,1)S(1)}, u32[]{:S(2)}, u32[]{:S(2)}) collective-permute-start(bf16[672,128]{1,0:T(8,128)(2,1)S(1)} %get-tuple-element.57), channel_id=1, source_target_pairs={{0,24},{8,16},{16,8},{24,0},{1,25},{9,17},{17,9},{25,1},{2,26},{10... | collective-permute-start | bytes 516104 | tf_op jit(solution)/shard_map/ppermute | solution.py:324
  (1 other events, 0.7 us)

commit v6 on v5

--- a/solution.py
+++ b/solution.py
@@ -228,21 +228,31 @@
         store_tiles(outs, value, tiles, per, 0, main)
 
 
-def transposed_weights_kernel(
-    me_of, channels, members, group, scale, s_ref, ovt_ref, w_ref, high_ref, low_ref
+def early_gradient_kernel(
+    me_of, count, main, per, last, channels, members, group, scale, s_ref, ovt_ref, *refs
 ):
+    grads, (w_ref, high_ref, low_ref, value_ref) = refs[:count], refs[count:]
     rows = ovt_ref.shape[0]
     picks = member_of_row(me_of(), rows, channels, members, group).astype(jnp.bfloat16)
     weights = softmax(s_ref[...] * scale)
     w_ref[...] = weights
-    high_ref[...], low_ref[...] = two_parts(spread_t(weights, picks) * ovt_ref[...])
+    high, low = two_parts(spread_t(weights, picks) * ovt_ref[...])
+    high_ref[...], low_ref[...] = high, low
+    at = 0
+    for tiles in tile_groups(0, last, 0):
+        c = gather_tiles(grads, tiles, per, main)
+        value_ref[:, at:at + len(tiles) * LANES] = mm(high, c, ((1,), (0,))) + mm(
+            low, c, ((1,), (0,))
+        )
+        at += len(tiles) * LANES
 
 
 def grad_kernel(
-    me_of, count, main, half, per, group, channels, members, scale, first, last, waits,
-    w_ref, qk_ref, qkt_ref, a_high_ref, a_low_ref, *refs,
+    me_of, count, main, half, per, group, channels, members, scale, first, last, waits, early,
+    w_ref, qk_ref, qkt_ref, *refs,
 ):
     me = me_of()
+    known, refs = refs[:1 if early else 2], refs[1 if early else 2:]
     fields, grads, sums = refs[:count], refs[count:2 * count], refs[2 * count:3 * count]
     outs = refs[3 * count + waits:]
     rows = count * per
@@ -253,15 +263,18 @@
     d_high, d_low = two_parts(
         spread(slope, picks) * qk_ref[...] + spread_t(slope, picks) * qkt_ref[...]
     )
-    a_high, a_low = a_high_ref[...], a_low_ref[...]
+    at = 0
     for tiles in tile_groups(first, last, half):
         e = gather_tiles(fields, tiles, per, main)
-        c = gather_tiles(grads, tiles, per, main)
-        value = (
-            mm(d_high, e, ((1,), (0,))) + mm(d_low, e, ((1,), (0,)))
-            + mm(a_high, c, ((1,), (0,))) + mm(a_low, c, ((1,), (0,)))
-        )
+        value = mm(d_high, e, ((1,), (0,))) + mm(d_low, e, ((1,), (0,)))
+        if early:
+            value = value + known[0][:, at:at + len(tiles) * LANES]
+        else:
+            c = gather_tiles(grads, tiles, per, main)
+            for weight in known:
+                value = value + mm(weight[...], c, ((1,), (0,)))
         store_tiles(outs, value, tiles, per, first, last)
+        at += len(tiles) * LANES
 
 
 def finish_kernel(
@@ -457,37 +470,40 @@
     pairs = join(pairs, "space", space_steps[-1], branch_home[first:first + 1])
     pair_parts = [pairs] + [swap(pairs, s, count) for s in order]
 
-    weights, a_high, a_low = pl.pallas_call(
+    mid = (main + 1 + half) // 2
+    weights, a_high, a_low, early = pl.pallas_call(
         functools.partial(
-            transposed_weights_kernel, me_of, channels, members, group, scale
+            early_gradient_kernel, me_of, count, main, per, mid, channels, members, group,
+            scale,
         ),
-        out_shape=[pair] + [jax.ShapeDtypeStruct((rows, rows), bf)] * 2,
-        in_specs=[whole] * 2,
-        out_specs=[whole] * 3,
+        out_shape=[pair]
+        + [jax.ShapeDtypeStruct((rows, rows), bf)] * 2
+        + [jax.ShapeDtypeStruct((rows, mid * LANES), f32)],
+        in_specs=[whole] * (count + 2),
+        out_specs=[whole] * 4,
         compiler_params=params,
         cost_estimate=cost(10**8, 8 * rows * rows),
-        name="transposed_weights",
-    )(scores, ovt)
-
-    def gradient(begin, end, with_half, awaited, name):
+        name="early_gradient",
+    )(scores, ovt, *c_cells)
+
+    def gradient(begin, end, with_half, known, awaited, name):
         size = (end - begin) * LANES
         parts = pl.pallas_call(
             functools.partial(
                 grad_kernel, me_of, count, main, with_half, per, group, channels, members, scale,
-                begin, end, len(awaited),
+                begin, end, len(awaited), len(known) == 1,
             ),
             out_shape=[packed(end - begin, with_half)] * count,
-            in_specs=[whole] * (3 * count + 5) + [anywhere] * len(awaited),
+            in_specs=[whole] * (3 * count + 3 + len(known)) + [anywhere] * len(awaited),
             out_specs=[whole] * count,
             compiler_params=params,
             cost_estimate=cost(8 * rows * rows * size, 6 * rows * size),
             name=name,
-        )(weights, qk, qkt, a_high, a_low, *e_cells, *c_cells, *pair_parts, *awaited)
+        )(weights, qk, qkt, *known, *e_cells, *c_cells, *pair_parts, *awaited)
         return exchange(parts)
 
-    mid = (main + 1 + half) // 2
-    grad_a = gradient(0, mid, 0, branch_home[1:], "input_gradient_a")
-    grad_b = gradient(mid, main, half, branch_home[1:], "input_gradient_b")
+    grad_a = gradient(0, mid, 0, [early], branch_home[1:], "input_gradient_a")
+    grad_b = gradient(mid, main, half, [a_high, a_low], branch_home[1:], "input_gradient_b")
     serial = count * main - length // LANES > main - mid
 
     def finish(base, extra, stages, halves, before, after, name):

time: 82.1 us -> 81.7 us (level)
  transfers between devices with their start and end apart: 27 -> 27, of which waited for: 18 -> 18; matrix products, arithmetic and copies ran while one was open for 0% -> 0% of each run, Pallas kernels for 12% -> 13%
where the time goes in v6:
time: 81.7 us; the launch traced here: 81.4 us
  starting transfers between devices  34.1 us (42%)
  waiting for transfers between devices  27.1 us (33%)
  Pallas kernels  14 us (17%)
  local copies, waits for them, and re-layouts  5.48 us (7%)
    ppermute x21, starting transfers between devices, swap(): return lax.ppermute(value, 'mem', [(i, i ^ step) for i in range(count)])  25.8 us
    ppermute x21, waiting for transfers between devices, swap(): return lax.ppermute(value, 'mem', [(i, i ^ step) for i in range(count)])  16.6 us
    ppermute x4, waiting for transfers between devices, sum_steps(): lax.ppermute(value, name, [(i, i ^ step) for i in range(size)])  6.52 us
    unnamed x12, local copies, waits for them, and re-layouts  5.48 us
    pallas_call x3, Pallas kernels, finish(): pl.pallas_call(functools.partial(finish_kernel, me_of, count, main, per,...  5.38 us
    ppermute x2, starting transfers between devices, join(): other = lax.ppermute(value, name, [(i, i ^ step) for i in range(size)])  5.16 us
    ppermute x2, waiting for transfers between devices, join(): other = lax.ppermute(value, name, [(i, i ^ step) for i in range(size)])  3.93 us
    ppermute x4, starting transfers between devices, sum_steps(): lax.ppermute(value, name, [(i, i ^ step) for i in range(size)])  3.15 us
  transfers between devices with their start and end apart: 27, of which 18 were waited for; matrix products, arithmetic and copies ran while one was open for 0% of the time, Pallas kernels for 13%

profile of v6, /device:TPU:0, one launch (start us, length us, event | category | flops | bytes accessed | tf_op | source)
XLA Modules:
  0.0 81.4 jit_solution(7358739342566251908)
XLA Ops:
  2.3 3.0 %collective-permute-start = (bf16[1440,128]{1,0:T(8,128)(2,1)S(1)}, bf16[1440,128]{1,0:T(8,128)(2,1)S(1)}, u32[]{:S(2)}, u32[]{:S(2)}) collective-permute-start(bf16[1440,128]{1,0:T(8,128)(2,1)S(1)} %get-tuple-element.34.refs_2_), channel_id=1, source_target_pairs={{0,8},{8,0},{16,24},{24,16},{1,9},{9,1},{17,25},{25,17},{2,10},{10... | collective-permute-start | bytes 1105928 | tf_op jit(solution)/shard_map/ppermute | solution.py:337
  5.3 1.5 %collective-permute-start.1 = (bf16[1440,128]{1,0:T(8,128)(2,1)S(1)}, bf16[1440,128]{1,0:T(8,128)(2,1)S(1)}, u32[]{:S(2)}, u32[]{:S(2)}) collective-permute-start(bf16[1440,128]{1,0:T(8,128)(2,1)S(1)} %get-tuple-element.35.refs_3_), channel_id=1, source_target_pairs={{0,16},{8,24},{16,0},{24,8},{1,17},{9,25},{17,1},{25,9},{2,18},{10... | collective-permute-start | bytes 1105928 | tf_op jit(solution)/shard_map/ppermute | solution.py:337
  10.9 3.8 %collective-permute-done.refs_1_.rest_0_.refs_5_.refs_2_.refs_3_ = bf16[1440,128]{1,0:T(8,128)(2,1)S(1)} collective-permute-done((bf16[1440,128]{1,0:T(8,128)(2,1)S(1)}, bf16[1440,128]{1,0:T(8,128)(2,1)S(1)}, u32[]{:S(2)}, u32[]{:S(2)}) %collective-permute-start) | collective-permute-done | bytes 368672 | tf_op jit(solution)/shard_map/ppermute | solution.py:337
  14.7 1.4 %copy-done.1 = bf16[4,16,11520]{2,1,0:T(8,128)(2,1)S(1)} copy-done((bf16[4,16,11520]{2,1,0:T(8,128)(2,1)S(1)}, bf16[4,16,11520]{2,1,0:T(8,128)(2,1)}, u32[]{:S(2)}) %copy-start.1) | copy-done | bytes 1474584
  16.4 2.1 %collective-permute-start.6 = (bf16[1440,128]{1,0:T(8,128)(2,1)S(1)}, bf16[1440,128]{1,0:T(8,128)(2,1)S(1)}, u32[]{:S(2)}, u32[]{:S(2)}) collective-permute-start(bf16[1440,128]{1,0:T(8,128)(2,1)S(1)} %get-tuple-element.37.refs_1_.refs_2_), channel_id=1, source_target_pairs={{0,8},{8,0},{16,24},{24,16},{1,9},{9,1},{17,25},{25,17},{2,10},{10... | collective-permute-start | bytes 1105928 | tf_op jit(solution)/shard_map/ppermute | solution.py:337
  18.5 1.5 %collective-permute-start.10 = (bf16[1440,128]{1,0:T(8,128)(2,1)S(1)}, bf16[1440,128]{1,0:T(8,128)(2,1)S(1)}, u32[]{:S(2)}, u32[]{:S(2)}) collective-permute-start(bf16[1440,128]{1,0:T(8,128)(2,1)S(1)} %get-tuple-element.39.refs_2_.refs_3_), channel_id=1, source_target_pairs={{0,16},{8,24},{16,0},{24,8},{1,17},{9,25},{17,1},{25,9},{2,18},{10... | collective-permute-start | bytes 1105928 | tf_op jit(solution)/shard_map/ppermute | solution.py:337
  20.1 3.6 %collective-permute-done.1.refs_2_.refs_6_.refs_3_.refs_4_ = bf16[1440,128]{1,0:T(8,128)(2,1)S(1)} collective-permute-done((bf16[1440,128]{1,0:T(8,128)(2,1)S(1)}, bf16[1440,128]{1,0:T(8,128)(2,1)S(1)}, u32[]{:S(2)}, u32[]{:S(2)}) %collective-permute-start.1) | collective-permute-done | bytes 368672 | tf_op jit(solution)/shard_map/ppermute | solution.py:337
  26.4 1.6 %collective-permute-start.4 = (f32[16,16]{1,0:T(8,128)S(1)}, f32[16,16]{1,0:T(8,128)S(1)}, u32[]{:S(2)}, u32[]{:S(2)}) collective-permute-start(f32[16,16]{1,0:T(8,128)S(1)} %add.12), channel_id=1, source_target_pairs={{0,2},{1,3},{2,0},{3,1},{4,6},{5,7},{6,4},{7,5},{8,10},{9,11},{10,... | collective-permute-start | bytes 3080 | tf_op jit(solution)/shard_map/ppermute | solution.py:348
  28.0 2.1 %collective-permute-done.4 = f32[16,16]{1,0:T(8,128)S(1)} collective-permute-done((f32[16,16]{1,0:T(8,128)S(1)}, f32[16,16]{1,0:T(8,128)S(1)}, u32[]{:S(2)}, u32[]{:S(2)}) %collective-permute-start.4) | collective-permute-done | bytes 1056 | tf_op jit(solution)/shard_map/ppermute | solution.py:348
  30.0 2.6 %collective-permute-start.5 = (f32[16,16]{1,0:T(8,128)S(1)}, f32[16,16]{1,0:T(8,128)S(1)}, u32[]{:S(2)}, u32[]{:S(2)}) collective-permute-start(f32[16,16]{1,0:T(8,128)S(1)} %add.13.a_ref), channel_id=1, source_target_pairs={{0,4},{1,5},{2,6},{3,7},{4,0},{5,1},{6,2},{7,3},{8,12},{9,13},{10,... | collective-permute-start | bytes 3080 | tf_op jit(solution)/shard_map/ppermute | solution.py:417
  32.6 2.0 %collective-permute-done.5.b_ref = f32[16,16]{1,0:T(8,128)S(1)} collective-permute-done((f32[16,16]{1,0:T(8,128)S(1)}, f32[16,16]{1,0:T(8,128)S(1)}, u32[]{:S(2)}, u32[]{:S(2)}) %collective-permute-start.5) | collective-permute-done | bytes 1056 | tf_op jit(solution)/shard_map/ppermute | solution.py:417
  34.6 1.9 %collective-permute-start.9 = (f32[16,16]{1,0:T(8,128)S(1)}, f32[16,16]{1,0:T(8,128)S(1)}, u32[]{:S(2)}, u32[]{:S(2)}) collective-permute-start(f32[16,16]{1,0:T(8,128)S(1)} %join_sums.2.refs_8_.refs_0_), channel_id=1, source_target_pairs={{0,16},{8,24},{16,0},{24,8},{1,17},{9,25},{17,1},{25,9},{2,18},{10... | collective-permute-start | bytes 3080 | tf_op jit(solution)/shard_map/ppermute | solution.py:337
  36.6 1.5 %collective-permute-start.7 = (f32[16,16]{1,0:T(8,128)S(1)}, f32[16,16]{1,0:T(8,128)S(1)}, u32[]{:S(2)}, u32[]{:S(2)}) collective-permute-start(f32[16,16]{1,0:T(8,128)S(1)} %join_sums.2.refs_8_.refs_0_), channel_id=1, source_target_pairs={{0,24},{8,16},{16,8},{24,0},{1,25},{9,17},{17,9},{25,1},{2,26},{10... | collective-permute-start | bytes 3080 | tf_op jit(solution)/shard_map/ppermute | solution.py:337
  41.1 1.4 %branch.1 = (f32[16,16]{1,0:T(8,128)S(1)}, bf16[1440,128]{1,0:T(8,128)(2,1)S(1)}, bf16[1440,128]{1,0:T(8,128)(2,1)S(1)}, bf16[1440,128]{1,0:T(8,128)(2,1)S(1)}, bf16[1440,128]{1,0:T(8,128)(2,1)S(1)}) custom-call(f32[256,256]{1,0:T(8,128)S(1)} %get-tuple-element.31.tile_ref.ov_ref, f32[16,16]{1,0:T(8,128)S(1)} %join_sums.2.refs_8_.refs_0_, ...), custom_call_target="tpu_custom_call" | custom-call | flops 754974720 | bytes 2949120 | tf_op jit(solution)/shard_map/branch/pallas_call | solution.py:456
  42.6 2.0 %collective-permute-start.15 = (bf16[1440,128]{1,0:T(8,128)(2,1)S(1)}, bf16[1440,128]{1,0:T(8,128)(2,1)S(1)}, u32[]{:S(2)}, u32[]{:S(2)}) collective-permute-start(bf16[1440,128]{1,0:T(8,128)(2,1)S(1)} %get-tuple-element.46), channel_id=1, source_target_pairs={{0,8},{8,0},{16,24},{24,16},{1,9},{9,1},{17,25},{25,17},{2,10},{10... | collective-permute-start | bytes 1105928 | tf_op jit(solution)/shard_map/ppermute | solution.py:337
  44.7 1.4 %collective-permute-start.20 = (bf16[1440,128]{1,0:T(8,128)(2,1)S(1)}, bf16[1440,128]{1,0:T(8,128)(2,1)S(1)}, u32[]{:S(2)}, u32[]{:S(2)}) collective-permute-start(bf16[1440,128]{1,0:T(8,128)(2,1)S(1)} %get-tuple-element.48), channel_id=1, source_target_pairs={{0,24},{8,16},{16,8},{24,0},{1,25},{9,17},{17,9},{25,1},{2,26},{10... | collective-permute-start | bytes 1105928 | tf_op jit(solution)/shard_map/ppermute | solution.py:337
  47.3 1.6 %collective-permute-start.13 = (f32[16,16]{1,0:T(8,128)S(1)}, f32[16,16]{1,0:T(8,128)S(1)}, u32[]{:S(2)}, u32[]{:S(2)}) collective-permute-start(f32[16,16]{1,0:T(8,128)S(1)} %add.14), channel_id=1, source_target_pairs={{0,2},{1,3},{2,0},{3,1},{4,6},{5,7},{6,4},{7,5},{8,10},{9,11},{10,... | collective-permute-start | bytes 3080 | tf_op jit(solution)/shard_map/ppermute | solution.py:348
  48.9 2.1 %collective-permute-done.13 = f32[16,16]{1,0:T(8,128)S(1)} collective-permute-done((f32[16,16]{1,0:T(8,128)S(1)}, f32[16,16]{1,0:T(8,128)S(1)}, u32[]{:S(2)}, u32[]{:S(2)}) %collective-permute-start.13) | collective-permute-done | bytes 1056 | tf_op jit(solution)/shard_map/ppermute | solution.py:348
  51.0 2.6 %collective-permute-start.14 = (f32[16,16]{1,0:T(8,128)S(1)}, f32[16,16]{1,0:T(8,128)S(1)}, u32[]{:S(2)}, u32[]{:S(2)}) collective-permute-start(f32[16,16]{1,0:T(8,128)S(1)} %add.15.a_ref), channel_id=1, source_target_pairs={{0,4},{1,5},{2,6},{3,7},{4,0},{5,1},{6,2},{7,3},{8,12},{9,13},{10,... | collective-permute-start | bytes 3080 | tf_op jit(solution)/shard_map/ppermute | solution.py:417
  53.6 2.0 %collective-permute-done.14.b_ref = f32[16,16]{1,0:T(8,128)S(1)} collective-permute-done((f32[16,16]{1,0:T(8,128)S(1)}, f32[16,16]{1,0:T(8,128)S(1)}, u32[]{:S(2)}, u32[]{:S(2)}) %collective-permute-start.14) | collective-permute-done | bytes 1056 | tf_op jit(solution)/shard_map/ppermute | solution.py:417
  55.5 1.5 %collective-permute-start.18 = (f32[16,16]{1,0:T(8,128)S(1)}, f32[16,16]{1,0:T(8,128)S(1)}, u32[]{:S(2)}, u32[]{:S(2)}) collective-permute-start(f32[16,16]{1,0:T(8,128)S(1)} %join_sums.3.refs_9_.refs_10_), channel_id=1, source_target_pairs={{0,16},{8,24},{16,0},{24,8},{1,17},{9,25},{17,1},{25,9},{2,18},{10... | collective-permute-start | bytes 3080 | tf_op jit(solution)/shard_map/ppermute | solution.py:337
  57.6 1.4 %collective-permute-start.16 = (f32[16,16]{1,0:T(8,128)S(1)}, f32[16,16]{1,0:T(8,128)S(1)}, u32[]{:S(2)}, u32[]{:S(2)}) collective-permute-start(f32[16,16]{1,0:T(8,128)S(1)} %join_sums.3.refs_9_.refs_10_), channel_id=1, source_target_pairs={{0,24},{8,16},{16,8},{24,0},{1,25},{9,17},{17,9},{25,1},{2,26},{10... | collective-permute-start | bytes 3080 | tf_op jit(solution)/shard_map/ppermute | solution.py:337
  60.7 1.4 %collective-permute-done.16.refs_10_.refs_11_ = f32[16,16]{1,0:T(8,128)S(1)} collective-permute-done((f32[16,16]{1,0:T(8,128)S(1)}, f32[16,16]{1,0:T(8,128)S(1)}, u32[]{:S(2)}, u32[]{:S(2)}) %collective-permute-start.16) | collective-permute-done | bytes 1056 | tf_op jit(solution)/shard_map/ppermute | solution.py:337
  63.0 1.6 %collective-permute-start.21 = (bf16[768,128]{1,0:T(8,128)(2,1)S(1)}, bf16[768,128]{1,0:T(8,128)(2,1)S(1)}, u32[]{:S(2)}, u32[]{:S(2)}) collective-permute-start(bf16[768,128]{1,0:T(8,128)(2,1)S(1)} %get-tuple-element.49), channel_id=1, source_target_pairs={{0,8},{8,0},{16,24},{24,16},{1,9},{9,1},{17,25},{25,17},{2,10},{10... | collective-permute-start | bytes 589832 | tf_op jit(solution)/shard_map/ppermute | solution.py:337
  65.1 1.5 %collective-permute-start.23 = (bf16[768,128]{1,0:T(8,128)(2,1)S(1)}, bf16[768,128]{1,0:T(8,128)(2,1)S(1)}, u32[]{:S(2)}, u32[]{:S(2)}) collective-permute-start(bf16[768,128]{1,0:T(8,128)(2,1)S(1)} %get-tuple-element.53), channel_id=1, source_target_pairs={{0,24},{8,16},{16,8},{24,0},{1,25},{9,17},{17,9},{25,1},{2,26},{10... | collective-permute-start | bytes 589832 | tf_op jit(solution)/shard_map/ppermute | solution.py:337
  66.6 1.4 %input_gradient_b.1 = (bf16[672,128]{1,0:T(8,128)(2,1)S(1)}, bf16[672,128]{1,0:T(8,128)(2,1)S(1)}, bf16[672,128]{1,0:T(8,128)(2,1)S(1)}, bf16[672,128]{1,0:T(8,128)(2,1)S(1)}) custom-call(f32[16,16]{1,0:T(8,128)S(1)} %get-tuple-element.43.w_ref, f32[256,256]{1,0:T(8,128)S(1)} %get-tuple-element.32.tile_ref.rest_1_.qk_ref, ...), custom_call_target="tpu_custom_call" | custom-call | flops 671088640 | bytes 1966080 | tf_op jit(solution)/shard_map/input_gradient_b/pallas_call | solution.py:491
  68.0 1.5 %collective-permute-start.24 = (bf16[672,128]{1,0:T(8,128)(2,1)S(1)}, bf16[672,128]{1,0:T(8,128)(2,1)S(1)}, u32[]{:S(2)}, u32[]{:S(2)}) collective-permute-start(bf16[672,128]{1,0:T(8,128)(2,1)S(1)} %get-tuple-element.57), channel_id=1, source_target_pairs={{0,8},{8,0},{16,24},{24,16},{1,9},{9,1},{17,25},{25,17},{2,10},{10... | collective-permute-start | bytes 516104 | tf_op jit(solution)/shard_map/ppermute | solution.py:337
  70.9 1.4 %collective-permute-start.26 = (bf16[672,128]{1,0:T(8,128)(2,1)S(1)}, bf16[672,128]{1,0:T(8,128)(2,1)S(1)}, u32[]{:S(2)}, u32[]{:S(2)}) collective-permute-start(bf16[672,128]{1,0:T(8,128)(2,1)S(1)} %get-tuple-element.59), channel_id=1, source_target_pairs={{0,24},{8,16},{16,8},{24,0},{1,25},{9,17},{17,9},{25,1},{2,26},{10... | collective-permute-start | bytes 516104 | tf_op jit(solution)/shard_map/ppermute | solution.py:337
  72.3 2.4 %updated.1 = f32[64,11520]{1,0:T(8,128)} custom-call(bf16[768,128]{1,0:T(8,128)(2,1)S(1)} %collective-permute-done.21.refs_0_.refs_5_, bf16[1440,128]{1,0:T(8,128)(2,1)S(1)} %get-tuple-element.33.refs_0_.refs_4_.refs_1_.refs_2_, bf16[1440,128]{1,0:T(8,128)(2,1)S(1)} %get-tuple-element.34.refs_2_, bf16[1440,128]{1,0:T(8,128)(2,1)S(1)} %get-tuple-element.35.refs_3_, ...), custom_call_target="tpu_custom_call" | custom-call | flops 737280 | bytes 5898240 | tf_op jit(solution)/shard_map/updated/pallas_call | solution.py:512
  74.7 2.0 %collective-permute-done.22.refs_6_ = bf16[768,128]{1,0:T(8,128)(2,1)S(1)} collective-permute-done((bf16[768,128]{1,0:T(8,128)(2,1)S(1)}, bf16[768,128]{1,0:T(8,128)(2,1)S(1)}, u32[]{:S(2)}, u32[]{:S(2)}) %collective-permute-start.22) | collective-permute-done | bytes 196640 | tf_op jit(solution)/shard_map/ppermute | solution.py:337
  76.7 2.0 %ensemble_grad_early.1.refs_0_ = f32[64,11520]{1,0:T(8,128)} custom-call(bf16[1440,128]{1,0:T(8,128)(2,1)S(1)} %get-tuple-element.38.refs_4_.refs_0_.refs_5_.refs_6_.refs_1_, bf16[1440,128]{1,0:T(8,128)(2,1)S(1)} %get-tuple-element.37.refs_1_.refs_2_, bf16[1440,128]{1,0:T(8,128)(2,1)S(1)} %get-tuple-element.39.refs_2_.refs_3_, ...), custom_call_target="tpu_custom_call" | custom-call | flops 737280 | bytes 5898240 | tf_op jit(solution)/shard_map/ensemble_grad_early/pallas_call | solution.py:512
  78.6 1.7 %collective-permute-done.25.refs_7_ = bf16[672,128]{1,0:T(8,128)(2,1)S(1)} collective-permute-done((bf16[672,128]{1,0:T(8,128)(2,1)S(1)}, bf16[672,128]{1,0:T(8,128)(2,1)S(1)}, u32[]{:S(2)}, u32[]{:S(2)}) %collective-permute-start.25) | collective-permute-done | bytes 172064 | tf_op jit(solution)/shard_map/ppermute | solution.py:337
  (52 shorter events, 19.2 us)
Async XLA Ops:
  0.6 1.4 %copy-start = (bf16[4,16,11520]{2,1,0:T(8,128)(2,1)S(1)}, bf16[4,16,11520]{2,1,0:T(8,128)(2,1)}, u32[]{:S(2)}) copy-start(bf16[4,16,11520]{2,1,0:T(8,128)(2,1)} %param.6) | copy-start | bytes 4423684
  2.3 12.4 %collective-permute-start = (bf16[1440,128]{1,0:T(8,128)(2,1)S(1)}, bf16[1440,128]{1,0:T(8,128)(2,1)S(1)}, u32[]{:S(2)}, u32[]{:S(2)}) collective-permute-start(bf16[1440,128]{1,0:T(8,128)(2,1)S(1)} %get-tuple-element.34.refs_2_), channel_id=1, source_target_pairs={{0,8},{8,0},{16,24},{24,16},{1,9},{9,1},{17,25},{25,17},{2,10},{10... | collective-permute-start | bytes 1105928 | tf_op jit(solution)/shard_map/ppermute | solution.py:337
  5.3 18.3 %collective-permute-start.1 = (bf16[1440,128]{1,0:T(8,128)(2,1)S(1)}, bf16[1440,128]{1,0:T(8,128)(2,1)S(1)}, u32[]{:S(2)}, u32[]{:S(2)}) collective-permute-start(bf16[1440,128]{1,0:T(8,128)(2,1)S(1)} %get-tuple-element.35.refs_3_), channel_id=1, source_target_pairs={{0,16},{8,24},{16,0},{24,8},{1,17},{9,25},{17,1},{25,9},{2,18},{10... | collective-permute-start | bytes 1105928 | tf_op jit(solution)/shard_map/ppermute | solution.py:337
  6.8 17.4 %collective-permute-start.2 = (bf16[1440,128]{1,0:T(8,128)(2,1)S(1)}, bf16[1440,128]{1,0:T(8,128)(2,1)S(1)}, u32[]{:S(2)}, u32[]{:S(2)}) collective-permute-start(bf16[1440,128]{1,0:T(8,128)(2,1)S(1)} %get-tuple-element.36.refs_4_), channel_id=1, source_target_pairs={{0,24},{8,16},{16,8},{24,0},{1,25},{9,17},{17,9},{25,1},{2,26},{10... | collective-permute-start | bytes 1105928 | tf_op jit(solution)/shard_map/ppermute | solution.py:337
  6.9 0.7 copy-start.2
  7.5 0.7 copy-start.3
  8.2 0.7 copy-start.4
  14.7 1.4 %copy-start.1 = (bf16[4,16,11520]{2,1,0:T(8,128)(2,1)S(1)}, bf16[4,16,11520]{2,1,0:T(8,128)(2,1)}, u32[]{:S(2)}) copy-start(bf16[4,16,11520]{2,1,0:T(8,128)(2,1)} %param.7) | copy-start | bytes 4423684
  16.4 18.2 %collective-permute-start.6 = (bf16[1440,128]{1,0:T(8,128)(2,1)S(1)}, bf16[1440,128]{1,0:T(8,128)(2,1)S(1)}, u32[]{:S(2)}, u32[]{:S(2)}) collective-permute-start(bf16[1440,128]{1,0:T(8,128)(2,1)S(1)} %get-tuple-element.37.refs_1_.refs_2_), channel_id=1, source_target_pairs={{0,8},{8,0},{16,24},{24,16},{1,9},{9,1},{17,25},{25,17},{2,10},{10... | collective-permute-start | bytes 1105928 | tf_op jit(solution)/shard_map/ppermute | solution.py:337
  18.5 20.7 %collective-permute-start.10 = (bf16[1440,128]{1,0:T(8,128)(2,1)S(1)}, bf16[1440,128]{1,0:T(8,128)(2,1)S(1)}, u32[]{:S(2)}, u32[]{:S(2)}) collective-permute-start(bf16[1440,128]{1,0:T(8,128)(2,1)S(1)} %get-tuple-element.39.refs_2_.refs_3_), channel_id=1, source_target_pairs={{0,16},{8,24},{16,0},{24,8},{1,17},{9,25},{17,1},{25,9},{2,18},{10... | collective-permute-start | bytes 1105928 | tf_op jit(solution)/shard_map/ppermute | solution.py:337
  20.1 19.2 %collective-permute-start.11 = (bf16[1440,128]{1,0:T(8,128)(2,1)S(1)}, bf16[1440,128]{1,0:T(8,128)(2,1)S(1)}, u32[]{:S(2)}, u32[]{:S(2)}) collective-permute-start(bf16[1440,128]{1,0:T(8,128)(2,1)S(1)} %get-tuple-element.40.refs_3_.refs_4_), channel_id=1, source_target_pairs={{0,24},{8,16},{16,8},{24,0},{1,25},{9,17},{17,9},{25,1},{2,26},{10... | collective-permute-start | bytes 1105928 | tf_op jit(solution)/shard_map/ppermute | solution.py:337
  25.2 1.2 %collective-permute-start.3 = (f32[16,16]{1,0:T(8,128)S(1)}, f32[16,16]{1,0:T(8,128)S(1)}, u32[]{:S(2)}, u32[]{:S(2)}) collective-permute-start(f32[16,16]{1,0:T(8,128)S(1)} %score_sums.1), channel_id=1, source_target_pairs={{0,1},{1,0},{2,3},{3,2},{4,5},{5,4},{6,7},{7,6},{8,9},{9,8},{10,11... | collective-permute-start | bytes 3080 | tf_op jit(solution)/shard_map/ppermute | solution.py:348
  26.4 3.7 %collective-permute-start.4 = (f32[16,16]{1,0:T(8,128)S(1)}, f32[16,16]{1,0:T(8,128)S(1)}, u32[]{:S(2)}, u32[]{:S(2)}) collective-permute-start(f32[16,16]{1,0:T(8,128)S(1)} %add.12), channel_id=1, source_target_pairs={{0,2},{1,3},{2,0},{3,1},{4,6},{5,7},{6,4},{7,5},{8,10},{9,11},{10,... | collective-permute-start | bytes 3080 | tf_op jit(solution)/shard_map/ppermute | solution.py:348
  30.0 4.5 %collective-permute-start.5 = (f32[16,16]{1,0:T(8,128)S(1)}, f32[16,16]{1,0:T(8,128)S(1)}, u32[]{:S(2)}, u32[]{:S(2)}) collective-permute-start(f32[16,16]{1,0:T(8,128)S(1)} %add.13.a_ref), channel_id=1, source_target_pairs={{0,4},{1,5},{2,6},{3,7},{4,0},{5,1},{6,2},{7,3},{8,12},{9,13},{10,... | collective-permute-start | bytes 3080 | tf_op jit(solution)/shard_map/ppermute | solution.py:417
  34.6 5.6 %collective-permute-start.9 = (f32[16,16]{1,0:T(8,128)S(1)}, f32[16,16]{1,0:T(8,128)S(1)}, u32[]{:S(2)}, u32[]{:S(2)}) collective-permute-start(f32[16,16]{1,0:T(8,128)S(1)} %join_sums.2.refs_8_.refs_0_), channel_id=1, source_target_pairs={{0,16},{8,24},{16,0},{24,8},{1,17},{9,25},{17,1},{25,9},{2,18},{10... | collective-permute-start | bytes 3080 | tf_op jit(solution)/shard_map/ppermute | solution.py:337
  36.5 3.7 %collective-permute-start.8 = (f32[16,16]{1,0:T(8,128)S(1)}, f32[16,16]{1,0:T(8,128)S(1)}, u32[]{:S(2)}, u32[]{:S(2)}) collective-permute-start(f32[16,16]{1,0:T(8,128)S(1)} %join_sums.2.refs_8_.refs_0_), channel_id=1, source_target_pairs={{0,8},{8,0},{16,24},{24,16},{1,9},{9,1},{17,25},{25,17},{2,10},{10... | collective-permute-start | bytes 3080 | tf_op jit(solution)/shard_map/ppermute | solution.py:337
  36.6 4.5 %collective-permute-start.7 = (f32[16,16]{1,0:T(8,128)S(1)}, f32[16,16]{1,0:T(8,128)S(1)}, u32[]{:S(2)}, u32[]{:S(2)}) collective-permute-start(f32[16,16]{1,0:T(8,128)S(1)} %join_sums.2.refs_8_.refs_0_), channel_id=1, source_target_pairs={{0,24},{8,16},{16,8},{24,0},{1,25},{9,17},{17,9},{25,1},{2,26},{10... | collective-permute-start | bytes 3080 | tf_op jit(solution)/shard_map/ppermute | solution.py:337
  42.6 12.9 %collective-permute-start.15 = (bf16[1440,128]{1,0:T(8,128)(2,1)S(1)}, bf16[1440,128]{1,0:T(8,128)(2,1)S(1)}, u32[]{:S(2)}, u32[]{:S(2)}) collective-permute-start(bf16[1440,128]{1,0:T(8,128)(2,1)S(1)} %get-tuple-element.46), channel_id=1, source_target_pairs={{0,8},{8,0},{16,24},{24,16},{1,9},{9,1},{17,25},{25,17},{2,10},{10... | collective-permute-start | bytes 1105928 | tf_op jit(solution)/shard_map/ppermute | solution.py:337
  44.6 15.5 %collective-permute-start.19 = (bf16[1440,128]{1,0:T(8,128)(2,1)S(1)}, bf16[1440,128]{1,0:T(8,128)(2,1)S(1)}, u32[]{:S(2)}, u32[]{:S(2)}) collective-permute-start(bf16[1440,128]{1,0:T(8,128)(2,1)S(1)} %get-tuple-element.47), channel_id=1, source_target_pairs={{0,16},{8,24},{16,0},{24,8},{1,17},{9,25},{17,1},{25,9},{2,18},{10... | collective-permute-start | bytes 1105928 | tf_op jit(solution)/shard_map/ppermute | solution.py:337
  44.7 15.5 %collective-permute-start.20 = (bf16[1440,128]{1,0:T(8,128)(2,1)S(1)}, bf16[1440,128]{1,0:T(8,128)(2,1)S(1)}, u32[]{:S(2)}, u32[]{:S(2)}) collective-permute-start(bf16[1440,128]{1,0:T(8,128)(2,1)S(1)} %get-tuple-element.48), channel_id=1, source_target_pairs={{0,24},{8,16},{16,8},{24,0},{1,25},{9,17},{17,9},{25,1},{2,26},{10... | collective-permute-start | bytes 1105928 | tf_op jit(solution)/shard_map/ppermute | solution.py:337
  46.1 1.2 %collective-permute-start.12 = (f32[16,16]{1,0:T(8,128)S(1)}, f32[16,16]{1,0:T(8,128)S(1)}, u32[]{:S(2)}, u32[]{:S(2)}) collective-permute-start(f32[16,16]{1,0:T(8,128)S(1)} %pair_sums.1.refs_8_), channel_id=1, source_target_pairs={{0,1},{1,0},{2,3},{3,2},{4,5},{5,4},{6,7},{7,6},{8,9},{9,8},{10,11... | collective-permute-start | bytes 3080 | tf_op jit(solution)/shard_map/ppermute | solution.py:348
  47.3 3.7 %collective-permute-start.13 = (f32[16,16]{1,0:T(8,128)S(1)}, f32[16,16]{1,0:T(8,128)S(1)}, u32[]{:S(2)}, u32[]{:S(2)}) collective-permute-start(f32[16,16]{1,0:T(8,128)S(1)} %add.14), channel_id=1, source_target_pairs={{0,2},{1,3},{2,0},{3,1},{4,6},{5,7},{6,4},{7,5},{8,10},{9,11},{10,... | collective-permute-start | bytes 3080 | tf_op jit(solution)/shard_map/ppermute | solution.py:348
  51.0 4.5 %collective-permute-start.14 = (f32[16,16]{1,0:T(8,128)S(1)}, f32[16,16]{1,0:T(8,128)S(1)}, u32[]{:S(2)}, u32[]{:S(2)}) collective-permute-start(f32[16,16]{1,0:T(8,128)S(1)} %add.15.a_ref), channel_id=1, source_target_pairs={{0,4},{1,5},{2,6},{3,7},{4,0},{5,1},{6,2},{7,3},{8,12},{9,13},{10,... | collective-permute-start | bytes 3080 | tf_op jit(solution)/shard_map/ppermute | solution.py:417
  55.5 4.7 %collective-permute-start.18 = (f32[16,16]{1,0:T(8,128)S(1)}, f32[16,16]{1,0:T(8,128)S(1)}, u32[]{:S(2)}, u32[]{:S(2)}) collective-permute-start(f32[16,16]{1,0:T(8,128)S(1)} %join_sums.3.refs_9_.refs_10_), channel_id=1, source_target_pairs={{0,16},{8,24},{16,0},{24,8},{1,17},{9,25},{17,1},{25,9},{2,18},{10... | collective-permute-start | bytes 3080 | tf_op jit(solution)/shard_map/ppermute | solution.py:337
  57.0 3.7 %collective-permute-start.17 = (f32[16,16]{1,0:T(8,128)S(1)}, f32[16,16]{1,0:T(8,128)S(1)}, u32[]{:S(2)}, u32[]{:S(2)}) collective-permute-start(f32[16,16]{1,0:T(8,128)S(1)} %join_sums.3.refs_9_.refs_10_), channel_id=1, source_target_pairs={{0,8},{8,0},{16,24},{24,16},{1,9},{9,1},{17,25},{25,17},{2,10},{10... | collective-permute-start | bytes 3080 | tf_op jit(solution)/shard_map/ppermute | solution.py:337
  57.6 4.5 %collective-permute-start.16 = (f32[16,16]{1,0:T(8,128)S(1)}, f32[16,16]{1,0:T(8,128)S(1)}, u32[]{:S(2)}, u32[]{:S(2)}) collective-permute-start(f32[16,16]{1,0:T(8,128)S(1)} %join_sums.3.refs_9_.refs_10_), channel_id=1, source_target_pairs={{0,24},{8,16},{16,8},{24,0},{1,25},{9,17},{17,9},{25,1},{2,26},{10... | collective-permute-start | bytes 3080 | tf_op jit(solution)/shard_map/ppermute | solution.py:337
  63.0 7.8 %collective-permute-start.21 = (bf16[768,128]{1,0:T(8,128)(2,1)S(1)}, bf16[768,128]{1,0:T(8,128)(2,1)S(1)}, u32[]{:S(2)}, u32[]{:S(2)}) collective-permute-start(bf16[768,128]{1,0:T(8,128)(2,1)S(1)} %get-tuple-element.49), channel_id=1, source_target_pairs={{0,8},{8,0},{16,24},{24,16},{1,9},{9,1},{17,25},{25,17},{2,10},{10... | collective-permute-start | bytes 589832 | tf_op jit(solution)/shard_map/ppermute | solution.py:337
  64.6 12.0 %collective-permute-start.22 = (bf16[768,128]{1,0:T(8,128)(2,1)S(1)}, bf16[768,128]{1,0:T(8,128)(2,1)S(1)}, u32[]{:S(2)}, u32[]{:S(2)}) collective-permute-start(bf16[768,128]{1,0:T(8,128)(2,1)S(1)} %get-tuple-element.52), channel_id=1, source_target_pairs={{0,16},{8,24},{16,0},{24,8},{1,17},{9,25},{17,1},{25,9},{2,18},{10... | collective-permute-start | bytes 589832 | tf_op jit(solution)/shard_map/ppermute | solution.py:337
  65.1 11.5 %collective-permute-start.23 = (bf16[768,128]{1,0:T(8,128)(2,1)S(1)}, bf16[768,128]{1,0:T(8,128)(2,1)S(1)}, u32[]{:S(2)}, u32[]{:S(2)}) collective-permute-start(bf16[768,128]{1,0:T(8,128)(2,1)S(1)} %get-tuple-element.53), channel_id=1, source_target_pairs={{0,24},{8,16},{16,8},{24,0},{1,25},{9,17},{17,9},{25,1},{2,26},{10... | collective-permute-start | bytes 589832 | tf_op jit(solution)/shard_map/ppermute | solution.py:337
  68.0 10.7 %collective-permute-start.24 = (bf16[672,128]{1,0:T(8,128)(2,1)S(1)}, bf16[672,128]{1,0:T(8,128)(2,1)S(1)}, u32[]{:S(2)}, u32[]{:S(2)}) collective-permute-start(bf16[672,128]{1,0:T(8,128)(2,1)S(1)} %get-tuple-element.57), channel_id=1, source_target_pairs={{0,8},{8,0},{16,24},{24,16},{1,9},{9,1},{17,25},{25,17},{2,10},{10... | collective-permute-start | bytes 516104 | tf_op jit(solution)/shard_map/ppermute | solution.py:337
  69.5 10.8 %collective-permute-start.25 = (bf16[672,128]{1,0:T(8,128)(2,1)S(1)}, bf16[672,128]{1,0:T(8,128)(2,1)S(1)}, u32[]{:S(2)}, u32[]{:S(2)}) collective-permute-start(bf16[672,128]{1,0:T(8,128)(2,1)S(1)} %get-tuple-element.58), channel_id=1, source_target_pairs={{0,16},{8,24},{16,0},{24,8},{1,17},{9,25},{17,1},{25,9},{2,18},{10... | collective-permute-start | bytes 516104 | tf_op jit(solution)/shard_map/ppermute | solution.py:337
  70.9 9.5 %collective-permute-start.26 = (bf16[672,128]{1,0:T(8,128)(2,1)S(1)}, bf16[672,128]{1,0:T(8,128)(2,1)S(1)}, u32[]{:S(2)}, u32[]{:S(2)}) collective-permute-start(bf16[672,128]{1,0:T(8,128)(2,1)S(1)} %get-tuple-element.59), channel_id=1, source_target_pairs={{0,24},{8,16},{16,8},{24,0},{1,25},{9,17},{17,9},{25,1},{2,26},{10... | collective-permute-start | bytes 516104 | tf_op jit(solution)/shard_map/ppermute | solution.py:337
  (1 other events, 0.7 us)

commit v7 on v6

--- a/solution.py
+++ b/solution.py
@@ -95,20 +95,50 @@
     return (member == col).astype(jnp.float32)
 
 
-def split_kernel(me_of, count, main, half, length, x_ref, *rest):
-    outs = rest[-count:]
+def split_kernel(me_of, steps, count, main, half, length, x_ref, *rest):
+    outs = rest[-len(steps):]
     me = me_of()
     per = x_ref.shape[0]
-    for s in range(count):
+    for out, s in zip(outs, steps):
         owner = partner(me, s)
         start = chunk_start(owner, main * LANES, length)
         for tile in range(main):
             place = pl.multiple_of(start + tile * LANES, LANES)
-            outs[s][tile * per:(tile + 1) * per, :] = x_ref[:, pl.ds(place, LANES)]
+            out[tile * per:(tile + 1) * per, :] = x_ref[:, pl.ds(place, LANES)]
         if half:
             place = pl.multiple_of((main * count + owner // 2) * LANES, LANES)
             shared = x_ref[:, pl.ds(place, LANES)].astype(jnp.float32)
-            outs[s][main * per:, :] = pack(shared, owner % 2).astype(jnp.bfloat16)
+            out[main * per:, :] = pack(shared, owner % 2).astype(jnp.bfloat16)
+
+
+def direct_split_kernel(me_of, steps, count, main, half, length, x_ref, *rest):
+    outs, (held, shared, sem) = rest[:len(steps)], rest[len(steps):]
+    me = me_of()
+    per = x_ref.shape[0]
+    copies = []
+    for at, s in enumerate(steps):
+        owner = partner(me, s)
+        start = chunk_start(owner, main * LANES, length)
+        copies.append(pltpu.make_async_copy(
+            x_ref.at[:, pl.ds(start, main * LANES)], held.at[at], sem.at[2 * at]
+        ))
+        if half:
+            place = pl.multiple_of((main * count + owner // 2) * LANES, LANES)
+            copies.append(pltpu.make_async_copy(
+                x_ref.at[:, pl.ds(place, LANES)], shared.at[at], sem.at[2 * at + 1]
+            ))
+    for copy in copies:
+        copy.start()
+    for copy in copies:
+        copy.wait()
+    for at, s in enumerate(steps):
+        for tile in range(main):
+            outs[at][tile * per:(tile + 1) * per, :] = held[
+                at, :, tile * LANES:(tile + 1) * LANES
+            ]
+        if half:
+            tile = shared[at].astype(jnp.float32)
+            outs[at][main * per:, :] = pack(tile, partner(me, s) % 2).astype(jnp.bfloat16)
 
 
 def tiled(small, rows, channels):
@@ -387,17 +417,38 @@
 
     first = min(1, count - 1)
 
-    def split(operands, name):
+    def split(operands, steps, name):
         return pl.pallas_call(
-            functools.partial(split_kernel, me_of, count, main, half, length),
-            out_shape=[part] * count,
+            functools.partial(split_kernel, me_of, steps, count, main, half, length),
+            out_shape=[part] * len(steps),
             in_specs=[whole] + [anywhere] * (len(operands) - 1),
-            out_specs=[whole] * count,
+            out_specs=[whole] * len(steps),
             compiler_params=params,
             name=name,
         )(*operands)
 
-    e_mine = split([fields], "split_fields")
+    steps = list(range(count))
+    ends = sorted({0, count - 1})
+    middle = steps[1:-1]
+    near = []
+    if middle:
+        near = list(pl.pallas_call(
+            functools.partial(
+                direct_split_kernel, me_of, middle, count, main, half, length
+            ),
+            out_shape=[part] * len(middle),
+            in_specs=[in_hbm],
+            out_specs=[whole] * len(middle),
+            scratch_shapes=[
+                pltpu.VMEM((len(middle), per, main * LANES), bf),
+                pltpu.VMEM((len(middle), per, LANES), bf),
+                pltpu.SemaphoreType.DMA((2 * len(middle),)),
+            ],
+            compiler_params=params,
+            name="split_fields_near",
+        )(pltpu.with_memory_space_constraint(fields, pltpu.HBM)))
+    far = list(split([fields] + near[:1], ends, "split_fields_far"))
+    e_mine = far[:1] + near + far[1:]
     e_cells = exchange(e_mine)
     qk, qkt, ov, ovt = pl.pallas_call(
         functools.partial(tiles_kernel, rows, channels),
@@ -408,7 +459,7 @@
         cost_estimate=cost(10**8, 4 * 4 * rows * rows),
         name="weight_tiles",
     )(w_query, w_key, w_value, w_out)
-    c_mine = split([grads, e_cells[first], qk], "split_grads")
+    c_mine = split([grads, e_cells[first], qk], steps, "split_grads")
     c_cells = exchange(c_mine)
     space_steps = doubling(lax.axis_size("space"))
 
@@ -527,7 +578,6 @@
             name=name,
         )(*waited, *base, *extra)
 
-    steps = list(range(count))
     first_part = [(s, 0, mid, s, 0) for s in steps]
     updated = finish(
         e_mine, branch_home, [first_part, [(s, mid, main, s, 0) for s in steps]],

time: 81.7 us -> 81.5 us (level)
  local copies, waits for them, and re-layouts: 5.48 us -> 3.43 us
  Pallas kernels: 14 us -> 15.3 us
    unnamed x12, local copies, waits for them, and re-layouts: 5.48 us -> 3.43 us
    pallas_call x2 -> x3, Pallas kernels: 0.61 us -> 1.93 us  [the longest x1 1.47 us: shards(): pl.pallas_call(functools.partial(direct_split_kernel, me_of, middle, coun...]
where the time goes in v7:
time: 81.5 us; the launch traced here: 81.2 us
  starting transfers between devices  34.2 us (42%)
  waiting for transfers between devices  27.5 us (34%)
  Pallas kernels  15.3 us (19%)
  local copies, waits for them, and re-layouts  3.43 us (4%)
    ppermute x21, starting transfers between devices, swap(): return lax.ppermute(value, 'mem', [(i, i ^ step) for i in range(count)])  25.9 us
    ppermute x21, waiting for transfers between devices, swap(): return lax.ppermute(value, 'mem', [(i, i ^ step) for i in range(count)])  17.1 us
    ppermute x4, waiting for transfers between devices, sum_steps(): lax.ppermute(value, name, [(i, i ^ step) for i in range(size)])  6.52 us
    pallas_call x3, Pallas kernels, finish(): pl.pallas_call(functools.partial(finish_kernel, me_of, count, main, per,...  5.38 us
    ppermute x2, starting transfers between devices, join(): other = lax.ppermute(value, name, [(i, i ^ step) for i in range(size)])  5.16 us
    ppermute x2, waiting for transfers between devices, join(): other = lax.ppermute(value, name, [(i, i ^ step) for i in range(size)])  3.93 us
    unnamed x12, local copies, waits for them, and re-layouts  3.43 us
    ppermute x4, starting transfers between devices, sum_steps(): lax.ppermute(value, name, [(i, i ^ step) for i in range(size)])  3.15 us
  transfers between devices with their start and end apart: 27, of which 18 were waited for; matrix products, arithmetic and copies ran while one was open for 0% of the time, Pallas kernels for 13%

profile of v7, /device:TPU:0, one launch (start us, length us, event | category | flops | bytes accessed | tf_op | source)
XLA Modules:
  0.0 81.2 jit_solution(12060152878259201617)
XLA Ops:
  0.6 1.5 %split_fields_near.1 = (bf16[1440,128]{1,0:T(8,128)(2,1)S(1)}, bf16[1440,128]{1,0:T(8,128)(2,1)S(1)}) custom-call(bf16[64,11520]{1,0:T(8,128)(2,1)} %bitcast.4), custom_call_target="tpu_custom_call" | custom-call | tf_op jit(solution)/shard_map/split_fields_near/pallas_call | solution.py:435
  2.1 3.0 %collective-permute-start = (bf16[1440,128]{1,0:T(8,128)(2,1)S(1)}, bf16[1440,128]{1,0:T(8,128)(2,1)S(1)}, u32[]{:S(2)}, u32[]{:S(2)}) collective-permute-start(bf16[1440,128]{1,0:T(8,128)(2,1)S(1)} %get-tuple-element.33.rest_0_.refs_2_), channel_id=1, source_target_pairs={{0,8},{8,0},{16,24},{24,16},{1,9},{9,1},{17,25},{25,17},{2,10},{10... | collective-permute-start | bytes 1105928 | tf_op jit(solution)/shard_map/ppermute | solution.py:367
  5.1 1.5 %collective-permute-start.1 = (bf16[1440,128]{1,0:T(8,128)(2,1)S(1)}, bf16[1440,128]{1,0:T(8,128)(2,1)S(1)}, u32[]{:S(2)}, u32[]{:S(2)}) collective-permute-start(bf16[1440,128]{1,0:T(8,128)(2,1)S(1)} %get-tuple-element.35.refs_3_), channel_id=1, source_target_pairs={{0,16},{8,24},{16,0},{24,8},{1,17},{9,25},{17,1},{25,9},{2,18},{10... | collective-permute-start | bytes 1105928 | tf_op jit(solution)/shard_map/ppermute | solution.py:367
  11.7 2.9 %collective-permute-done.refs_1_.rest_0_.refs_5_.refs_2_.refs_3_ = bf16[1440,128]{1,0:T(8,128)(2,1)S(1)} collective-permute-done((bf16[1440,128]{1,0:T(8,128)(2,1)S(1)}, bf16[1440,128]{1,0:T(8,128)(2,1)S(1)}, u32[]{:S(2)}, u32[]{:S(2)}) %collective-permute-start) | collective-permute-done | bytes 368672 | tf_op jit(solution)/shard_map/ppermute | solution.py:367
  14.9 2.1 %collective-permute-start.6 = (bf16[1440,128]{1,0:T(8,128)(2,1)S(1)}, bf16[1440,128]{1,0:T(8,128)(2,1)S(1)}, u32[]{:S(2)}, u32[]{:S(2)}) collective-permute-start(bf16[1440,128]{1,0:T(8,128)(2,1)S(1)} %get-tuple-element.37.refs_1_.refs_2_), channel_id=1, source_target_pairs={{0,8},{8,0},{16,24},{24,16},{1,9},{9,1},{17,25},{25,17},{2,10},{10... | collective-permute-start | bytes 1105928 | tf_op jit(solution)/shard_map/ppermute | solution.py:367
  17.0 1.5 %collective-permute-start.10 = (bf16[1440,128]{1,0:T(8,128)(2,1)S(1)}, bf16[1440,128]{1,0:T(8,128)(2,1)S(1)}, u32[]{:S(2)}, u32[]{:S(2)}) collective-permute-start(bf16[1440,128]{1,0:T(8,128)(2,1)S(1)} %get-tuple-element.39.refs_2_.refs_3_), channel_id=1, source_target_pairs={{0,16},{8,24},{16,0},{24,8},{1,17},{9,25},{17,1},{25,9},{2,18},{10... | collective-permute-start | bytes 1105928 | tf_op jit(solution)/shard_map/ppermute | solution.py:367
  18.5 4.9 %collective-permute-done.1.refs_2_.refs_6_.refs_3_.refs_4_ = bf16[1440,128]{1,0:T(8,128)(2,1)S(1)} collective-permute-done((bf16[1440,128]{1,0:T(8,128)(2,1)S(1)}, bf16[1440,128]{1,0:T(8,128)(2,1)S(1)}, u32[]{:S(2)}, u32[]{:S(2)}) %collective-permute-start.1) | collective-permute-done | bytes 368672 | tf_op jit(solution)/shard_map/ppermute | solution.py:367
  26.2 1.6 %collective-permute-start.4 = (f32[16,16]{1,0:T(8,128)S(1)}, f32[16,16]{1,0:T(8,128)S(1)}, u32[]{:S(2)}, u32[]{:S(2)}) collective-permute-start(f32[16,16]{1,0:T(8,128)S(1)} %add.12), channel_id=1, source_target_pairs={{0,2},{1,3},{2,0},{3,1},{4,6},{5,7},{6,4},{7,5},{8,10},{9,11},{10,... | collective-permute-start | bytes 3080 | tf_op jit(solution)/shard_map/ppermute | solution.py:378
  27.8 2.1 %collective-permute-done.4 = f32[16,16]{1,0:T(8,128)S(1)} collective-permute-done((f32[16,16]{1,0:T(8,128)S(1)}, f32[16,16]{1,0:T(8,128)S(1)}, u32[]{:S(2)}, u32[]{:S(2)}) %collective-permute-start.4) | collective-permute-done | bytes 1056 | tf_op jit(solution)/shard_map/ppermute | solution.py:378
  29.9 2.6 %collective-permute-start.5 = (f32[16,16]{1,0:T(8,128)S(1)}, f32[16,16]{1,0:T(8,128)S(1)}, u32[]{:S(2)}, u32[]{:S(2)}) collective-permute-start(f32[16,16]{1,0:T(8,128)S(1)} %add.13.a_ref), channel_id=1, source_target_pairs={{0,4},{1,5},{2,6},{3,7},{4,0},{5,1},{6,2},{7,3},{8,12},{9,13},{10,... | collective-permute-start | bytes 3080 | tf_op jit(solution)/shard_map/ppermute | solution.py:468
  32.4 2.0 %collective-permute-done.5.b_ref = f32[16,16]{1,0:T(8,128)S(1)} collective-permute-done((f32[16,16]{1,0:T(8,128)S(1)}, f32[16,16]{1,0:T(8,128)S(1)}, u32[]{:S(2)}, u32[]{:S(2)}) %collective-permute-start.5) | collective-permute-done | bytes 1056 | tf_op jit(solution)/shard_map/ppermute | solution.py:468
  34.4 1.9 %collective-permute-start.9 = (f32[16,16]{1,0:T(8,128)S(1)}, f32[16,16]{1,0:T(8,128)S(1)}, u32[]{:S(2)}, u32[]{:S(2)}) collective-permute-start(f32[16,16]{1,0:T(8,128)S(1)} %join_sums.2.refs_8_.refs_0_), channel_id=1, source_target_pairs={{0,16},{8,24},{16,0},{24,8},{1,17},{9,25},{17,1},{25,9},{2,18},{10... | collective-permute-start | bytes 3080 | tf_op jit(solution)/shard_map/ppermute | solution.py:367
  36.4 1.5 %collective-permute-start.7 = (f32[16,16]{1,0:T(8,128)S(1)}, f32[16,16]{1,0:T(8,128)S(1)}, u32[]{:S(2)}, u32[]{:S(2)}) collective-permute-start(f32[16,16]{1,0:T(8,128)S(1)} %join_sums.2.refs_8_.refs_0_), channel_id=1, source_target_pairs={{0,24},{8,16},{16,8},{24,0},{1,25},{9,17},{17,9},{25,1},{2,26},{10... | collective-permute-start | bytes 3080 | tf_op jit(solution)/shard_map/ppermute | solution.py:367
  41.0 1.4 %branch.1 = (f32[16,16]{1,0:T(8,128)S(1)}, bf16[1440,128]{1,0:T(8,128)(2,1)S(1)}, bf16[1440,128]{1,0:T(8,128)(2,1)S(1)}, bf16[1440,128]{1,0:T(8,128)(2,1)S(1)}, bf16[1440,128]{1,0:T(8,128)(2,1)S(1)}) custom-call(f32[256,256]{1,0:T(8,128)S(1)} %get-tuple-element.31.tile_ref.ov_ref, f32[16,16]{1,0:T(8,128)S(1)} %join_sums.2.refs_8_.refs_0_, ...), custom_call_target="tpu_custom_call" | custom-call | flops 754974720 | bytes 2949120 | tf_op jit(solution)/shard_map/branch/pallas_call | solution.py:507
  42.4 2.0 %collective-permute-start.15 = (bf16[1440,128]{1,0:T(8,128)(2,1)S(1)}, bf16[1440,128]{1,0:T(8,128)(2,1)S(1)}, u32[]{:S(2)}, u32[]{:S(2)}) collective-permute-start(bf16[1440,128]{1,0:T(8,128)(2,1)S(1)} %get-tuple-element.46), channel_id=1, source_target_pairs={{0,8},{8,0},{16,24},{24,16},{1,9},{9,1},{17,25},{25,17},{2,10},{10... | collective-permute-start | bytes 1105928 | tf_op jit(solution)/shard_map/ppermute | solution.py:367
  44.5 1.4 %collective-permute-start.20 = (bf16[1440,128]{1,0:T(8,128)(2,1)S(1)}, bf16[1440,128]{1,0:T(8,128)(2,1)S(1)}, u32[]{:S(2)}, u32[]{:S(2)}) collective-permute-start(bf16[1440,128]{1,0:T(8,128)(2,1)S(1)} %get-tuple-element.48), channel_id=1, source_target_pairs={{0,24},{8,16},{16,8},{24,0},{1,25},{9,17},{17,9},{25,1},{2,26},{10... | collective-permute-start | bytes 1105928 | tf_op jit(solution)/shard_map/ppermute | solution.py:367
  47.1 1.6 %collective-permute-start.13 = (f32[16,16]{1,0:T(8,128)S(1)}, f32[16,16]{1,0:T(8,128)S(1)}, u32[]{:S(2)}, u32[]{:S(2)}) collective-permute-start(f32[16,16]{1,0:T(8,128)S(1)} %add.14), channel_id=1, source_target_pairs={{0,2},{1,3},{2,0},{3,1},{4,6},{5,7},{6,4},{7,5},{8,10},{9,11},{10,... | collective-permute-start | bytes 3080 | tf_op jit(solution)/shard_map/ppermute | solution.py:378
  48.7 2.1 %collective-permute-done.13 = f32[16,16]{1,0:T(8,128)S(1)} collective-permute-done((f32[16,16]{1,0:T(8,128)S(1)}, f32[16,16]{1,0:T(8,128)S(1)}, u32[]{:S(2)}, u32[]{:S(2)}) %collective-permute-start.13) | collective-permute-done | bytes 1056 | tf_op jit(solution)/shard_map/ppermute | solution.py:378
  50.8 2.6 %collective-permute-start.14 = (f32[16,16]{1,0:T(8,128)S(1)}, f32[16,16]{1,0:T(8,128)S(1)}, u32[]{:S(2)}, u32[]{:S(2)}) collective-permute-start(f32[16,16]{1,0:T(8,128)S(1)} %add.15.a_ref), channel_id=1, source_target_pairs={{0,4},{1,5},{2,6},{3,7},{4,0},{5,1},{6,2},{7,3},{8,12},{9,13},{10,... | collective-permute-start | bytes 3080 | tf_op jit(solution)/shard_map/ppermute | solution.py:468
  53.4 2.0 %collective-permute-done.14.b_ref = f32[16,16]{1,0:T(8,128)S(1)} collective-permute-done((f32[16,16]{1,0:T(8,128)S(1)}, f32[16,16]{1,0:T(8,128)S(1)}, u32[]{:S(2)}, u32[]{:S(2)}) %collective-permute-start.14) | collective-permute-done | bytes 1056 | tf_op jit(solution)/shard_map/ppermute | solution.py:468
  55.3 1.5 %collective-permute-start.18 = (f32[16,16]{1,0:T(8,128)S(1)}, f32[16,16]{1,0:T(8,128)S(1)}, u32[]{:S(2)}, u32[]{:S(2)}) collective-permute-start(f32[16,16]{1,0:T(8,128)S(1)} %join_sums.3.refs_9_.refs_10_), channel_id=1, source_target_pairs={{0,16},{8,24},{16,0},{24,8},{1,17},{9,25},{17,1},{25,9},{2,18},{10... | collective-permute-start | bytes 3080 | tf_op jit(solution)/shard_map/ppermute | solution.py:367
  57.4 1.4 %collective-permute-start.16 = (f32[16,16]{1,0:T(8,128)S(1)}, f32[16,16]{1,0:T(8,128)S(1)}, u32[]{:S(2)}, u32[]{:S(2)}) collective-permute-start(f32[16,16]{1,0:T(8,128)S(1)} %join_sums.3.refs_9_.refs_10_), channel_id=1, source_target_pairs={{0,24},{8,16},{16,8},{24,0},{1,25},{9,17},{17,9},{25,1},{2,26},{10... | collective-permute-start | bytes 3080 | tf_op jit(solution)/shard_map/ppermute | solution.py:367
  60.5 1.4 %collective-permute-done.16.refs_10_.refs_11_ = f32[16,16]{1,0:T(8,128)S(1)} collective-permute-done((f32[16,16]{1,0:T(8,128)S(1)}, f32[16,16]{1,0:T(8,128)S(1)}, u32[]{:S(2)}, u32[]{:S(2)}) %collective-permute-start.16) | collective-permute-done | bytes 1056 | tf_op jit(solution)/shard_map/ppermute | solution.py:367
  62.9 1.6 %collective-permute-start.21 = (bf16[768,128]{1,0:T(8,128)(2,1)S(1)}, bf16[768,128]{1,0:T(8,128)(2,1)S(1)}, u32[]{:S(2)}, u32[]{:S(2)}) collective-permute-start(bf16[768,128]{1,0:T(8,128)(2,1)S(1)} %get-tuple-element.49), channel_id=1, source_target_pairs={{0,8},{8,0},{16,24},{24,16},{1,9},{9,1},{17,25},{25,17},{2,10},{10... | collective-permute-start | bytes 589832 | tf_op jit(solution)/shard_map/ppermute | solution.py:367
  64.9 1.5 %collective-permute-start.23 = (bf16[768,128]{1,0:T(8,128)(2,1)S(1)}, bf16[768,128]{1,0:T(8,128)(2,1)S(1)}, u32[]{:S(2)}, u32[]{:S(2)}) collective-permute-start(bf16[768,128]{1,0:T(8,128)(2,1)S(1)} %get-tuple-element.53), channel_id=1, source_target_pairs={{0,24},{8,16},{16,8},{24,0},{1,25},{9,17},{17,9},{25,1},{2,26},{10... | collective-permute-start | bytes 589832 | tf_op jit(solution)/shard_map/ppermute | solution.py:367
  66.4 1.4 %input_gradient_b.1 = (bf16[672,128]{1,0:T(8,128)(2,1)S(1)}, bf16[672,128]{1,0:T(8,128)(2,1)S(1)}, bf16[672,128]{1,0:T(8,128)(2,1)S(1)}, bf16[672,128]{1,0:T(8,128)(2,1)S(1)}) custom-call(f32[16,16]{1,0:T(8,128)S(1)} %get-tuple-element.43.w_ref, f32[256,256]{1,0:T(8,128)S(1)} %get-tuple-element.32.tile_ref.rest_1_.qk_ref, ...), custom_call_target="tpu_custom_call" | custom-call | flops 671088640 | bytes 1966080 | tf_op jit(solution)/shard_map/input_gradient_b/pallas_call | solution.py:542
  67.8 1.5 %collective-permute-start.24 = (bf16[672,128]{1,0:T(8,128)(2,1)S(1)}, bf16[672,128]{1,0:T(8,128)(2,1)S(1)}, u32[]{:S(2)}, u32[]{:S(2)}) collective-permute-start(bf16[672,128]{1,0:T(8,128)(2,1)S(1)} %get-tuple-element.57), channel_id=1, source_target_pairs={{0,8},{8,0},{16,24},{24,16},{1,9},{9,1},{17,25},{25,17},{2,10},{10... | collective-permute-start | bytes 516104 | tf_op jit(solution)/shard_map/ppermute | solution.py:367
  70.7 1.4 %collective-permute-start.26 = (bf16[672,128]{1,0:T(8,128)(2,1)S(1)}, bf16[672,128]{1,0:T(8,128)(2,1)S(1)}, u32[]{:S(2)}, u32[]{:S(2)}) collective-permute-start(bf16[672,128]{1,0:T(8,128)(2,1)S(1)} %get-tuple-element.59), channel_id=1, source_target_pairs={{0,24},{8,16},{16,8},{24,0},{1,25},{9,17},{17,9},{25,1},{2,26},{10... | collective-permute-start | bytes 516104 | tf_op jit(solution)/shard_map/ppermute | solution.py:367
  72.1 2.4 %updated.1 = f32[64,11520]{1,0:T(8,128)} custom-call(bf16[768,128]{1,0:T(8,128)(2,1)S(1)} %collective-permute-done.21.refs_0_.refs_5_, bf16[1440,128]{1,0:T(8,128)(2,1)S(1)} %get-tuple-element.34.refs_0_.refs_4_.refs_1_.refs_2_, bf16[1440,128]{1,0:T(8,128)(2,1)S(1)} %get-tuple-element.33.rest_0_.refs_2_, bf16[1440,128]{1,0:T(8,128)(2,1)S(1)} %get-tuple-element.35.refs_3_, ...), custom_call_target="tpu_custom_call" | custom-call | flops 737280 | bytes 5898240 | tf_op jit(solution)/shard_map/updated/pallas_call | solution.py:563
  74.5 2.0 %collective-permute-done.22.refs_6_ = bf16[768,128]{1,0:T(8,128)(2,1)S(1)} collective-permute-done((bf16[768,128]{1,0:T(8,128)(2,1)S(1)}, bf16[768,128]{1,0:T(8,128)(2,1)S(1)}, u32[]{:S(2)}, u32[]{:S(2)}) %collective-permute-start.22) | collective-permute-done | bytes 196640 | tf_op jit(solution)/shard_map/ppermute | solution.py:367
  76.5 2.0 %ensemble_grad_early.1.refs_0_ = f32[64,11520]{1,0:T(8,128)} custom-call(bf16[1440,128]{1,0:T(8,128)(2,1)S(1)} %get-tuple-element.38.refs_4_.refs_0_.refs_5_.refs_6_.refs_1_, bf16[1440,128]{1,0:T(8,128)(2,1)S(1)} %get-tuple-element.37.refs_1_.refs_2_, bf16[1440,128]{1,0:T(8,128)(2,1)S(1)} %get-tuple-element.39.refs_2_.refs_3_, ...), custom_call_target="tpu_custom_call" | custom-call | flops 737280 | bytes 5898240 | tf_op jit(solution)/shard_map/ensemble_grad_early/pallas_call | solution.py:563
  78.5 1.7 %collective-permute-done.25.refs_7_ = bf16[672,128]{1,0:T(8,128)(2,1)S(1)} collective-permute-done((bf16[672,128]{1,0:T(8,128)(2,1)S(1)}, bf16[672,128]{1,0:T(8,128)(2,1)S(1)}, u32[]{:S(2)}, u32[]{:S(2)}) %collective-permute-start.25) | collective-permute-done | bytes 172064 | tf_op jit(solution)/shard_map/ppermute | solution.py:367
  (53 shorter events, 18.5 us)
Async XLA Ops:
  0.6 7.6 %copy-start.2 = (bf16[16,16]{1,0:T(8,128)(2,1)S(1)}, bf16[16,16]{1,0:T(8,128)(2,1)}, u32[]{:S(2)}) copy-start(bf16[16,16]{1,0:T(8,128)(2,1)} %wq_ref.1) | copy-start | bytes 1540
  0.6 13.9 %copy-start.1 = (bf16[4,16,11520]{2,1,0:T(8,128)(2,1)S(1)}, bf16[4,16,11520]{2,1,0:T(8,128)(2,1)}, u32[]{:S(2)}) copy-start(bf16[4,16,11520]{2,1,0:T(8,128)(2,1)} %param.7) | copy-start | bytes 4423684
  2.1 12.4 %collective-permute-start = (bf16[1440,128]{1,0:T(8,128)(2,1)S(1)}, bf16[1440,128]{1,0:T(8,128)(2,1)S(1)}, u32[]{:S(2)}, u32[]{:S(2)}) collective-permute-start(bf16[1440,128]{1,0:T(8,128)(2,1)S(1)} %get-tuple-element.33.rest_0_.refs_2_), channel_id=1, source_target_pairs={{0,8},{8,0},{16,24},{24,16},{1,9},{9,1},{17,25},{25,17},{2,10},{10... | collective-permute-start | bytes 1105928 | tf_op jit(solution)/shard_map/ppermute | solution.py:367
  5.1 18.3 %collective-permute-start.1 = (bf16[1440,128]{1,0:T(8,128)(2,1)S(1)}, bf16[1440,128]{1,0:T(8,128)(2,1)S(1)}, u32[]{:S(2)}, u32[]{:S(2)}) collective-permute-start(bf16[1440,128]{1,0:T(8,128)(2,1)S(1)} %get-tuple-element.35.refs_3_), channel_id=1, source_target_pairs={{0,16},{8,24},{16,0},{24,8},{1,17},{9,25},{17,1},{25,9},{2,18},{10... | collective-permute-start | bytes 1105928 | tf_op jit(solution)/shard_map/ppermute | solution.py:367
  6.7 1.4 %copy-start = (bf16[4,16,11520]{2,1,0:T(8,128)(2,1)S(1)}, bf16[4,16,11520]{2,1,0:T(8,128)(2,1)}, u32[]{:S(2)}) copy-start(bf16[4,16,11520]{2,1,0:T(8,128)(2,1)} %param.6) | copy-start | bytes 4423684
  8.2 15.8 %collective-permute-start.2 = (bf16[1440,128]{1,0:T(8,128)(2,1)S(1)}, bf16[1440,128]{1,0:T(8,128)(2,1)S(1)}, u32[]{:S(2)}, u32[]{:S(2)}) collective-permute-start(bf16[1440,128]{1,0:T(8,128)(2,1)S(1)} %get-tuple-element.36.refs_4_), channel_id=1, source_target_pairs={{0,24},{8,16},{16,8},{24,0},{1,25},{9,17},{17,9},{25,1},{2,26},{10... | collective-permute-start | bytes 1105928 | tf_op jit(solution)/shard_map/ppermute | solution.py:367
  8.3 0.7 copy-start.3
  9.0 0.7 copy-start.4
  14.9 19.5 %collective-permute-start.6 = (bf16[1440,128]{1,0:T(8,128)(2,1)S(1)}, bf16[1440,128]{1,0:T(8,128)(2,1)S(1)}, u32[]{:S(2)}, u32[]{:S(2)}) collective-permute-start(bf16[1440,128]{1,0:T(8,128)(2,1)S(1)} %get-tuple-element.37.refs_1_.refs_2_), channel_id=1, source_target_pairs={{0,8},{8,0},{16,24},{24,16},{1,9},{9,1},{17,25},{25,17},{2,10},{10... | collective-permute-start | bytes 1105928 | tf_op jit(solution)/shard_map/ppermute | solution.py:367
  17.0 22.1 %collective-permute-start.10 = (bf16[1440,128]{1,0:T(8,128)(2,1)S(1)}, bf16[1440,128]{1,0:T(8,128)(2,1)S(1)}, u32[]{:S(2)}, u32[]{:S(2)}) collective-permute-start(bf16[1440,128]{1,0:T(8,128)(2,1)S(1)} %get-tuple-element.39.refs_2_.refs_3_), channel_id=1, source_target_pairs={{0,16},{8,24},{16,0},{24,8},{1,17},{9,25},{17,1},{25,9},{2,18},{10... | collective-permute-start | bytes 1105928 | tf_op jit(solution)/shard_map/ppermute | solution.py:367
  18.5 20.5 %collective-permute-start.11 = (bf16[1440,128]{1,0:T(8,128)(2,1)S(1)}, bf16[1440,128]{1,0:T(8,128)(2,1)S(1)}, u32[]{:S(2)}, u32[]{:S(2)}) collective-permute-start(bf16[1440,128]{1,0:T(8,128)(2,1)S(1)} %get-tuple-element.40.refs_3_.refs_4_), channel_id=1, source_target_pairs={{0,24},{8,16},{16,8},{24,0},{1,25},{9,17},{17,9},{25,1},{2,26},{10... | collective-permute-start | bytes 1105928 | tf_op jit(solution)/shard_map/ppermute | solution.py:367
  25.0 1.2 %collective-permute-start.3 = (f32[16,16]{1,0:T(8,128)S(1)}, f32[16,16]{1,0:T(8,128)S(1)}, u32[]{:S(2)}, u32[]{:S(2)}) collective-permute-start(f32[16,16]{1,0:T(8,128)S(1)} %score_sums.1), channel_id=1, source_target_pairs={{0,1},{1,0},{2,3},{3,2},{4,5},{5,4},{6,7},{7,6},{8,9},{9,8},{10,11... | collective-permute-start | bytes 3080 | tf_op jit(solution)/shard_map/ppermute | solution.py:378
  26.2 3.7 %collective-permute-start.4 = (f32[16,16]{1,0:T(8,128)S(1)}, f32[16,16]{1,0:T(8,128)S(1)}, u32[]{:S(2)}, u32[]{:S(2)}) collective-permute-start(f32[16,16]{1,0:T(8,128)S(1)} %add.12), channel_id=1, source_target_pairs={{0,2},{1,3},{2,0},{3,1},{4,6},{5,7},{6,4},{7,5},{8,10},{9,11},{10,... | collective-permute-start | bytes 3080 | tf_op jit(solution)/shard_map/ppermute | solution.py:378
  29.9 4.5 %collective-permute-start.5 = (f32[16,16]{1,0:T(8,128)S(1)}, f32[16,16]{1,0:T(8,128)S(1)}, u32[]{:S(2)}, u32[]{:S(2)}) collective-permute-start(f32[16,16]{1,0:T(8,128)S(1)} %add.13.a_ref), channel_id=1, source_target_pairs={{0,4},{1,5},{2,6},{3,7},{4,0},{5,1},{6,2},{7,3},{8,12},{9,13},{10,... | collective-permute-start | bytes 3080 | tf_op jit(solution)/shard_map/ppermute | solution.py:468
  34.4 5.6 %collective-permute-start.9 = (f32[16,16]{1,0:T(8,128)S(1)}, f32[16,16]{1,0:T(8,128)S(1)}, u32[]{:S(2)}, u32[]{:S(2)}) collective-permute-start(f32[16,16]{1,0:T(8,128)S(1)} %join_sums.2.refs_8_.refs_0_), channel_id=1, source_target_pairs={{0,16},{8,24},{16,0},{24,8},{1,17},{9,25},{17,1},{25,9},{2,18},{10... | collective-permute-start | bytes 3080 | tf_op jit(solution)/shard_map/ppermute | solution.py:367
  36.3 3.7 %collective-permute-start.8 = (f32[16,16]{1,0:T(8,128)S(1)}, f32[16,16]{1,0:T(8,128)S(1)}, u32[]{:S(2)}, u32[]{:S(2)}) collective-permute-start(f32[16,16]{1,0:T(8,128)S(1)} %join_sums.2.refs_8_.refs_0_), channel_id=1, source_target_pairs={{0,8},{8,0},{16,24},{24,16},{1,9},{9,1},{17,25},{25,17},{2,10},{10... | collective-permute-start | bytes 3080 | tf_op jit(solution)/shard_map/ppermute | solution.py:367
  36.4 4.5 %collective-permute-start.7 = (f32[16,16]{1,0:T(8,128)S(1)}, f32[16,16]{1,0:T(8,128)S(1)}, u32[]{:S(2)}, u32[]{:S(2)}) collective-permute-start(f32[16,16]{1,0:T(8,128)S(1)} %join_sums.2.refs_8_.refs_0_), channel_id=1, source_target_pairs={{0,24},{8,16},{16,8},{24,0},{1,25},{9,17},{17,9},{25,1},{2,26},{10... | collective-permute-start | bytes 3080 | tf_op jit(solution)/shard_map/ppermute | solution.py:367
  42.4 12.9 %collective-permute-start.15 = (bf16[1440,128]{1,0:T(8,128)(2,1)S(1)}, bf16[1440,128]{1,0:T(8,128)(2,1)S(1)}, u32[]{:S(2)}, u32[]{:S(2)}) collective-permute-start(bf16[1440,128]{1,0:T(8,128)(2,1)S(1)} %get-tuple-element.46), channel_id=1, source_target_pairs={{0,8},{8,0},{16,24},{24,16},{1,9},{9,1},{17,25},{25,17},{2,10},{10... | collective-permute-start | bytes 1105928 | tf_op jit(solution)/shard_map/ppermute | solution.py:367
  44.4 15.5 %collective-permute-start.19 = (bf16[1440,128]{1,0:T(8,128)(2,1)S(1)}, bf16[1440,128]{1,0:T(8,128)(2,1)S(1)}, u32[]{:S(2)}, u32[]{:S(2)}) collective-permute-start(bf16[1440,128]{1,0:T(8,128)(2,1)S(1)} %get-tuple-element.47), channel_id=1, source_target_pairs={{0,16},{8,24},{16,0},{24,8},{1,17},{9,25},{17,1},{25,9},{2,18},{10... | collective-permute-start | bytes 1105928 | tf_op jit(solution)/shard_map/ppermute | solution.py:367
  44.5 15.5 %collective-permute-start.20 = (bf16[1440,128]{1,0:T(8,128)(2,1)S(1)}, bf16[1440,128]{1,0:T(8,128)(2,1)S(1)}, u32[]{:S(2)}, u32[]{:S(2)}) collective-permute-start(bf16[1440,128]{1,0:T(8,128)(2,1)S(1)} %get-tuple-element.48), channel_id=1, source_target_pairs={{0,24},{8,16},{16,8},{24,0},{1,25},{9,17},{17,9},{25,1},{2,26},{10... | collective-permute-start | bytes 1105928 | tf_op jit(solution)/shard_map/ppermute | solution.py:367
  46.0 1.2 %collective-permute-start.12 = (f32[16,16]{1,0:T(8,128)S(1)}, f32[16,16]{1,0:T(8,128)S(1)}, u32[]{:S(2)}, u32[]{:S(2)}) collective-permute-start(f32[16,16]{1,0:T(8,128)S(1)} %pair_sums.1.refs_8_), channel_id=1, source_target_pairs={{0,1},{1,0},{2,3},{3,2},{4,5},{5,4},{6,7},{7,6},{8,9},{9,8},{10,11... | collective-permute-start | bytes 3080 | tf_op jit(solution)/shard_map/ppermute | solution.py:378
  47.1 3.7 %collective-permute-start.13 = (f32[16,16]{1,0:T(8,128)S(1)}, f32[16,16]{1,0:T(8,128)S(1)}, u32[]{:S(2)}, u32[]{:S(2)}) collective-permute-start(f32[16,16]{1,0:T(8,128)S(1)} %add.14), channel_id=1, source_target_pairs={{0,2},{1,3},{2,0},{3,1},{4,6},{5,7},{6,4},{7,5},{8,10},{9,11},{10,... | collective-permute-start | bytes 3080 | tf_op jit(solution)/shard_map/ppermute | solution.py:378
  50.8 4.5 %collective-permute-start.14 = (f32[16,16]{1,0:T(8,128)S(1)}, f32[16,16]{1,0:T(8,128)S(1)}, u32[]{:S(2)}, u32[]{:S(2)}) collective-permute-start(f32[16,16]{1,0:T(8,128)S(1)} %add.15.a_ref), channel_id=1, source_target_pairs={{0,4},{1,5},{2,6},{3,7},{4,0},{5,1},{6,2},{7,3},{8,12},{9,13},{10,... | collective-permute-start | bytes 3080 | tf_op jit(solution)/shard_map/ppermute | solution.py:468
  55.3 4.7 %collective-permute-start.18 = (f32[16,16]{1,0:T(8,128)S(1)}, f32[16,16]{1,0:T(8,128)S(1)}, u32[]{:S(2)}, u32[]{:S(2)}) collective-permute-start(f32[16,16]{1,0:T(8,128)S(1)} %join_sums.3.refs_9_.refs_10_), channel_id=1, source_target_pairs={{0,16},{8,24},{16,0},{24,8},{1,17},{9,25},{17,1},{25,9},{2,18},{10... | collective-permute-start | bytes 3080 | tf_op jit(solution)/shard_map/ppermute | solution.py:367
  56.9 3.7 %collective-permute-start.17 = (f32[16,16]{1,0:T(8,128)S(1)}, f32[16,16]{1,0:T(8,128)S(1)}, u32[]{:S(2)}, u32[]{:S(2)}) collective-permute-start(f32[16,16]{1,0:T(8,128)S(1)} %join_sums.3.refs_9_.refs_10_), channel_id=1, source_target_pairs={{0,8},{8,0},{16,24},{24,16},{1,9},{9,1},{17,25},{25,17},{2,10},{10... | collective-permute-start | bytes 3080 | tf_op jit(solution)/shard_map/ppermute | solution.py:367
  57.4 4.5 %collective-permute-start.16 = (f32[16,16]{1,0:T(8,128)S(1)}, f32[16,16]{1,0:T(8,128)S(1)}, u32[]{:S(2)}, u32[]{:S(2)}) collective-permute-start(f32[16,16]{1,0:T(8,128)S(1)} %join_sums.3.refs_9_.refs_10_), channel_id=1, source_target_pairs={{0,24},{8,16},{16,8},{24,0},{1,25},{9,17},{17,9},{25,1},{2,26},{10... | collective-permute-start | bytes 3080 | tf_op jit(solution)/shard_map/ppermute | solution.py:367
  62.9 7.8 %collective-permute-start.21 = (bf16[768,128]{1,0:T(8,128)(2,1)S(1)}, bf16[768,128]{1,0:T(8,128)(2,1)S(1)}, u32[]{:S(2)}, u32[]{:S(2)}) collective-permute-start(bf16[768,128]{1,0:T(8,128)(2,1)S(1)} %get-tuple-element.49), channel_id=1, source_target_pairs={{0,8},{8,0},{16,24},{24,16},{1,9},{9,1},{17,25},{25,17},{2,10},{10... | collective-permute-start | bytes 589832 | tf_op jit(solution)/shard_map/ppermute | solution.py:367
  64.4 12.0 %collective-permute-start.22 = (bf16[768,128]{1,0:T(8,128)(2,1)S(1)}, bf16[768,128]{1,0:T(8,128)(2,1)S(1)}, u32[]{:S(2)}, u32[]{:S(2)}) collective-permute-start(bf16[768,128]{1,0:T(8,128)(2,1)S(1)} %get-tuple-element.52), channel_id=1, source_target_pairs={{0,16},{8,24},{16,0},{24,8},{1,17},{9,25},{17,1},{25,9},{2,18},{10... | collective-permute-start | bytes 589832 | tf_op jit(solution)/shard_map/ppermute | solution.py:367
  64.9 11.5 %collective-permute-start.23 = (bf16[768,128]{1,0:T(8,128)(2,1)S(1)}, bf16[768,128]{1,0:T(8,128)(2,1)S(1)}, u32[]{:S(2)}, u32[]{:S(2)}) collective-permute-start(bf16[768,128]{1,0:T(8,128)(2,1)S(1)} %get-tuple-element.53), channel_id=1, source_target_pairs={{0,24},{8,16},{16,8},{24,0},{1,25},{9,17},{17,9},{25,1},{2,26},{10... | collective-permute-start | bytes 589832 | tf_op jit(solution)/shard_map/ppermute | solution.py:367
  67.8 10.7 %collective-permute-start.24 = (bf16[672,128]{1,0:T(8,128)(2,1)S(1)}, bf16[672,128]{1,0:T(8,128)(2,1)S(1)}, u32[]{:S(2)}, u32[]{:S(2)}) collective-permute-start(bf16[672,128]{1,0:T(8,128)(2,1)S(1)} %get-tuple-element.57), channel_id=1, source_target_pairs={{0,8},{8,0},{16,24},{24,16},{1,9},{9,1},{17,25},{25,17},{2,10},{10... | collective-permute-start | bytes 516104 | tf_op jit(solution)/shard_map/ppermute | solution.py:367
  69.3 10.8 %collective-permute-start.25 = (bf16[672,128]{1,0:T(8,128)(2,1)S(1)}, bf16[672,128]{1,0:T(8,128)(2,1)S(1)}, u32[]{:S(2)}, u32[]{:S(2)}) collective-permute-start(bf16[672,128]{1,0:T(8,128)(2,1)S(1)} %get-tuple-element.58), channel_id=1, source_target_pairs={{0,16},{8,24},{16,0},{24,8},{1,17},{9,25},{17,1},{25,9},{2,18},{10... | collective-permute-start | bytes 516104 | tf_op jit(solution)/shard_map/ppermute | solution.py:367
  70.7 9.5 %collective-permute-start.26 = (bf16[672,128]{1,0:T(8,128)(2,1)S(1)}, bf16[672,128]{1,0:T(8,128)(2,1)S(1)}, u32[]{:S(2)}, u32[]{:S(2)}) collective-permute-start(bf16[672,128]{1,0:T(8,128)(2,1)S(1)} %get-tuple-element.59), channel_id=1, source_target_pairs={{0,24},{8,16},{16,8},{24,0},{1,25},{9,17},{17,9},{25,1},{2,26},{10... | collective-permute-start | bytes 516104 | tf_op jit(solution)/shard_map/ppermute | solution.py:367
  (1 other events, 0.7 us)

commit v8 on v7

--- a/solution.py
+++ b/solution.py
@@ -252,9 +252,10 @@
     picks = member_of_row(me, rows, channels, members, group).astype(jnp.bfloat16)
     weights = softmax(total * scale)
     high, low = two_parts(spread(weights, picks) * ov_ref[...])
+    both = jnp.concatenate([high, low], axis=1)
     for tiles in tile_groups(0, main, half):
         e = gather_tiles(fields, tiles, per, main)
-        value = mm(high, e, ((1,), (0,))) + mm(low, e, ((1,), (0,)))
+        value = mm(both, jnp.concatenate([e, e], axis=0), ((1,), (0,)))
         store_tiles(outs, value, tiles, per, 0, main)
 
 

time: 81.5 us -> 81.4 us (level)
  no operation moved by 1% of the time
where the time goes in v8:
time: 81.4 us; the launch traced here: 81.2 us
  starting transfers between devices  34.2 us (42%)
  waiting for transfers between devices  27.5 us (34%)
  Pallas kernels  15.3 us (19%)
  local copies, waits for them, and re-layouts  3.43 us (4%)
    ppermute x21, starting transfers between devices, swap(): return lax.ppermute(value, 'mem', [(i, i ^ step) for i in range(count)])  25.9 us
    ppermute x21, waiting for transfers between devices, swap(): return lax.ppermute(value, 'mem', [(i, i ^ step) for i in range(count)])  17 us
    ppermute x4, waiting for transfers between devices, sum_steps(): lax.ppermute(value, name, [(i, i ^ step) for i in range(size)])  6.52 us
    pallas_call x3, Pallas kernels, finish(): pl.pallas_call(functools.partial(finish_kernel, me_of, count, main, per,...  5.38 us
    ppermute x2, starting transfers between devices, join(): other = lax.ppermute(value, name, [(i, i ^ step) for i in range(size)])  5.16 us
    ppermute x2, waiting for transfers between devices, join(): other = lax.ppermute(value, name, [(i, i ^ step) for i in range(size)])  3.93 us
    unnamed x12, local copies, waits for them, and re-layouts  3.43 us
    ppermute x4, starting transfers between devices, sum_steps(): lax.ppermute(value, name, [(i, i ^ step) for i in range(size)])  3.14 us
  transfers between devices with their start and end apart: 27, of which 18 were waited for; matrix products, arithmetic and copies ran while one was open for 0% of the time, Pallas kernels for 13%

profile of v8, /device:TPU:0, one launch (start us, length us, event | category | flops | bytes accessed | tf_op | source)
XLA Modules:
  0.0 81.2 jit_solution(8198106735687011597)
XLA Ops:
  0.6 1.5 %split_fields_near.1 = (bf16[1440,128]{1,0:T(8,128)(2,1)S(1)}, bf16[1440,128]{1,0:T(8,128)(2,1)S(1)}) custom-call(bf16[64,11520]{1,0:T(8,128)(2,1)} %bitcast.4), custom_call_target="tpu_custom_call" | custom-call | tf_op jit(solution)/shard_map/split_fields_near/pallas_call | solution.py:436
  2.1 3.0 %collective-permute-start = (bf16[1440,128]{1,0:T(8,128)(2,1)S(1)}, bf16[1440,128]{1,0:T(8,128)(2,1)S(1)}, u32[]{:S(2)}, u32[]{:S(2)}) collective-permute-start(bf16[1440,128]{1,0:T(8,128)(2,1)S(1)} %get-tuple-element.33.rest_0_.refs_2_), channel_id=1, source_target_pairs={{0,8},{8,0},{16,24},{24,16},{1,9},{9,1},{17,25},{25,17},{2,10},{10... | collective-permute-start | bytes 1105928 | tf_op jit(solution)/shard_map/ppermute | solution.py:368
  5.1 1.5 %collective-permute-start.1 = (bf16[1440,128]{1,0:T(8,128)(2,1)S(1)}, bf16[1440,128]{1,0:T(8,128)(2,1)S(1)}, u32[]{:S(2)}, u32[]{:S(2)}) collective-permute-start(bf16[1440,128]{1,0:T(8,128)(2,1)S(1)} %get-tuple-element.35.refs_3_), channel_id=1, source_target_pairs={{0,16},{8,24},{16,0},{24,8},{1,17},{9,25},{17,1},{25,9},{2,18},{10... | collective-permute-start | bytes 1105928 | tf_op jit(solution)/shard_map/ppermute | solution.py:368
  11.7 2.9 %collective-permute-done.refs_1_.rest_0_.refs_5_.refs_2_.refs_3_ = bf16[1440,128]{1,0:T(8,128)(2,1)S(1)} collective-permute-done((bf16[1440,128]{1,0:T(8,128)(2,1)S(1)}, bf16[1440,128]{1,0:T(8,128)(2,1)S(1)}, u32[]{:S(2)}, u32[]{:S(2)}) %collective-permute-start) | collective-permute-done | bytes 368672 | tf_op jit(solution)/shard_map/ppermute | solution.py:368
  14.9 2.1 %collective-permute-start.6 = (bf16[1440,128]{1,0:T(8,128)(2,1)S(1)}, bf16[1440,128]{1,0:T(8,128)(2,1)S(1)}, u32[]{:S(2)}, u32[]{:S(2)}) collective-permute-start(bf16[1440,128]{1,0:T(8,128)(2,1)S(1)} %get-tuple-element.37.refs_1_.refs_2_), channel_id=1, source_target_pairs={{0,8},{8,0},{16,24},{24,16},{1,9},{9,1},{17,25},{25,17},{2,10},{10... | collective-permute-start | bytes 1105928 | tf_op jit(solution)/shard_map/ppermute | solution.py:368
  17.0 1.5 %collective-permute-start.10 = (bf16[1440,128]{1,0:T(8,128)(2,1)S(1)}, bf16[1440,128]{1,0:T(8,128)(2,1)S(1)}, u32[]{:S(2)}, u32[]{:S(2)}) collective-permute-start(bf16[1440,128]{1,0:T(8,128)(2,1)S(1)} %get-tuple-element.39.refs_2_.refs_3_), channel_id=1, source_target_pairs={{0,16},{8,24},{16,0},{24,8},{1,17},{9,25},{17,1},{25,9},{2,18},{10... | collective-permute-start | bytes 1105928 | tf_op jit(solution)/shard_map/ppermute | solution.py:368
  18.5 4.9 %collective-permute-done.1.refs_2_.refs_6_.refs_3_.refs_4_ = bf16[1440,128]{1,0:T(8,128)(2,1)S(1)} collective-permute-done((bf16[1440,128]{1,0:T(8,128)(2,1)S(1)}, bf16[1440,128]{1,0:T(8,128)(2,1)S(1)}, u32[]{:S(2)}, u32[]{:S(2)}) %collective-permute-start.1) | collective-permute-done | bytes 368672 | tf_op jit(solution)/shard_map/ppermute | solution.py:368
  26.2 1.6 %collective-permute-start.4 = (f32[16,16]{1,0:T(8,128)S(1)}, f32[16,16]{1,0:T(8,128)S(1)}, u32[]{:S(2)}, u32[]{:S(2)}) collective-permute-start(f32[16,16]{1,0:T(8,128)S(1)} %add.12), channel_id=1, source_target_pairs={{0,2},{1,3},{2,0},{3,1},{4,6},{5,7},{6,4},{7,5},{8,10},{9,11},{10,... | collective-permute-start | bytes 3080 | tf_op jit(solution)/shard_map/ppermute | solution.py:379
  27.8 2.1 %collective-permute-done.4 = f32[16,16]{1,0:T(8,128)S(1)} collective-permute-done((f32[16,16]{1,0:T(8,128)S(1)}, f32[16,16]{1,0:T(8,128)S(1)}, u32[]{:S(2)}, u32[]{:S(2)}) %collective-permute-start.4) | collective-permute-done | bytes 1056 | tf_op jit(solution)/shard_map/ppermute | solution.py:379
  29.9 2.6 %collective-permute-start.5 = (f32[16,16]{1,0:T(8,128)S(1)}, f32[16,16]{1,0:T(8,128)S(1)}, u32[]{:S(2)}, u32[]{:S(2)}) collective-permute-start(f32[16,16]{1,0:T(8,128)S(1)} %add.13.a_ref), channel_id=1, source_target_pairs={{0,4},{1,5},{2,6},{3,7},{4,0},{5,1},{6,2},{7,3},{8,12},{9,13},{10,... | collective-permute-start | bytes 3080 | tf_op jit(solution)/shard_map/ppermute | solution.py:469
  32.4 2.0 %collective-permute-done.5.b_ref = f32[16,16]{1,0:T(8,128)S(1)} collective-permute-done((f32[16,16]{1,0:T(8,128)S(1)}, f32[16,16]{1,0:T(8,128)S(1)}, u32[]{:S(2)}, u32[]{:S(2)}) %collective-permute-start.5) | collective-permute-done | bytes 1056 | tf_op jit(solution)/shard_map/ppermute | solution.py:469
  34.4 1.9 %collective-permute-start.9 = (f32[16,16]{1,0:T(8,128)S(1)}, f32[16,16]{1,0:T(8,128)S(1)}, u32[]{:S(2)}, u32[]{:S(2)}) collective-permute-start(f32[16,16]{1,0:T(8,128)S(1)} %join_sums.2.refs_8_.refs_0_), channel_id=1, source_target_pairs={{0,16},{8,24},{16,0},{24,8},{1,17},{9,25},{17,1},{25,9},{2,18},{10... | collective-permute-start | bytes 3080 | tf_op jit(solution)/shard_map/ppermute | solution.py:368
  36.4 1.5 %collective-permute-start.7 = (f32[16,16]{1,0:T(8,128)S(1)}, f32[16,16]{1,0:T(8,128)S(1)}, u32[]{:S(2)}, u32[]{:S(2)}) collective-permute-start(f32[16,16]{1,0:T(8,128)S(1)} %join_sums.2.refs_8_.refs_0_), channel_id=1, source_target_pairs={{0,24},{8,16},{16,8},{24,0},{1,25},{9,17},{17,9},{25,1},{2,26},{10... | collective-permute-start | bytes 3080 | tf_op jit(solution)/shard_map/ppermute | solution.py:368
  41.0 1.4 %branch.1 = (f32[16,16]{1,0:T(8,128)S(1)}, bf16[1440,128]{1,0:T(8,128)(2,1)S(1)}, bf16[1440,128]{1,0:T(8,128)(2,1)S(1)}, bf16[1440,128]{1,0:T(8,128)(2,1)S(1)}, bf16[1440,128]{1,0:T(8,128)(2,1)S(1)}) custom-call(f32[256,256]{1,0:T(8,128)S(1)} %get-tuple-element.31.tile_ref.ov_ref, f32[16,16]{1,0:T(8,128)S(1)} %join_sums.2.refs_8_.refs_0_, ...), custom_call_target="tpu_custom_call" | custom-call | flops 754974720 | bytes 2949120 | tf_op jit(solution)/shard_map/branch/pallas_call | solution.py:508
  42.4 2.0 %collective-permute-start.15 = (bf16[1440,128]{1,0:T(8,128)(2,1)S(1)}, bf16[1440,128]{1,0:T(8,128)(2,1)S(1)}, u32[]{:S(2)}, u32[]{:S(2)}) collective-permute-start(bf16[1440,128]{1,0:T(8,128)(2,1)S(1)} %get-tuple-element.46), channel_id=1, source_target_pairs={{0,8},{8,0},{16,24},{24,16},{1,9},{9,1},{17,25},{25,17},{2,10},{10... | collective-permute-start | bytes 1105928 | tf_op jit(solution)/shard_map/ppermute | solution.py:368
  44.5 1.4 %collective-permute-start.20 = (bf16[1440,128]{1,0:T(8,128)(2,1)S(1)}, bf16[1440,128]{1,0:T(8,128)(2,1)S(1)}, u32[]{:S(2)}, u32[]{:S(2)}) collective-permute-start(bf16[1440,128]{1,0:T(8,128)(2,1)S(1)} %get-tuple-element.48), channel_id=1, source_target_pairs={{0,24},{8,16},{16,8},{24,0},{1,25},{9,17},{17,9},{25,1},{2,26},{10... | collective-permute-start | bytes 1105928 | tf_op jit(solution)/shard_map/ppermute | solution.py:368
  47.1 1.6 %collective-permute-start.13 = (f32[16,16]{1,0:T(8,128)S(1)}, f32[16,16]{1,0:T(8,128)S(1)}, u32[]{:S(2)}, u32[]{:S(2)}) collective-permute-start(f32[16,16]{1,0:T(8,128)S(1)} %add.14), channel_id=1, source_target_pairs={{0,2},{1,3},{2,0},{3,1},{4,6},{5,7},{6,4},{7,5},{8,10},{9,11},{10,... | collective-permute-start | bytes 3080 | tf_op jit(solution)/shard_map/ppermute | solution.py:379
  48.7 2.1 %collective-permute-done.13 = f32[16,16]{1,0:T(8,128)S(1)} collective-permute-done((f32[16,16]{1,0:T(8,128)S(1)}, f32[16,16]{1,0:T(8,128)S(1)}, u32[]{:S(2)}, u32[]{:S(2)}) %collective-permute-start.13) | collective-permute-done | bytes 1056 | tf_op jit(solution)/shard_map/ppermute | solution.py:379
  50.8 2.6 %collective-permute-start.14 = (f32[16,16]{1,0:T(8,128)S(1)}, f32[16,16]{1,0:T(8,128)S(1)}, u32[]{:S(2)}, u32[]{:S(2)}) collective-permute-start(f32[16,16]{1,0:T(8,128)S(1)} %add.15.a_ref), channel_id=1, source_target_pairs={{0,4},{1,5},{2,6},{3,7},{4,0},{5,1},{6,2},{7,3},{8,12},{9,13},{10,... | collective-permute-start | bytes 3080 | tf_op jit(solution)/shard_map/ppermute | solution.py:469
  53.4 2.0 %collective-permute-done.14.b_ref = f32[16,16]{1,0:T(8,128)S(1)} collective-permute-done((f32[16,16]{1,0:T(8,128)S(1)}, f32[16,16]{1,0:T(8,128)S(1)}, u32[]{:S(2)}, u32[]{:S(2)}) %collective-permute-start.14) | collective-permute-done | bytes 1056 | tf_op jit(solution)/shard_map/ppermute | solution.py:469
  55.3 1.5 %collective-permute-start.18 = (f32[16,16]{1,0:T(8,128)S(1)}, f32[16,16]{1,0:T(8,128)S(1)}, u32[]{:S(2)}, u32[]{:S(2)}) collective-permute-start(f32[16,16]{1,0:T(8,128)S(1)} %join_sums.3.refs_9_.refs_10_), channel_id=1, source_target_pairs={{0,16},{8,24},{16,0},{24,8},{1,17},{9,25},{17,1},{25,9},{2,18},{10... | collective-permute-start | bytes 3080 | tf_op jit(solution)/shard_map/ppermute | solution.py:368
  57.4 1.4 %collective-permute-start.16 = (f32[16,16]{1,0:T(8,128)S(1)}, f32[16,16]{1,0:T(8,128)S(1)}, u32[]{:S(2)}, u32[]{:S(2)}) collective-permute-start(f32[16,16]{1,0:T(8,128)S(1)} %join_sums.3.refs_9_.refs_10_), channel_id=1, source_target_pairs={{0,24},{8,16},{16,8},{24,0},{1,25},{9,17},{17,9},{25,1},{2,26},{10... | collective-permute-start | bytes 3080 | tf_op jit(solution)/shard_map/ppermute | solution.py:368
  60.5 1.4 %collective-permute-done.16.refs_10_.refs_11_ = f32[16,16]{1,0:T(8,128)S(1)} collective-permute-done((f32[16,16]{1,0:T(8,128)S(1)}, f32[16,16]{1,0:T(8,128)S(1)}, u32[]{:S(2)}, u32[]{:S(2)}) %collective-permute-start.16) | collective-permute-done | bytes 1056 | tf_op jit(solution)/shard_map/ppermute | solution.py:368
  62.8 1.5 %collective-permute-start.21 = (bf16[768,128]{1,0:T(8,128)(2,1)S(1)}, bf16[768,128]{1,0:T(8,128)(2,1)S(1)}, u32[]{:S(2)}, u32[]{:S(2)}) collective-permute-start(bf16[768,128]{1,0:T(8,128)(2,1)S(1)} %get-tuple-element.49), channel_id=1, source_target_pairs={{0,8},{8,0},{16,24},{24,16},{1,9},{9,1},{17,25},{25,17},{2,10},{10... | collective-permute-start | bytes 589832 | tf_op jit(solution)/shard_map/ppermute | solution.py:368
  64.9 1.5 %collective-permute-start.23 = (bf16[768,128]{1,0:T(8,128)(2,1)S(1)}, bf16[768,128]{1,0:T(8,128)(2,1)S(1)}, u32[]{:S(2)}, u32[]{:S(2)}) collective-permute-start(bf16[768,128]{1,0:T(8,128)(2,1)S(1)} %get-tuple-element.53), channel_id=1, source_target_pairs={{0,24},{8,16},{16,8},{24,0},{1,25},{9,17},{17,9},{25,1},{2,26},{10... | collective-permute-start | bytes 589832 | tf_op jit(solution)/shard_map/ppermute | solution.py:368
  66.4 1.4 %input_gradient_b.1 = (bf16[672,128]{1,0:T(8,128)(2,1)S(1)}, bf16[672,128]{1,0:T(8,128)(2,1)S(1)}, bf16[672,128]{1,0:T(8,128)(2,1)S(1)}, bf16[672,128]{1,0:T(8,128)(2,1)S(1)}) custom-call(f32[16,16]{1,0:T(8,128)S(1)} %get-tuple-element.43.w_ref, f32[256,256]{1,0:T(8,128)S(1)} %get-tuple-element.32.tile_ref.rest_1_.qk_ref, ...), custom_call_target="tpu_custom_call" | custom-call | flops 671088640 | bytes 1966080 | tf_op jit(solution)/shard_map/input_gradient_b/pallas_call | solution.py:543
  67.8 1.6 %collective-permute-start.24 = (bf16[672,128]{1,0:T(8,128)(2,1)S(1)}, bf16[672,128]{1,0:T(8,128)(2,1)S(1)}, u32[]{:S(2)}, u32[]{:S(2)}) collective-permute-start(bf16[672,128]{1,0:T(8,128)(2,1)S(1)} %get-tuple-element.57), channel_id=1, source_target_pairs={{0,8},{8,0},{16,24},{24,16},{1,9},{9,1},{17,25},{25,17},{2,10},{10... | collective-permute-start | bytes 516104 | tf_op jit(solution)/shard_map/ppermute | solution.py:368
  70.7 1.4 %collective-permute-start.26 = (bf16[672,128]{1,0:T(8,128)(2,1)S(1)}, bf16[672,128]{1,0:T(8,128)(2,1)S(1)}, u32[]{:S(2)}, u32[]{:S(2)}) collective-permute-start(bf16[672,128]{1,0:T(8,128)(2,1)S(1)} %get-tuple-element.59), channel_id=1, source_target_pairs={{0,24},{8,16},{16,8},{24,0},{1,25},{9,17},{17,9},{25,1},{2,26},{10... | collective-permute-start | bytes 516104 | tf_op jit(solution)/shard_map/ppermute | solution.py:368
  72.1 2.4 %updated.1 = f32[64,11520]{1,0:T(8,128)} custom-call(bf16[768,128]{1,0:T(8,128)(2,1)S(1)} %collective-permute-done.21.refs_0_.refs_5_, bf16[1440,128]{1,0:T(8,128)(2,1)S(1)} %get-tuple-element.34.refs_0_.refs_4_.refs_1_.refs_2_, bf16[1440,128]{1,0:T(8,128)(2,1)S(1)} %get-tuple-element.33.rest_0_.refs_2_, bf16[1440,128]{1,0:T(8,128)(2,1)S(1)} %get-tuple-element.35.refs_3_, ...), custom_call_target="tpu_custom_call" | custom-call | flops 737280 | bytes 5898240 | tf_op jit(solution)/shard_map/updated/pallas_call | solution.py:564
  74.5 1.9 %collective-permute-done.22.refs_6_ = bf16[768,128]{1,0:T(8,128)(2,1)S(1)} collective-permute-done((bf16[768,128]{1,0:T(8,128)(2,1)S(1)}, bf16[768,128]{1,0:T(8,128)(2,1)S(1)}, u32[]{:S(2)}, u32[]{:S(2)}) %collective-permute-start.22) | collective-permute-done | bytes 196640 | tf_op jit(solution)/shard_map/ppermute | solution.py:368
  76.5 2.0 %ensemble_grad_early.1.refs_0_ = f32[64,11520]{1,0:T(8,128)} custom-call(bf16[1440,128]{1,0:T(8,128)(2,1)S(1)} %get-tuple-element.38.refs_4_.refs_0_.refs_5_.refs_6_.refs_1_, bf16[1440,128]{1,0:T(8,128)(2,1)S(1)} %get-tuple-element.37.refs_1_.refs_2_, bf16[1440,128]{1,0:T(8,128)(2,1)S(1)} %get-tuple-element.39.refs_2_.refs_3_, ...), custom_call_target="tpu_custom_call" | custom-call | flops 737280 | bytes 5898240 | tf_op jit(solution)/shard_map/ensemble_grad_early/pallas_call | solution.py:564
  78.4 1.7 %collective-permute-done.25.refs_7_ = bf16[672,128]{1,0:T(8,128)(2,1)S(1)} collective-permute-done((bf16[672,128]{1,0:T(8,128)(2,1)S(1)}, bf16[672,128]{1,0:T(8,128)(2,1)S(1)}, u32[]{:S(2)}, u32[]{:S(2)}) %collective-permute-start.25) | collective-permute-done | bytes 172064 | tf_op jit(solution)/shard_map/ppermute | solution.py:368
  (53 shorter events, 18.5 us)
Async XLA Ops:
  0.6 7.6 %copy-start.2 = (bf16[16,16]{1,0:T(8,128)(2,1)S(1)}, bf16[16,16]{1,0:T(8,128)(2,1)}, u32[]{:S(2)}) copy-start(bf16[16,16]{1,0:T(8,128)(2,1)} %wq_ref.1) | copy-start | bytes 1540
  0.6 13.9 %copy-start.1 = (bf16[4,16,11520]{2,1,0:T(8,128)(2,1)S(1)}, bf16[4,16,11520]{2,1,0:T(8,128)(2,1)}, u32[]{:S(2)}) copy-start(bf16[4,16,11520]{2,1,0:T(8,128)(2,1)} %param.7) | copy-start | bytes 4423684
  2.1 12.4 %collective-permute-start = (bf16[1440,128]{1,0:T(8,128)(2,1)S(1)}, bf16[1440,128]{1,0:T(8,128)(2,1)S(1)}, u32[]{:S(2)}, u32[]{:S(2)}) collective-permute-start(bf16[1440,128]{1,0:T(8,128)(2,1)S(1)} %get-tuple-element.33.rest_0_.refs_2_), channel_id=1, source_target_pairs={{0,8},{8,0},{16,24},{24,16},{1,9},{9,1},{17,25},{25,17},{2,10},{10... | collective-permute-start | bytes 1105928 | tf_op jit(solution)/shard_map/ppermute | solution.py:368
  5.1 18.3 %collective-permute-start.1 = (bf16[1440,128]{1,0:T(8,128)(2,1)S(1)}, bf16[1440,128]{1,0:T(8,128)(2,1)S(1)}, u32[]{:S(2)}, u32[]{:S(2)}) collective-permute-start(bf16[1440,128]{1,0:T(8,128)(2,1)S(1)} %get-tuple-element.35.refs_3_), channel_id=1, source_target_pairs={{0,16},{8,24},{16,0},{24,8},{1,17},{9,25},{17,1},{25,9},{2,18},{10... | collective-permute-start | bytes 1105928 | tf_op jit(solution)/shard_map/ppermute | solution.py:368
  6.7 1.4 %copy-start = (bf16[4,16,11520]{2,1,0:T(8,128)(2,1)S(1)}, bf16[4,16,11520]{2,1,0:T(8,128)(2,1)}, u32[]{:S(2)}) copy-start(bf16[4,16,11520]{2,1,0:T(8,128)(2,1)} %param.6) | copy-start | bytes 4423684
  8.2 15.8 %collective-permute-start.2 = (bf16[1440,128]{1,0:T(8,128)(2,1)S(1)}, bf16[1440,128]{1,0:T(8,128)(2,1)S(1)}, u32[]{:S(2)}, u32[]{:S(2)}) collective-permute-start(bf16[1440,128]{1,0:T(8,128)(2,1)S(1)} %get-tuple-element.36.refs_4_), channel_id=1, source_target_pairs={{0,24},{8,16},{16,8},{24,0},{1,25},{9,17},{17,9},{25,1},{2,26},{10... | collective-permute-start | bytes 1105928 | tf_op jit(solution)/shard_map/ppermute | solution.py:368
  8.3 0.7 copy-start.3
  9.7 0.7 copy-start.5
  14.9 19.5 %collective-permute-start.6 = (bf16[1440,128]{1,0:T(8,128)(2,1)S(1)}, bf16[1440,128]{1,0:T(8,128)(2,1)S(1)}, u32[]{:S(2)}, u32[]{:S(2)}) collective-permute-start(bf16[1440,128]{1,0:T(8,128)(2,1)S(1)} %get-tuple-element.37.refs_1_.refs_2_), channel_id=1, source_target_pairs={{0,8},{8,0},{16,24},{24,16},{1,9},{9,1},{17,25},{25,17},{2,10},{10... | collective-permute-start | bytes 1105928 | tf_op jit(solution)/shard_map/ppermute | solution.py:368
  17.0 22.1 %collective-permute-start.10 = (bf16[1440,128]{1,0:T(8,128)(2,1)S(1)}, bf16[1440,128]{1,0:T(8,128)(2,1)S(1)}, u32[]{:S(2)}, u32[]{:S(2)}) collective-permute-start(bf16[1440,128]{1,0:T(8,128)(2,1)S(1)} %get-tuple-element.39.refs_2_.refs_3_), channel_id=1, source_target_pairs={{0,16},{8,24},{16,0},{24,8},{1,17},{9,25},{17,1},{25,9},{2,18},{10... | collective-permute-start | bytes 1105928 | tf_op jit(solution)/shard_map/ppermute | solution.py:368
  18.5 20.5 %collective-permute-start.11 = (bf16[1440,128]{1,0:T(8,128)(2,1)S(1)}, bf16[1440,128]{1,0:T(8,128)(2,1)S(1)}, u32[]{:S(2)}, u32[]{:S(2)}) collective-permute-start(bf16[1440,128]{1,0:T(8,128)(2,1)S(1)} %get-tuple-element.40.refs_3_.refs_4_), channel_id=1, source_target_pairs={{0,24},{8,16},{16,8},{24,0},{1,25},{9,17},{17,9},{25,1},{2,26},{10... | collective-permute-start | bytes 1105928 | tf_op jit(solution)/shard_map/ppermute | solution.py:368
  25.0 1.2 %collective-permute-start.3 = (f32[16,16]{1,0:T(8,128)S(1)}, f32[16,16]{1,0:T(8,128)S(1)}, u32[]{:S(2)}, u32[]{:S(2)}) collective-permute-start(f32[16,16]{1,0:T(8,128)S(1)} %score_sums.1), channel_id=1, source_target_pairs={{0,1},{1,0},{2,3},{3,2},{4,5},{5,4},{6,7},{7,6},{8,9},{9,8},{10,11... | collective-permute-start | bytes 3080 | tf_op jit(solution)/shard_map/ppermute | solution.py:379
  26.2 3.7 %collective-permute-start.4 = (f32[16,16]{1,0:T(8,128)S(1)}, f32[16,16]{1,0:T(8,128)S(1)}, u32[]{:S(2)}, u32[]{:S(2)}) collective-permute-start(f32[16,16]{1,0:T(8,128)S(1)} %add.12), channel_id=1, source_target_pairs={{0,2},{1,3},{2,0},{3,1},{4,6},{5,7},{6,4},{7,5},{8,10},{9,11},{10,... | collective-permute-start | bytes 3080 | tf_op jit(solution)/shard_map/ppermute | solution.py:379
  29.9 4.5 %collective-permute-start.5 = (f32[16,16]{1,0:T(8,128)S(1)}, f32[16,16]{1,0:T(8,128)S(1)}, u32[]{:S(2)}, u32[]{:S(2)}) collective-permute-start(f32[16,16]{1,0:T(8,128)S(1)} %add.13.a_ref), channel_id=1, source_target_pairs={{0,4},{1,5},{2,6},{3,7},{4,0},{5,1},{6,2},{7,3},{8,12},{9,13},{10,... | collective-permute-start | bytes 3080 | tf_op jit(solution)/shard_map/ppermute | solution.py:469
  34.4 5.6 %collective-permute-start.9 = (f32[16,16]{1,0:T(8,128)S(1)}, f32[16,16]{1,0:T(8,128)S(1)}, u32[]{:S(2)}, u32[]{:S(2)}) collective-permute-start(f32[16,16]{1,0:T(8,128)S(1)} %join_sums.2.refs_8_.refs_0_), channel_id=1, source_target_pairs={{0,16},{8,24},{16,0},{24,8},{1,17},{9,25},{17,1},{25,9},{2,18},{10... | collective-permute-start | bytes 3080 | tf_op jit(solution)/shard_map/ppermute | solution.py:368
  36.3 3.7 %collective-permute-start.8 = (f32[16,16]{1,0:T(8,128)S(1)}, f32[16,16]{1,0:T(8,128)S(1)}, u32[]{:S(2)}, u32[]{:S(2)}) collective-permute-start(f32[16,16]{1,0:T(8,128)S(1)} %join_sums.2.refs_8_.refs_0_), channel_id=1, source_target_pairs={{0,8},{8,0},{16,24},{24,16},{1,9},{9,1},{17,25},{25,17},{2,10},{10... | collective-permute-start | bytes 3080 | tf_op jit(solution)/shard_map/ppermute | solution.py:368
  36.4 4.5 %collective-permute-start.7 = (f32[16,16]{1,0:T(8,128)S(1)}, f32[16,16]{1,0:T(8,128)S(1)}, u32[]{:S(2)}, u32[]{:S(2)}) collective-permute-start(f32[16,16]{1,0:T(8,128)S(1)} %join_sums.2.refs_8_.refs_0_), channel_id=1, source_target_pairs={{0,24},{8,16},{16,8},{24,0},{1,25},{9,17},{17,9},{25,1},{2,26},{10... | collective-permute-start | bytes 3080 | tf_op jit(solution)/shard_map/ppermute | solution.py:368
  42.4 12.9 %collective-permute-start.15 = (bf16[1440,128]{1,0:T(8,128)(2,1)S(1)}, bf16[1440,128]{1,0:T(8,128)(2,1)S(1)}, u32[]{:S(2)}, u32[]{:S(2)}) collective-permute-start(bf16[1440,128]{1,0:T(8,128)(2,1)S(1)} %get-tuple-element.46), channel_id=1, source_target_pairs={{0,8},{8,0},{16,24},{24,16},{1,9},{9,1},{17,25},{25,17},{2,10},{10... | collective-permute-start | bytes 1105928 | tf_op jit(solution)/shard_map/ppermute | solution.py:368
  44.4 15.5 %collective-permute-start.19 = (bf16[1440,128]{1,0:T(8,128)(2,1)S(1)}, bf16[1440,128]{1,0:T(8,128)(2,1)S(1)}, u32[]{:S(2)}, u32[]{:S(2)}) collective-permute-start(bf16[1440,128]{1,0:T(8,128)(2,1)S(1)} %get-tuple-element.47), channel_id=1, source_target_pairs={{0,16},{8,24},{16,0},{24,8},{1,17},{9,25},{17,1},{25,9},{2,18},{10... | collective-permute-start | bytes 1105928 | tf_op jit(solution)/shard_map/ppermute | solution.py:368
  44.5 15.4 %collective-permute-start.20 = (bf16[1440,128]{1,0:T(8,128)(2,1)S(1)}, bf16[1440,128]{1,0:T(8,128)(2,1)S(1)}, u32[]{:S(2)}, u32[]{:S(2)}) collective-permute-start(bf16[1440,128]{1,0:T(8,128)(2,1)S(1)} %get-tuple-element.48), channel_id=1, source_target_pairs={{0,24},{8,16},{16,8},{24,0},{1,25},{9,17},{17,9},{25,1},{2,26},{10... | collective-permute-start | bytes 1105928 | tf_op jit(solution)/shard_map/ppermute | solution.py:368
  46.0 1.2 %collective-permute-start.12 = (f32[16,16]{1,0:T(8,128)S(1)}, f32[16,16]{1,0:T(8,128)S(1)}, u32[]{:S(2)}, u32[]{:S(2)}) collective-permute-start(f32[16,16]{1,0:T(8,128)S(1)} %pair_sums.1.refs_8_), channel_id=1, source_target_pairs={{0,1},{1,0},{2,3},{3,2},{4,5},{5,4},{6,7},{7,6},{8,9},{9,8},{10,11... | collective-permute-start | bytes 3080 | tf_op jit(solution)/shard_map/ppermute | solution.py:379
  47.1 3.7 %collective-permute-start.13 = (f32[16,16]{1,0:T(8,128)S(1)}, f32[16,16]{1,0:T(8,128)S(1)}, u32[]{:S(2)}, u32[]{:S(2)}) collective-permute-start(f32[16,16]{1,0:T(8,128)S(1)} %add.14), channel_id=1, source_target_pairs={{0,2},{1,3},{2,0},{3,1},{4,6},{5,7},{6,4},{7,5},{8,10},{9,11},{10,... | collective-permute-start | bytes 3080 | tf_op jit(solution)/shard_map/ppermute | solution.py:379
  50.8 4.5 %collective-permute-start.14 = (f32[16,16]{1,0:T(8,128)S(1)}, f32[16,16]{1,0:T(8,128)S(1)}, u32[]{:S(2)}, u32[]{:S(2)}) collective-permute-start(f32[16,16]{1,0:T(8,128)S(1)} %add.15.a_ref), channel_id=1, source_target_pairs={{0,4},{1,5},{2,6},{3,7},{4,0},{5,1},{6,2},{7,3},{8,12},{9,13},{10,... | collective-permute-start | bytes 3080 | tf_op jit(solution)/shard_map/ppermute | solution.py:469
  55.3 4.7 %collective-permute-start.18 = (f32[16,16]{1,0:T(8,128)S(1)}, f32[16,16]{1,0:T(8,128)S(1)}, u32[]{:S(2)}, u32[]{:S(2)}) collective-permute-start(f32[16,16]{1,0:T(8,128)S(1)} %join_sums.3.refs_9_.refs_10_), channel_id=1, source_target_pairs={{0,16},{8,24},{16,0},{24,8},{1,17},{9,25},{17,1},{25,9},{2,18},{10... | collective-permute-start | bytes 3080 | tf_op jit(solution)/shard_map/ppermute | solution.py:368
  56.8 3.7 %collective-permute-start.17 = (f32[16,16]{1,0:T(8,128)S(1)}, f32[16,16]{1,0:T(8,128)S(1)}, u32[]{:S(2)}, u32[]{:S(2)}) collective-permute-start(f32[16,16]{1,0:T(8,128)S(1)} %join_sums.3.refs_9_.refs_10_), channel_id=1, source_target_pairs={{0,8},{8,0},{16,24},{24,16},{1,9},{9,1},{17,25},{25,17},{2,10},{10... | collective-permute-start | bytes 3080 | tf_op jit(solution)/shard_map/ppermute | solution.py:368
  57.4 4.5 %collective-permute-start.16 = (f32[16,16]{1,0:T(8,128)S(1)}, f32[16,16]{1,0:T(8,128)S(1)}, u32[]{:S(2)}, u32[]{:S(2)}) collective-permute-start(f32[16,16]{1,0:T(8,128)S(1)} %join_sums.3.refs_9_.refs_10_), channel_id=1, source_target_pairs={{0,24},{8,16},{16,8},{24,0},{1,25},{9,17},{17,9},{25,1},{2,26},{10... | collective-permute-start | bytes 3080 | tf_op jit(solution)/shard_map/ppermute | solution.py:368
  62.8 7.8 %collective-permute-start.21 = (bf16[768,128]{1,0:T(8,128)(2,1)S(1)}, bf16[768,128]{1,0:T(8,128)(2,1)S(1)}, u32[]{:S(2)}, u32[]{:S(2)}) collective-permute-start(bf16[768,128]{1,0:T(8,128)(2,1)S(1)} %get-tuple-element.49), channel_id=1, source_target_pairs={{0,8},{8,0},{16,24},{24,16},{1,9},{9,1},{17,25},{25,17},{2,10},{10... | collective-permute-start | bytes 589832 | tf_op jit(solution)/shard_map/ppermute | solution.py:368
  64.4 12.1 %collective-permute-start.22 = (bf16[768,128]{1,0:T(8,128)(2,1)S(1)}, bf16[768,128]{1,0:T(8,128)(2,1)S(1)}, u32[]{:S(2)}, u32[]{:S(2)}) collective-permute-start(bf16[768,128]{1,0:T(8,128)(2,1)S(1)} %get-tuple-element.52), channel_id=1, source_target_pairs={{0,16},{8,24},{16,0},{24,8},{1,17},{9,25},{17,1},{25,9},{2,18},{10... | collective-permute-start | bytes 589832 | tf_op jit(solution)/shard_map/ppermute | solution.py:368
  64.9 11.5 %collective-permute-start.23 = (bf16[768,128]{1,0:T(8,128)(2,1)S(1)}, bf16[768,128]{1,0:T(8,128)(2,1)S(1)}, u32[]{:S(2)}, u32[]{:S(2)}) collective-permute-start(bf16[768,128]{1,0:T(8,128)(2,1)S(1)} %get-tuple-element.53), channel_id=1, source_target_pairs={{0,24},{8,16},{16,8},{24,0},{1,25},{9,17},{17,9},{25,1},{2,26},{10... | collective-permute-start | bytes 589832 | tf_op jit(solution)/shard_map/ppermute | solution.py:368
  67.8 10.7 %collective-permute-start.24 = (bf16[672,128]{1,0:T(8,128)(2,1)S(1)}, bf16[672,128]{1,0:T(8,128)(2,1)S(1)}, u32[]{:S(2)}, u32[]{:S(2)}) collective-permute-start(bf16[672,128]{1,0:T(8,128)(2,1)S(1)} %get-tuple-element.57), channel_id=1, source_target_pairs={{0,8},{8,0},{16,24},{24,16},{1,9},{9,1},{17,25},{25,17},{2,10},{10... | collective-permute-start | bytes 516104 | tf_op jit(solution)/shard_map/ppermute | solution.py:368
  69.3 10.8 %collective-permute-start.25 = (bf16[672,128]{1,0:T(8,128)(2,1)S(1)}, bf16[672,128]{1,0:T(8,128)(2,1)S(1)}, u32[]{:S(2)}, u32[]{:S(2)}) collective-permute-start(bf16[672,128]{1,0:T(8,128)(2,1)S(1)} %get-tuple-element.58), channel_id=1, source_target_pairs={{0,16},{8,24},{16,0},{24,8},{1,17},{9,25},{17,1},{25,9},{2,18},{10... | collective-permute-start | bytes 516104 | tf_op jit(solution)/shard_map/ppermute | solution.py:368
  70.7 9.5 %collective-permute-start.26 = (bf16[672,128]{1,0:T(8,128)(2,1)S(1)}, bf16[672,128]{1,0:T(8,128)(2,1)S(1)}, u32[]{:S(2)}, u32[]{:S(2)}) collective-permute-start(bf16[672,128]{1,0:T(8,128)(2,1)S(1)} %get-tuple-element.59), channel_id=1, source_target_pairs={{0,24},{8,16},{16,8},{24,0},{1,25},{9,17},{17,9},{25,1},{2,26},{10... | collective-permute-start | bytes 516104 | tf_op jit(solution)/shard_map/ppermute | solution.py:368
  (1 other events, 0.7 us)
